TPU v7x, 32 devices: a whole 2x2x4 slice. The times are simulated.
32 devices in a mesh: replica: 4 (over z), fsdp: 8 (over y, x, core).
Axes of the slice: x: 2, y: 2, z: 4, core: 2. Of those that a mesh axis runs over, the one named last changes fastest.
Arguments:
- tokens_in: bfloat16 [16384, 1024], P(('replica', 'fsdp')), may hold values from -6 to 6
- cotangent: bfloat16 [16384, 1024], P(('replica', 'fsdp')), may hold values from -6 to 6
- document_lengths: int32 [32, 4], P(('replica', 'fsdp')), may hold values from 4 to 256, as said below
- expert_choice: int32 [16384, 8], P(('replica', 'fsdp')), may hold values from 0 to 15, all different within a row; in each aligned block of 512 rows (0 to 511, 512 to 1023, ...) at most 384 rows name the same one
- norm_gains: float32 [2, 1024], P(None, 'fsdp'), may hold values from 0.5 to 1.5
- gains_first: float32 [2, 1024], P(None, 'fsdp'), may hold values from -128 to 128
- gains_second: float32 [2, 1024], P(None, 'fsdp'), may hold values from 2621.44 to 10321.92
- query_weight: float32 [1024, 1024], P('fsdp'), may hold values from -0.1875 to 0.1875
- query_first: float32 [1024, 1024], P('fsdp'), may hold values from -80 to 80
- query_second: float32 [1024, 1024], P('fsdp'), may hold values from 868.352 to 3440.64
- keyvalue_weight: float32 [2, 1024, 512], P(None, 'fsdp'), may hold values from -0.1875 to 0.1875
- keyvalue_first_moment: float32 [2, 1024, 512], P(None, 'fsdp'), may hold values from -128 to 128
- keyvalue_second_moment: float32 [2, 1024, 512], P(None, 'fsdp'), may hold values from 1720.32 to 6881.28
- output_weight: float32 [1024, 1024], P('fsdp'), may hold values from -0.75 to 0.75
- output_first: float32 [1024, 1024], P('fsdp'), may hold values from -20 to 20
- output_second: float32 [1024, 1024], P('fsdp'), may hold values from 52.4288 to 206.4384
- router_weight: float32 [1024, 16], P('fsdp'), may hold values from -0.09375 to 0.09375
- router_first: float32 [1024, 16], P('fsdp'), may hold values from -640 to 640
- router_second: float32 [1024, 16], P('fsdp'), may hold values from 42598.4 to 172032
- gateup_weight: float32 [16, 2, 1024, 512], P(None, None, 'fsdp'), may hold values from -0.1875 to 0.1875
- gateup_first: float32 [16, 2, 1024, 512], P(None, None, 'fsdp'), may hold values from -28 to 28
- gateup_second: float32 [16, 2, 1024, 512], P(None, None, 'fsdp'), may hold values from 103.2192 to 409.6
- down_weight: float32 [16, 512, 1024], P(None, None, 'fsdp'), may hold values from -1 to 1
- down_first: float32 [16, 512, 1024], P(None, None, 'fsdp'), may hold values from -4 to 4
- down_second: float32 [16, 512, 1024], P(None, None, 'fsdp'), may hold values from 2.12992 to 8.68352
Outputs:
- block_output: bfloat16 [16384, 1024], P(('replica', 'fsdp'))
- input_gradient: float32 [16384, 1024], P(('replica', 'fsdp'))
- gains_moment: float32 [2, 1024], P(None, 'fsdp')
- gains_square: float32 [2, 1024], P(None, 'fsdp')
- gains_renewed: float32 [2, 1024], P(None, 'fsdp')
- query_moment: float32 [1024, 1024], P('fsdp')
- query_square: float32 [1024, 1024], P('fsdp')
- query_renewed: float32 [1024, 1024], P('fsdp')
- keyval_moment: float32 [2, 1024, 512], P(None, 'fsdp')
- keyval_square: float32 [2, 1024, 512], P(None, 'fsdp')
- keyval_renewed: float32 [2, 1024, 512], P(None, 'fsdp')
- output_moment: float32 [1024, 1024], P('fsdp')
- output_square: float32 [1024, 1024], P('fsdp')
- output_renewed: float32 [1024, 1024], P('fsdp')
- router_moment: float32 [1024, 16], P('fsdp')
- router_square: float32 [1024, 16], P('fsdp')
- router_renewed: float32 [1024, 16], P('fsdp')
- gateup_moment: float32 [16, 2, 1024, 512], P(None, None, 'fsdp')
- gateup_square: float32 [16, 2, 1024, 512], P(None, None, 'fsdp')
- gateup_renewed: float32 [16, 2, 1024, 512], P(None, None, 'fsdp')
- down_moment: float32 [16, 512, 1024], P(None, None, 'fsdp')
- down_square: float32 [16, 512, 1024], P(None, None, 'fsdp')
- down_renewed: float32 [16, 512, 1024], P(None, None, 'fsdp')
Inputs may be any that keep to these rules, and one draw needn't show every extreme that they name: `document_lengths`: each row holds the lengths of one device's 4 documents, packed from its first slot; one of them has exactly 256 tokens, the others 4 to 85; slots after their sum are padding. `expert_choice`: among the rows of one device no expert is named more than 384 times, and on some devices an expert is named exactly 384 times.
All inputs are finite; a program needn't handle non-finite values.
Results may differ from a plain program's by a relative error of at most 0.014.
The roundings to bfloat16 on the way count: a program that leaves them out, or rounds other values in their place, can miss the bound.
Values may be sent and summed in bfloat16 or wider, within the bound.
No kernel may reach another device: no remote copies, remote signals or barrier semaphores. Data moves between devices by JAX's collectives and lax.ppermute only.
A program may use at most 320 MiB of HBM per device.

v0:
```python
import math

import jax
import jax.numpy as jnp
from jax import lax
from jax.sharding import PartitionSpec as P

MODEL_WIDTH = 1024
QUERY_HEADS = 16
KEYVALUE_HEADS = 8
HEAD_SIZE = 64
F = 512
TOPK = 8
EXPERTS = 16
ADAM_STEP = 5
CAP = 384


norm_eps = 1e-06
rope_base = 10000.0
beta_one = 0.9
beta_two = 0.95
adam_eps = 1e-08
decay_rate = 0.1
gain_rate = 0.25
masked_value = -1e30


def layout(lengths, count_of_rows):
    document_ends = jnp.cumsum(lengths)
    row_index = jnp.arange(count_of_rows, dtype=jnp.int32)
    passed = row_index[:, None] >= document_ends[None, :]
    segment = jnp.sum(passed.astype(jnp.int32), axis=1)
    start_row = jnp.sum(jnp.where(passed, lengths[None, :], 0), axis=1)
    position = (row_index - start_row).astype(jnp.float32)
    alive_mask = (segment < lengths.shape[0]).astype(jnp.float32)
    allowed = (segment[:, None] == segment[None, :]) & (row_index[None, :] <= row_index[:, None])
    return (position, alive_mask, allowed)


def rope_tables(position):
    half_width = HEAD_SIZE // 2
    exponents = jnp.arange(half_width, dtype=jnp.float32) * (2.0 / HEAD_SIZE)
    inverse = jnp.exp(exponents * -math.log(rope_base))
    angles = position[:, None] * inverse[None, :]
    return (jnp.cos(angles)[:, None, :], jnp.sin(angles)[:, None, :])


def apply_rotary(values, cosine_lookup, sine_lookup):
    half_width = values.shape[-1] // 2
    front_half = values[..., :half_width]
    back_half = values[..., half_width:]
    return jnp.concatenate(
        [
            front_half * cosine_lookup - back_half * sine_lookup,
            back_half * cosine_lookup + front_half * sine_lookup,
        ],
        axis=-1,
    )


def normalize(values):
    inverse = lax.rsqrt(jnp.mean(values * values, axis=-1, keepdims=True) + norm_eps)
    return (values * inverse, inverse)


def norm_back(upstream, scaled_rows, inverse, gain_row):
    weighted = upstream * gain_row
    gain_part = jnp.sum(upstream * scaled_rows, axis=0)
    inner = jnp.mean(weighted * scaled_rows, axis=-1, keepdims=True)
    return (inverse * (weighted - scaled_rows * inner), gain_part)


def product(left, right):
    return jnp.dot(left, right, preferred_element_type=jnp.float32)


def times_transposed(left, right):
    return lax.dot_general(
        left, right, (((1,), (1,)), ((), ())), preferred_element_type=jnp.float32
    )


def transposed_times(left, right):
    return lax.dot_general(
        left, right, (((0,), (0,)), ((), ())), preferred_element_type=jnp.float32
    )


def expert_forward(rows, gateup_full, down_full):
    gate_linear = jnp.einsum(
        "ecd,edf->ecf", rows, gateup_full[:, 0], preferred_element_type=jnp.float32
    )
    up_linear = jnp.einsum(
        "ecd,edf->ecf", rows, gateup_full[:, 1], preferred_element_type=jnp.float32
    )
    sigmoid_gate = jax.nn.sigmoid(gate_linear)
    silu_gate = gate_linear * sigmoid_gate
    activated = (silu_gate * up_linear).astype(jnp.bfloat16)
    expert_result = jnp.einsum(
        "ecf,efd->ecd", activated, down_full, preferred_element_type=jnp.float32
    )
    return ((gate_linear, up_linear, sigmoid_gate, silu_gate, activated), expert_result)


def expert_backward(rows, d_result, kept, gateup_full, down_full):
    gate_linear, up_linear, sigmoid_gate, silu_gate, activated = kept
    down_grad = jnp.einsum("ecf,ecd->efd", activated, d_result, preferred_element_type=jnp.float32)
    d_activated = jnp.einsum(
        "ecd,efd->ecf", d_result, down_full, preferred_element_type=jnp.float32
    )
    d_gate_linear = (
        d_activated * up_linear * sigmoid_gate * (1.0 + gate_linear * (1.0 - sigmoid_gate))
    ).astype(jnp.bfloat16)
    d_up_linear = (d_activated * silu_gate).astype(jnp.bfloat16)
    gateup_grad = jnp.stack(
        [
            jnp.einsum("ecd,ecf->edf", rows, d_gate_linear, preferred_element_type=jnp.float32),
            jnp.einsum("ecd,ecf->edf", rows, d_up_linear, preferred_element_type=jnp.float32),
        ],
        axis=1,
    )
    d_rows = jnp.einsum(
        "ecf,edf->ecd", d_gate_linear, gateup_full[:, 0], preferred_element_type=jnp.float32
    ) + jnp.einsum(
        "ecf,edf->ecd", d_up_linear, gateup_full[:, 1], preferred_element_type=jnp.float32
    )
    return (gateup_grad, down_grad, d_rows)


def adamw_step(weight, moment_old, square_old, gradient, step_rate, shrink):
    moment = beta_one * moment_old + (1.0 - beta_one) * gradient
    square = beta_two * square_old + (1.0 - beta_two) * gradient * gradient
    moment_hat = moment / (1.0 - beta_one**ADAM_STEP)
    square_hat = square / (1.0 - beta_two**ADAM_STEP)
    renewed = weight - step_rate * (
        moment_hat / (jnp.sqrt(square_hat) + adam_eps) + shrink * weight
    )
    return (moment, square, renewed)


def body(
    tokens_in,
    cotangent,
    document_lengths,
    expert_choice,
    norm_gains,
    gains_first,
    gains_second,
    query_weight,
    query_first,
    query_second,
    keyvalue_weight,
    keyvalue_first_moment,
    keyvalue_second_moment,
    output_weight,
    output_first,
    output_second,
    router_weight,
    router_first,
    router_second,
    gateup_weight,
    gateup_first,
    gateup_second,
    down_weight,
    down_first,
    down_second,
):
    brain_floating = jnp.bfloat16
    count_of_rows = tokens_in.shape[0]
    heads_per_group = QUERY_HEADS // KEYVALUE_HEADS
    score_scale = HEAD_SIZE ** (-0.5)
    attention_shards = (
        norm_gains.astype(brain_floating),
        query_weight.astype(brain_floating),
        keyvalue_weight.astype(brain_floating),
        output_weight.astype(brain_floating),
        router_weight.astype(brain_floating),
    )
    expert_shards = (gateup_weight.astype(brain_floating), down_weight.astype(brain_floating))
    gains_full, query_full, keyval_full, output_full, router_full = (
        lax.all_gather(attention_shards[0], "fsdp", axis=1, tiled=True),
        lax.all_gather(attention_shards[1], "fsdp", axis=0, tiled=True),
        lax.all_gather(attention_shards[2], "fsdp", axis=1, tiled=True),
        lax.all_gather(attention_shards[3], "fsdp", axis=0, tiled=True),
        lax.all_gather(attention_shards[4], "fsdp", axis=0, tiled=True),
    )
    gains_value = gains_full.astype(jnp.float32)
    position, alive_mask, allowed = layout(document_lengths[0], count_of_rows)
    cosine_lookup, sine_lookup = rope_tables(position)
    alive_rows = alive_mask[:, None]
    inputs = tokens_in.astype(jnp.float32)
    scaled_one, inverse_one = normalize(inputs)
    normed = (scaled_one * gains_value[0]).astype(brain_floating)
    query_projected = product(normed, query_full)
    key_projected = product(normed, keyval_full[0])
    value_projected = product(normed, keyval_full[1])
    query_rows = (
        apply_rotary(
            query_projected.reshape(count_of_rows, QUERY_HEADS, HEAD_SIZE),
            cosine_lookup,
            sine_lookup,
        )
        .astype(brain_floating)
        .reshape(count_of_rows, KEYVALUE_HEADS, heads_per_group, HEAD_SIZE)
    )
    rows_of_keys = apply_rotary(
        key_projected.reshape(count_of_rows, KEYVALUE_HEADS, HEAD_SIZE), cosine_lookup, sine_lookup
    ).astype(brain_floating)
    rows_of_values = value_projected.reshape(count_of_rows, KEYVALUE_HEADS, HEAD_SIZE).astype(
        brain_floating
    )

    def score_block():
        raw_scores = (
            jnp.einsum(
                "qhgd,khd->hgqk", query_rows, rows_of_keys, preferred_element_type=jnp.float32
            )
            * score_scale
        )
        return jnp.where(allowed[None, None], raw_scores, masked_value)

    scores = score_block()
    row_peak = jnp.max(scores, axis=-1, keepdims=True)
    exponentials = jnp.exp(scores - row_peak)
    totals = jnp.sum(exponentials, axis=-1, keepdims=True)
    soft_weights = exponentials / totals
    log_totals = row_peak + jnp.log(totals)
    mixed_heads = (
        jnp.einsum(
            "hgqk,khd->qhgd",
            soft_weights.astype(brain_floating),
            rows_of_values,
            preferred_element_type=jnp.float32,
        )
        .reshape(count_of_rows, QUERY_HEADS * HEAD_SIZE)
        .astype(brain_floating)
    )
    attended = product(mixed_heads, output_full)
    middle = inputs + alive_rows * attended
    scaled_two, inverse_two = normalize(middle)
    normed_two = (scaled_two * gains_value[1]).astype(brain_floating)
    logits = product(normed_two, router_full)
    expert_row = jnp.arange(EXPERTS, dtype=jnp.int32)
    onehot = (expert_choice[:, :, None] == expert_row[None, None, :]).astype(jnp.float32)
    chosen = jnp.sum(onehot * logits[:, None, :], axis=-1)
    gate_weights = jax.nn.softmax(chosen, axis=-1)
    flat_expert = expert_choice.reshape(-1)
    flat_hot = (flat_expert[:, None] == expert_row[None, :]).astype(jnp.int32)
    rank_rows = jnp.cumsum(flat_hot, axis=0) - flat_hot
    slot_index = jnp.sum(rank_rows * flat_hot, axis=1)
    buffers = (
        jnp.zeros((EXPERTS, CAP, MODEL_WIDTH), brain_floating)
        .at[flat_expert, slot_index]
        .set(jnp.repeat(normed_two, TOPK, axis=0))
    )
    gateup_full, down_full = (
        lax.all_gather(expert_shards[0], "fsdp", axis=2, tiled=True),
        lax.all_gather(expert_shards[1], "fsdp", axis=2, tiled=True),
    )
    kept, expert_out = expert_forward(buffers, gateup_full, down_full)
    picked_rows = expert_out[flat_expert, slot_index].reshape(count_of_rows, TOPK, MODEL_WIDTH)
    mixture = jnp.sum(gate_weights[:, :, None] * picked_rows, axis=1)
    block_output = (middle + alive_rows * mixture).astype(brain_floating)
    upstream = cotangent.astype(jnp.float32)
    branch_back = alive_rows * upstream
    d_gate_logit = jnp.sum(picked_rows * branch_back[:, None, :], axis=-1)
    d_chosen = gate_weights * (
        d_gate_logit - jnp.sum(gate_weights * d_gate_logit, axis=-1, keepdims=True)
    )
    d_logits = jnp.sum(onehot * d_chosen[:, :, None], axis=1).astype(brain_floating)
    d_rows = (
        (gate_weights[:, :, None] * branch_back[:, None, :])
        .reshape(-1, MODEL_WIDTH)
        .astype(brain_floating)
    )
    d_expert_out = (
        jnp.zeros((EXPERTS, CAP, MODEL_WIDTH), brain_floating)
        .at[flat_expert, slot_index]
        .set(d_rows)
    )
    gains_back, query_back, keyval_back, output_back, router_back = (
        lax.all_gather(attention_shards[0], "fsdp", axis=1, tiled=True),
        lax.all_gather(attention_shards[1], "fsdp", axis=0, tiled=True),
        lax.all_gather(attention_shards[2], "fsdp", axis=1, tiled=True),
        lax.all_gather(attention_shards[3], "fsdp", axis=0, tiled=True),
        lax.all_gather(attention_shards[4], "fsdp", axis=0, tiled=True),
    )
    gateup_back, down_back = (
        lax.all_gather(expert_shards[0], "fsdp", axis=2, tiled=True),
        lax.all_gather(expert_shards[1], "fsdp", axis=2, tiled=True),
    )
    gateup_grad, down_grad, d_buffers = expert_backward(
        buffers, d_expert_out, kept, gateup_back, down_back
    )
    gateup_part, down_part = (
        lax.psum_scatter(gateup_grad, "fsdp", scatter_dimension=2, tiled=True),
        lax.psum_scatter(down_grad, "fsdp", scatter_dimension=2, tiled=True),
    )
    d_normed_two = jnp.sum(
        d_buffers[flat_expert, slot_index].reshape(count_of_rows, TOPK, MODEL_WIDTH), axis=1
    ) + times_transposed(d_logits, router_back)
    router_grad = transposed_times(normed_two, d_logits)
    gains_again = gains_back.astype(jnp.float32)
    d_middle_norm, gain_two = norm_back(d_normed_two, scaled_two, inverse_two, gains_again[1])
    d_middle = upstream + d_middle_norm
    d_attended = (alive_rows * d_middle).astype(brain_floating)
    output_grad = transposed_times(mixed_heads, d_attended)
    d_mixed = (
        times_transposed(d_attended, output_back)
        .astype(brain_floating)
        .reshape(count_of_rows, KEYVALUE_HEADS, heads_per_group, HEAD_SIZE)
    )
    scores = score_block()
    soft_again = jnp.exp(scores - log_totals)
    d_soft = jnp.einsum(
        "qhgd,khd->hgqk", d_mixed, rows_of_values, preferred_element_type=jnp.float32
    )
    d_scores = (
        soft_again * (d_soft - jnp.sum(soft_again * d_soft, axis=-1, keepdims=True))
    ).astype(brain_floating)
    d_queries = (
        jnp.einsum("hgqk,khd->qhgd", d_scores, rows_of_keys, preferred_element_type=jnp.float32)
        * score_scale
    )
    key_gradients = (
        jnp.einsum("hgqk,qhgd->khd", d_scores, query_rows, preferred_element_type=jnp.float32)
        * score_scale
    )
    value_gradients = jnp.einsum(
        "hgqk,qhgd->khd",
        soft_again.astype(brain_floating),
        d_mixed,
        preferred_element_type=jnp.float32,
    )
    d_query_linear = (
        apply_rotary(
            d_queries.reshape(count_of_rows, QUERY_HEADS, HEAD_SIZE), cosine_lookup, -sine_lookup
        )
        .reshape(count_of_rows, QUERY_HEADS * HEAD_SIZE)
        .astype(brain_floating)
    )
    d_key_linear = (
        apply_rotary(key_gradients, cosine_lookup, -sine_lookup)
        .reshape(count_of_rows, KEYVALUE_HEADS * HEAD_SIZE)
        .astype(brain_floating)
    )
    value_projection_gradient = value_gradients.reshape(
        count_of_rows, KEYVALUE_HEADS * HEAD_SIZE
    ).astype(brain_floating)
    query_grad = transposed_times(normed, d_query_linear)
    keyval_grad = jnp.stack(
        [
            transposed_times(normed, d_key_linear),
            transposed_times(normed, value_projection_gradient),
        ]
    )
    d_normed = (
        times_transposed(d_query_linear, query_back)
        + times_transposed(d_key_linear, keyval_back[0])
        + times_transposed(value_projection_gradient, keyval_back[1])
    )
    d_input_norm, gain_one = norm_back(d_normed, scaled_one, inverse_one, gains_again[0])
    input_gradient = d_middle + d_input_norm
    gains_grad = jnp.stack([gain_one, gain_two])
    gains_part, query_part, keyval_part, output_part, router_part = (
        lax.psum_scatter(gains_grad, "fsdp", scatter_dimension=1, tiled=True),
        lax.psum_scatter(query_grad, "fsdp", scatter_dimension=0, tiled=True),
        lax.psum_scatter(keyval_grad, "fsdp", scatter_dimension=1, tiled=True),
        lax.psum_scatter(output_grad, "fsdp", scatter_dimension=0, tiled=True),
        lax.psum_scatter(router_grad, "fsdp", scatter_dimension=0, tiled=True),
    )
    summed = lax.psum(
        (gains_part, query_part, keyval_part, output_part, router_part, gateup_part, down_part),
        "replica",
    )
    settings = (
        (norm_gains, gains_first, gains_second, gain_rate, 0.0),
        (query_weight, query_first, query_second, MODEL_WIDTH ** (-0.5), decay_rate),
        (
            keyvalue_weight,
            keyvalue_first_moment,
            keyvalue_second_moment,
            MODEL_WIDTH ** (-0.5),
            decay_rate,
        ),
        (
            output_weight,
            output_first,
            output_second,
            (QUERY_HEADS * HEAD_SIZE // 16) ** (-0.5),
            decay_rate,
        ),
        (router_weight, router_first, router_second, (4 * MODEL_WIDTH) ** (-0.5), decay_rate),
        (gateup_weight, gateup_first, gateup_second, MODEL_WIDTH ** (-0.5), decay_rate),
        (down_weight, down_first, down_second, (F // 16) ** (-0.5), decay_rate),
    )
    updated = []
    for gradient, setting in zip(summed, settings):
        updated.extend(
            adamw_step(setting[0], setting[1], setting[2], gradient, setting[3], setting[4])
        )
    return (block_output, input_gradient) + tuple(updated)


def solution(mesh):
    in_specs = (
        P(("replica", "fsdp"), None),
        P(("replica", "fsdp"), None),
        P(("replica", "fsdp"), None),
        P(("replica", "fsdp"), None),
        P(None, "fsdp"),
        P(None, "fsdp"),
        P(None, "fsdp"),
        P("fsdp", None),
        P("fsdp", None),
        P("fsdp", None),
        P(None, "fsdp", None),
        P(None, "fsdp", None),
        P(None, "fsdp", None),
        P("fsdp", None),
        P("fsdp", None),
        P("fsdp", None),
        P("fsdp", None),
        P("fsdp", None),
        P("fsdp", None),
        P(None, None, "fsdp", None),
        P(None, None, "fsdp", None),
        P(None, None, "fsdp", None),
        P(None, None, "fsdp"),
        P(None, None, "fsdp"),
        P(None, None, "fsdp"),
    )
    out_specs = (
        P(("replica", "fsdp"), None),
        P(("replica", "fsdp"), None),
        P(None, "fsdp"),
        P(None, "fsdp"),
        P(None, "fsdp"),
        P("fsdp", None),
        P("fsdp", None),
        P("fsdp", None),
        P(None, "fsdp", None),
        P(None, "fsdp", None),
        P(None, "fsdp", None),
        P("fsdp", None),
        P("fsdp", None),
        P("fsdp", None),
        P("fsdp", None),
        P("fsdp", None),
        P("fsdp", None),
        P(None, None, "fsdp", None),
        P(None, None, "fsdp", None),
        P(None, None, "fsdp", None),
        P(None, None, "fsdp"),
        P(None, None, "fsdp"),
        P(None, None, "fsdp"),
    )
    return jax.shard_map(body, mesh=mesh, in_specs=in_specs, out_specs=out_specs, check_vma=False)
```

profile of v0, /device:TPU:2, one launch (start us, length us, event | category | flops | bytes accessed | tf_op | source)
XLA Modules:
  0.0 2008.9 jit_solution(18135123997074087179)
XLA Ops:
  29.3 8.7 all_gather.28
  38.0 9.1 all_gather.32
  81.2 8.2 fusion.6
  90.1 9.0 fusion.41
  107.4 26.2 %scatter_custom_fusion = bf16[6144,1024]{1,0:T(8,128)(2,1)} fusion(s32[4096]{0:T(1024)} %broadcast_select_fusion, bf16[]{:T(256)} %constant.35.clone.1, bf16[512,1024]{1,0:T(8,128)(2,1)S(1)} %multiply_convert_fusion.4), kind=kCustom, calls=%fused_computation.40 | custom fusion | bytes 13632000
  133.7 27.6 %scatter_custom_fusion.1 = bf16[6144,1024]{1,0:T(8,128)(2,1)} fusion(s32[4096]{0:T(1024)} %broadcast_select_fusion, f32[512,1024]{1,0:T(8,128)S(1)} %convert_multiply_fusion.2, f32[4096]{0:T(1024)S(1)} %div.142, bf16[]{:T(256)} %constant.35.clone.1), kind=kCustom, calls=%fused_computation.39 | custom fusion | flops 8388608 | bytes 14696960
  161.3 102.4 %all-gather.12.cloned.1.call-done = bf16[16,2,1024,512]{3,2,0,1:T(8,128)(2,1)} async-done(((bf16[16,2,128,512]{3,2,0,1:T(8,128)(2,1)}), bf16[16,2,1024,512]{3,2,0,1:T(8,128)(2,1)}) %all-gather.12.cloned.1.call-update) | async-done | bytes 33554448 | tf_op jit(solution)/shard_map/all_gather | solution.py:258
  263.7 17.2 fusion.10
  280.9 17.2 fusion.8
  298.1 61.1 %all-gather.14.cloned.1.call-done = bf16[16,512,1024]{2,1,0:T(8,128)(2,1)} async-done(((bf16[16,512,128]{2,1,0:T(8,128)(2,1)}), bf16[16,512,1024]{2,1,0:T(8,128)(2,1)}) %all-gather.14.cloned.1.call-update) | async-done | bytes 16777232 | tf_op jit(solution)/shard_map/all_gather | solution.py:259
  359.1 26.2 %multiply_convert_fusion = (bf16[16,384,512]{2,1,0:T(8,128)(2,1)}, bf16[16,384,512]{2,1,0:T(8,128)(2,1)}, bf16[16,384,512]{2,1,0:T(8,128)(2,1)}) fusion(f32[16,384,512]{2,1,0:T(8,128)} %fusion.8, f32[16,384,512]{2,1,0:T(8,128)} %fusion.10, bf16[16,384,1024]{2,1,0:T(8,128)(2,1)} %bitcast.192, bf16[16,512,1024]{2,1,0:T(8,128)(2,1)} %all-gather.14.cloned.1.call-done), kind=kOutput, calls=%fused_computation.32 | convolution fusion | flops 6489636864 | bytes 73400320 | tf_op jit(solution)/shard_map/ecd,efd->ecf/dot_general | solution.py:109
  385.4 18.4 fusion.98
  403.8 80.5 %gather_fusion = f32[4096,1024]{1,0:T(8,128)} fusion(f32[16,384,1024]{2,1,0:T(8,128)} %fusion.98, s32[4096]{0:T(1024)S(1)} %bitcast.184), kind=kCustom, calls=%fused_computation | custom fusion | bytes 33587200 | tf_op jit(solution)/shard_map/gather | solution.py:262
  484.3 10.8 fusion.5
  495.4 18.2 fusion.7
  513.6 23.9 %fusion.25 = f32[16,384,1024]{2,1,0:T(8,128)} fusion(f32[16,384,1024]{2,1,0:T(8,128)} %fusion.7, bf16[16,384,512]{2,1,0:T(8,128)(2,1)} %get-tuple-element.174, bf16[16,2,1024,512]{3,2,0,1:T(8,128)(2,1)} %all-gather.12.cloned.1.call-done), kind=kOutput, calls=%fused_computation.51 | convolution fusion | flops 6448742400 | bytes 73400320 | tf_op jit(solution)/shard_map/ecf,edf->ecd/dot_general | solution.py:125
  537.5 80.3 %gather_fusion.1 = f32[4096,1024]{1,0:T(8,128)} fusion(f32[16,384,1024]{2,1,0:T(8,128)} %fusion.25, s32[4096]{0:T(1024)S(1)} %bitcast.185), kind=kCustom, calls=%fused_computation.1 | custom fusion | bytes 33587200 | tf_op jit(solution)/shard_map/gather | solution.py:301
  617.7 8.2 bitcast_reduce_fusion
  639.7 15.2 fusion
  658.5 11.0 fusion.2
  695.7 23.1 %fusion.100 = f32[16,512,1024]{2,1,0:T(8,128)} fusion(bf16[16,384,512]{2,1,0:T(8,128)(2,1)} %get-tuple-element.176, bf16[16,384,1024]{2,1,0:T(8,128)(2,1)} %bitcast.193), kind=kOutput, calls=%fused_computation.193 | convolution fusion | flops 6442450944 | bytes 52428800 | tf_op jit(solution)/shard_map/ecf,ecd->efd/dot_general | solution.py:108
  719.0 19.9 convolution_bitcast_fusion
  738.9 20.9 %convolution_bitcast_fusion.1 = f32[16,1,1024,512]{3,2,0,1:T(8,128)} fusion(bf16[16,384,1024]{2,1,0:T(8,128)(2,1)} %bitcast.191, bf16[16,384,512]{2,1,0:T(8,128)(2,1)} %get-tuple-element.175), kind=kOutput, calls=%fused_computation.30 | convolution fusion | flops 6442450944 | bytes 52428800 | tf_op jit(solution)/shard_map/ecd,ecf->edf/dot_general | solution.py:118
  759.8 43.8 %pad_maximum_fusion = f32[16,2,1024,512]{3,2,0,1:T(8,128)} fusion(f32[16,1,1024,512]{3,2,0,1:T(8,128)} %convolution_bitcast_fusion, f32[16,1,1024,512]{3,2,0,1:T(8,128)} %convolution_bitcast_fusion.1), kind=kLoop, calls=%fused_computation.4 | loop fusion | flops 16777216 | bytes 134217728 | tf_op jit(solution)/shard_map/stack | solution.py:116
  815.1 189.5 %reduce-scatter.20.cloned.1.call-done = f32[16,512,128]{2,1,0:T(8,128)} async-done(((f32[16,512,1024]{2,1,0:T(8,128)}), f32[16,512,128]{2,1,0:T(8,128)}) %reduce-scatter.20.cloned.1.call-update) | async-done | bytes 4194320 | tf_op jit(solution)/shard_map/reduce_scatter | solution.py:298
  1004.6 387.2 %reduce-scatter.18.cloned.1.call-done = f32[16,2,128,512]{3,2,0,1:T(8,128)} async-done(((f32[16,2,1024,512]{3,2,0,1:T(8,128)}), f32[16,2,128,512]{3,2,0,1:T(8,128)}) %reduce-scatter.18.cloned.1.call-update) | async-done | bytes 8388624 | tf_op jit(solution)/shard_map/reduce_scatter | solution.py:297
  1396.1 33.9 %reduce-scatter.22.cloned.1.call-done = f32[128,2]{1,0:T(8,128)} async-done(((f32[1024,2]{1,0:T(8,128)}), f32[128,2]{1,0:T(8,128)}) %reduce-scatter.22.cloned.1.call-update) | async-done | bytes 1040
  1430.9 34.0 %reduce-scatter.16.cloned.1.call-done = f32[128,16]{0,1:T(8,128)} async-done(((f32[1024,16]{0,1:T(8,128)}), f32[128,16]{0,1:T(8,128)}) %reduce-scatter.16.cloned.1.call-update) | async-done | bytes 8208 | tf_op jit(solution)/shard_map/reduce_scatter | solution.py:371
  1464.9 12.5 all-reduce
  1478.6 469.2 %all-reduce.4.cloned.1.call-done = (f32[128,1024]{1,0:T(8,128)}, f32[2,128,512]{2,1,0:T(8,128)}, f32[128,1024]{1,0:T(8,128)}, f32[16,2,128,512]{3,2,0,1:T(8,128)}, f32[16,512,128]{2,1,0:T(8,128)}) async-done(((f32[128,1024]{1,0:T(8,128)}, f32[2,128,512]{2,1,0:T(8,128)}, f32[128,1024]{1,0:T(8,128)}, f32[16,2,128,512]{3,2,0,1:T(8,128)}, f32[16,512,128]{2,1,0:T(8,128)}), (f32[128,1024]{1,0:T(8,128)}, ...) | async-done | bytes 14155792 | tf_op jit(solution)/shard_map/psum | solution.py:373
  1947.9 22.3 %multiply_subtract_fusion = (f32[16,2,128,512]{3,2,0,1:T(8,128)}, f32[16,2,128,512]{3,2,0,1:T(8,128)}, f32[16,2,128,512]{3,2,0,1:T(8,128)}) fusion(f32[16,2,128,512]{3,2,1,0:T(8,128)} %param.44, f32[16,2,128,512]{3,2,0,1:T(8,128)} %get-tuple-element.151, f32[16,2,128,512]{3,2,1,0:T(8,128)} %param.46, f32[16,2,128,512]{3,2,1,0:T(8,128)} %param.45), kind=kLoop, calls=%fused_computation.45 | loop fusion | flops 31457280 | bytes 58720256 | tf_op jit(solution)/shard_map/sub | solution.py:136
  1970.2 8.9 copy.173
  (307 shorter events, 148.6 us)
Async XLA Ops:
  7.2 45.6 %all-gather.6.cloned.1.call-start = ((), (), s32[]{:S(2)}) async-start(), calls=%async_computation.7 | async-start | bytes 2359296 | tf_op jit(solution)/shard_map/all_gather | solution.py:184
  9.0 61.1 %all-gather.8.cloned.1.call-start = ((), (), s32[]{:S(2)}) async-start(), calls=%async_computation.8 | async-start | bytes 2359296 | tf_op jit(solution)/shard_map/all_gather | solution.py:183
  10.9 89.6 %all-gather.10.cloned.1.call-start = ((), (), s32[]{:S(2)}) async-start(), calls=%async_computation.9 | async-start | bytes 2359296 | tf_op jit(solution)/shard_map/all_gather | solution.py:185
  12.8 250.9 %all-gather.12.cloned.1.call-start = ((), (), s32[]{:S(2)}) async-start(), calls=%async_computation.10 | async-start | bytes 37748736 | tf_op jit(solution)/shard_map/all_gather | solution.py:258
  18.9 28.8 %copy-start.84 = (s32[2]{0:T(128)S(1)}, s32[2]{0:T(128)}, u32[]{:S(2)}) copy-start(s32[2]{0:T(128)} %constant.51) | copy-start | bytes 28
  18.9 28.9 %copy-start.83 = (s32[2]{0:T(128)S(1)}, s32[2]{0:T(128)}, u32[]{:S(2)}) copy-start(s32[2]{0:T(128)} %constant.54) | copy-start | bytes 28
  18.9 29.1 %copy-start = (bf16[512,1024]{1,0:T(8,128)(2,1)S(1)}, bf16[512,1024]{1,0:T(8,128)(2,1)}, u32[]{:S(2)}) copy-start(bf16[512,1024]{1,0:T(8,128)(2,1)} %param.25) | copy-start | bytes 3145732
  18.9 340.2 %all-gather.14.cloned.1.call-start = ((), (), s32[]{:S(2)}) async-start(), calls=%async_computation.11 | async-start | bytes 18874368 | tf_op jit(solution)/shard_map/all_gather | solution.py:259
  23.1 792.0 %reduce-scatter.14.cloned.1.call-start = ((), (), s32[]{:S(2)}) async-start(), calls=%async_computation.14 | async-start | bytes 4718592 | tf_op jit(solution)/shard_map/reduce_scatter | solution.py:370
  48.2 14.4 copy-start.66
  48.3 14.3 copy-start.49
  50.4 22.8 %copy-start.23 = (f32[512,32]{0,1:T(8,128)}, f32[512,32]{0,1:T(8,128)S(1)}, u32[]{:S(2)}) copy-start(f32[512,32]{0,1:T(8,128)S(1)} %get-tuple-element.196) | copy-start | bytes 196612
  105.5 28.2 %copy-start.7 = (bf16[512,1024]{1,0:T(8,128)(2,1)}, bf16[512,1024]{1,0:T(8,128)(2,1)S(1)}, u32[]{:S(2)}) copy-start(bf16[512,1024]{1,0:T(8,128)(2,1)S(1)} %multiply_convert_fusion.4) | copy-start | bytes 3145732
  495.3 130.6 %copy-start.53 = (bf16[512,16]{0,1:T(8,128)(2,1)}, bf16[512,16]{0,1:T(8,128)(2,1)S(1)}, u32[]{:S(2)}) copy-start(bf16[512,16]{0,1:T(8,128)(2,1)S(1)} %select_reduce_fusion) | copy-start | bytes 49156
  633.0 182.1 %reduce-scatter.12.cloned.1.call-start = ((), (), s32[]{:S(2)}) async-start(), calls=%async_computation.13 | async-start | bytes 4718592 | tf_op jit(solution)/shard_map/reduce_scatter | solution.py:369
  639.7 15.3 slice-start
  639.7 15.3 slice-start.1
  639.7 17.6 slice-start.2
  639.7 18.8 slice-start.3
  639.7 18.8 copy-start.46
  685.7 129.4 %reduce-scatter.10.cloned.1.call-start = ((), (), s32[]{:S(2)}) async-start(), calls=%async_computation.12 | async-start | bytes 4718592 | tf_op jit(solution)/shard_map/reduce_scatter | solution.py:368
  695.7 308.9 %reduce-scatter.20.cloned.1.call-start = ((), (), s32[]{:S(2)}) async-start(), calls=%async_computation.17 | async-start | bytes 37748736 | tf_op jit(solution)/shard_map/reduce_scatter | solution.py:298
  718.9 672.9 %reduce-scatter.18.cloned.1.call-start = ((), (), s32[]{:S(2)}) async-start(), calls=%async_computation.16 | async-start | bytes 75497472 | tf_op jit(solution)/shard_map/reduce_scatter | solution.py:297
  803.7 626.3 %reduce-scatter.22.cloned.1.call-start = ((), (), s32[]{:S(2)}) async-start(), calls=%async_computation.18 | async-start | bytes 589824
  814.0 650.9 %reduce-scatter.16.cloned.1.call-start = ((), (), s32[]{:S(2)}) async-start(), calls=%async_computation.15 | async-start | bytes 73728 | tf_op jit(solution)/shard_map/reduce_scatter | solution.py:371
  815.0 1132.8 %all-reduce.4.cloned.1.call-start = ((), (), s32[]{:S(2)}) async-start(), calls=%async_computation.19 | async-start | bytes 28311552 | tf_op jit(solution)/shard_map/psum | solution.py:373
  1391.9 85.5 %copy-start.80 = (f32[2,128]{1,0:T(2,128)S(1)}, f32[2,128]{1,0:T(2,128)}, u32[]{:S(2)}) copy-start(f32[2,128]{1,0:T(2,128)} %param.29) | copy-start | bytes 3076
  1391.9 85.5 %copy-start.81 = (f32[2,128]{1,0:T(2,128)S(1)}, f32[2,128]{1,0:T(2,128)}, u32[]{:S(2)}) copy-start(f32[2,128]{1,0:T(2,128)} %param.31) | copy-start | bytes 3076
  1391.9 85.5 %copy-start.82 = (f32[2,128]{1,0:T(2,128)S(1)}, f32[2,128]{1,0:T(2,128)}, u32[]{:S(2)}) copy-start(f32[2,128]{1,0:T(2,128)} %param.30) | copy-start | bytes 3076
  1391.9 86.1 %copy-start.73 = (f32[128,16]{0,1:T(8,128)S(1)}, f32[128,16]{0,1:T(8,128)}, u32[]{:S(2)}) copy-start(f32[128,16]{0,1:T(8,128)} %param.41) | copy-start | bytes 24580
  1391.9 86.1 %copy-start.77 = (f32[128,16]{0,1:T(8,128)S(1)}, f32[128,16]{0,1:T(8,128)}, u32[]{:S(2)}) copy-start(f32[128,16]{0,1:T(8,128)} %param.43) | copy-start | bytes 24580
  1391.9 86.1 %copy-start.78 = (f32[128,16]{0,1:T(8,128)S(1)}, f32[128,16]{0,1:T(8,128)}, u32[]{:S(2)}) copy-start(f32[128,16]{0,1:T(8,128)} %param.42) | copy-start | bytes 24580
  (73 other events, 430.2 us)
Sparse Core Ops, SparseCore 0:
  10.5 29.1 all-gather.5
  42.2 27.9 all-gather.7
  72.6 27.8 all-gather.9
  102.9 160.7 all-gather.11
  266.0 93.1 all-gather.13
  633.1 51.3 reduce-scatter.13
  688.7 51.3 reduce-scatter.11
  744.0 51.3 reduce-scatter.9
  799.4 205.2 reduce-scatter.19
  1008.1 383.7 reduce-scatter.17
  1395.8 34.1 reduce-scatter.21
  1433.4 31.4 reduce-scatter.15
  1468.3 479.4 all-reduce.3
where the time goes:
time: 2020 us; the launch traced here: 2010 us
  waiting for transfers between devices  1280 us (63%)
  matrix products  268 us (13%)
  local copies, waits for them, and re-layouts  235 us (12%)
  other arithmetic  178 us (9%)
  blocking collectives  30.4 us (2%)
    psum x1, waiting for transfers between devices, body(): lax.psum((gains_part, query_part, keyval_part, output_part, router_part,...  469 us
    reduce_scatter x1, waiting for transfers between devices, body(): lax.psum_scatter(gateup_grad, 'fsdp', scatter_dimension=2, tiled=True)  387 us
    reduce_scatter x1, waiting for transfers between devices, body(): lax.psum_scatter(down_grad, 'fsdp', scatter_dimension=2, tiled=True)  190 us
    all_gather x1, waiting for transfers between devices, body(): lax.all_gather(expert_shards[0], 'fsdp', axis=2, tiled=True)  102 us
    gather x1, local copies, waits for them, and re-layouts, body(): expert_out[flat_expert, slot_index]  80.5 us
    gather x1, local copies, waits for them, and re-layouts, body(): d_buffers[flat_expert, slot_index].reshape(count_of_rows, TOPK, MODEL_WIDTH)  80.3 us
    unnamed x192, local copies, waits for them, and re-layouts  62.3 us
    all_gather x1, waiting for transfers between devices, body(): lax.all_gather(expert_shards[1], 'fsdp', axis=2, tiled=True)  61.1 us
  transfers between devices with their start and end apart: 13, of which 9 were waited for; matrix products, arithmetic and copies ran while one was open for 17% of the time, Pallas kernels for 0%

commit v1 on v0

v1 whole, which is shorter than its diff:
```python
import functools
import math

import jax
import jax.numpy as jnp
from jax import lax
from jax.experimental import pallas as pl
from jax.experimental.pallas import tpu as pltpu
from jax.sharding import Mesh
from jax.sharding import PartitionSpec as P

MODEL_WIDTH = 1024
QUERY_HEADS = 16
KEYVALUE_HEADS = 8
HEAD_SIZE = 64
F = 512
TOPK = 8
EXPERTS = 16
ADAM_STEP = 5
GROUP = 8
LOCAL = EXPERTS // GROUP
EXTRA = 128
CHUNKS = 2
TILE = 512
SPAN = 256
LANES = 128
WIDTH = QUERY_HEADS * HEAD_SIZE
KV_WIDTH = KEYVALUE_HEADS * HEAD_SIZE
PROJECTED = WIDTH + 2 * KV_WIDTH
SCORE_SCALE = HEAD_SIZE ** (-0.5)
ROUTER_BLOCK = (PROJECTED + MODEL_WIDTH) // EXTRA


norm_eps = 1e-06
rope_base = 10000.0
beta_one = 0.9
beta_two = 0.95
adam_eps = 1e-08
decay_rate = 0.1
gain_rate = 0.25
masked_value = -1e30
brain_floating = jnp.bfloat16


def layout(lengths, count_of_rows):
    document_ends = jnp.cumsum(lengths)
    row_index = jnp.arange(count_of_rows, dtype=jnp.int32)
    passed = row_index[:, None] >= document_ends[None, :]
    segment = jnp.sum(passed.astype(jnp.int32), axis=1)
    start_row = jnp.sum(jnp.where(passed, lengths[None, :], 0), axis=1)
    position = (row_index - start_row).astype(jnp.float32)
    alive_mask = (segment < lengths.shape[0]).astype(jnp.float32)
    allowed = (segment[:, None] == segment[None, :]) & (row_index[None, :] <= row_index[:, None])
    return (position, alive_mask, allowed)


def rope_tables(position):
    half_width = HEAD_SIZE // 2
    exponents = jnp.arange(half_width, dtype=jnp.float32) * (2.0 / HEAD_SIZE)
    inverse = jnp.exp(exponents * -math.log(rope_base))
    angles = position[:, None] * inverse[None, :]
    cosine, sine = (jnp.cos(angles), jnp.sin(angles))
    return (
        jnp.concatenate([cosine] * 4, axis=1),
        jnp.concatenate([-sine, sine, -sine, sine], axis=1),
    )


def product(left, right):
    return jnp.dot(left, right, preferred_element_type=jnp.float32)


def times_transposed(left, right):
    return lax.dot_general(
        left, right, (((1,), (1,)), ((), ())), preferred_element_type=jnp.float32
    )


def transposed_times(left, right):
    return lax.dot_general(
        left, right, (((0,), (0,)), ((), ())), preferred_element_type=jnp.float32
    )


def normalize(values):
    inverse = lax.rsqrt(jnp.mean(values * values, axis=-1, keepdims=True) + norm_eps)
    return (values * inverse, inverse)


def norm_back(upstream, scaled_rows, inverse, gain_row):
    weighted = upstream * gain_row
    inner = jnp.mean(weighted * scaled_rows, axis=-1, keepdims=True)
    return inverse * (weighted - scaled_rows * inner)


def column_sums(values):
    ones = jnp.ones((values.shape[0], LANES), brain_floating)
    high = values.astype(brain_floating)
    low = (values - high.astype(jnp.float32)).astype(brain_floating)
    return transposed_times(high, ones) + transposed_times(low, ones)


def lanes_of(shape):
    return lax.broadcasted_iota(jnp.int32, shape, 1)


def rotate(values, cosine, sine):
    half = HEAD_SIZE // 2
    front = lax.rem(lanes_of(values.shape), HEAD_SIZE) < half
    swapped = jnp.where(
        front, pltpu.roll(values, LANES - half, 1), pltpu.roll(values, half, 1)
    )
    return values * cosine + swapped * sine


def both_halves(values, which):
    turned = pltpu.roll(values, HEAD_SIZE, 1)
    first = lanes_of(values.shape) < HEAD_SIZE
    return jnp.where(first == (which == 0), values, turned)


def only_half(values, which):
    first = lanes_of(values.shape) < HEAD_SIZE
    return jnp.where(first == (which == 0), values, 0.0)


def gates_of(rows, router, mask):
    logits = product(rows, router)
    peak = jnp.max(jnp.where(mask, logits, masked_value), axis=1, keepdims=True)
    weights = jnp.where(mask, jnp.exp(logits - peak), 0.0)
    return weights / jnp.sum(weights, axis=1, keepdims=True)


def adamw_step(weight, moment_old, square_old, gradient, step_rate, shrink):
    moment = beta_one * moment_old + (1.0 - beta_one) * gradient
    square = beta_two * square_old + (1.0 - beta_two) * gradient * gradient
    moment_hat = moment / (1.0 - beta_one**ADAM_STEP)
    square_hat = square / (1.0 - beta_two**ADAM_STEP)
    renewed = weight - step_rate * (
        moment_hat / (jnp.sqrt(square_hat) + adam_eps) + shrink * weight
    )
    return (moment, square, renewed)


MIB = 1024 * 1024
ANYWHERE = pl.BlockSpec(memory_space=pl.ANY)


def whole(shape):
    return pl.BlockSpec(shape, lambda *_: (0,) * len(shape), pipeline_mode=pl.Buffered(1))


def part(shape, place):
    return pl.BlockSpec(shape, lambda *_: place, pipeline_mode=pl.Buffered(1))


def out(shape, dtype):
    return jax.ShapeDtypeStruct(shape, dtype)


def split_kernel(gateup_ref, down_ref, out_ref):
    out_ref[0, 0, 0] = gateup_ref[0, 0].astype(brain_floating)
    out_ref[0, 0, 1] = gateup_ref[0, 1].astype(brain_floating)
    out_ref[0, 0, 2] = down_ref[0].T.astype(brain_floating)


def split_by_owner(gateup, down):
    shard = gateup.shape[2]
    return pl.pallas_call(
        split_kernel,
        grid=(EXPERTS,),
        in_specs=[
            pl.BlockSpec((1, 2, shard, F), lambda e: (e, 0, 0, 0)),
            pl.BlockSpec((1, F, shard), lambda e: (e, 0, 0)),
        ],
        out_specs=pl.BlockSpec(
            (1, 1, 3, shard, F), lambda e: (lax.rem(e, GROUP), e // GROUP, 0, 0, 0)
        ),
        out_shape=out((GROUP, LOCAL, 3, shard, F), brain_floating),
        name="split",
    )(gateup, down)


def front_kernel(
    x_ref, pack_ref, gains_ref, alive_ref, bias_ref, cos_ref, sin_ref, wait_ref,
    normed_ref, qkv_ref, mixed_ref, totals_ref, middle_ref, normed_two_ref, linear_ref,
):
    rows = x_ref.shape[0]
    scaled, _ = normalize(x_ref[...].astype(jnp.float32))
    normed = (scaled * gains_ref[0:1, :]).astype(brain_floating)
    normed_ref[...] = normed
    linear_ref[...] = product(normed, pack_ref[:, :PROJECTED])
    cosine, sine = (cos_ref[...], sin_ref[...])
    for at in range(0, WIDTH + KV_WIDTH, LANES):
        qkv_ref[:, at : at + LANES] = rotate(
            linear_ref[:, at : at + LANES], cosine, sine
        ).astype(brain_floating)
    qkv_ref[:, WIDTH + KV_WIDTH :] = linear_ref[:, WIDTH + KV_WIDTH :].astype(brain_floating)
    totals_ref[...] = jnp.zeros_like(totals_ref)

    @pl.loop(0, KEYVALUE_HEADS // 2)
    def _(pair):
        at = pl.multiple_of(pair * LANES, LANES)
        keys = qkv_ref[:, pl.ds(WIDTH + at, LANES)].astype(jnp.float32)
        values = qkv_ref[:, pl.ds(WIDTH + KV_WIDTH + at, LANES)].astype(jnp.float32)
        for a in range(2):
            head_keys = both_halves(keys, a).astype(brain_floating)
            head_values = both_halves(values, a)
            place = pl.multiple_of((2 * pair + a) * LANES, LANES)
            queries = qkv_ref[:, pl.ds(place, LANES)].astype(jnp.float32)
            for start in range(0, rows, SPAN):
                seen = min(start + SPAN, rows)
                mixed = jnp.zeros((SPAN, LANES), jnp.float32)
                for j in range(2):
                    head = 2 * (2 * pair + a) + j
                    query = only_half(queries[start : start + SPAN], j).astype(brain_floating)
                    scores = (
                        times_transposed(query, head_keys[:seen]) * SCORE_SCALE
                        + bias_ref[start : start + SPAN, :seen]
                    )
                    peak = jnp.max(scores, axis=1, keepdims=True)
                    weights = jnp.exp(scores - peak)
                    total = jnp.sum(weights, axis=1, keepdims=True)
                    probs = (weights * (1.0 / total)).astype(brain_floating)
                    mixed += product(probs, only_half(head_values[:seen], j).astype(brain_floating))
                    held = totals_ref[start : start + SPAN, :]
                    totals_ref[start : start + SPAN, :] = jnp.where(
                        lanes_of(held.shape) == head, peak + jnp.log(total), held
                    )
                mixed_ref[start : start + SPAN, pl.ds(place, LANES)] = mixed.astype(brain_floating)

    attended = product(mixed_ref[...], pack_ref[:, PROJECTED : PROJECTED + MODEL_WIDTH])
    middle = x_ref[...].astype(jnp.float32) + alive_ref[...] * attended
    middle_ref[...] = middle
    scaled_two, _ = normalize(middle)
    normed_two_ref[...] = (scaled_two * gains_ref[1:2, :]).astype(brain_floating)


def run_front(x, pack, gains, alive, bias, cosine, sine, wait):
    rows = x.shape[0]
    return pl.pallas_call(
        front_kernel,
        in_specs=[pl.BlockSpec(memory_space=pltpu.VMEM)] * 7 + [ANYWHERE],
        out_shape=[
            out((rows, MODEL_WIDTH), brain_floating),
            out((rows, PROJECTED), brain_floating),
            out((rows, WIDTH), brain_floating),
            out((rows, LANES), jnp.float32),
            out((rows, MODEL_WIDTH), jnp.float32),
            out((rows, MODEL_WIDTH), brain_floating),
        ],
        scratch_shapes=[pltpu.VMEM((rows, PROJECTED), jnp.float32)],
        compiler_params=pltpu.CompilerParams(vmem_limit_bytes=52 * MIB),
        name="front",
    )(x, pack, gains, alive, bias, cosine, sine, wait)


def middle_kernel(
    dx_one_ref, dx_two_ref, normed_two_ref, middle_ref, cot_ref, mask_ref, alive_ref, gains_ref,
    router_ref, output_ref, mixed_ref, wait_ref, d_middle_ref, d_mixed_ref, grads_ref,
):
    dx = jnp.concatenate([dx_one_ref[...], dx_two_ref[...]], axis=0).astype(jnp.float32)
    normed_two = normed_two_ref[...]
    mask = mask_ref[...].astype(jnp.float32) > 0.5
    gates = gates_of(normed_two, router_ref[...], mask)
    extra = dx[:, MODEL_WIDTH:]
    d_gates = extra + pltpu.roll(extra, LANES - EXPERTS, 1)
    d_logits = (
        gates * (d_gates - jnp.sum(gates * d_gates, axis=1, keepdims=True))
    ).astype(brain_floating)
    d_normed = dx[:, :MODEL_WIDTH] + times_transposed(d_logits, router_ref[...])
    scaled, inverse = normalize(middle_ref[...])
    d_middle = cot_ref[...].astype(jnp.float32) + norm_back(
        d_normed, scaled, inverse, gains_ref[1:2, :]
    )
    d_middle_ref[...] = d_middle
    d_attended = (alive_ref[...] * d_middle).astype(brain_floating)
    grads_ref[:, :MODEL_WIDTH] = transposed_times(mixed_ref[...], d_attended).astype(brain_floating)
    small = transposed_times(normed_two, d_logits)
    small = jnp.where(lanes_of(small.shape) == EXPERTS, column_sums(d_normed * scaled), small)
    grads_ref[:, MODEL_WIDTH:] = small.astype(brain_floating)
    d_mixed_ref[...] = times_transposed(d_attended, output_ref[...]).astype(brain_floating)


def run_middle(dx_one, dx_two, normed_two, middle, cot, mask, alive, gains, pack, mixed, wait):
    rows = middle.shape[0]
    full = [whole(v.shape) for v in (dx_one, dx_two, normed_two, middle, cot, mask, alive, gains)]
    return pl.pallas_call(
        middle_kernel,
        grid=(1,),
        in_specs=full
        + [
            part((MODEL_WIDTH, EXTRA), (0, ROUTER_BLOCK)),
            part((WIDTH, MODEL_WIDTH), (0, PROJECTED // MODEL_WIDTH)),
            whole(mixed.shape),
            ANYWHERE,
        ],
        out_specs=[
            whole((rows, MODEL_WIDTH)),
            whole((rows, WIDTH)),
            whole((MODEL_WIDTH, MODEL_WIDTH + EXTRA)),
        ],
        out_shape=[
            out((rows, MODEL_WIDTH), jnp.float32),
            out((rows, WIDTH), brain_floating),
            out((MODEL_WIDTH, MODEL_WIDTH + EXTRA), brain_floating),
        ],
        compiler_params=pltpu.CompilerParams(vmem_limit_bytes=52 * MIB),
        name="middle_back",
    )(dx_one, dx_two, normed_two, middle, cot, mask, alive, gains, pack, pack, mixed, wait)


def back_kernel(
    d_mixed_ref, qkv_ref, totals_ref, bias_ref, cos_ref, sin_ref, normed_ref, x_ref, d_middle_ref,
    gains_ref, pack_ref, wait_ref, grads_ref, d_input_ref, d_linear_ref, d_keys_ref, d_values_ref,
):
    rows = x_ref.shape[0]
    cosine, sine = (cos_ref[...], -sin_ref[...])

    @pl.loop(0, KEYVALUE_HEADS // 2)
    def _(pair):
        at = pl.multiple_of(pair * LANES, LANES)
        keys = qkv_ref[:, pl.ds(WIDTH + at, LANES)].astype(jnp.float32)
        values = qkv_ref[:, pl.ds(WIDTH + KV_WIDTH + at, LANES)].astype(jnp.float32)
        pair_keys = jnp.zeros((rows, LANES), jnp.float32)
        pair_values = jnp.zeros((rows, LANES), jnp.float32)
        for a in range(2):
            both_keys = both_halves(keys, a)
            head_keys = both_keys.astype(brain_floating)
            head_values = both_halves(values, a).astype(brain_floating)
            place = pl.multiple_of((2 * pair + a) * LANES, LANES)
            queries = qkv_ref[:, pl.ds(place, LANES)].astype(jnp.float32)
            d_outs = d_mixed_ref[:, pl.ds(place, LANES)].astype(jnp.float32)
            d_keys_ref[...] = jnp.zeros_like(d_keys_ref)
            d_values_ref[...] = jnp.zeros_like(d_values_ref)
            for start in range(0, rows, SPAN):
                seen = min(start + SPAN, rows)
                d_query = jnp.zeros((SPAN, LANES), jnp.float32)
                for j in range(2):
                    head = 2 * (2 * pair + a) + j
                    query = only_half(queries[start : start + SPAN], j).astype(brain_floating)
                    d_out = only_half(d_outs[start : start + SPAN], j).astype(brain_floating)
                    held = totals_ref[start : start + SPAN, :]
                    total = jnp.sum(
                        jnp.where(lanes_of(held.shape) == head, held, 0.0), axis=1, keepdims=True
                    )
                    scores = (
                        times_transposed(query, head_keys[:seen]) * SCORE_SCALE
                        + bias_ref[start : start + SPAN, :seen]
                    )
                    probs = jnp.exp(scores - total)
                    d_probs = times_transposed(d_out, head_values[:seen])
                    inner = jnp.sum(probs * d_probs, axis=1, keepdims=True)
                    d_scores = (probs * (d_probs - inner)).astype(brain_floating)
                    d_query += product(
                        d_scores, only_half(both_keys[:seen], j).astype(brain_floating)
                    )
                    d_keys_ref[:seen, :] += transposed_times(d_scores, query)
                    d_values_ref[:seen, :] += transposed_times(probs.astype(brain_floating), d_out)
                d_linear_ref[start : start + SPAN, pl.ds(place, LANES)] = rotate(
                    d_query * SCORE_SCALE,
                    cosine[start : start + SPAN],
                    sine[start : start + SPAN],
                ).astype(brain_floating)
            d_keys = d_keys_ref[...]
            d_values = d_values_ref[...]
            pair_keys += only_half(d_keys + pltpu.roll(d_keys, HEAD_SIZE, 1), a)
            pair_values += only_half(d_values + pltpu.roll(d_values, HEAD_SIZE, 1), a)
        d_linear_ref[:, pl.ds(WIDTH + at, LANES)] = rotate(
            pair_keys * SCORE_SCALE, cosine, sine
        ).astype(brain_floating)
        d_linear_ref[:, pl.ds(WIDTH + KV_WIDTH + at, LANES)] = pair_values.astype(brain_floating)

    normed = normed_ref[...]
    for at in range(0, PROJECTED, 512):
        grads_ref[:, at : at + 512] = transposed_times(
            normed, d_linear_ref[:, at : at + 512]
        ).astype(brain_floating)
    d_normed = times_transposed(d_linear_ref[...], pack_ref[...])
    scaled, inverse = normalize(x_ref[...].astype(jnp.float32))
    sums = column_sums(d_normed * scaled)
    grads_ref[:, PROJECTED:] = jnp.where(lanes_of(sums.shape) == 0, sums, 0.0).astype(
        brain_floating
    )
    d_input_ref[...] = d_middle_ref[...] + norm_back(d_normed, scaled, inverse, gains_ref[0:1, :])


def run_back(d_mixed, qkv, totals, bias, cosine, sine, normed, x, d_middle, gains, pack, wait):
    rows = x.shape[0]
    held = (d_mixed, qkv, totals, bias, cosine, sine, normed, x, d_middle, gains)
    return pl.pallas_call(
        back_kernel,
        grid=(1,),
        in_specs=[whole(v.shape) for v in held]
        + [part((MODEL_WIDTH, PROJECTED), (0, 0)), ANYWHERE],
        out_specs=[whole((MODEL_WIDTH, PROJECTED + EXTRA)), whole((rows, MODEL_WIDTH))],
        out_shape=[
            out((MODEL_WIDTH, PROJECTED + EXTRA), brain_floating),
            out((rows, MODEL_WIDTH), jnp.float32),
        ],
        scratch_shapes=[
            pltpu.VMEM((rows, PROJECTED), brain_floating),
            pltpu.VMEM((rows, LANES), jnp.float32),
            pltpu.VMEM((rows, LANES), jnp.float32),
        ],
        compiler_params=pltpu.CompilerParams(vmem_limit_bytes=52 * MIB),
        name="attention_back",
    )(*held, pack, wait)


def expert_kernel(me_ref, x_ref, b_ref, w_ref, router_ref, ga_ref, dgu_ref, dx_ref):
    x = x_ref[...]
    branch = b_ref[:, :MODEL_WIDTH]
    mask = b_ref[:, MODEL_WIDTH:].astype(jnp.float32) > 0.5
    gates = gates_of(x, router_ref[...], mask)
    lane = lanes_of(gates.shape)
    d_gates = jnp.zeros_like(gates)
    dx = jnp.zeros((x.shape[0], MODEL_WIDTH), jnp.float32)
    for local in range(LOCAL):
        expert = me_ref[0] + GROUP * local
        gate_weight, up_weight, down_weight = (
            w_ref[:, local, p].reshape(MODEL_WIDTH, F) for p in range(3)
        )
        gate = jnp.sum(jnp.where(lane == expert, gates, 0.0), axis=1, keepdims=True)
        gate_linear = product(x, gate_weight)
        up_linear = product(x, up_weight)
        back = product(branch, down_weight)
        sig = jax.nn.sigmoid(gate_linear)
        silu = gate_linear * sig
        act = silu * up_linear
        ga_ref[:, local * F : (local + 1) * F] = (gate * act).astype(brain_floating)
        d_gate = jnp.sum(act * back, axis=1, keepdims=True)
        high = d_gate.astype(brain_floating).astype(jnp.float32)
        d_gates += jnp.where(lane == expert, high, 0.0)
        d_gates += jnp.where(lane == expert + EXPERTS, d_gate - high, 0.0)
        d_act = gate * back
        d_gl = (d_act * up_linear * (sig + silu * (1.0 - sig))).astype(brain_floating)
        d_ul = (d_act * silu).astype(brain_floating)
        dgu_ref[:, 2 * local * F : (2 * local + 1) * F] = d_gl
        dgu_ref[:, (2 * local + 1) * F : (2 * local + 2) * F] = d_ul
        dx += times_transposed(d_gl, gate_weight) + times_transposed(d_ul, up_weight)
    dx_ref[:, :MODEL_WIDTH] = dx.astype(brain_floating)
    dx_ref[:, MODEL_WIDTH:] = d_gates.astype(brain_floating)


def run_experts(me, x, b, weights, pack):
    rows = x.shape[0]
    tile = min(TILE, rows)
    wide = MODEL_WIDTH + EXTRA

    def rowed(width):
        return pl.BlockSpec((tile, width), lambda i, me_ref: (i, 0))

    return pl.pallas_call(
        expert_kernel,
        grid_spec=pltpu.PrefetchScalarGridSpec(
            num_scalar_prefetch=1,
            grid=(rows // tile,),
            in_specs=[
                rowed(MODEL_WIDTH),
                rowed(wide),
                whole(weights.shape),
                part((MODEL_WIDTH, EXTRA), (0, ROUTER_BLOCK)),
            ],
            out_specs=[rowed(LOCAL * F), rowed(2 * LOCAL * F), rowed(wide)],
        ),
        out_shape=[
            out((rows, LOCAL * F), brain_floating),
            out((rows, 2 * LOCAL * F), brain_floating),
            out((rows, wide), brain_floating),
        ],
        compiler_params=pltpu.CompilerParams(vmem_limit_bytes=56 * MIB),
        name="experts",
    )(me, x, b, weights, pack)


def chunked_specs(count, tile, steps, width, column):
    def index(c):
        return lambda i, *_: (jnp.clip(i - c * steps, 0, steps - 1), column)

    return [pl.BlockSpec((tile, width), index(c)) for c in range(count)]


def grads_kernel(steps, *refs):
    ins, wait_ref, outs, sums = (refs[:-7], refs[-7], refs[-6:-3], refs[-3:])
    i = pl.program_id(0)

    @pl.when(i == 0)
    def _():
        for total in sums:
            total[...] = jnp.zeros_like(total)

    for c in range(CHUNKS):

        @pl.when(i // steps == c)
        def _():
            x_ref, b_ref, ga_ref, dgu_ref = ins[4 * c : 4 * c + 4]
            x = x_ref[...]
            sums[0][...] += transposed_times(x, dgu_ref[:, :F])
            sums[1][...] += transposed_times(x, dgu_ref[:, F:])
            sums[2][...] += transposed_times(b_ref[...], ga_ref[...])

    @pl.when(i == CHUNKS * steps - 1)
    def _():
        for result, total in zip(outs, sums):
            result[...] = total[...].astype(brain_floating)


def run_grads(local, xs, bs, gas, dgus, wait):
    tile = min(TILE, xs[0].shape[0])
    steps = xs[0].shape[0] // tile
    columns = (
        chunked_specs(CHUNKS, tile, steps, MODEL_WIDTH, 0),
        chunked_specs(CHUNKS, tile, steps, MODEL_WIDTH, 0),
        chunked_specs(CHUNKS, tile, steps, F, local),
        chunked_specs(CHUNKS, tile, steps, 2 * F, local),
    )
    return pl.pallas_call(
        functools.partial(grads_kernel, steps),
        grid=(CHUNKS * steps,),
        in_specs=[columns[k][c] for c in range(CHUNKS) for k in range(4)] + [ANYWHERE],
        out_specs=[whole((MODEL_WIDTH, F))] * 3,
        out_shape=[out((MODEL_WIDTH, F), brain_floating)] * 3,
        scratch_shapes=[pltpu.VMEM((MODEL_WIDTH, F), jnp.float32)] * 3,
        compiler_params=pltpu.CompilerParams(vmem_limit_bytes=52 * MIB),
        name="grads",
    )(*[v[c] for c in range(CHUNKS) for v in (xs, bs, gas, dgus)], wait)


def mix_kernel(steps, *refs):
    gas, w_ref, out_ref = (refs[:CHUNKS], refs[CHUNKS], refs[-1])
    i = pl.program_id(0)
    for c in range(CHUNKS):

        @pl.when(i // steps == c)
        def _():
            total = jnp.zeros((gas[c].shape[0], MODEL_WIDTH), jnp.float32)
            for local in range(LOCAL):
                total += times_transposed(
                    gas[c][:, local * F : (local + 1) * F],
                    w_ref[:, local, 0].reshape(MODEL_WIDTH, F),
                )
            out_ref[0] = total.astype(brain_floating)


def run_mix(gas, weights, wait):
    rows = gas[0].shape[0]
    tile = min(TILE, rows)
    steps = rows // tile
    blocks, _, _, shard, _ = weights.shape
    return pl.pallas_call(
        functools.partial(mix_kernel, steps),
        grid=(CHUNKS * steps,),
        in_specs=chunked_specs(CHUNKS, tile, steps, LOCAL * F, 0)
        + [part((blocks, LOCAL, 1, shard, F), (0, 0, 2, 0, 0)), ANYWHERE],
        out_specs=pl.BlockSpec(
            (1, tile, MODEL_WIDTH), lambda i: (i // steps, lax.rem(i, steps), 0)
        ),
        out_shape=out((CHUNKS, rows, MODEL_WIDTH), brain_floating),
        compiler_params=pltpu.CompilerParams(vmem_limit_bytes=52 * MIB),
        name="mixture",
    )(*gas, weights, wait)


def sums_kernel(count, waits, *refs):
    ins, outs = (refs[: 2 * count], refs[2 * count + waits :])
    for k in range(count):
        left, right = (ins[2 * k][...], ins[2 * k + 1][...])
        outs[k][...] = (left.astype(jnp.float32) + right.astype(jnp.float32)).astype(
            brain_floating
        )


def run_sums(pairs, waits):
    flat = [v for pair in pairs for v in pair]
    return pl.pallas_call(
        functools.partial(sums_kernel, len(pairs), len(waits)),
        in_specs=[pl.BlockSpec(memory_space=pltpu.VMEM)] * len(flat) + [ANYWHERE] * len(waits),
        out_shape=[out(pair[0].shape, brain_floating) for pair in pairs],
        compiler_params=pltpu.CompilerParams(vmem_limit_bytes=40 * MIB),
        name="sums",
    )(*flat, *waits)


def adam_kernel(turned, rate, shrink, place_ref, t_ref, r_ref, w_ref, m_ref, v_ref, *rest):
    m_out, v_out, w_out = rest[-3:]
    inner = (place_ref[0] == 1) | (place_ref[0] == 2)
    for k in range(t_ref.shape[0]):
        gradient = jnp.where(inner, t_ref[k].astype(jnp.float32), r_ref[k].astype(jnp.float32))
        if turned:
            at = (k,)
            gradient = gradient.T
        else:
            at = (k, 0)
        moment, square, renewed = adamw_step(
            w_ref[at], m_ref[at], v_ref[at], gradient, rate, shrink
        )
        m_out[at] = moment
        v_out[at] = square
        w_out[at] = renewed


def adam_part(place, total, ends, state, local, side, rate, before, wait):
    weight, first, second = state
    turned = side == 2
    shard = total.shape[1]
    held = [] if before is None else list(before)
    if turned:
        spec = pl.BlockSpec((2, F, shard), lambda i, _: (i + local * (GROUP // 2), 0, 0))
    else:
        spec = pl.BlockSpec((2, 1, shard, F), lambda i, _: (i + local * (GROUP // 2), side, 0, 0))
    piece = pl.BlockSpec((2, shard, F), lambda i, _: (i, 0, 0))
    return pl.pallas_call(
        functools.partial(adam_kernel, turned, rate, decay_rate),
        grid_spec=pltpu.PrefetchScalarGridSpec(
            num_scalar_prefetch=1,
            grid=(GROUP // 2,),
            in_specs=[piece, piece, spec, spec, spec] + [ANYWHERE] * (len(held) + 1),
            out_specs=[spec] * 3,
        ),
        out_shape=[out(weight.shape, jnp.float32)] * 3,
        input_output_aliases={6 + i: i for i in range(len(held))},
        compiler_params=pltpu.CompilerParams(vmem_limit_bytes=40 * MIB),
        name="adam",
    )(place, total, ends, weight, first, second, *held, wait)


fsdp = ("outer", "inner")


def body(
    sizes,
    tokens_in,
    cotangent,
    document_lengths,
    expert_choice,
    norm_gains,
    gains_first,
    gains_second,
    query_weight,
    query_first,
    query_second,
    keyvalue_weight,
    keyvalue_first_moment,
    keyvalue_second_moment,
    output_weight,
    output_first,
    output_second,
    router_weight,
    router_first,
    router_second,
    gateup_weight,
    gateup_first,
    gateup_second,
    down_weight,
    down_first,
    down_second,
):
    replicas, outer = sizes
    count_of_rows = tokens_in.shape[0]
    shard = query_weight.shape[0]
    me = lax.axis_index("inner").astype(jnp.int32).reshape(1)
    place = lax.axis_index("replica").astype(jnp.int32).reshape(1)

    pack_own = jnp.concatenate(
        [
            query_weight,
            keyvalue_weight[0],
            keyvalue_weight[1],
            output_weight,
            router_weight,
            norm_gains.T,
            jnp.zeros((shard, EXTRA - EXPERTS - 2), jnp.float32),
        ],
        axis=1,
    ).astype(brain_floating)
    pack = lax.all_gather(pack_own, fsdp, axis=0, tiled=True)
    at = PROJECTED + MODEL_WIDTH + EXPERTS
    gains_value = pack[:, at : at + 2].astype(jnp.float32).T

    weights = lax.all_to_all(split_by_owner(gateup_weight, down_weight), "inner", 0, 0)
    if outer > 1:
        weights = lax.all_gather(weights, "outer", axis=0, tiled=True)

    position, alive_mask, allowed = layout(document_lengths[0], count_of_rows)
    cosine, sine = rope_tables(position)
    alive = alive_mask[:, None]
    bias = jnp.where(allowed, 0.0, masked_value)

    expert_row = jnp.arange(EXPERTS, dtype=jnp.int32)
    chosen = jnp.any(expert_choice[:, :, None] == expert_row[None, None, :], axis=1)
    mask = jnp.concatenate(
        [
            chosen.astype(brain_floating),
            jnp.zeros((count_of_rows, EXTRA - EXPERTS), brain_floating),
        ],
        axis=1,
    )
    branch = (alive * cotangent.astype(jnp.float32)).astype(brain_floating)
    branch_pack = jnp.concatenate([branch, mask], axis=1)
    part_rows = count_of_rows // CHUNKS

    def gathered(values, c):
        return lax.all_gather(
            values[c * part_rows : (c + 1) * part_rows], "inner", axis=0, tiled=True
        )

    branch_all = [gathered(branch_pack, c) for c in range(CHUNKS)]

    normed, qkv, mixed, totals, middle, normed_two = run_front(
        tokens_in, pack, gains_value, alive, bias, cosine, sine, weights
    )

    x_all, ga_all, dgu_all, dx_parts = ([], [], [], [])
    for c in range(CHUNKS):
        x_part = gathered(normed_two, c)
        ga, dgu, dx = run_experts(me, x_part, branch_all[c], weights, pack)
        x_all.append(x_part)
        ga_all.append(ga)
        dgu_all.append(dgu)
        dx_parts.append(lax.psum_scatter(dx, "inner", scatter_dimension=0, tiled=True))

    def to_owner(grad):
        parts = grad.reshape(GROUP * outer, shard, F)
        if outer > 1:
            parts = lax.psum_scatter(parts, "outer", scatter_dimension=0, tiled=True)
        return lax.all_to_all(parts, "inner", 0, 0)

    def inward(values):
        return lax.ppermute(values, "replica", [(0, 1), (3, 2)])

    def across(values):
        return lax.ppermute(values, "replica", [(1, 2), (2, 1)])

    def outward(values):
        return lax.ppermute(values, "replica", [(1, 0), (2, 3)])

    grads = [list(run_grads(0, x_all, branch_all, ga_all, dgu_all, dgu_all[-1])), None]
    queue = {0: (to_owner(grads[0][0]),)}
    gateup_new, down_new = (None, None)
    held = {"token": grads[0][0]}
    halves, sums, ends = ({}, {}, {})
    root = MODEL_WIDTH ** (-0.5)
    gateup_state = (gateup_weight, gateup_first, gateup_second)
    down_state = (down_weight, down_first, down_second)

    def adam_of(k, wait):
        nonlocal gateup_new, down_new
        local, side = divmod(k, 3)
        if side == 2:
            down_new = adam_part(
                place, sums[k][0], ends[k][0], down_state, local, side, (F // 16) ** (-0.5),
                down_new, wait,
            )
            return down_new[0]
        gateup_new = adam_part(
            place, sums[k][0], ends[k][0], gateup_state, local, side, root, gateup_new, wait
        )
        return gateup_new[0]

    count = 3 * LOCAL + 1
    token = grads[0][2]
    for k in range(-1, count + 2):
        arrived, waits = ([], [])
        if k in queue:
            halves[k] = tuple(inward(v) for v in queue[k])
            arrived += list(zip(queue[k], halves[k]))
        if k - 1 in queue:
            crossed = tuple(across(v) for v in sums[k - 1])
            arrived += list(zip(sums[k - 1], crossed))
        if k - 2 in queue:
            ends[k - 2] = tuple(outward(v) for v in sums[k - 2])
            waits += list(ends[k - 2])
        if 0 <= k + 1 < 3 * LOCAL and k + 1 not in queue:
            local, side = divmod(k + 1, 3)
            queue[k + 1] = (to_owner(grads[local][side]),)
        if k + 1 in queue:
            waits += list(queue[k + 1])

        if k == -1:
            grads[1] = list(run_grads(1, x_all, branch_all, ga_all, dgu_all, token))
            waits += [grads[1][0]]
        elif k == 0:
            mixture = run_mix(ga_all, weights, token)
            waits += [mixture]
        elif k == 1:
            d_middle, d_mixed, second_grads = run_middle(
                dx_parts[0], dx_parts[1], normed_two, middle, cotangent, mask, alive, gains_value,
                pack, mixed, token,
            )
            second_part = lax.psum_scatter(second_grads, fsdp, scatter_dimension=0, tiled=True)
            waits += [d_mixed]
        elif k == 2:
            first_grads, input_gradient = run_back(
                d_mixed, qkv, totals, bias, cosine, sine, normed, tokens_in, d_middle, gains_value,
                pack, token,
            )
            first_part = lax.psum_scatter(first_grads, fsdp, scatter_dimension=0, tiled=True)
            queue[count - 1] = (first_part, second_part)
            waits += [input_gradient]
        elif k - 3 in ends and k - 3 < 3 * LOCAL:
            waits += [adam_of(k - 3, token)]

        if not arrived:
            continue
        results = run_sums(arrived, waits)
        token = results[0]
        if k in queue:
            size = len(queue[k])
            sums[k] = None
            halves[k], results = (tuple(results[:size]), results[size:])
        if k - 1 in queue:
            crossed_sums = tuple(results)
        if k - 1 in queue:
            sums[k - 1] = crossed_sums
        if k in queue:
            sums[k] = halves[k]
    for k in range(3 * LOCAL):
        if k + 3 > count + 1:
            adam_of(k, token)

    mixture_own = lax.psum_scatter(mixture, "inner", scatter_dimension=1, tiled=True)
    mixture_own = mixture_own.reshape(count_of_rows, MODEL_WIDTH).astype(jnp.float32)
    block_output = (middle + alive * mixture_own).astype(brain_floating)

    inner = (place[0] == 1) | (place[0] == 2)
    first_sum, second_sum = (
        jnp.where(inner, total, end).astype(jnp.float32)
        for total, end in zip(sums[count - 1], ends[count - 1])
    )
    gains_part = jnp.stack([first_sum[:, PROJECTED], second_sum[:, MODEL_WIDTH + EXPERTS]])
    keyval_part = jnp.stack(
        [first_sum[:, WIDTH : WIDTH + KV_WIDTH], first_sum[:, WIDTH + KV_WIDTH : PROJECTED]]
    )
    settings = (
        (gains_part, norm_gains, gains_first, gains_second, gain_rate, 0.0),
        (first_sum[:, :WIDTH], query_weight, query_first, query_second, root, decay_rate),
        (
            keyval_part,
            keyvalue_weight,
            keyvalue_first_moment,
            keyvalue_second_moment,
            root,
            decay_rate,
        ),
        (
            second_sum[:, :MODEL_WIDTH],
            output_weight,
            output_first,
            output_second,
            (WIDTH // 16) ** (-0.5),
            decay_rate,
        ),
        (
            second_sum[:, MODEL_WIDTH : MODEL_WIDTH + EXPERTS],
            router_weight,
            router_first,
            router_second,
            (4 * MODEL_WIDTH) ** (-0.5),
            decay_rate,
        ),
    )
    updated = []
    for gradient, weight, first, second, rate, shrink in settings:
        updated.extend(adamw_step(weight, first, second, gradient, rate, shrink))
    return (block_output, input_gradient) + tuple(updated) + tuple(gateup_new) + tuple(down_new)


def solution(mesh):
    replicas, shards = (mesh.shape["replica"], mesh.shape["fsdp"])
    outer = shards // GROUP
    split = Mesh(mesh.devices.reshape(replicas, outer, GROUP), ("replica",) + fsdp)
    rows = P(("replica",) + fsdp, None)
    by_first = P(fsdp, None)
    by_second = P(None, fsdp)
    by_middle = P(None, fsdp, None)
    by_third = P(None, None, fsdp, None)
    by_last = P(None, None, fsdp)
    weights = (by_second, by_first, by_middle, by_first, by_first, by_third, by_last)
    states = tuple(spec for spec in weights for _ in range(3))
    return jax.shard_map(
        functools.partial(body, (replicas, outer)),
        mesh=split,
        in_specs=(rows,) * 4 + states,
        out_specs=(rows,) * 2 + states,
        check_vma=False,
    )
```

time: 2020 us -> 740 us (0.37)
  waiting for transfers between devices: 1280 us -> 250 us
  matrix products: 268 us -> 0 us
  Pallas kernels: 0 us -> 250 us
  local copies, waits for them, and re-layouts: 235 us -> 45.2 us
  other arithmetic: 178 us -> 20.4 us
  starting transfers between devices: 0.54 us -> 77.1 us
  blocking collectives: 30.4 us -> 71.6 us
    reduce_scatter x6 -> x5, waiting for transfers between devices: 611 us -> 14.8 us  [the longest x2 14.8 us: body(): lax.psum_scatter(dx, 'inner', scatter_dimension=0, tiled=True)]
    psum x1 -> x0, waiting for transfers between devices: 469 us -> none  [body(): lax.psum((gains_part, query_part, keyval_part, output_part, router_part,...]
    dot_general x30 -> x0, matrix products: 268 us -> none  [the longest x1 26.2 us: expert_backward(): jnp.einsum('ecd,efd->ecf', d_result, down_full, preferred_element_type=jn...]
    pallas_call x0 -> x23, Pallas kernels: none -> 250 us  [the longest x2 66.7 us: run_experts(): pl.pallas_call(expert_kernel, grid_spec=pltpu.PrefetchScalarGridSpec(num_...]
    gather x2 -> x0, local copies, waits for them, and re-layouts: 161 us -> none  [the longest x1 80.5 us: body(): expert_out[flat_expert, slot_index]]
    all_to_all x0 -> x4, blocking collectives: none -> 71.6 us  [to_owner(): return lax.all_to_all(parts, 'inner', 0, 0)]
    ppermute x0 -> x24, starting transfers between devices: none -> 60.7 us  [the longest x8 41.7 us: inward(): return lax.ppermute(values, 'replica', [(0, 1), (3, 2)])]
    another operation x10 -> x5, other arithmetic: 53 us -> 4.17 us  [the longest x1 43.8 us: expert_backward(): jnp.stack([jnp.einsum('ecd,ecf->edf', rows, d_gate_linear, preferred_elem...]
  transfers between devices with their start and end apart: 13 -> 37, of which waited for: 9 -> 16; matrix products, arithmetic and copies ran while one was open for 17% -> 3% of each run, Pallas kernels for 0% -> 33%
where the time goes in v1:
time: 740 us; the launch traced here: 730 us
  waiting for transfers between devices  250 us (34%)
  Pallas kernels  250 us (34%)
  starting transfers between devices  77.1 us (10%)
  blocking collectives  71.6 us (10%)
  local copies, waits for them, and re-layouts  45.2 us (6%)
  other arithmetic  20.4 us (3%)
  between operations  15.6 us (2%)
    all_gather x4, waiting for transfers between devices, gathered(): lax.all_gather(values[c * part_rows:(c + 1) * part_rows], 'inner', axis=0...  92.5 us
    all_to_all x4, blocking collectives, to_owner(): return lax.all_to_all(parts, 'inner', 0, 0)  71.6 us
    all_gather x1, waiting for transfers between devices, body(): pack = lax.all_gather(pack_own, fsdp, axis=0, tiled=True)  70.4 us
    pallas_call x2, Pallas kernels, run_experts(): pl.pallas_call(expert_kernel, grid_spec=pltpu.PrefetchScalarGridSpec(num_...  66.7 us
    pallas_call x2, Pallas kernels, run_grads(): pl.pallas_call(functools.partial(grads_kernel, steps), grid=(CHUNKS * ste...  42.9 us
    ppermute x8, starting transfers between devices, inward(): return lax.ppermute(values, 'replica', [(0, 1), (3, 2)])  41.7 us
    pallas_call x6, Pallas kernels, adam_part(): pl.pallas_call(functools.partial(adam_kernel, turned, rate, decay_rate),...  37.1 us
    unnamed x126, local copies, waits for them, and re-layouts  35.3 us
  transfers between devices with their start and end apart: 37, of which 16 were waited for; matrix products, arithmetic and copies ran while one was open for 3% of the time, Pallas kernels for 33%

profile of v1, /device:TPU:2, one launch (start us, length us, event | category | flops | bytes accessed | tf_op | source)
XLA Modules:
  0.0 729.5 jit_solution(7279384925527983356)
XLA Ops:
  17.3 12.8 %split.1 = bf16[8,2,3,128,512]{4,3,2,1,0:T(8,128)(2,1)} custom-call(f32[16,2,128,512]{3,2,1,0:T(8,128)} %w_ref.10, f32[16,512,128]{2,1,0:T(8,128)} %w_ref.11), custom_call_target="tpu_custom_call" | custom-call | tf_op jit(solution)/shard_map/split/pallas_call | solution.py:169
  37.7 70.4 %all-gather.6.cloned.1.call-done.pack_ref.router_ref.output_ref = bf16[1024,3200]{1,0:T(8,128)(2,1)} async-done(((bf16[128,3200]{1,0:T(8,128)(2,1)}), bf16[1024,3200]{1,0:T(8,128)(2,1)}) %all-gather.6.cloned.1.call-update) | async-done | bytes 6553616 | tf_op jit(solution)/shard_map/all_gather | solution.py:677
  109.3 13.0 %all-to-all-done.wait_ref.w_ref.refs_2_ = bf16[8,2,3,128,512]{4,3,2,1,0:T(8,128)(2,1)} async-done(((bf16[8,2,3,128,512]{4,3,2,1,0:T(8,128)(2,1)}), bf16[8,2,3,128,512]{4,3,2,1,0:T(8,128)(2,1)}, u32[]{:S(2)}, u32[]{:S(2)}) %all-to-all-start) | async-done | bytes 6291488 | tf_op jit(solution)/shard_map/all_to_all | solution.py:681
  122.3 19.1 %front.1 = (bf16[512,1024]{1,0:T(8,128)(2,1)}, bf16[512,2048]{1,0:T(8,128)(2,1)}, bf16[512,1024]{1,0:T(8,128)(2,1)}, f32[512,128]{1,0:T(8,128)S(1)}, f32[512,1024]{1,0:T(8,128)}, /*index=5*/bf16[512,1024]{1,0:T(8,128)(2,1)}) custom-call(bf16[512,1024]{1,0:T(8,128)(2,1)} %x_ref.3, ...), custom_call_target="tpu_custom_call" | custom-call | tf_op jit(solution)/shard_map/front/pallas_call | solution.py:241
  145.2 6.6 all-gather.10.cloned.1.call-done.b_ref.refs_1_
  151.9 39.2 %all-gather.8.cloned.1.call-done.x_ref.refs_0_ = bf16[2048,1024]{1,0:T(8,128)(2,1)} async-done(((bf16[256,1024]{1,0:T(8,128)(2,1)}), bf16[2048,1024]{1,0:T(8,128)(2,1)}) %all-gather.8.cloned.1.call-update) | async-done | bytes 4194320 | tf_op jit(solution)/shard_map/all_gather | solution.py:704
  191.1 33.3 %experts.2 = (bf16[2048,1024]{1,0:T(8,128)(2,1)}, bf16[2048,2048]{1,0:T(8,128)(2,1)}, bf16[2048,1152]{1,0:T(8,128)(2,1)}) custom-call(s32[1]{0:T(128)} %bitcast.8.me_ref, bf16[2048,1024]{1,0:T(8,128)(2,1)} %all-gather.8.cloned.1.call-done.x_ref.refs_0_, bf16[2048,1152]{1,0:T(8,128)(2,1)} %all-gather.10.cloned.1.call-done.b_ref.refs_1_, ...), custom_call_target="tpu_custom_call" | custom-call | tf_op jit(solution)/shard_map/experts/pallas_call | solution.py:454
  224.7 7.6 %all-gather.14.cloned.1.call-done.b_ref.refs_5_ = bf16[2048,1152]{1,0:T(8,128)(2,1)} async-done(((bf16[256,1152]{1,0:T(8,128)(2,1)}), bf16[2048,1152]{1,0:T(8,128)(2,1)}) %all-gather.14.cloned.1.call-update) | async-done | bytes 4718608 | tf_op jit(solution)/shard_map/all_gather | solution.py:704
  232.3 39.1 %all-gather.12.cloned.1.call-done.x_ref.refs_4_ = bf16[2048,1024]{1,0:T(8,128)(2,1)} async-done(((bf16[256,1024]{1,0:T(8,128)(2,1)}), bf16[2048,1024]{1,0:T(8,128)(2,1)}) %all-gather.12.cloned.1.call-update) | async-done | bytes 4194320 | tf_op jit(solution)/shard_map/all_gather | solution.py:704
  271.4 33.3 %experts.3 = (bf16[2048,1024]{1,0:T(8,128)(2,1)}, bf16[2048,2048]{1,0:T(8,128)(2,1)}, bf16[2048,1152]{1,0:T(8,128)(2,1)}) custom-call(s32[1]{0:T(128)} %bitcast.8.me_ref, bf16[2048,1024]{1,0:T(8,128)(2,1)} %all-gather.12.cloned.1.call-done.x_ref.refs_4_, bf16[2048,1152]{1,0:T(8,128)(2,1)} %all-gather.14.cloned.1.call-done.b_ref.refs_5_, ...), custom_call_target="tpu_custom_call" | custom-call | tf_op jit(solution)/shard_map/experts/pallas_call | solution.py:454
  304.8 20.7 %grads.2 = (bf16[1024,512]{1,0:T(8,128)(2,1)S(1)}, bf16[1024,512]{1,0:T(8,128)(2,1)}, bf16[1024,512]{1,0:T(8,128)(2,1)}) custom-call(bf16[2048,1024]{1,0:T(8,128)(2,1)} %all-gather.8.cloned.1.call-done.x_ref.refs_0_, bf16[2048,1152]{1,0:T(8,128)(2,1)} %all-gather.10.cloned.1.call-done.b_ref.refs_1_, bf16[2048,1024]{1,0:T(8,128)(2,1)} %get-tuple-element.81.refs_2_.refs_0_, ...), custom_call_target="tpu_custom_call" | custom-call | tf_op jit(solution)/shard_map/grads/pallas_call | solution.py:518
  325.5 17.5 %all_to_all.35.refs_0_ = bf16[8,128,512]{2,1,0:T(8,128)(2,1)S(1)} all-to-all(bf16[8,128,512]{2,1,0:T(8,128)(2,1)S(1)} %bitcast.32), channel_id=1, replica_groups=mesh['replica'=4,'fsdp'=8] {'fsdp'}, dimensions={0} | all-to-all | bytes 2097152 | tf_op jit(solution)/shard_map/all_to_all | solution.py:727
  353.6 14.7 %mixture.1.refs_3_ = bf16[2,2048,1024]{2,1,0:T(8,128)(2,1)} custom-call(bf16[2048,1024]{1,0:T(8,128)(2,1)} %get-tuple-element.81.refs_2_.refs_0_, bf16[2048,1024]{1,0:T(8,128)(2,1)} %get-tuple-element.82.refs_6_.refs_1_, bf16[8,2,3,128,512]{4,3,2,1,0:T(8,128)(2,1)} %all-to-all-done.wait_ref.w_ref.refs_2_, bf16[1024,512]{1,0:T(8,128)(2,1)S(1)} %copy-done.10), custom_call_target="tpu_custom_call" | custom-call | tf_op jit(solution)/shard_map/mixture/pallas_call | solution.py:551
  379.5 14.8 %reduce-scatter.10.cloned.1.call-done.dx_two_ref = bf16[256,1152]{1,0:T(8,128)(2,1)} async-done(((bf16[2048,1152]{1,0:T(8,128)(2,1)}), bf16[256,1152]{1,0:T(8,128)(2,1)}) %reduce-scatter.10.cloned.1.call-update) | async-done | bytes 589840 | tf_op jit(solution)/shard_map/reduce_scatter | solution.py:721
  396.4 10.2 %middle_back.1 = (f32[512,1024]{1,0:T(8,128)}, bf16[512,1024]{1,0:T(8,128)(2,1)}, bf16[1024,1152]{1,0:T(8,128)(2,1)}) custom-call(bf16[256,1152]{1,0:T(8,128)(2,1)S(1)} %copy-done.32, bf16[256,1152]{1,0:T(8,128)(2,1)S(1)} %copy-done.33, bf16[512,1024]{1,0:T(8,128)(2,1)} %get-tuple-element.80.normed_two_ref, f32[512,1024]{1,0:T(8,128)} %get-tuple-element.79.middle_ref, ...), custom_call_target="tpu_custom_call" | custom-call | tf_op jit(solution)/shard_map/middle_back/pallas_call | solution.py:288
  410.9 17.3 %all_to_all.36.refs_4_.refs_0_ = bf16[8,128,512]{2,1,0:T(8,128)(2,1)S(1)} all-to-all(bf16[8,128,512]{2,1,0:T(8,128)(2,1)S(1)} %bitcast.30), channel_id=1, replica_groups=mesh['replica'=4,'fsdp'=8] {'fsdp'}, dimensions={0} | all-to-all | bytes 2097152 | tf_op jit(solution)/shard_map/all_to_all | solution.py:727
  436.1 32.2 %attention_back.1 = (bf16[1024,2176]{1,0:T(8,128)(2,1)}, f32[512,1024]{1,0:T(8,128)}) custom-call(bf16[512,1024]{1,0:T(8,128)(2,1)S(1)} %copy-done.16, bf16[512,2048]{1,0:T(8,128)(2,1)} %get-tuple-element.92.qkv_ref, f32[512,128]{1,0:T(8,128)S(1)} %copy-done.35, f32[512,512]{1,0:T(8,128)} %fusion.3.bias_ref, f32[512,128]{1,0:T(8,128)S(1)} %copy-done.22, ...), custom_call_target="tpu_custom_call" | custom-call | tf_op jit(solution)/shard_map/attention_back/pallas_call | solution.py:391
  477.7 22.2 %grads.3 = (bf16[1024,512]{1,0:T(8,128)(2,1)S(1)}, bf16[1024,512]{1,0:T(8,128)(2,1)}, bf16[1024,512]{1,0:T(8,128)(2,1)}) custom-call(bf16[2048,1024]{1,0:T(8,128)(2,1)} %all-gather.8.cloned.1.call-done.x_ref.refs_0_, bf16[2048,1152]{1,0:T(8,128)(2,1)} %all-gather.10.cloned.1.call-done.b_ref.refs_1_, bf16[2048,1024]{1,0:T(8,128)(2,1)} %get-tuple-element.81.refs_2_.refs_0_, ...), custom_call_target="tpu_custom_call" | custom-call | tf_op jit(solution)/shard_map/grads/pallas_call | solution.py:518
  499.8 17.8 %all_to_all.37.refs_5_.refs_0_ = bf16[8,128,512]{2,1,0:T(8,128)(2,1)S(1)} all-to-all(bf16[8,128,512]{2,1,0:T(8,128)(2,1)S(1)} %bitcast.31), channel_id=1, replica_groups=mesh['replica'=4,'fsdp'=8] {'fsdp'}, dimensions={0} | all-to-all | bytes 2097152 | tf_op jit(solution)/shard_map/all_to_all | solution.py:727
  517.6 7.5 %collective-permute-start.7 = (bf16[8,128,512]{2,1,0:T(8,128)(2,1)S(1)}, bf16[8,128,512]{2,1,0:T(8,128)(2,1)}, u32[]{:S(2)}, u32[]{:S(2)}) collective-permute-start(bf16[8,128,512]{2,1,0:T(8,128)(2,1)S(1)} %all_to_all.37.refs_5_.refs_0_), channel_id=1, source_target_pairs={{0,8},{24,16},{1,9},{25,17},{2,10},{26,18},{3,11},{27,19},{4,12},{... | collective-permute-start | bytes 3145736 | tf_op jit(solution)/shard_map/ppermute | solution.py:730
  535.3 13.9 %all-to-all-done.5.refs_5_.refs_0_ = bf16[8,128,512]{2,1,0:T(8,128)(2,1)S(1)} async-done(((bf16[8,128,512]{2,1,0:T(8,128)(2,1)}), bf16[8,128,512]{2,1,0:T(8,128)(2,1)S(1)}, u32[]{:S(2)}, u32[]{:S(2)}) %all-to-all-start.5) | async-done | bytes 1048608 | tf_op jit(solution)/shard_map/all_to_all | solution.py:727
  549.2 5.9 collective-permute-start.6
  559.9 6.6 adam.6
  571.6 19.0 %all_to_all.38.refs_5_.refs_0_ = bf16[8,128,512]{2,1,0:T(8,128)(2,1)S(1)} all-to-all(bf16[8,128,512]{2,1,0:T(8,128)(2,1)S(1)} %bitcast.33), channel_id=1, replica_groups=mesh['replica'=4,'fsdp'=8] {'fsdp'}, dimensions={0} | all-to-all | bytes 2097152 | tf_op jit(solution)/shard_map/all_to_all | solution.py:727
  590.6 5.9 collective-permute-start.5
  596.5 6.5 adam.7
  619.9 12.0 %collective-permute-done.16.refs_4_.r_ref = bf16[8,128,512]{2,1,0:T(8,128)(2,1)S(1)} collective-permute-done((bf16[8,128,512]{2,1,0:T(8,128)(2,1)}, bf16[8,128,512]{2,1,0:T(8,128)(2,1)S(1)}, u32[]{:S(2)}, u32[]{:S(2)}) %collective-permute-start.16) | collective-permute-done | bytes 1048608 | tf_op jit(solution)/shard_map/ppermute | solution.py:736
  639.0 7.6 %collective-permute-start.3 = (bf16[128,2176]{1,0:T(8,128)(2,1)}, bf16[128,2176]{1,0:T(8,128)(2,1)S(1)}, u32[]{:S(2)}, u32[]{:S(2)}) collective-permute-start(bf16[128,2176]{1,0:T(8,128)(2,1)} %reduce-scatter.12.cloned.1.call-done.refs_5_.refs_0_), channel_id=1, source_target_pairs={{0,8},{24,16},{1,9},{25,17},{2,10},{26,18},{3,11},{27,19},{4,12},{... | collective-permute-start | bytes 1671176 | tf_op jit(solution)/shard_map/ppermute | solution.py:730
  651.3 6.5 adam.9
  677.3 6.2 adam.10
  683.6 8.6 %collective-permute-done.21.refs_4_.r_ref = bf16[8,128,512]{2,1,0:T(8,128)(2,1)S(1)} collective-permute-done((bf16[8,128,512]{2,1,0:T(8,128)(2,1)}, bf16[8,128,512]{2,1,0:T(8,128)(2,1)S(1)}, u32[]{:S(2)}, u32[]{:S(2)}) %collective-permute-start.21) | collective-permute-done | bytes 1048608 | tf_op jit(solution)/shard_map/ppermute | solution.py:736
  704.9 5.8 adam.11
  (252 shorter events, 160.1 us)
Async XLA Ops:
  7.2 100.8 %all-gather.6.cloned.1.call-start = ((), (), s32[]{:S(2)}) async-start(), calls=%async_computation.12 | async-start | bytes 7372800 | tf_op jit(solution)/shard_map/all_gather | solution.py:677
  14.0 137.8 %all-gather.10.cloned.1.call-start = ((), (), s32[]{:S(2)}) async-start(), calls=%async_computation.14 | async-start | bytes 5308416 | tf_op jit(solution)/shard_map/all_gather | solution.py:704
  30.1 92.2 %all-to-all-start = ((bf16[8,2,3,128,512]{4,3,2,1,0:T(8,128)(2,1)}), bf16[8,2,3,128,512]{4,3,2,1,0:T(8,128)(2,1)}, u32[]{:S(2)}, u32[]{:S(2)}) async-start(bf16[8,2,3,128,512]{4,3,2,1,0:T(8,128)(2,1)} %split.1), calls=%async_computation | async-start | bytes 12582912 | tf_op jit(solution)/shard_map/all_to_all | solution.py:681
  34.8 156.3 %all-gather.8.cloned.1.call-start = ((), (), s32[]{:S(2)}) async-start(), calls=%async_computation.13 | async-start | bytes 4718592 | tf_op jit(solution)/shard_map/all_gather | solution.py:704
  143.8 88.5 %all-gather.14.cloned.1.call-start = ((), (), s32[]{:S(2)}) async-start(), calls=%async_computation.16 | async-start | bytes 5308416 | tf_op jit(solution)/shard_map/all_gather | solution.py:704
  144.4 127.0 %all-gather.12.cloned.1.call-start = ((), (), s32[]{:S(2)}) async-start(), calls=%async_computation.15 | async-start | bytes 4718592 | tf_op jit(solution)/shard_map/all_gather | solution.py:704
  145.0 234.5 %reduce-scatter.8.cloned.1.call-start = ((), (), s32[]{:S(2)}) async-start(), calls=%async_computation.18 | async-start | bytes 5308416 | tf_op jit(solution)/shard_map/reduce_scatter | solution.py:721
  224.4 169.9 %reduce-scatter.10.cloned.1.call-start = ((), (), s32[]{:S(2)}) async-start(), calls=%async_computation.19 | async-start | bytes 5308416 | tf_op jit(solution)/shard_map/reduce_scatter | solution.py:721
  342.9 30.7 %collective-permute-start = (bf16[8,128,512]{2,1,0:T(8,128)(2,1)S(1)}, bf16[8,128,512]{2,1,0:T(8,128)(2,1)}, u32[]{:S(2)}, u32[]{:S(2)}) collective-permute-start(bf16[8,128,512]{2,1,0:T(8,128)(2,1)S(1)} %all_to_all.35.refs_0_), channel_id=1, source_target_pairs={{0,8},{24,16},{1,9},{25,17},{2,10},{26,18},{3,11},{27,19},{4,12},{... | collective-permute-start | bytes 3145736 | tf_op jit(solution)/shard_map/ppermute | solution.py:730
  347.3 26.3 %all-to-all-start.2 = ((bf16[8,128,512]{2,1,0:T(8,128)(2,1)}), bf16[8,128,512]{2,1,0:T(8,128)(2,1)S(1)}, u32[]{:S(2)}, u32[]{:S(2)}) async-start(bf16[8,128,512]{2,1,0:T(8,128)(2,1)} %bitcast.35), calls=%async_computation.5 | async-start | bytes 2097152 | tf_op jit(solution)/shard_map/all_to_all | solution.py:727
  352.2 267.6 %reduce-scatter.14.cloned.1.call-start = ((), (), s32[]{:S(2)}) async-start(), calls=%async_computation.21 | async-start | bytes 2654208 | tf_op jit(solution)/shard_map/reduce_scatter | solution.py:791
  406.6 225.2 %reduce-scatter.12.cloned.1.call-start = ((), (), s32[]{:S(2)}) async-start(), calls=%async_computation.20 | async-start | bytes 5013504 | tf_op jit(solution)/shard_map/reduce_scatter | solution.py:798
  406.7 25.8 %collective-permute-start.1 = (bf16[8,128,512]{2,1,0:T(8,128)(2,1)S(1)}, bf16[8,128,512]{2,1,0:T(8,128)(2,1)S(1)}, u32[]{:S(2)}, u32[]{:S(2)}) collective-permute-start(bf16[8,128,512]{2,1,0:T(8,128)(2,1)S(1)} %all-to-all-done.2.refs_2_.refs_0_), channel_id=1, source_target_pairs={{0,8},{24,16},{1,9},{25,17},{2,10},{26,18},{3,11},{27,19},{4,12},{... | collective-permute-start | bytes 3145736 | tf_op jit(solution)/shard_map/ppermute | solution.py:730
  410.1 22.3 %collective-permute-start.2 = (bf16[8,128,512]{2,1,0:T(8,128)(2,1)S(1)}, bf16[8,128,512]{2,1,0:T(8,128)(2,1)S(1)}, u32[]{:S(2)}, u32[]{:S(2)}) collective-permute-start(bf16[8,128,512]{2,1,0:T(8,128)(2,1)S(1)} %copy-done.12), channel_id=1, source_target_pairs={{8,16},{16,8},{9,17},{17,9},{10,18},{18,10},{11,19},{19,11},{12,20... | collective-permute-start | bytes 3145736 | tf_op jit(solution)/shard_map/ppermute | solution.py:733
  468.4 229.7 %reduce-scatter.6.cloned.1.call-start = ((), (), s32[]{:S(2)}) async-start(), calls=%async_computation.17 | async-start | bytes 9437184 | tf_op jit(solution)/shard_map/reduce_scatter | solution.py:822
  469.6 55.5 %collective-permute-start.8 = (bf16[8,128,512]{2,1,0:T(8,128)(2,1)S(1)}, bf16[8,128,512]{2,1,0:T(8,128)(2,1)S(1)}, u32[]{:S(2)}, u32[]{:S(2)}) collective-permute-start(bf16[8,128,512]{2,1,0:T(8,128)(2,1)S(1)} %copy-done.14), channel_id=1, source_target_pairs={{0,8},{24,16},{1,9},{25,17},{2,10},{26,18},{3,11},{27,19},{4,12},{... | collective-permute-start | bytes 3145736 | tf_op jit(solution)/shard_map/ppermute | solution.py:730
  475.3 49.8 %collective-permute-start.10 = (bf16[8,128,512]{2,1,0:T(8,128)(2,1)}, bf16[8,128,512]{2,1,0:T(8,128)(2,1)S(1)}, u32[]{:S(2)}, u32[]{:S(2)}) collective-permute-start(bf16[8,128,512]{2,1,0:T(8,128)(2,1)} %get-tuple-element.103.t_ref), channel_id=1, source_target_pairs={{8,0},{16,24},{9,1},{17,25},{10,2},{18,26},{11,3},{19,27},{12,4},{... | collective-permute-start | bytes 3145736 | tf_op jit(solution)/shard_map/ppermute | solution.py:736
  476.7 48.4 %collective-permute-start.9 = (bf16[8,128,512]{2,1,0:T(8,128)(2,1)S(1)}, bf16[8,128,512]{2,1,0:T(8,128)(2,1)S(1)}, u32[]{:S(2)}, u32[]{:S(2)}) collective-permute-start(bf16[8,128,512]{2,1,0:T(8,128)(2,1)S(1)} %copy-done.18), channel_id=1, source_target_pairs={{8,16},{16,8},{9,17},{17,9},{10,18},{18,10},{11,19},{19,11},{12,20... | collective-permute-start | bytes 3145736 | tf_op jit(solution)/shard_map/ppermute | solution.py:733
  517.6 48.9 %collective-permute-start.7 = (bf16[8,128,512]{2,1,0:T(8,128)(2,1)S(1)}, bf16[8,128,512]{2,1,0:T(8,128)(2,1)}, u32[]{:S(2)}, u32[]{:S(2)}) collective-permute-start(bf16[8,128,512]{2,1,0:T(8,128)(2,1)S(1)} %all_to_all.37.refs_5_.refs_0_), channel_id=1, source_target_pairs={{0,8},{24,16},{1,9},{25,17},{2,10},{26,18},{3,11},{27,19},{4,12},{... | collective-permute-start | bytes 3145736 | tf_op jit(solution)/shard_map/ppermute | solution.py:730
  526.8 39.6 %collective-permute-start.12 = (bf16[8,128,512]{2,1,0:T(8,128)(2,1)}, bf16[8,128,512]{2,1,0:T(8,128)(2,1)S(1)}, u32[]{:S(2)}, u32[]{:S(2)}) collective-permute-start(bf16[8,128,512]{2,1,0:T(8,128)(2,1)} %get-tuple-element.105.t_ref), channel_id=1, source_target_pairs={{8,0},{16,24},{9,1},{17,25},{10,2},{18,26},{11,3},{19,27},{12,4},{... | collective-permute-start | bytes 3145736 | tf_op jit(solution)/shard_map/ppermute | solution.py:736
  528.1 38.4 %collective-permute-start.11 = (bf16[8,128,512]{2,1,0:T(8,128)(2,1)}, bf16[8,128,512]{2,1,0:T(8,128)(2,1)}, u32[]{:S(2)}, u32[]{:S(2)}) collective-permute-start(bf16[8,128,512]{2,1,0:T(8,128)(2,1)} %get-tuple-element.104.rest_0_.refs_2_), channel_id=1, source_target_pairs={{8,16},{16,8},{9,17},{17,9},{10,18},{18,10},{11,19},{19,11},{12,20... | collective-permute-start | bytes 3145736 | tf_op jit(solution)/shard_map/ppermute | solution.py:733
  529.8 19.5 %all-to-all-start.5 = ((bf16[8,128,512]{2,1,0:T(8,128)(2,1)}), bf16[8,128,512]{2,1,0:T(8,128)(2,1)S(1)}, u32[]{:S(2)}, u32[]{:S(2)}) async-start(bf16[8,128,512]{2,1,0:T(8,128)(2,1)} %bitcast.34), calls=%async_computation.10 | async-start | bytes 2097152 | tf_op jit(solution)/shard_map/all_to_all | solution.py:727
  549.2 53.8 %collective-permute-start.6 = (bf16[8,128,512]{2,1,0:T(8,128)(2,1)S(1)}, bf16[8,128,512]{2,1,0:T(8,128)(2,1)S(1)}, u32[]{:S(2)}, u32[]{:S(2)}) collective-permute-start(bf16[8,128,512]{2,1,0:T(8,128)(2,1)S(1)} %all-to-all-done.5.refs_5_.refs_0_), channel_id=1, source_target_pairs={{0,8},{24,16},{1,9},{25,17},{2,10},{26,18},{3,11},{27,19},{4,12},{... | collective-permute-start | bytes 3145736 | tf_op jit(solution)/shard_map/ppermute | solution.py:730
  569.1 33.9 %collective-permute-start.14 = (bf16[8,128,512]{2,1,0:T(8,128)(2,1)S(1)}, bf16[8,128,512]{2,1,0:T(8,128)(2,1)S(1)}, u32[]{:S(2)}, u32[]{:S(2)}) collective-permute-start(bf16[8,128,512]{2,1,0:T(8,128)(2,1)S(1)} %get-tuple-element.108.t_ref), channel_id=1, source_target_pairs={{8,0},{16,24},{9,1},{17,25},{10,2},{18,26},{11,3},{19,27},{12,4},{... | collective-permute-start | bytes 3145736 | tf_op jit(solution)/shard_map/ppermute | solution.py:736
  570.7 32.3 %collective-permute-start.13 = (bf16[8,128,512]{2,1,0:T(8,128)(2,1)S(1)}, bf16[8,128,512]{2,1,0:T(8,128)(2,1)S(1)}, u32[]{:S(2)}, u32[]{:S(2)}) collective-permute-start(bf16[8,128,512]{2,1,0:T(8,128)(2,1)S(1)} %get-tuple-element.107.rest_3_.refs_2_), channel_id=1, source_target_pairs={{8,16},{16,8},{9,17},{17,9},{10,18},{18,10},{11,19},{19,11},{12,20... | collective-permute-start | bytes 3145736 | tf_op jit(solution)/shard_map/ppermute | solution.py:733
  590.6 28.3 %collective-permute-start.5 = (bf16[8,128,512]{2,1,0:T(8,128)(2,1)S(1)}, bf16[8,128,512]{2,1,0:T(8,128)(2,1)S(1)}, u32[]{:S(2)}, u32[]{:S(2)}) collective-permute-start(bf16[8,128,512]{2,1,0:T(8,128)(2,1)S(1)} %all_to_all.38.refs_5_.refs_0_), channel_id=1, source_target_pairs={{0,8},{24,16},{1,9},{25,17},{2,10},{26,18},{3,11},{27,19},{4,12},{... | collective-permute-start | bytes 3145736 | tf_op jit(solution)/shard_map/ppermute | solution.py:730
  604.8 27.1 %collective-permute-start.16 = (bf16[8,128,512]{2,1,0:T(8,128)(2,1)}, bf16[8,128,512]{2,1,0:T(8,128)(2,1)S(1)}, u32[]{:S(2)}, u32[]{:S(2)}) collective-permute-start(bf16[8,128,512]{2,1,0:T(8,128)(2,1)} %get-tuple-element.113.t_ref), channel_id=1, source_target_pairs={{8,0},{16,24},{9,1},{17,25},{10,2},{18,26},{11,3},{19,27},{12,4},{... | collective-permute-start | bytes 3145736 | tf_op jit(solution)/shard_map/ppermute | solution.py:736
  606.3 25.5 %collective-permute-start.15 = (bf16[8,128,512]{2,1,0:T(8,128)(2,1)}, bf16[8,128,512]{2,1,0:T(8,128)(2,1)S(1)}, u32[]{:S(2)}, u32[]{:S(2)}) collective-permute-start(bf16[8,128,512]{2,1,0:T(8,128)(2,1)} %get-tuple-element.112.rest_0_.refs_2_), channel_id=1, source_target_pairs={{8,16},{16,8},{9,17},{17,9},{10,18},{18,10},{11,19},{19,11},{12,20... | collective-permute-start | bytes 3145736 | tf_op jit(solution)/shard_map/ppermute | solution.py:733
  637.0 26.8 %collective-permute-start.18 = (bf16[8,128,512]{2,1,0:T(8,128)(2,1)S(1)}, bf16[8,128,512]{2,1,0:T(8,128)(2,1)S(1)}, u32[]{:S(2)}, u32[]{:S(2)}) collective-permute-start(bf16[8,128,512]{2,1,0:T(8,128)(2,1)S(1)} %get-tuple-element.116.t_ref), channel_id=1, source_target_pairs={{8,0},{16,24},{9,1},{17,25},{10,2},{18,26},{11,3},{19,27},{12,4},{... | collective-permute-start | bytes 3145736 | tf_op jit(solution)/shard_map/ppermute | solution.py:736
  638.3 25.5 %collective-permute-start.17 = (bf16[8,128,512]{2,1,0:T(8,128)(2,1)S(1)}, bf16[8,128,512]{2,1,0:T(8,128)(2,1)S(1)}, u32[]{:S(2)}, u32[]{:S(2)}) collective-permute-start(bf16[8,128,512]{2,1,0:T(8,128)(2,1)S(1)} %get-tuple-element.115.rest_3_.refs_4_), channel_id=1, source_target_pairs={{8,16},{16,8},{9,17},{17,9},{10,18},{18,10},{11,19},{19,11},{12,20... | collective-permute-start | bytes 3145736 | tf_op jit(solution)/shard_map/ppermute | solution.py:733
  639.0 24.4 %collective-permute-start.3 = (bf16[128,2176]{1,0:T(8,128)(2,1)}, bf16[128,2176]{1,0:T(8,128)(2,1)S(1)}, u32[]{:S(2)}, u32[]{:S(2)}) collective-permute-start(bf16[128,2176]{1,0:T(8,128)(2,1)} %reduce-scatter.12.cloned.1.call-done.refs_5_.refs_0_), channel_id=1, source_target_pairs={{0,8},{24,16},{1,9},{25,17},{2,10},{26,18},{3,11},{27,19},{4,12},{... | collective-permute-start | bytes 1671176 | tf_op jit(solution)/shard_map/ppermute | solution.py:730
  666.1 26.0 %collective-permute-start.21 = (bf16[8,128,512]{2,1,0:T(8,128)(2,1)}, bf16[8,128,512]{2,1,0:T(8,128)(2,1)S(1)}, u32[]{:S(2)}, u32[]{:S(2)}) collective-permute-start(bf16[8,128,512]{2,1,0:T(8,128)(2,1)} %get-tuple-element.122.t_ref), channel_id=1, source_target_pairs={{8,0},{16,24},{9,1},{17,25},{10,2},{18,26},{11,3},{19,27},{12,4},{... | collective-permute-start | bytes 3145736 | tf_op jit(solution)/shard_map/ppermute | solution.py:736
  (66 other events, 904.9 us)
Sparse Core Ops, SparseCore 0:
  14.2 93.8 all-gather.5
  110.5 41.3 all-gather.9
  154.3 36.7 all-gather.7
  193.4 38.9 all-gather.13
  234.6 36.7 all-gather.11
  275.3 53.8 reduce-scatter.7
  332.9 61.3 reduce-scatter.9
  406.7 42.4 reduce-scatter.13
  468.5 57.8 reduce-scatter.11
  529.7 76.3 reduce-scatter.5

commit v2 on v1

--- a/solution.py
+++ b/solution.py
@@ -146,6 +146,12 @@
 ANYWHERE = pl.BlockSpec(memory_space=pl.ANY)
 
 
+def takes(microseconds):
+    return pl.CostEstimate(
+        flops=int(microseconds * 1e9), bytes_accessed=int(microseconds * 3.6e6), transcendentals=0
+    )
+
+
 def whole(shape):
     return pl.BlockSpec(shape, lambda *_: (0,) * len(shape), pipeline_mode=pl.Buffered(1))
 
@@ -159,22 +165,24 @@
 
 
 def split_kernel(gateup_ref, down_ref, out_ref):
-    out_ref[0, 0, 0] = gateup_ref[0, 0].astype(brain_floating)
-    out_ref[0, 0, 1] = gateup_ref[0, 1].astype(brain_floating)
-    out_ref[0, 0, 2] = down_ref[0].T.astype(brain_floating)
+    for k in range(2):
+        out_ref[k, 0, 0] = gateup_ref[k, 0].astype(brain_floating)
+        out_ref[k, 0, 1] = gateup_ref[k, 1].astype(brain_floating)
+        out_ref[k, 0, 2] = down_ref[k].T.astype(brain_floating)
 
 
 def split_by_owner(gateup, down):
     shard = gateup.shape[2]
+    steps = GROUP // 2
     return pl.pallas_call(
         split_kernel,
-        grid=(EXPERTS,),
+        grid=(EXPERTS // 2,),
         in_specs=[
-            pl.BlockSpec((1, 2, shard, F), lambda e: (e, 0, 0, 0)),
-            pl.BlockSpec((1, F, shard), lambda e: (e, 0, 0)),
+            pl.BlockSpec((2, 2, shard, F), lambda e: (e, 0, 0, 0)),
+            pl.BlockSpec((2, F, shard), lambda e: (e, 0, 0)),
         ],
         out_specs=pl.BlockSpec(
-            (1, 1, 3, shard, F), lambda e: (lax.rem(e, GROUP), e // GROUP, 0, 0, 0)
+            (2, 1, 3, shard, F), lambda e: (lax.rem(e, steps), e // steps, 0, 0, 0)
         ),
         out_shape=out((GROUP, LOCAL, 3, shard, F), brain_floating),
         name="split",
@@ -306,13 +314,14 @@
             out((MODEL_WIDTH, MODEL_WIDTH + EXTRA), brain_floating),
         ],
         compiler_params=pltpu.CompilerParams(vmem_limit_bytes=52 * MIB),
+        cost_estimate=takes(30),
         name="middle_back",
     )(dx_one, dx_two, normed_two, middle, cot, mask, alive, gains, pack, pack, mixed, wait)
 
 
 def back_kernel(
     d_mixed_ref, qkv_ref, totals_ref, bias_ref, cos_ref, sin_ref, normed_ref, x_ref, d_middle_ref,
-    gains_ref, pack_ref, wait_ref, grads_ref, d_input_ref, d_linear_ref, d_keys_ref, d_values_ref,
+    gains_ref, other_ref, pack_ref, wait_ref, also_ref, grads_ref, d_input_ref, d_linear_ref, d_keys_ref, d_values_ref,
 ):
     rows = x_ref.shape[0]
     cosine, sine = (cos_ref[...], -sin_ref[...])
@@ -379,23 +388,27 @@
     d_normed = times_transposed(d_linear_ref[...], pack_ref[...])
     scaled, inverse = normalize(x_ref[...].astype(jnp.float32))
     sums = column_sums(d_normed * scaled)
-    grads_ref[:, PROJECTED:] = jnp.where(lanes_of(sums.shape) == 0, sums, 0.0).astype(
-        brain_floating
-    )
+    grads_ref[:, PROJECTED : PROJECTED + EXTRA] = jnp.where(
+        lanes_of(sums.shape) == 0, sums, 0.0
+    ).astype(brain_floating)
+    grads_ref[:, PROJECTED + EXTRA :] = other_ref[...]
     d_input_ref[...] = d_middle_ref[...] + norm_back(d_normed, scaled, inverse, gains_ref[0:1, :])
 
 
-def run_back(d_mixed, qkv, totals, bias, cosine, sine, normed, x, d_middle, gains, pack, wait):
+def run_back(
+    d_mixed, qkv, totals, bias, cosine, sine, normed, x, d_middle, gains, other, pack, wait, also
+):
     rows = x.shape[0]
-    held = (d_mixed, qkv, totals, bias, cosine, sine, normed, x, d_middle, gains)
+    held = (d_mixed, qkv, totals, bias, cosine, sine, normed, x, d_middle, gains, other)
+    width = PROJECTED + EXTRA + other.shape[1]
     return pl.pallas_call(
         back_kernel,
         grid=(1,),
         in_specs=[whole(v.shape) for v in held]
-        + [part((MODEL_WIDTH, PROJECTED), (0, 0)), ANYWHERE],
-        out_specs=[whole((MODEL_WIDTH, PROJECTED + EXTRA)), whole((rows, MODEL_WIDTH))],
+        + [part((MODEL_WIDTH, PROJECTED), (0, 0)), ANYWHERE, ANYWHERE],
+        out_specs=[whole((MODEL_WIDTH, width)), whole((rows, MODEL_WIDTH))],
         out_shape=[
-            out((MODEL_WIDTH, PROJECTED + EXTRA), brain_floating),
+            out((MODEL_WIDTH, width), brain_floating),
             out((rows, MODEL_WIDTH), jnp.float32),
         ],
         scratch_shapes=[
@@ -404,14 +417,15 @@
             pltpu.VMEM((rows, LANES), jnp.float32),
         ],
         compiler_params=pltpu.CompilerParams(vmem_limit_bytes=52 * MIB),
+        cost_estimate=takes(30),
         name="attention_back",
-    )(*held, pack, wait)
+    )(*held, pack, wait, also)
 
 
 def expert_kernel(me_ref, x_ref, b_ref, w_ref, router_ref, ga_ref, dgu_ref, dx_ref):
     x = x_ref[...]
-    branch = b_ref[:, :MODEL_WIDTH]
-    mask = b_ref[:, MODEL_WIDTH:].astype(jnp.float32) > 0.5
+    branch = b_ref[:, 0, :, :MODEL_WIDTH].reshape(x.shape)
+    mask = b_ref[:, 0, :, MODEL_WIDTH:].reshape(x.shape[0], EXTRA).astype(jnp.float32) > 0.5
     gates = gates_of(x, router_ref[...], mask)
     lane = lanes_of(gates.shape)
     d_gates = jnp.zeros_like(gates)
@@ -443,9 +457,10 @@
     dx_ref[:, MODEL_WIDTH:] = d_gates.astype(brain_floating)
 
 
-def run_experts(me, x, b, weights, pack):
+def run_experts(me, c, x, b, weights, pack):
     rows = x.shape[0]
-    tile = min(TILE, rows)
+    part_rows = b.shape[2]
+    tile = 2 * part_rows
     wide = MODEL_WIDTH + EXTRA
 
     def rowed(width):
@@ -458,7 +473,7 @@
             grid=(rows // tile,),
             in_specs=[
                 rowed(MODEL_WIDTH),
-                rowed(wide),
+                pl.BlockSpec((2, 1, part_rows, wide), lambda i, me_ref: (i, c, 0, 0)),
                 whole(weights.shape),
                 part((MODEL_WIDTH, EXTRA), (0, ROUTER_BLOCK)),
             ],
@@ -474,15 +489,20 @@
     )(me, x, b, weights, pack)
 
 
-def chunked_specs(count, tile, steps, width, column):
+def chunked_specs(steps, shape, place):
     def index(c):
-        return lambda i, *_: (jnp.clip(i - c * steps, 0, steps - 1), column)
-
-    return [pl.BlockSpec((tile, width), index(c)) for c in range(count)]
-
-
-def grads_kernel(steps, *refs):
-    ins, wait_ref, outs, sums = (refs[:-7], refs[-7], refs[-6:-3], refs[-3:])
+        return lambda i, *_: place(jnp.clip(i - c * steps, 0, steps - 1), c)
+
+    return [pl.BlockSpec(shape, index(c)) for c in range(CHUNKS)]
+
+
+def grads_kernel(steps, sides, *refs):
+    count = len(sides)
+    ins, outs, sums = (
+        refs[: CHUNKS * 2 * count],
+        refs[CHUNKS * 2 * count + 1 : -count],
+        refs[-count:],
+    )
     i = pl.program_id(0)
 
     @pl.when(i == 0)
@@ -494,11 +514,11 @@
 
         @pl.when(i // steps == c)
         def _():
-            x_ref, b_ref, ga_ref, dgu_ref = ins[4 * c : 4 * c + 4]
-            x = x_ref[...]
-            sums[0][...] += transposed_times(x, dgu_ref[:, :F])
-            sums[1][...] += transposed_times(x, dgu_ref[:, F:])
-            sums[2][...] += transposed_times(b_ref[...], ga_ref[...])
+            for k in range(count):
+                left, right = (ins[2 * (k * CHUNKS + c)], ins[2 * (k * CHUNKS + c) + 1])
+                sums[k][...] += transposed_times(
+                    left[...].reshape(right.shape[0], MODEL_WIDTH), right[...]
+                )
 
     @pl.when(i == CHUNKS * steps - 1)
     def _():
@@ -506,80 +526,103 @@
             result[...] = total[...].astype(brain_floating)
 
 
-def run_grads(local, xs, bs, gas, dgus, wait):
-    tile = min(TILE, xs[0].shape[0])
-    steps = xs[0].shape[0] // tile
-    columns = (
-        chunked_specs(CHUNKS, tile, steps, MODEL_WIDTH, 0),
-        chunked_specs(CHUNKS, tile, steps, MODEL_WIDTH, 0),
-        chunked_specs(CHUNKS, tile, steps, F, local),
-        chunked_specs(CHUNKS, tile, steps, 2 * F, local),
-    )
+def run_grads(local, sides, xs, b, gas, dgus, wait, cost):
+    rows, part_rows = (xs[0].shape[0], b.shape[2])
+    tile = 2 * part_rows
+    steps = rows // tile
+    specs, arrays = ([], [])
+    for side in sides:
+        if side == 2:
+            left = chunked_specs(
+                steps, (2, 1, part_rows, MODEL_WIDTH), lambda i, c: (i, c, 0, 0)
+            )
+            right = chunked_specs(steps, (tile, F), lambda i, c: (i, local))
+        else:
+            left = chunked_specs(steps, (tile, MODEL_WIDTH), lambda i, c: (i, 0))
+            right = chunked_specs(
+                steps, (tile, F), lambda i, c, side=side: (i, 2 * local + side)
+            )
+        for c in range(CHUNKS):
+            specs += [left[c], right[c]]
+            arrays += [b, gas[c]] if side == 2 else [xs[c], dgus[c]]
     return pl.pallas_call(
-        functools.partial(grads_kernel, steps),
+        functools.partial(grads_kernel, steps, sides),
         grid=(CHUNKS * steps,),
-        in_specs=[columns[k][c] for c in range(CHUNKS) for k in range(4)] + [ANYWHERE],
-        out_specs=[whole((MODEL_WIDTH, F))] * 3,
-        out_shape=[out((MODEL_WIDTH, F), brain_floating)] * 3,
-        scratch_shapes=[pltpu.VMEM((MODEL_WIDTH, F), jnp.float32)] * 3,
+        in_specs=specs + [ANYWHERE],
+        out_specs=[whole((MODEL_WIDTH, F))] * len(sides),
+        out_shape=[out((MODEL_WIDTH, F), brain_floating)] * len(sides),
+        scratch_shapes=[pltpu.VMEM((MODEL_WIDTH, F), jnp.float32)] * len(sides),
         compiler_params=pltpu.CompilerParams(vmem_limit_bytes=52 * MIB),
+        cost_estimate=takes(cost),
         name="grads",
-    )(*[v[c] for c in range(CHUNKS) for v in (xs, bs, gas, dgus)], wait)
-
-
-def mix_kernel(steps, *refs):
-    gas, w_ref, out_ref = (refs[:CHUNKS], refs[CHUNKS], refs[-1])
-    i = pl.program_id(0)
-    for c in range(CHUNKS):
-
-        @pl.when(i // steps == c)
-        def _():
-            total = jnp.zeros((gas[c].shape[0], MODEL_WIDTH), jnp.float32)
-            for local in range(LOCAL):
-                total += times_transposed(
-                    gas[c][:, local * F : (local + 1) * F],
-                    w_ref[:, local, 0].reshape(MODEL_WIDTH, F),
-                )
-            out_ref[0] = total.astype(brain_floating)
-
-
-def run_mix(gas, weights, wait):
-    rows = gas[0].shape[0]
+    )(*arrays, wait)
+
+
+def mix_kernel(ga_ref, w_ref, wait_ref, out_ref):
+    total = jnp.zeros((ga_ref.shape[0], MODEL_WIDTH), jnp.float32)
+    for local in range(LOCAL):
+        total += times_transposed(
+            ga_ref[:, local * F : (local + 1) * F], w_ref[:, local, 0].reshape(MODEL_WIDTH, F)
+        )
+    out_ref[...] = total.astype(brain_floating)
+
+
+def run_mix(ga, weights, wait, cost):
+    rows = ga.shape[0]
     tile = min(TILE, rows)
-    steps = rows // tile
     blocks, _, _, shard, _ = weights.shape
     return pl.pallas_call(
-        functools.partial(mix_kernel, steps),
-        grid=(CHUNKS * steps,),
-        in_specs=chunked_specs(CHUNKS, tile, steps, LOCAL * F, 0)
-        + [part((blocks, LOCAL, 1, shard, F), (0, 0, 2, 0, 0)), ANYWHERE],
-        out_specs=pl.BlockSpec(
-            (1, tile, MODEL_WIDTH), lambda i: (i // steps, lax.rem(i, steps), 0)
-        ),
-        out_shape=out((CHUNKS, rows, MODEL_WIDTH), brain_floating),
+        mix_kernel,
+        grid=(rows // tile,),
+        in_specs=[
+            pl.BlockSpec((tile, LOCAL * F), lambda i: (i, 0)),
+            part((blocks, LOCAL, 1, shard, F), (0, 0, 2, 0, 0)),
+            ANYWHERE,
+        ],
+        out_specs=pl.BlockSpec((tile, MODEL_WIDTH), lambda i: (i, 0)),
+        out_shape=out((rows, MODEL_WIDTH), brain_floating),
         compiler_params=pltpu.CompilerParams(vmem_limit_bytes=52 * MIB),
+        cost_estimate=takes(cost),
         name="mixture",
-    )(*gas, weights, wait)
-
-
-def sums_kernel(count, waits, *refs):
-    ins, outs = (refs[: 2 * count], refs[2 * count + waits :])
+    )(ga, weights, wait)
+
+
+def sums_kernel(count, copies, waits, *refs):
+    ins, outs = (refs[: 2 * count + copies], refs[2 * count + copies + waits :])
     for k in range(count):
         left, right = (ins[2 * k][...], ins[2 * k + 1][...])
         outs[k][...] = (left.astype(jnp.float32) + right.astype(jnp.float32)).astype(
             brain_floating
         )
-
-
-def run_sums(pairs, waits):
-    flat = [v for pair in pairs for v in pair]
+    for k in range(copies):
+        outs[count + k][...] = ins[2 * count + k][...]
+
+
+def run_sums(pairs, copies, waits):
+    flat = [v for pair in pairs for v in pair] + list(copies)
     return pl.pallas_call(
-        functools.partial(sums_kernel, len(pairs), len(waits)),
+        functools.partial(sums_kernel, len(pairs), len(copies), len(waits)),
         in_specs=[pl.BlockSpec(memory_space=pltpu.VMEM)] * len(flat) + [ANYWHERE] * len(waits),
-        out_shape=[out(pair[0].shape, brain_floating) for pair in pairs],
+        out_shape=[out(v.shape, brain_floating) for v in [pair[0] for pair in pairs] + list(copies)],
         compiler_params=pltpu.CompilerParams(vmem_limit_bytes=40 * MIB),
+        cost_estimate=takes(2),
         name="sums",
     )(*flat, *waits)
+
+
+def after_kernel(values_ref, wait_ref, out_ref):
+    del values_ref, wait_ref, out_ref
+
+
+def after(values, wait):
+    return pl.pallas_call(
+        after_kernel,
+        in_specs=[ANYWHERE] * 2,
+        out_specs=ANYWHERE,
+        out_shape=out(values.shape, values.dtype),
+        input_output_aliases={0: 0},
+        name="after",
+    )(values, wait)
 
 
 def adam_kernel(turned, rate, shrink, place_ref, t_ref, r_ref, w_ref, m_ref, v_ref, *rest):
@@ -600,7 +643,7 @@
         w_out[at] = renewed
 
 
-def adam_part(place, total, ends, state, local, side, rate, before, wait):
+def adam_part(place, total, ends, state, local, side, rate, before, wait, cost):
     weight, first, second = state
     turned = side == 2
     shard = total.shape[1]
@@ -621,6 +664,7 @@
         out_shape=[out(weight.shape, jnp.float32)] * 3,
         input_output_aliases={6 + i: i for i in range(len(held))},
         compiler_params=pltpu.CompilerParams(vmem_limit_bytes=40 * MIB),
+        cost_estimate=takes(cost),
         name="adam",
     )(place, total, ends, weight, first, second, *held, wait)
 
@@ -705,7 +749,9 @@
             values[c * part_rows : (c + 1) * part_rows], "inner", axis=0, tiled=True
         )
 
-    branch_all = [gathered(branch_pack, c) for c in range(CHUNKS)]
+    branch_all = lax.all_gather(branch_pack, "inner", axis=0, tiled=True).reshape(
+        GROUP, CHUNKS, part_rows, MODEL_WIDTH + EXTRA
+    )
 
     normed, qkv, mixed, totals, middle, normed_two = run_front(
         tokens_in, pack, gains_value, alive, bias, cosine, sine, weights
@@ -714,7 +760,7 @@
     x_all, ga_all, dgu_all, dx_parts = ([], [], [], [])
     for c in range(CHUNKS):
         x_part = gathered(normed_two, c)
-        ga, dgu, dx = run_experts(me, x_part, branch_all[c], weights, pack)
+        ga, dgu, dx = run_experts(me, c, x_part, branch_all, weights, pack)
         x_all.append(x_part)
         ga_all.append(ga)
         dgu_all.append(dgu)
@@ -735,99 +781,102 @@
     def outward(values):
         return lax.ppermute(values, "replica", [(1, 0), (2, 3)])
 
-    grads = [list(run_grads(0, x_all, branch_all, ga_all, dgu_all, dgu_all[-1])), None]
-    queue = {0: (to_owner(grads[0][0]),)}
-    gateup_new, down_new = (None, None)
-    held = {"token": grads[0][0]}
-    halves, sums, ends = ({}, {}, {})
+    def grads_of(local, sides, wait, cost):
+        return run_grads(local, sides, x_all, branch_all, ga_all, dgu_all, wait, cost)
+
+    chunks = [(local, side) for local in range(LOCAL) for side in (2, 0, 1)]
+    last = len(chunks) + 1
     root = MODEL_WIDTH ** (-0.5)
-    gateup_state = (gateup_weight, gateup_first, gateup_second)
-    down_state = (down_weight, down_first, down_second)
-
-    def adam_of(k, wait):
-        nonlocal gateup_new, down_new
-        local, side = divmod(k, 3)
-        if side == 2:
-            down_new = adam_part(
-                place, sums[k][0], ends[k][0], down_state, local, side, (F // 16) ** (-0.5),
-                down_new, wait,
-            )
-            return down_new[0]
-        gateup_new = adam_part(
-            place, sums[k][0], ends[k][0], gateup_state, local, side, root, gateup_new, wait
+    states = (
+        (gateup_weight, gateup_first, gateup_second),
+        (down_weight, down_first, down_second),
+    )
+    renewed = [None, None]
+    totals_of, ends = ({}, {})
+
+    def adam_of(k, wait, cost):
+        local, side = chunks[k]
+        which = side // 2
+        renewed[which] = adam_part(
+            place, totals_of[k], ends[k], states[which], local, side,
+            (F // 16) ** (-0.5) if which else root, renewed[which], wait, cost,
         )
-        return gateup_new[0]
-
-    count = 3 * LOCAL + 1
-    token = grads[0][2]
-    for k in range(-1, count + 2):
-        arrived, waits = ([], [])
-        if k in queue:
-            halves[k] = tuple(inward(v) for v in queue[k])
-            arrived += list(zip(queue[k], halves[k]))
-        if k - 1 in queue:
-            crossed = tuple(across(v) for v in sums[k - 1])
-            arrived += list(zip(sums[k - 1], crossed))
-        if k - 2 in queue:
-            ends[k - 2] = tuple(outward(v) for v in sums[k - 2])
-            waits += list(ends[k - 2])
-        if 0 <= k + 1 < 3 * LOCAL and k + 1 not in queue:
-            local, side = divmod(k + 1, 3)
-            queue[k + 1] = (to_owner(grads[local][side]),)
-        if k + 1 in queue:
-            waits += list(queue[k + 1])
-
+        return renewed[which][0]
+
+    first = grads_of(0, (2,), dgu_all[-1], 1)
+    ready = {0: first[0]}
+    token = first[0]
+    mine, by_pairs = ({}, {})
+    mixtures_own = []
+
+    def mix_of(c, wait, cost):
+        rows = run_mix(ga_all[c], weights, wait, cost)
+        mixtures_own.append(lax.psum_scatter(rows, "inner", scatter_dimension=0, tiled=True))
+        return rows
+
+    for k in range(-1, last + 3):
+        pairs, copies, waits, keep = ([], [], [], [])
+        if k in mine:
+            pairs.append((mine[k], inward(mine[k])))
+            keep.append((by_pairs, k))
+        if k - 1 in by_pairs:
+            pairs.append((by_pairs[k - 1], across(by_pairs[k - 1])))
+            keep.append((totals_of, k - 1))
+        if k - 2 in totals_of:
+            ends[k - 2] = outward(totals_of[k - 2])
+            waits.append(ends[k - 2])
+
+        arrived = None
+        if 0 <= k + 1 < len(chunks):
+            arrived = to_owner(after(ready[k + 1], token) if k >= 0 else ready[k + 1])
         if k == -1:
-            grads[1] = list(run_grads(1, x_all, branch_all, ga_all, dgu_all, token))
-            waits += [grads[1][0]]
+            ready[1], ready[2] = grads_of(0, (0, 1), token, 1)
+            done = ready[1]
         elif k == 0:
-            mixture = run_mix(ga_all, weights, token)
-            waits += [mixture]
+            ready[3], ready[4], ready[5] = grads_of(1, (2, 0, 1), token, 6)
+            done = ready[3]
         elif k == 1:
+            done = mix_of(0, token, 6)
+        elif k == 2:
             d_middle, d_mixed, second_grads = run_middle(
                 dx_parts[0], dx_parts[1], normed_two, middle, cotangent, mask, alive, gains_value,
                 pack, mixed, token,
             )
-            second_part = lax.psum_scatter(second_grads, fsdp, scatter_dimension=0, tiled=True)
-            waits += [d_mixed]
-        elif k == 2:
-            first_grads, input_gradient = run_back(
+            done = d_mixed
+        elif k == 3:
+            rest_grads, input_gradient = run_back(
                 d_mixed, qkv, totals, bias, cosine, sine, normed, tokens_in, d_middle, gains_value,
-                pack, token,
+                second_grads, pack, token, token,
             )
-            first_part = lax.psum_scatter(first_grads, fsdp, scatter_dimension=0, tiled=True)
-            queue[count - 1] = (first_part, second_part)
-            waits += [input_gradient]
-        elif k - 3 in ends and k - 3 < 3 * LOCAL:
-            waits += [adam_of(k - 3, token)]
-
-        if not arrived:
-            continue
-        results = run_sums(arrived, waits)
-        token = results[0]
-        if k in queue:
-            size = len(queue[k])
-            sums[k] = None
-            halves[k], results = (tuple(results[:size]), results[size:])
-        if k - 1 in queue:
-            crossed_sums = tuple(results)
-        if k - 1 in queue:
-            sums[k - 1] = crossed_sums
-        if k in queue:
-            sums[k] = halves[k]
-    for k in range(3 * LOCAL):
-        if k + 3 > count + 1:
-            adam_of(k, token)
-
-    mixture_own = lax.psum_scatter(mixture, "inner", scatter_dimension=1, tiled=True)
-    mixture_own = mixture_own.reshape(count_of_rows, MODEL_WIDTH).astype(jnp.float32)
+            rest_own = lax.psum_scatter(rest_grads, fsdp, scatter_dimension=0, tiled=True)
+            waits.append(mixtures_own[0])
+            done = input_gradient
+        elif k == 4:
+            done = adam_of(0, mix_of(1, token, 200), 1)
+        elif k == 5:
+            done = adam_of(2, adam_of(1, token, 200), 1)
+        elif k - 3 < len(chunks):
+            done = adam_of(k - 3, token, 200)
+        waits.append(done)
+
+        if 0 <= k + 1 < len(chunks):
+            copies.append(arrived)
+            keep.append((mine, k + 1))
+        elif k + 1 == last:
+            copies.append(rest_own)
+            keep.append((mine, k + 1))
+        if pairs or copies:
+            results = run_sums(pairs, copies, waits)
+            token = results[0]
+            for (kept, at), value in zip(keep, results):
+                kept[at] = value
+
+    mixture_own = jnp.concatenate(mixtures_own, axis=0).astype(jnp.float32)
     block_output = (middle + alive * mixture_own).astype(brain_floating)
 
     inner = (place[0] == 1) | (place[0] == 2)
-    first_sum, second_sum = (
-        jnp.where(inner, total, end).astype(jnp.float32)
-        for total, end in zip(sums[count - 1], ends[count - 1])
-    )
+    rest_sum = jnp.where(inner, totals_of[last], ends[last]).astype(jnp.float32)
+    first_sum, second_sum = (rest_sum[:, : PROJECTED + EXTRA], rest_sum[:, PROJECTED + EXTRA :])
     gains_part = jnp.stack([first_sum[:, PROJECTED], second_sum[:, MODEL_WIDTH + EXPERTS]])
     keyval_part = jnp.stack(
         [first_sum[:, WIDTH : WIDTH + KV_WIDTH], first_sum[:, WIDTH + KV_WIDTH : PROJECTED]]
@@ -863,7 +912,7 @@
     updated = []
     for gradient, weight, first, second, rate, shrink in settings:
         updated.extend(adamw_step(weight, first, second, gradient, rate, shrink))
-    return (block_output, input_gradient) + tuple(updated) + tuple(gateup_new) + tuple(down_new)
+    return (block_output, input_gradient) + tuple(updated) + tuple(renewed[0]) + tuple(renewed[1])
 
 
 def solution(mesh):

time: 740 us -> 714 us (0.965)
  blocking collectives: 71.6 us -> 0 us
  Pallas kernels: 250 us -> 284 us
  starting transfers between devices: 77.1 us -> 86 us
  waiting for transfers between devices: 250 us -> 242 us
    all_to_all x4 -> x0, blocking collectives: 71.6 us -> none  [to_owner(): return lax.all_to_all(parts, 'inner', 0, 0)]
    all_gather x4 -> x2, waiting for transfers between devices: 92.5 us -> 44.5 us  [gathered(): lax.all_gather(values[c * part_rows:(c + 1) * part_rows], 'inner', axis=0...]
    ppermute x8 -> x7, waiting for transfers between devices: 22.5 us -> 56.1 us  [outward(): return lax.ppermute(values, 'replica', [(1, 0), (2, 3)])]
    all_gather x0 -> x1, waiting for transfers between devices: none -> 32.9 us  [body(): lax.all_gather(branch_pack, 'inner', axis=0, tiled=True)]
    pallas_call x12 -> x21, Pallas kernels: 84.5 us -> 115 us  [the longest x3 56.3 us: run_grads(): pl.pallas_call(functools.partial(grads_kernel, steps, sides), grid=(CHUNK...]
    all_to_all x2 -> x6, starting transfers between devices: 10.5 us -> 26.6 us  [to_owner(): return lax.all_to_all(parts, 'inner', 0, 0)]
    reduce_scatter x2, waiting for transfers between devices: 14.8 us -> 0.04 us  [body(): lax.psum_scatter(dx, 'inner', scatter_dimension=0, tiled=True)]
    ppermute x8 -> x7, starting transfers between devices: 41.7 us -> 32.6 us  [inward(): return lax.ppermute(values, 'replica', [(0, 1), (3, 2)])]
  transfers between devices with their start and end apart: 37 -> 37, of which waited for: 16 -> 14; matrix products, arithmetic and copies ran while one was open for 3% -> 3% of each run, Pallas kernels for 33% -> 40%
where the time goes in v2:
time: 714 us; the launch traced here: 701 us
  Pallas kernels  284 us (40%)
  waiting for transfers between devices  242 us (34%)
  starting transfers between devices  86 us (12%)
  local copies, waits for them, and re-layouts  52.2 us (7%)
  other arithmetic  22 us (3%)
  between operations  14.9 us (2%)
    all_gather x1, waiting for transfers between devices, body(): pack = lax.all_gather(pack_own, fsdp, axis=0, tiled=True)  79.4 us
    pallas_call x2, Pallas kernels, run_experts(): pl.pallas_call(expert_kernel, grid_spec=pltpu.PrefetchScalarGridSpec(num_...  66.7 us
    pallas_call x3, Pallas kernels, run_grads(): pl.pallas_call(functools.partial(grads_kernel, steps, sides), grid=(CHUNK...  56.3 us
    ppermute x7, waiting for transfers between devices, outward(): return lax.ppermute(values, 'replica', [(1, 0), (2, 3)])  56.1 us
    all_gather x2, waiting for transfers between devices, gathered(): lax.all_gather(values[c * part_rows:(c + 1) * part_rows], 'inner', axis=0...  44.5 us
    unnamed x89, local copies, waits for them, and re-layouts  43 us
    pallas_call x6, Pallas kernels, adam_part(): pl.pallas_call(functools.partial(adam_kernel, turned, rate, decay_rate),...  39.7 us
    pallas_call x1, Pallas kernels, run_back(): pl.pallas_call(back_kernel, grid=(1,), in_specs=[whole(v.shape) for v in...  33.6 us
  transfers between devices with their start and end apart: 37, of which 14 were waited for; matrix products, arithmetic and copies ran while one was open for 3% of the time, Pallas kernels for 40%

profile of v2, /device:TPU:2, one launch (start us, length us, event | category | flops | bytes accessed | tf_op | source)
XLA Modules:
  0.0 701.0 jit_solution(2378850776533262080)
XLA Ops:
  16.9 9.9 %split.1 = bf16[8,2,3,128,512]{4,3,2,1,0:T(8,128)(2,1)} custom-call(f32[16,2,128,512]{3,2,1,0:T(8,128)} %w_ref.11, f32[16,512,128]{2,1,0:T(8,128)} %w_ref.9), custom_call_target="tpu_custom_call" | custom-call | tf_op jit(solution)/shard_map/split/pallas_call | solution.py:177
  34.5 79.4 %all-gather.5.cloned.1.call-done.pack_ref.router_ref.output_ref = bf16[1024,3200]{1,0:T(8,128)(2,1)} async-done(((bf16[128,3200]{1,0:T(8,128)(2,1)}), bf16[1024,3200]{1,0:T(8,128)(2,1)}) %all-gather.5.cloned.1.call-update) | async-done | bytes 6553616 | tf_op jit(solution)/shard_map/all_gather | solution.py:721
  120.0 19.2 %front.1 = (bf16[512,1024]{1,0:T(8,128)(2,1)}, bf16[512,2048]{1,0:T(8,128)(2,1)}, bf16[512,1024]{1,0:T(8,128)(2,1)}, f32[512,128]{1,0:T(8,128)S(1)}, f32[512,1024]{1,0:T(8,128)}, /*index=5*/bf16[512,1024]{1,0:T(8,128)(2,1)}) custom-call(bf16[512,1024]{1,0:T(8,128)(2,1)} %x_ref.3, ...), custom_call_target="tpu_custom_call" | custom-call | tf_op jit(solution)/shard_map/front/pallas_call | solution.py:249
  142.3 32.9 %all-gather.9.cloned.1.call-done = bf16[4096,1152]{1,0:T(8,128)(2,1)} async-done(((bf16[512,1152]{1,0:T(8,128)(2,1)}), bf16[4096,1152]{1,0:T(8,128)(2,1)}) %all-gather.9.cloned.1.call-update) | async-done | bytes 9437200 | tf_op jit(solution)/shard_map/all_gather | solution.py:752
  175.2 39.2 %all-gather.11.cloned.1.call-done.x_ref.refs_2_.refs_6_.refs_10_ = bf16[2048,1024]{1,0:T(8,128)(2,1)} async-done(((bf16[256,1024]{1,0:T(8,128)(2,1)}), bf16[2048,1024]{1,0:T(8,128)(2,1)}) %all-gather.11.cloned.1.call-update) | async-done | bytes 4194320 | tf_op jit(solution)/shard_map/all_gather | solution.py:748
  214.4 33.3 %experts.3 = (bf16[2048,1024]{1,0:T(8,128)(2,1)}, bf16[2048,2048]{1,0:T(8,128)(2,1)}, bf16[2048,1152]{1,0:T(8,128)(2,1)}) custom-call(s32[1]{0:T(128)} %bitcast.8.me_ref, bf16[2048,1024]{1,0:T(8,128)(2,1)} %all-gather.11.cloned.1.call-done.x_ref.refs_2_.refs_6_.refs_10_, bf16[8,2,256,1152]{3,2,1,0:T(8,128)(2,1)} %bitcast.30, ...), custom_call_target="tpu_custom_call" | custom-call | tf_op jit(solution)/shard_map/experts/pallas_call | solution.py:469
  248.2 5.3 all-gather.7.cloned.1.call-done.x_ref.refs_0_.refs_4_.refs_8_
  253.5 33.3 %experts.2 = (bf16[2048,1024]{1,0:T(8,128)(2,1)}, bf16[2048,2048]{1,0:T(8,128)(2,1)}, bf16[2048,1152]{1,0:T(8,128)(2,1)}) custom-call(s32[1]{0:T(128)} %bitcast.8.me_ref, bf16[2048,1024]{1,0:T(8,128)(2,1)} %all-gather.7.cloned.1.call-done.x_ref.refs_0_.refs_4_.refs_8_, bf16[8,2,256,1152]{3,2,1,0:T(8,128)(2,1)} %bitcast.31, ...), custom_call_target="tpu_custom_call" | custom-call | tf_op jit(solution)/shard_map/experts/pallas_call | solution.py:469
  286.9 11.3 %grads.3.refs_8_ = bf16[1024,512]{1,0:T(8,128)(2,1)} custom-call(bf16[8,2,256,1152]{3,2,1,0:T(8,128)(2,1)} %bitcast.32, bf16[2048,1024]{1,0:T(8,128)(2,1)} %get-tuple-element.83.refs_1_.ga_ref, bf16[8,2,256,1152]{3,2,1,0:T(8,128)(2,1)} %bitcast.33, bf16[2048,1024]{1,0:T(8,128)(2,1)} %get-tuple-element.84.refs_3_.ga_ref, ...), custom_call_target="tpu_custom_call" | custom-call | flops 1000000000 | bytes 3600000 | tf_op jit(solution)/shard_map/grads/pallas_call | solution.py:548
  302.2 19.1 %grads.4 = (bf16[1024,512]{1,0:T(8,128)(2,1)S(1)}, bf16[1024,512]{1,0:T(8,128)(2,1)}) custom-call(bf16[2048,1024]{1,0:T(8,128)(2,1)} %all-gather.7.cloned.1.call-done.x_ref.refs_0_.refs_4_.refs_8_, bf16[2048,2048]{1,0:T(8,128)(2,1)} %get-tuple-element.86.refs_1_.refs_5_.refs_9_, ...), custom_call_target="tpu_custom_call" | custom-call | flops 1000000000 | bytes 3600000 | tf_op jit(solution)/shard_map/grads/pallas_call | solution.py:548
  326.8 5.0 all-to-all-start.2
  331.8 25.9 %grads.5 = (bf16[1024,512]{1,0:T(8,128)(2,1)S(1)}, bf16[1024,512]{1,0:T(8,128)(2,1)}, bf16[1024,512]{1,0:T(8,128)(2,1)}) custom-call(bf16[8,2,256,1152]{3,2,1,0:T(8,128)(2,1)} %bitcast.34, bf16[2048,1024]{1,0:T(8,128)(2,1)} %get-tuple-element.83.refs_1_.ga_ref, bf16[8,2,256,1152]{3,2,1,0:T(8,128)(2,1)} %bitcast.35, ...), custom_call_target="tpu_custom_call" | custom-call | flops 6000000000 | bytes 21600000 | tf_op jit(solution)/shard_map/grads/pallas_call | solution.py:548
  370.9 8.5 %mixture.2.refs_5_ = bf16[2048,1024]{1,0:T(8,128)(2,1)} custom-call(bf16[2048,1024]{1,0:T(8,128)(2,1)} %get-tuple-element.83.refs_1_.ga_ref, bf16[8,2,3,128,512]{4,3,2,1,0:T(8,128)(2,1)} %all-to-all-done.wait_ref.w_ref, bf16[8,128,512]{2,1,0:T(8,128)(2,1)} %get-tuple-element.89.wait_ref.refs_2_), custom_call_target="tpu_custom_call" | custom-call | flops 6000000000 | bytes 21600000 | tf_op jit(solution)/shard_map/mixture/pallas_call | solution.py:574
  379.5 10.5 %all-to-all-done.3.refs_4_ = bf16[8,128,512]{2,1,0:T(8,128)(2,1)S(1)} async-done(((bf16[8,128,512]{2,1,0:T(8,128)(2,1)}), bf16[8,128,512]{2,1,0:T(8,128)(2,1)S(1)}, u32[]{:S(2)}, u32[]{:S(2)}) %all-to-all-start.3) | async-done | bytes 1048608 | tf_op jit(solution)/shard_map/all_to_all | solution.py:773
  398.3 4.9 all-to-all-start.4
  411.1 10.2 %middle_back.1 = (f32[512,1024]{1,0:T(8,128)}, bf16[512,1024]{1,0:T(8,128)(2,1)}, bf16[1024,1152]{1,0:T(8,128)(2,1)}) custom-call(bf16[256,1152]{1,0:T(8,128)(2,1)S(1)} %copy-done.23, bf16[256,1152]{1,0:T(8,128)(2,1)S(1)} %copy-done.22, bf16[512,1024]{1,0:T(8,128)(2,1)} %get-tuple-element.82.normed_two_ref, f32[512,1024]{1,0:T(8,128)} %get-tuple-element.81.middle_ref, ...), custom_call_target="tpu_custom_call" | custom-call | flops 30000001024 | bytes 108000000 | tf_op jit(solution)/shard_map/middle_back/pallas_call | solution.py:296
  421.3 8.3 %collective-permute-done.3.refs_1_ = bf16[8,128,512]{2,1,0:T(8,128)(2,1)} collective-permute-done((bf16[8,128,512]{2,1,0:T(8,128)(2,1)}, bf16[8,128,512]{2,1,0:T(8,128)(2,1)}, u32[]{:S(2)}, u32[]{:S(2)}) %collective-permute-start.3) | collective-permute-done | bytes 1048608 | tf_op jit(solution)/shard_map/ppermute | solution.py:776
  429.7 5.1 collective-permute-done.5.refs_5_.r_ref
  451.3 33.6 %attention_back.1 = (bf16[1024,3328]{1,0:T(8,128)(2,1)}, f32[512,1024]{1,0:T(8,128)}) custom-call(bf16[512,1024]{1,0:T(8,128)(2,1)S(1)} %copy-done.25, bf16[512,2048]{1,0:T(8,128)(2,1)} %get-tuple-element.103.qkv_ref, f32[512,128]{1,0:T(8,128)S(1)} %get-tuple-element.104.totals_ref, f32[512,512]{1,0:T(8,128)} %fusion.1.bias_ref, ...), custom_call_target="tpu_custom_call" | custom-call | flops 30000001024 | bytes 108000000 | tf_op jit(solution)/shard_map/attention_back/pallas_call | solution.py:404
  497.5 7.3 %collective-permute-start.9 = (bf16[8,128,512]{2,1,0:T(8,128)(2,1)}, bf16[8,128,512]{2,1,0:T(8,128)(2,1)}, u32[]{:S(2)}, u32[]{:S(2)}) collective-permute-start(bf16[8,128,512]{2,1,0:T(8,128)(2,1)} %get-tuple-element.110.refs_0_), channel_id=1, source_target_pairs={{0,8},{24,16},{1,9},{25,17},{2,10},{26,18},{3,11},{27,19},{4,12},{... | collective-permute-start | bytes 3145736 | tf_op jit(solution)/shard_map/ppermute | solution.py:776
  506.3 8.6 %mixture.3.rest_0_ = bf16[2048,1024]{1,0:T(8,128)(2,1)} custom-call(bf16[2048,1024]{1,0:T(8,128)(2,1)} %get-tuple-element.84.refs_3_.ga_ref, bf16[8,2,3,128,512]{4,3,2,1,0:T(8,128)(2,1)} %all-to-all-done.wait_ref.w_ref, bf16[8,128,512]{2,1,0:T(8,128)(2,1)} %get-tuple-element.109.wait_ref.refs_2_), custom_call_target="tpu_custom_call" | custom-call | flops 199999995904 | bytes 720000000 | tf_op jit(solution)/shard_map/mixture/pallas_call | solution.py:574
  519.5 6.1 adam.6
  526.8 5.1 collective-permute-done.11.refs_5_.r_ref
  544.0 6.7 adam.7
  560.0 7.1 %adam.8 = (f32[16,2,128,512]{3,2,1,0:T(8,128)}, f32[16,2,128,512]{3,2,1,0:T(8,128)}, f32[16,2,128,512]{3,2,1,0:T(8,128)}) custom-call(s32[1]{0:T(128)} %bitcast.16.place_ref, bf16[8,128,512]{2,1,0:T(8,128)(2,1)} %get-tuple-element.112.t_ref, ...), custom_call_target="tpu_custom_call", output_to_operand_aliasing={{0}: (6, {}), {1}: (7, {}), {2}: (8, {})} | custom-call | flops 1000000000 | bytes 3600000 | tf_op jit(solution)/shard_map/adam/pallas_call | solution.py:656
  574.3 6.2 adam.9
  580.5 19.1 %collective-permute-done.16.refs_3_.r_ref = bf16[8,128,512]{2,1,0:T(8,128)(2,1)} collective-permute-done((bf16[8,128,512]{2,1,0:T(8,128)(2,1)}, bf16[8,128,512]{2,1,0:T(8,128)(2,1)}, u32[]{:S(2)}, u32[]{:S(2)}) %collective-permute-start.16) | collective-permute-done | bytes 1048608 | tf_op jit(solution)/shard_map/ppermute | solution.py:782
  606.1 7.5 %collective-permute-start.17 = (bf16[128,3328]{1,0:T(8,128)(2,1)}, bf16[128,3328]{1,0:T(8,128)(2,1)}, u32[]{:S(2)}, u32[]{:S(2)}) collective-permute-start(bf16[128,3328]{1,0:T(8,128)(2,1)} %get-tuple-element.127.refs_0_), channel_id=1, source_target_pairs={{0,8},{24,16},{1,9},{25,17},{2,10},{26,18},{3,11},{27,19},{4,12},{... | collective-permute-start | bytes 2555912 | tf_op jit(solution)/shard_map/ppermute | solution.py:776
  618.3 6.8 adam.10
  628.5 9.2 %collective-permute-done.18.refs_2_.r_ref = bf16[8,128,512]{2,1,0:T(8,128)(2,1)} collective-permute-done((bf16[8,128,512]{2,1,0:T(8,128)(2,1)}, bf16[8,128,512]{2,1,0:T(8,128)(2,1)}, u32[]{:S(2)}, u32[]{:S(2)}) %collective-permute-start.18) | collective-permute-done | bytes 1048608 | tf_op jit(solution)/shard_map/ppermute | solution.py:782
  645.5 6.8 adam.11
  665.6 17.5 %collective-permute-done.20 = bf16[128,3328]{1,0:T(8,128)(2,1)} collective-permute-done((bf16[128,3328]{1,0:T(8,128)(2,1)S(1)}, bf16[128,3328]{1,0:T(8,128)(2,1)}, u32[]{:S(2)}, u32[]{:S(2)}) %collective-permute-start.20) | collective-permute-done | bytes 852000 | tf_op jit(solution)/shard_map/ppermute | solution.py:782
  (215 shorter events, 177.0 us)
Async XLA Ops:
  7.2 106.7 %all-gather.5.cloned.1.call-start = ((), (), s32[]{:S(2)}) async-start(), calls=%async_computation.12 | async-start | bytes 7372800 | tf_op jit(solution)/shard_map/all_gather | solution.py:721
  14.0 161.2 %all-gather.9.cloned.1.call-start = ((), (), s32[]{:S(2)}) async-start(), calls=%async_computation.14 | async-start | bytes 10616832 | tf_op jit(solution)/shard_map/all_gather | solution.py:752
  26.8 93.2 %all-to-all-start = ((bf16[8,2,3,128,512]{4,3,2,1,0:T(8,128)(2,1)}), bf16[8,2,3,128,512]{4,3,2,1,0:T(8,128)(2,1)}, u32[]{:S(2)}, u32[]{:S(2)}) async-start(bf16[8,2,3,128,512]{4,3,2,1,0:T(8,128)(2,1)} %split.1), calls=%async_computation | async-start | bytes 12582912 | tf_op jit(solution)/shard_map/all_to_all | solution.py:725
  31.6 182.8 %all-gather.11.cloned.1.call-start = ((), (), s32[]{:S(2)}) async-start(), calls=%async_computation.15 | async-start | bytes 4718592 | tf_op jit(solution)/shard_map/all_gather | solution.py:748
  141.5 112.0 %all-gather.7.cloned.1.call-start = ((), (), s32[]{:S(2)}) async-start(), calls=%async_computation.13 | async-start | bytes 4718592 | tf_op jit(solution)/shard_map/all_gather | solution.py:748
  142.1 266.9 %reduce-scatter.10.cloned.1.call-start = ((), (), s32[]{:S(2)}) async-start(), calls=%async_computation.18 | async-start | bytes 5308416 | tf_op jit(solution)/shard_map/reduce_scatter | solution.py:767
  247.8 161.2 %reduce-scatter.8.cloned.1.call-start = ((), (), s32[]{:S(2)}) async-start(), calls=%async_computation.17 | async-start | bytes 5308416 | tf_op jit(solution)/shard_map/reduce_scatter | solution.py:767
  322.4 36.3 %collective-permute-start = (bf16[8,128,512]{2,1,0:T(8,128)(2,1)}, bf16[8,128,512]{2,1,0:T(8,128)(2,1)}, u32[]{:S(2)}, u32[]{:S(2)}) collective-permute-start(bf16[8,128,512]{2,1,0:T(8,128)(2,1)} %sums.10.wait_ref.refs_12_.refs_0_), channel_id=1, source_target_pairs={{0,8},{24,16},{1,9},{25,17},{2,10},{26,18},{3,11},{27,19},{4,12},{... | collective-permute-start | bytes 3145736 | tf_op jit(solution)/shard_map/ppermute | solution.py:776
  326.8 30.9 %all-to-all-start.2 = ((bf16[8,128,512]{2,1,0:T(8,128)(2,1)}), bf16[8,128,512]{2,1,0:T(8,128)(2,1)S(1)}, u32[]{:S(2)}, u32[]{:S(2)}) async-start(bf16[8,128,512]{2,1,0:T(8,128)(2,1)} %bitcast.29), calls=%async_computation.2 | async-start | bytes 2097152 | tf_op jit(solution)/shard_map/all_to_all | solution.py:773
  362.7 27.3 %collective-permute-start.1 = (bf16[8,128,512]{2,1,0:T(8,128)(2,1)S(1)}, bf16[8,128,512]{2,1,0:T(8,128)(2,1)}, u32[]{:S(2)}, u32[]{:S(2)}) collective-permute-start(bf16[8,128,512]{2,1,0:T(8,128)(2,1)S(1)} %get-tuple-element.90.refs_0_), channel_id=1, source_target_pairs={{0,8},{24,16},{1,9},{25,17},{2,10},{26,18},{3,11},{27,19},{4,12},{... | collective-permute-start | bytes 3145736 | tf_op jit(solution)/shard_map/ppermute | solution.py:776
  365.0 25.0 %collective-permute-start.2 = (bf16[8,128,512]{2,1,0:T(8,128)(2,1)}, bf16[8,128,512]{2,1,0:T(8,128)(2,1)}, u32[]{:S(2)}, u32[]{:S(2)}) collective-permute-start(bf16[8,128,512]{2,1,0:T(8,128)(2,1)} %get-tuple-element.89.wait_ref.refs_2_), channel_id=1, source_target_pairs={{8,16},{16,8},{9,17},{17,9},{10,18},{18,10},{11,19},{19,11},{12,20... | collective-permute-start | bytes 3145736 | tf_op jit(solution)/shard_map/ppermute | solution.py:779
  370.9 114.0 %reduce-scatter.6.cloned.1.call-start = ((), (), s32[]{:S(2)}) async-start(), calls=%async_computation.16 | async-start | bytes 4718592 | tf_op jit(solution)/shard_map/reduce_scatter | solution.py:814
  396.6 38.1 %collective-permute-start.4 = (bf16[8,128,512]{2,1,0:T(8,128)(2,1)}, bf16[8,128,512]{2,1,0:T(8,128)(2,1)}, u32[]{:S(2)}, u32[]{:S(2)}) collective-permute-start(bf16[8,128,512]{2,1,0:T(8,128)(2,1)} %copy-done.17), channel_id=1, source_target_pairs={{8,16},{16,8},{9,17},{17,9},{10,18},{18,10},{11,19},{19,11},{12,20... | collective-permute-start | bytes 3145736 | tf_op jit(solution)/shard_map/ppermute | solution.py:779
  403.2 26.5 %collective-permute-start.3 = (bf16[8,128,512]{2,1,0:T(8,128)(2,1)}, bf16[8,128,512]{2,1,0:T(8,128)(2,1)}, u32[]{:S(2)}, u32[]{:S(2)}) collective-permute-start(bf16[8,128,512]{2,1,0:T(8,128)(2,1)} %get-tuple-element.92.refs_0_), channel_id=1, source_target_pairs={{0,8},{24,16},{1,9},{25,17},{2,10},{26,18},{3,11},{27,19},{4,12},{... | collective-permute-start | bytes 3145736 | tf_op jit(solution)/shard_map/ppermute | solution.py:776
  407.6 27.1 %collective-permute-start.5 = (bf16[8,128,512]{2,1,0:T(8,128)(2,1)}, bf16[8,128,512]{2,1,0:T(8,128)(2,1)}, u32[]{:S(2)}, u32[]{:S(2)}) collective-permute-start(bf16[8,128,512]{2,1,0:T(8,128)(2,1)} %get-tuple-element.94.t_ref), channel_id=1, source_target_pairs={{8,0},{16,24},{9,1},{17,25},{10,2},{18,26},{11,3},{19,27},{12,4},{... | collective-permute-start | bytes 3145736 | tf_op jit(solution)/shard_map/ppermute | solution.py:782
  439.8 45.2 %collective-permute-start.7 = (bf16[8,128,512]{2,1,0:T(8,128)(2,1)}, bf16[8,128,512]{2,1,0:T(8,128)(2,1)}, u32[]{:S(2)}, u32[]{:S(2)}) collective-permute-start(bf16[8,128,512]{2,1,0:T(8,128)(2,1)} %get-tuple-element.100.wait_ref.also_ref.refs_2_), channel_id=1, source_target_pairs={{8,16},{16,8},{9,17},{17,9},{10,18},{18,10},{11,19},{19,11},{12,20... | collective-permute-start | bytes 3145736 | tf_op jit(solution)/shard_map/ppermute | solution.py:779
  441.6 43.3 %all-to-all-start.5 = ((bf16[8,128,512]{2,1,0:T(8,128)(2,1)}), bf16[8,128,512]{2,1,0:T(8,128)(2,1)S(1)}, u32[]{:S(2)}, u32[]{:S(2)}) async-start(bf16[8,128,512]{2,1,0:T(8,128)(2,1)} %bitcast.37), calls=%async_computation.8 | async-start | bytes 2097152 | tf_op jit(solution)/shard_map/all_to_all | solution.py:773
  445.8 153.9 %reduce-scatter.14.cloned.1.call-start = ((), (), s32[]{:S(2)}) async-start(), calls=%async_computation.20 | async-start | bytes 7667712 | tf_op jit(solution)/shard_map/reduce_scatter | solution.py:851
  445.8 39.1 %collective-permute-start.6 = (bf16[8,128,512]{2,1,0:T(8,128)(2,1)}, bf16[8,128,512]{2,1,0:T(8,128)(2,1)}, u32[]{:S(2)}, u32[]{:S(2)}) collective-permute-start(bf16[8,128,512]{2,1,0:T(8,128)(2,1)} %get-tuple-element.99.refs_0_), channel_id=1, source_target_pairs={{0,8},{24,16},{1,9},{25,17},{2,10},{26,18},{3,11},{27,19},{4,12},{... | collective-permute-start | bytes 3145736 | tf_op jit(solution)/shard_map/ppermute | solution.py:776
  450.0 34.9 %collective-permute-start.8 = (bf16[8,128,512]{2,1,0:T(8,128)(2,1)}, bf16[8,128,512]{2,1,0:T(8,128)(2,1)}, u32[]{:S(2)}, u32[]{:S(2)}) collective-permute-start(bf16[8,128,512]{2,1,0:T(8,128)(2,1)} %get-tuple-element.102.t_ref), channel_id=1, source_target_pairs={{8,0},{16,24},{9,1},{17,25},{10,2},{18,26},{11,3},{19,27},{12,4},{... | collective-permute-start | bytes 3145736 | tf_op jit(solution)/shard_map/ppermute | solution.py:782
  491.6 40.3 %collective-permute-start.10 = (bf16[8,128,512]{2,1,0:T(8,128)(2,1)}, bf16[8,128,512]{2,1,0:T(8,128)(2,1)}, u32[]{:S(2)}, u32[]{:S(2)}) collective-permute-start(bf16[8,128,512]{2,1,0:T(8,128)(2,1)} %get-tuple-element.109.wait_ref.refs_2_), channel_id=1, source_target_pairs={{8,16},{16,8},{9,17},{17,9},{10,18},{18,10},{11,19},{19,11},{12,20... | collective-permute-start | bytes 3145736 | tf_op jit(solution)/shard_map/ppermute | solution.py:779
  493.2 32.4 %all-to-all-start.6 = ((bf16[8,128,512]{2,1,0:T(8,128)(2,1)}), bf16[8,128,512]{2,1,0:T(8,128)(2,1)}, u32[]{:S(2)}, u32[]{:S(2)}) async-start(bf16[8,128,512]{2,1,0:T(8,128)(2,1)} %bitcast.36), calls=%async_computation.10 | async-start | bytes 2097152 | tf_op jit(solution)/shard_map/all_to_all | solution.py:773
  497.5 165.6 %reduce-scatter.12.cloned.1.call-start = ((), (), s32[]{:S(2)}) async-start(), calls=%async_computation.19 | async-start | bytes 4718592 | tf_op jit(solution)/shard_map/reduce_scatter | solution.py:814
  497.5 29.2 %collective-permute-start.9 = (bf16[8,128,512]{2,1,0:T(8,128)(2,1)}, bf16[8,128,512]{2,1,0:T(8,128)(2,1)}, u32[]{:S(2)}, u32[]{:S(2)}) collective-permute-start(bf16[8,128,512]{2,1,0:T(8,128)(2,1)} %get-tuple-element.110.refs_0_), channel_id=1, source_target_pairs={{0,8},{24,16},{1,9},{25,17},{2,10},{26,18},{3,11},{27,19},{4,12},{... | collective-permute-start | bytes 3145736 | tf_op jit(solution)/shard_map/ppermute | solution.py:776
  504.8 27.1 %collective-permute-start.11 = (bf16[8,128,512]{2,1,0:T(8,128)(2,1)}, bf16[8,128,512]{2,1,0:T(8,128)(2,1)}, u32[]{:S(2)}, u32[]{:S(2)}) collective-permute-start(bf16[8,128,512]{2,1,0:T(8,128)(2,1)} %get-tuple-element.112.t_ref), channel_id=1, source_target_pairs={{8,0},{16,24},{9,1},{17,25},{10,2},{18,26},{11,3},{19,27},{12,4},{... | collective-permute-start | bytes 3145736 | tf_op jit(solution)/shard_map/ppermute | solution.py:782
  538.5 28.6 %collective-permute-start.12 = (bf16[8,128,512]{2,1,0:T(8,128)(2,1)}, bf16[8,128,512]{2,1,0:T(8,128)(2,1)}, u32[]{:S(2)}, u32[]{:S(2)}) collective-permute-start(bf16[8,128,512]{2,1,0:T(8,128)(2,1)} %get-tuple-element.114.refs_0_), channel_id=1, source_target_pairs={{0,8},{24,16},{1,9},{25,17},{2,10},{26,18},{3,11},{27,19},{4,12},{... | collective-permute-start | bytes 3145736 | tf_op jit(solution)/shard_map/ppermute | solution.py:776
  541.0 26.1 %collective-permute-start.14 = (bf16[8,128,512]{2,1,0:T(8,128)(2,1)}, bf16[8,128,512]{2,1,0:T(8,128)(2,1)}, u32[]{:S(2)}, u32[]{:S(2)}) collective-permute-start(bf16[8,128,512]{2,1,0:T(8,128)(2,1)} %get-tuple-element.116.t_ref), channel_id=1, source_target_pairs={{8,0},{16,24},{9,1},{17,25},{10,2},{18,26},{11,3},{19,27},{12,4},{... | collective-permute-start | bytes 3145736 | tf_op jit(solution)/shard_map/ppermute | solution.py:782
  542.3 24.8 %collective-permute-start.13 = (bf16[8,128,512]{2,1,0:T(8,128)(2,1)}, bf16[8,128,512]{2,1,0:T(8,128)(2,1)}, u32[]{:S(2)}, u32[]{:S(2)}) collective-permute-start(bf16[8,128,512]{2,1,0:T(8,128)(2,1)} %get-tuple-element.115.rest_0_.refs_2_), channel_id=1, source_target_pairs={{8,16},{16,8},{9,17},{17,9},{10,18},{18,10},{11,19},{19,11},{12,20... | collective-permute-start | bytes 3145736 | tf_op jit(solution)/shard_map/ppermute | solution.py:779
  571.2 28.4 %collective-permute-start.16 = (bf16[8,128,512]{2,1,0:T(8,128)(2,1)}, bf16[8,128,512]{2,1,0:T(8,128)(2,1)}, u32[]{:S(2)}, u32[]{:S(2)}) collective-permute-start(bf16[8,128,512]{2,1,0:T(8,128)(2,1)} %get-tuple-element.123.t_ref), channel_id=1, source_target_pairs={{8,0},{16,24},{9,1},{17,25},{10,2},{18,26},{11,3},{19,27},{12,4},{... | collective-permute-start | bytes 3145736 | tf_op jit(solution)/shard_map/ppermute | solution.py:782
  572.7 27.0 %collective-permute-start.15 = (bf16[8,128,512]{2,1,0:T(8,128)(2,1)}, bf16[8,128,512]{2,1,0:T(8,128)(2,1)}, u32[]{:S(2)}, u32[]{:S(2)}) collective-permute-start(bf16[8,128,512]{2,1,0:T(8,128)(2,1)} %get-tuple-element.121.rest_3_.refs_0_), channel_id=1, source_target_pairs={{8,16},{16,8},{9,17},{17,9},{10,18},{18,10},{11,19},{19,11},{12,20... | collective-permute-start | bytes 3145736 | tf_op jit(solution)/shard_map/ppermute | solution.py:779
  613.6 24.1 %collective-permute-start.18 = (bf16[8,128,512]{2,1,0:T(8,128)(2,1)}, bf16[8,128,512]{2,1,0:T(8,128)(2,1)}, u32[]{:S(2)}, u32[]{:S(2)}) collective-permute-start(bf16[8,128,512]{2,1,0:T(8,128)(2,1)} %get-tuple-element.128.rest_3_.t_ref), channel_id=1, source_target_pairs={{8,0},{16,24},{9,1},{17,25},{10,2},{18,26},{11,3},{19,27},{12,4},{... | collective-permute-start | bytes 3145736 | tf_op jit(solution)/shard_map/ppermute | solution.py:782
  657.4 25.7 %collective-permute-start.20 = (bf16[128,3328]{1,0:T(8,128)(2,1)S(1)}, bf16[128,3328]{1,0:T(8,128)(2,1)}, u32[]{:S(2)}, u32[]{:S(2)}) collective-permute-start(bf16[128,3328]{1,0:T(8,128)(2,1)S(1)} %sums.19), channel_id=1, source_target_pairs={{8,0},{16,24},{9,1},{17,25},{10,2},{18,26},{11,3},{19,27},{12,4},{... | collective-permute-start | bytes 2555912 | tf_op jit(solution)/shard_map/ppermute | solution.py:782
  (47 other events, 450.2 us)
Sparse Core Ops, SparseCore 0:
  14.2 99.6 all-gather.4
  116.3 58.8 all-gather.8
  177.7 36.7 all-gather.10
  216.7 36.7 all-gather.6
  257.4 64.9 reduce-scatter.9
  326.0 65.0 reduce-scatter.7
  395.0 51.3 reduce-scatter.5
  485.0 66.2 reduce-scatter.13
  554.7 51.3 reduce-scatter.11

commit v3 on v2

--- a/solution.py
+++ b/solution.py
@@ -264,10 +264,10 @@
 
 
 def middle_kernel(
-    dx_one_ref, dx_two_ref, normed_two_ref, middle_ref, cot_ref, mask_ref, alive_ref, gains_ref,
-    router_ref, output_ref, mixed_ref, wait_ref, d_middle_ref, d_mixed_ref, grads_ref,
+    dx_ref, normed_two_ref, middle_ref, cot_ref, mask_ref, alive_ref, gains_ref, router_ref,
+    output_ref, mixed_ref, wait_ref, d_middle_ref, d_mixed_ref, grads_ref,
 ):
-    dx = jnp.concatenate([dx_one_ref[...], dx_two_ref[...]], axis=0).astype(jnp.float32)
+    dx = dx_ref[...].astype(jnp.float32)
     normed_two = normed_two_ref[...]
     mask = mask_ref[...].astype(jnp.float32) > 0.5
     gates = gates_of(normed_two, router_ref[...], mask)
@@ -285,14 +285,14 @@
     d_attended = (alive_ref[...] * d_middle).astype(brain_floating)
     grads_ref[:, :MODEL_WIDTH] = transposed_times(mixed_ref[...], d_attended).astype(brain_floating)
     small = transposed_times(normed_two, d_logits)
-    small = jnp.where(lanes_of(small.shape) == EXPERTS, column_sums(d_normed * scaled), small)
+    small = jnp.where(lanes_of(small.shape) == EXPERTS + 1, column_sums(d_normed * scaled), small)
     grads_ref[:, MODEL_WIDTH:] = small.astype(brain_floating)
     d_mixed_ref[...] = times_transposed(d_attended, output_ref[...]).astype(brain_floating)
 
 
-def run_middle(dx_one, dx_two, normed_two, middle, cot, mask, alive, gains, pack, mixed, wait):
+def run_middle(dx, normed_two, middle, cot, mask, alive, gains, pack, mixed, wait):
     rows = middle.shape[0]
-    full = [whole(v.shape) for v in (dx_one, dx_two, normed_two, middle, cot, mask, alive, gains)]
+    full = [whole(v.shape) for v in (dx, normed_two, middle, cot, mask, alive, gains)]
     return pl.pallas_call(
         middle_kernel,
         grid=(1,),
@@ -316,7 +316,7 @@
         compiler_params=pltpu.CompilerParams(vmem_limit_bytes=52 * MIB),
         cost_estimate=takes(30),
         name="middle_back",
-    )(dx_one, dx_two, normed_two, middle, cot, mask, alive, gains, pack, pack, mixed, wait)
+    )(dx, normed_two, middle, cot, mask, alive, gains, pack, pack, mixed, wait)
 
 
 def back_kernel(
@@ -388,10 +388,11 @@
     d_normed = times_transposed(d_linear_ref[...], pack_ref[...])
     scaled, inverse = normalize(x_ref[...].astype(jnp.float32))
     sums = column_sums(d_normed * scaled)
-    grads_ref[:, PROJECTED : PROJECTED + EXTRA] = jnp.where(
-        lanes_of(sums.shape) == 0, sums, 0.0
+    grads_ref[:, PROJECTED : PROJECTED + MODEL_WIDTH] = other_ref[:, :MODEL_WIDTH]
+    small = other_ref[:, MODEL_WIDTH:].astype(jnp.float32)
+    grads_ref[:, PROJECTED + MODEL_WIDTH :] = jnp.where(
+        lanes_of(sums.shape) == EXPERTS, sums, small
     ).astype(brain_floating)
-    grads_ref[:, PROJECTED + EXTRA :] = other_ref[...]
     d_input_ref[...] = d_middle_ref[...] + norm_back(d_normed, scaled, inverse, gains_ref[0:1, :])
 
 
@@ -400,7 +401,7 @@
 ):
     rows = x.shape[0]
     held = (d_mixed, qkv, totals, bias, cosine, sine, normed, x, d_middle, gains, other)
-    width = PROJECTED + EXTRA + other.shape[1]
+    width = PROJECTED + other.shape[1]
     return pl.pallas_call(
         back_kernel,
         grid=(1,),
@@ -422,7 +423,8 @@
     )(*held, pack, wait, also)
 
 
-def expert_kernel(me_ref, x_ref, b_ref, w_ref, router_ref, ga_ref, dgu_ref, dx_ref):
+def expert_kernel(me_ref, x_ref, b_ref, w_ref, router_ref, *refs):
+    ga_ref, dgu_ref, dx_ref = refs[-3:]
     x = x_ref[...]
     branch = b_ref[:, 0, :, :MODEL_WIDTH].reshape(x.shape)
     mask = b_ref[:, 0, :, MODEL_WIDTH:].reshape(x.shape[0], EXTRA).astype(jnp.float32) > 0.5
@@ -453,11 +455,16 @@
         dgu_ref[:, 2 * local * F : (2 * local + 1) * F] = d_gl
         dgu_ref[:, (2 * local + 1) * F : (2 * local + 2) * F] = d_ul
         dx += times_transposed(d_gl, gate_weight) + times_transposed(d_ul, up_weight)
-    dx_ref[:, :MODEL_WIDTH] = dx.astype(brain_floating)
-    dx_ref[:, MODEL_WIDTH:] = d_gates.astype(brain_floating)
-
-
-def run_experts(me, c, x, b, weights, pack):
+    blocks, _, part_rows, _ = dx_ref.shape
+    dx_ref[:, 0, :, :MODEL_WIDTH] = dx.astype(brain_floating).reshape(
+        blocks, part_rows, MODEL_WIDTH
+    )
+    dx_ref[:, 0, :, MODEL_WIDTH:] = d_gates.astype(brain_floating).reshape(
+        blocks, part_rows, EXTRA
+    )
+
+
+def run_experts(me, c, x, b, weights, pack, before):
     rows = x.shape[0]
     part_rows = b.shape[2]
     tile = 2 * part_rows
@@ -476,17 +483,23 @@
                 pl.BlockSpec((2, 1, part_rows, wide), lambda i, me_ref: (i, c, 0, 0)),
                 whole(weights.shape),
                 part((MODEL_WIDTH, EXTRA), (0, ROUTER_BLOCK)),
+            ]
+            + [ANYWHERE] * len(before),
+            out_specs=[
+                rowed(LOCAL * F),
+                rowed(2 * LOCAL * F),
+                pl.BlockSpec((2, 1, part_rows, wide), lambda i, me_ref: (i, c, 0, 0)),
             ],
-            out_specs=[rowed(LOCAL * F), rowed(2 * LOCAL * F), rowed(wide)],
         ),
         out_shape=[
             out((rows, LOCAL * F), brain_floating),
             out((rows, 2 * LOCAL * F), brain_floating),
-            out((rows, wide), brain_floating),
+            out((rows // part_rows, CHUNKS, part_rows, wide), brain_floating),
         ],
+        input_output_aliases={5 + i: 2 for i in range(len(before))},
         compiler_params=pltpu.CompilerParams(vmem_limit_bytes=56 * MIB),
         name="experts",
-    )(me, x, b, weights, pack)
+    )(me, x, b, weights, pack, *before)
 
 
 def chunked_specs(steps, shape, place):
@@ -498,11 +511,8 @@
 
 def grads_kernel(steps, sides, *refs):
     count = len(sides)
-    ins, outs, sums = (
-        refs[: CHUNKS * 2 * count],
-        refs[CHUNKS * 2 * count + 1 : -count],
-        refs[-count:],
-    )
+    ins, out_ref, sums = (refs[: CHUNKS * 2 * count], refs[-count - 1], refs[-count:])
+    blocks, _, shard, _ = out_ref.shape
     i = pl.program_id(0)
 
     @pl.when(i == 0)
@@ -522,11 +532,12 @@
 
     @pl.when(i == CHUNKS * steps - 1)
     def _():
-        for result, total in zip(outs, sums):
-            result[...] = total[...].astype(brain_floating)
-
-
-def run_grads(local, sides, xs, b, gas, dgus, wait, cost):
+        for k, total in enumerate(sums):
+            out_ref[:, k] = total[...].astype(brain_floating).reshape(blocks, shard, F)
+
+
+def run_grads(local, sides, shard, xs, b, gas, dgus, wait, cost):
+    blocks = MODEL_WIDTH // shard
     rows, part_rows = (xs[0].shape[0], b.shape[2])
     tile = 2 * part_rows
     steps = rows // tile
@@ -549,8 +560,8 @@
         functools.partial(grads_kernel, steps, sides),
         grid=(CHUNKS * steps,),
         in_specs=specs + [ANYWHERE],
-        out_specs=[whole((MODEL_WIDTH, F))] * len(sides),
-        out_shape=[out((MODEL_WIDTH, F), brain_floating)] * len(sides),
+        out_specs=whole((blocks, len(sides), shard, F)),
+        out_shape=out((blocks, len(sides), shard, F), brain_floating),
         scratch_shapes=[pltpu.VMEM((MODEL_WIDTH, F), jnp.float32)] * len(sides),
         compiler_params=pltpu.CompilerParams(vmem_limit_bytes=52 * MIB),
         cost_estimate=takes(cost),
@@ -558,56 +569,111 @@
     )(*arrays, wait)
 
 
-def mix_kernel(ga_ref, w_ref, wait_ref, out_ref):
-    total = jnp.zeros((ga_ref.shape[0], MODEL_WIDTH), jnp.float32)
-    for local in range(LOCAL):
-        total += times_transposed(
-            ga_ref[:, local * F : (local + 1) * F], w_ref[:, local, 0].reshape(MODEL_WIDTH, F)
-        )
-    out_ref[...] = total.astype(brain_floating)
-
-
-def run_mix(ga, weights, wait, cost):
-    rows = ga.shape[0]
-    tile = min(TILE, rows)
+def mix_kernel(steps, *refs):
+    gas, w_ref, out_ref = (refs[:CHUNKS], refs[CHUNKS], refs[-1])
+    for c in range(CHUNKS):
+
+        @pl.when(pl.program_id(0) // steps == c)
+        def _():
+            total = jnp.zeros((gas[c].shape[0], MODEL_WIDTH), jnp.float32)
+            for local in range(LOCAL):
+                total += times_transposed(
+                    gas[c][:, local * F : (local + 1) * F],
+                    w_ref[:, local, 0].reshape(MODEL_WIDTH, F),
+                )
+            out_ref[...] = total.astype(brain_floating).reshape(out_ref.shape)
+
+
+def run_mix(gas, weights, part_rows, wait, cost):
+    rows = gas[0].shape[0]
+    tile = 2 * part_rows
+    steps = rows // tile
     blocks, _, _, shard, _ = weights.shape
     return pl.pallas_call(
-        mix_kernel,
-        grid=(rows // tile,),
-        in_specs=[
-            pl.BlockSpec((tile, LOCAL * F), lambda i: (i, 0)),
-            part((blocks, LOCAL, 1, shard, F), (0, 0, 2, 0, 0)),
-            ANYWHERE,
-        ],
-        out_specs=pl.BlockSpec((tile, MODEL_WIDTH), lambda i: (i, 0)),
-        out_shape=out((rows, MODEL_WIDTH), brain_floating),
+        functools.partial(mix_kernel, steps),
+        grid=(CHUNKS * steps,),
+        in_specs=chunked_specs(steps, (tile, LOCAL * F), lambda i, c: (i, 0))
+        + [part((blocks, LOCAL, 1, shard, F), (0, 0, 2, 0, 0)), ANYWHERE],
+        out_specs=pl.BlockSpec(
+            (2, 1, part_rows, MODEL_WIDTH), lambda i: (lax.rem(i, steps), i // steps, 0, 0)
+        ),
+        out_shape=out((rows // part_rows, CHUNKS, part_rows, MODEL_WIDTH), brain_floating),
         compiler_params=pltpu.CompilerParams(vmem_limit_bytes=52 * MIB),
         cost_estimate=takes(cost),
         name="mixture",
-    )(ga, weights, wait)
-
-
-def sums_kernel(count, copies, waits, *refs):
-    ins, outs = (refs[: 2 * count + copies], refs[2 * count + copies + waits :])
-    for k in range(count):
-        left, right = (ins[2 * k][...], ins[2 * k + 1][...])
-        outs[k][...] = (left.astype(jnp.float32) + right.astype(jnp.float32)).astype(
-            brain_floating
-        )
-    for k in range(copies):
-        outs[count + k][...] = ins[2 * count + k][...]
-
-
-def run_sums(pairs, copies, waits):
-    flat = [v for pair in pairs for v in pair] + list(copies)
+    )(*gas, weights, wait)
+
+
+def at_inner(place_ref):
+    return (place_ref[0] == 1) | (place_ref[0] == 2)
+
+
+def round_kernel(kinds, waits, place_ref, *refs):
+    has_own, has_pair, has_next = kinds
+    refs = list(refs)
+
+    def take(count):
+        taken, refs[:count] = (refs[:count], [])
+        return [ref[...].astype(jnp.float32) for ref in taken]
+
+    own = take(2) if has_own else None
+    pair = take(2) if has_pair else None
+    following = take(1) if has_next else None
+    outs = refs[waits:]
+    edge = None
+    if has_next:
+        edge = following[0].reshape(outs[-1].shape)
+    if has_own:
+        outs.pop(0)[...] = (own[0].reshape(own[1].shape) + own[1]).astype(brain_floating)
+    if has_pair:
+        total = pair[0] + pair[1]
+        outs.pop(0)[...] = total.astype(brain_floating)
+        edge = total if edge is None else jnp.where(at_inner(place_ref), total, edge)
+    outs.pop(0)[...] = edge.astype(brain_floating)
+
+
+def run_round(place, own, pair, following, waits):
+    steps = GROUP // 2
+    arrays, specs, count = ([], [], 0)
+
+    def chunk_spec(source):
+        values, at = source
+        _, _, shard, width = values.shape
+        return pl.BlockSpec((2, 1, shard, width), lambda i, _: (i, at, 0, 0))
+
+    flat = None
+    for source in (own[:1] if own else ()) + ((following,) if following else ()):
+        flat = (GROUP,) + source[0].shape[2:]
+    if pair:
+        flat = pair[0].shape
+    piece = pl.BlockSpec((2,) + flat[1:], lambda i, _: (i, 0, 0))
+    if own:
+        arrays += [own[0][0], own[1]]
+        specs += [chunk_spec(own[0]), piece]
+        count += 1
+    if pair:
+        arrays += list(pair)
+        specs += [piece] * 2
+        count += 1
+    if following:
+        arrays.append(following[0])
+        specs.append(chunk_spec(following))
+    count += 1
     return pl.pallas_call(
-        functools.partial(sums_kernel, len(pairs), len(copies), len(waits)),
-        in_specs=[pl.BlockSpec(memory_space=pltpu.VMEM)] * len(flat) + [ANYWHERE] * len(waits),
-        out_shape=[out(v.shape, brain_floating) for v in [pair[0] for pair in pairs] + list(copies)],
+        functools.partial(
+            round_kernel, (bool(own), bool(pair), bool(following)), len(waits)
+        ),
+        grid_spec=pltpu.PrefetchScalarGridSpec(
+            num_scalar_prefetch=1,
+            grid=(steps,),
+            in_specs=specs + [ANYWHERE] * len(waits),
+            out_specs=[piece] * count,
+        ),
+        out_shape=[out(flat, brain_floating)] * count,
         compiler_params=pltpu.CompilerParams(vmem_limit_bytes=40 * MIB),
         cost_estimate=takes(2),
-        name="sums",
-    )(*flat, *waits)
+        name="round",
+    )(place, *arrays, *waits)
 
 
 def after_kernel(values_ref, wait_ref, out_ref):
@@ -627,7 +693,7 @@
 
 def adam_kernel(turned, rate, shrink, place_ref, t_ref, r_ref, w_ref, m_ref, v_ref, *rest):
     m_out, v_out, w_out = rest[-3:]
-    inner = (place_ref[0] == 1) | (place_ref[0] == 2)
+    inner = at_inner(place_ref)
     for k in range(t_ref.shape[0]):
         gradient = jnp.where(inner, t_ref[k].astype(jnp.float32), r_ref[k].astype(jnp.float32))
         if turned:
@@ -663,10 +729,46 @@
         ),
         out_shape=[out(weight.shape, jnp.float32)] * 3,
         input_output_aliases={6 + i: i for i in range(len(held))},
-        compiler_params=pltpu.CompilerParams(vmem_limit_bytes=40 * MIB),
+        compiler_params=pltpu.CompilerParams(vmem_limit_bytes=60 * MIB),
         cost_estimate=takes(cost),
         name="adam",
     )(place, total, ends, weight, first, second, *held, wait)
+
+
+def rest_kernel(rates, place_ref, t_ref, r_ref, *refs):
+    inner = at_inner(place_ref)
+    states, outs = (refs[:15], refs[15:])
+
+    def gradient(j):
+        return jnp.where(inner, t_ref[j].astype(jnp.float32), r_ref[j].astype(jnp.float32))
+
+    def step(which, at, gradient):
+        weight, first, second = states[3 * which : 3 * which + 3]
+        rate, shrink = rates[which]
+        results = adamw_step(weight[at], first[at], second[at], gradient, rate, shrink)
+        for ref, value in zip(outs[3 * which : 3 * which + 3], results):
+            ref[at] = value
+
+    small = gradient(PROJECTED // F + 2)[:, :EXTRA]
+    step(0, ..., small.T[EXPERTS : EXPERTS + 2, :])
+    step(4, ..., small[:, :EXPERTS])
+    for half in range(2):
+        at = (slice(None), slice(half * F, half * F + F))
+        step(1, at, gradient(half))
+        step(2, half, gradient(2 + half))
+        step(3, at, gradient(4 + half))
+
+
+def adam_rest(place, total, ends, states, rates):
+    flat = [v for state in states for v in state]
+    in_vmem = pl.BlockSpec(memory_space=pltpu.VMEM)
+    return pl.pallas_call(
+        functools.partial(rest_kernel, rates),
+        in_specs=[pl.BlockSpec(memory_space=pltpu.SMEM)] + [in_vmem] * (2 + len(flat)),
+        out_shape=[out(v.shape, jnp.float32) for v in flat],
+        compiler_params=pltpu.CompilerParams(vmem_limit_bytes=40 * MIB),
+        name="adam_rest",
+    )(place, total, ends, *flat)
 
 
 fsdp = ("outer", "inner")
@@ -757,42 +859,45 @@
         tokens_in, pack, gains_value, alive, bias, cosine, sine, weights
     )
 
-    x_all, ga_all, dgu_all, dx_parts = ([], [], [], [])
+    x_all, ga_all, dgu_all, dx = ([], [], [], None)
     for c in range(CHUNKS):
         x_part = gathered(normed_two, c)
-        ga, dgu, dx = run_experts(me, c, x_part, branch_all, weights, pack)
+        ga, dgu, dx = run_experts(
+            me, c, x_part, branch_all, weights, pack, () if dx is None else (dx,)
+        )
         x_all.append(x_part)
         ga_all.append(ga)
         dgu_all.append(dgu)
-        dx_parts.append(lax.psum_scatter(dx, "inner", scatter_dimension=0, tiled=True))
-
-    def to_owner(grad):
-        parts = grad.reshape(GROUP * outer, shard, F)
+    dx_own = lax.psum_scatter(
+        dx.reshape(GROUP * count_of_rows, MODEL_WIDTH + EXTRA),
+        "inner",
+        scatter_dimension=0,
+        tiled=True,
+    )
+
+    def to_owner(parts):
         if outer > 1:
             parts = lax.psum_scatter(parts, "outer", scatter_dimension=0, tiled=True)
         return lax.all_to_all(parts, "inner", 0, 0)
 
-    def inward(values):
-        return lax.ppermute(values, "replica", [(0, 1), (3, 2)])
+    def swapped(values):
+        return lax.ppermute(values, "replica", [(0, 1), (1, 0), (2, 3), (3, 2)])
 
     def across(values):
         return lax.ppermute(values, "replica", [(1, 2), (2, 1)])
 
-    def outward(values):
-        return lax.ppermute(values, "replica", [(1, 0), (2, 3)])
-
     def grads_of(local, sides, wait, cost):
-        return run_grads(local, sides, x_all, branch_all, ga_all, dgu_all, wait, cost)
+        return run_grads(local, sides, shard, x_all, branch_all, ga_all, dgu_all, wait, cost)
 
     chunks = [(local, side) for local in range(LOCAL) for side in (2, 0, 1)]
-    last = len(chunks) + 1
+    last = len(chunks)
     root = MODEL_WIDTH ** (-0.5)
     states = (
         (gateup_weight, gateup_first, gateup_second),
         (down_weight, down_first, down_second),
     )
     renewed = [None, None]
-    totals_of, ends = ({}, {})
+    by_pairs, totals_of, ends, edges = ({}, {}, {}, {})
 
     def adam_of(k, wait, cost):
         local, side = chunks[k]
@@ -804,114 +909,91 @@
         return renewed[which][0]
 
     first = grads_of(0, (2,), dgu_all[-1], 1)
-    ready = {0: first[0]}
-    token = first[0]
-    mine, by_pairs = ({}, {})
-    mixtures_own = []
-
-    def mix_of(c, wait, cost):
-        rows = run_mix(ga_all[c], weights, wait, cost)
-        mixtures_own.append(lax.psum_scatter(rows, "inner", scatter_dimension=0, tiled=True))
-        return rows
-
+    token = first
+    mine = {0: (to_owner(first), 0)}
     for k in range(-1, last + 3):
-        pairs, copies, waits, keep = ([], [], [], [])
-        if k in mine:
-            pairs.append((mine[k], inward(mine[k])))
-            keep.append((by_pairs, k))
+        own, pair, following, waits = (None, None, None, [])
+        if k in edges:
+            arrived = swapped(edges[k])
+            ends[k - 2] = arrived
+            if k <= last:
+                own = (mine[k], arrived)
+            else:
+                waits.append(arrived)
         if k - 1 in by_pairs:
-            pairs.append((by_pairs[k - 1], across(by_pairs[k - 1])))
-            keep.append((totals_of, k - 1))
-        if k - 2 in totals_of:
-            ends[k - 2] = outward(totals_of[k - 2])
-            waits.append(ends[k - 2])
-
-        arrived = None
-        if 0 <= k + 1 < len(chunks):
-            arrived = to_owner(after(ready[k + 1], token) if k >= 0 else ready[k + 1])
+            pair = (by_pairs[k - 1], across(by_pairs[k - 1]))
+
         if k == -1:
-            ready[1], ready[2] = grads_of(0, (0, 1), token, 1)
-            done = ready[1]
+            second = grads_of(0, (0, 1), token, 1)
+            done = second
         elif k == 0:
-            ready[3], ready[4], ready[5] = grads_of(1, (2, 0, 1), token, 6)
-            done = ready[3]
+            got = to_owner(after(second, token))
+            mine[1], mine[2] = ((got, 0), (got, 1))
+            third = grads_of(1, (2, 0, 1), token, 6)
+            done = third
         elif k == 1:
-            done = mix_of(0, token, 6)
-        elif k == 2:
+            got = to_owner(after(third, token))
+            mine[3], mine[4], mine[5] = ((got, 0), (got, 1), (got, 2))
             d_middle, d_mixed, second_grads = run_middle(
-                dx_parts[0], dx_parts[1], normed_two, middle, cotangent, mask, alive, gains_value,
-                pack, mixed, token,
+                dx_own, normed_two, middle, cotangent, mask, alive, gains_value, pack, mixed, token
             )
             done = d_mixed
-        elif k == 3:
+        elif k == 2:
             rest_grads, input_gradient = run_back(
                 d_mixed, qkv, totals, bias, cosine, sine, normed, tokens_in, d_middle, gains_value,
                 second_grads, pack, token, token,
             )
             rest_own = lax.psum_scatter(rest_grads, fsdp, scatter_dimension=0, tiled=True)
-            waits.append(mixtures_own[0])
+            rest_own = jnp.pad(rest_own, ((0, 0), (0, GROUP * F - rest_own.shape[1])))
+            rest_own = rest_own.reshape(shard, GROUP, F).swapaxes(0, 1)
+            mine[last] = (rest_own.reshape(GROUP, 1, shard, F), 0)
             done = input_gradient
+        elif k == 3:
+            done = adam_of(0, token, 60)
         elif k == 4:
-            done = adam_of(0, mix_of(1, token, 200), 1)
+            mixture = run_mix(ga_all, weights, part_rows, token, 60)
+            mixture_own = lax.psum_scatter(
+                mixture.reshape(GROUP * count_of_rows, MODEL_WIDTH),
+                "inner",
+                scatter_dimension=0,
+                tiled=True,
+            )
+            done = mixture
         elif k == 5:
-            done = adam_of(2, adam_of(1, token, 200), 1)
+            done = adam_of(2, adam_of(1, token, 60), 1)
         elif k - 3 < len(chunks):
-            done = adam_of(k - 3, token, 200)
+            done = adam_of(k - 3, token, 60)
         waits.append(done)
 
-        if 0 <= k + 1 < len(chunks):
-            copies.append(arrived)
-            keep.append((mine, k + 1))
-        elif k + 1 == last:
-            copies.append(rest_own)
-            keep.append((mine, k + 1))
-        if pairs or copies:
-            results = run_sums(pairs, copies, waits)
-            token = results[0]
-            for (kept, at), value in zip(keep, results):
-                kept[at] = value
-
-    mixture_own = jnp.concatenate(mixtures_own, axis=0).astype(jnp.float32)
-    block_output = (middle + alive * mixture_own).astype(brain_floating)
-
-    inner = (place[0] == 1) | (place[0] == 2)
-    rest_sum = jnp.where(inner, totals_of[last], ends[last]).astype(jnp.float32)
-    first_sum, second_sum = (rest_sum[:, : PROJECTED + EXTRA], rest_sum[:, PROJECTED + EXTRA :])
-    gains_part = jnp.stack([first_sum[:, PROJECTED], second_sum[:, MODEL_WIDTH + EXPERTS]])
-    keyval_part = jnp.stack(
-        [first_sum[:, WIDTH : WIDTH + KV_WIDTH], first_sum[:, WIDTH + KV_WIDTH : PROJECTED]]
-    )
-    settings = (
-        (gains_part, norm_gains, gains_first, gains_second, gain_rate, 0.0),
-        (first_sum[:, :WIDTH], query_weight, query_first, query_second, root, decay_rate),
-        (
-            keyval_part,
-            keyvalue_weight,
-            keyvalue_first_moment,
-            keyvalue_second_moment,
-            root,
-            decay_rate,
-        ),
-        (
-            second_sum[:, :MODEL_WIDTH],
-            output_weight,
-            output_first,
-            output_second,
-            (WIDTH // 16) ** (-0.5),
-            decay_rate,
-        ),
-        (
-            second_sum[:, MODEL_WIDTH : MODEL_WIDTH + EXPERTS],
-            router_weight,
-            router_first,
-            router_second,
-            (4 * MODEL_WIDTH) ** (-0.5),
-            decay_rate,
-        ),
-    )
-    updated = []
-    for gradient, weight, first, second, rate, shrink in settings:
-        updated.extend(adamw_step(weight, first, second, gradient, rate, shrink))
+        if k + 1 <= last:
+            following = mine[k + 1]
+        if k == last + 2:
+            continue
+        results = list(run_round(place, own, pair, following, waits))
+        token = results[0]
+        if own:
+            by_pairs[k] = results.pop(0)
+        if pair:
+            totals_of[k - 1] = results.pop(0)
+        edges[k + 1] = results.pop(0)
+
+    block_output = (middle + alive * mixture_own.astype(jnp.float32)).astype(brain_floating)
+
+    rest_states = (
+        (norm_gains, gains_first, gains_second),
+        (query_weight, query_first, query_second),
+        (keyvalue_weight, keyvalue_first_moment, keyvalue_second_moment),
+        (output_weight, output_first, output_second),
+        (router_weight, router_first, router_second),
+    )
+    rates = (
+        (gain_rate, 0.0),
+        (root, decay_rate),
+        (root, decay_rate),
+        ((WIDTH // 16) ** (-0.5), decay_rate),
+        ((4 * MODEL_WIDTH) ** (-0.5), decay_rate),
+    )
+    updated = adam_rest(place, totals_of[last], ends[last], rest_states, rates)
     return (block_output, input_gradient) + tuple(updated) + tuple(renewed[0]) + tuple(renewed[1])
 
 

time: 714 us -> 682 us (0.955)
  starting transfers between devices: 86 us -> 55 us
  local copies, waits for them, and re-layouts: 52.2 us -> 65.7 us
  other arithmetic: 22 us -> 12.1 us
    ppermute x14 -> x9, starting transfers between devices: 42 us -> 26.4 us  [swapped(): return lax.ppermute(values, 'replica', [(0, 1), (1, 0), (2, 3), (3, 2)])]
    reduce_scatter x4 -> x2, waiting for transfers between devices: 0.06 us -> 14.9 us  [the longest x1 14.9 us: body(): lax.psum_scatter(dx.reshape(GROUP * count_of_rows, MODEL_WIDTH + EXTRA),...]
    ppermute x14 -> x9, waiting for transfers between devices: 69.1 us -> 54.4 us  [swapped(): return lax.ppermute(values, 'replica', [(0, 1), (1, 0), (2, 3), (3, 2)])]
    all_to_all x6 -> x3, starting transfers between devices: 26.6 us -> 13.6 us  [to_owner(): return lax.all_to_all(parts, 'inner', 0, 0)]
    unnamed x89 -> x124, local copies, waits for them, and re-layouts: 43 us -> 54.4 us
    sub x4 -> x0, other arithmetic: 7.28 us -> none  [adamw_step(): weight - step_rate * (moment_hat / (jnp.sqrt(square_hat) + adam_eps) + sh...]
    pallas_call x12 -> x11, Pallas kernels: 48.3 us -> 47.6 us  [the longest x9 29.3 us: run_round(): pl.pallas_call(functools.partial(round_kernel, (bool(own), bool(pair), bo...]
  transfers between devices with their start and end apart: 37 -> 27, of which waited for: 14 -> 12; matrix products, arithmetic and copies ran while one was open for 3% -> 4% of each run, Pallas kernels for 40% -> 38%
where the time goes in v3:
time: 682 us; the launch traced here: 672 us
  Pallas kernels  288 us (42%)
  waiting for transfers between devices  236 us (35%)
  local copies, waits for them, and re-layouts  65.7 us (10%)
  starting transfers between devices  55 us (8%)
  between operations  14.9 us (2%)
  other arithmetic  12.1 us (2%)
    all_gather x1, waiting for transfers between devices, body(): pack = lax.all_gather(pack_own, fsdp, axis=0, tiled=True)  79.5 us
    pallas_call x2, Pallas kernels, run_experts(): pl.pallas_call(expert_kernel, grid_spec=pltpu.PrefetchScalarGridSpec(num_...  66.7 us
    pallas_call x3, Pallas kernels, run_grads(): pl.pallas_call(functools.partial(grads_kernel, steps, sides), grid=(CHUNK...  57.6 us
    unnamed x124, local copies, waits for them, and re-layouts  54.4 us
    ppermute x9, waiting for transfers between devices, swapped(): return lax.ppermute(values, 'replica', [(0, 1), (1, 0), (2, 3), (3, 2)])  54.4 us
    all_gather x2, waiting for transfers between devices, gathered(): lax.all_gather(values[c * part_rows:(c + 1) * part_rows], 'inner', axis=0...  45 us
    pallas_call x6, Pallas kernels, adam_part(): pl.pallas_call(functools.partial(adam_kernel, turned, rate, decay_rate),...  44.3 us
    pallas_call x1, Pallas kernels, run_back(): pl.pallas_call(back_kernel, grid=(1,), in_specs=[whole(v.shape) for v in...  33.5 us
  transfers between devices with their start and end apart: 27, of which 12 were waited for; matrix products, arithmetic and copies ran while one was open for 4% of the time, Pallas kernels for 38%

profile of v3, /device:TPU:2, one launch (start us, length us, event | category | flops | bytes accessed | tf_op | source)
XLA Modules:
  0.0 672.2 jit_solution(17343988212116086396)
XLA Ops:
  16.2 9.9 %split.1 = bf16[8,2,3,128,512]{4,3,2,1,0:T(8,128)(2,1)} custom-call(f32[16,2,128,512]{3,2,1,0:T(8,128)} %w_ref.11, f32[16,512,128]{2,1,0:T(8,128)} %w_ref.9), custom_call_target="tpu_custom_call" | custom-call | tf_op jit(solution)/shard_map/split/pallas_call | solution.py:177
  26.1 4.7 all-to-all-start
  33.7 79.5 %all-gather.5.cloned.1.call-done.pack_ref.router_ref.output_ref = bf16[1024,3200]{1,0:T(8,128)(2,1)} async-done(((bf16[128,3200]{1,0:T(8,128)(2,1)}), bf16[1024,3200]{1,0:T(8,128)(2,1)}) %all-gather.5.cloned.1.call-update) | async-done | bytes 6553616 | tf_op jit(solution)/shard_map/all_gather | solution.py:823
  114.5 4.8 all-to-all-done.wait_ref.w_ref.refs_2_
  119.4 19.3 %front.1 = (bf16[512,1024]{1,0:T(8,128)(2,1)}, bf16[512,2048]{1,0:T(8,128)(2,1)}, bf16[512,1024]{1,0:T(8,128)(2,1)}, f32[512,128]{1,0:T(8,128)S(1)}, f32[512,1024]{1,0:T(8,128)}, /*index=5*/bf16[512,1024]{1,0:T(8,128)(2,1)}) custom-call(bf16[512,1024]{1,0:T(8,128)(2,1)} %x_ref.3, ...), custom_call_target="tpu_custom_call" | custom-call | tf_op jit(solution)/shard_map/front/pallas_call | solution.py:249
  141.8 32.8 %all-gather.9.cloned.1.call-done = bf16[4096,1152]{1,0:T(8,128)(2,1)} async-done(((bf16[512,1152]{1,0:T(8,128)(2,1)}), bf16[4096,1152]{1,0:T(8,128)(2,1)}) %all-gather.9.cloned.1.call-update) | async-done | bytes 9437200 | tf_op jit(solution)/shard_map/all_gather | solution.py:854
  174.6 39.2 %all-gather.7.cloned.1.call-done.x_ref.refs_0_.refs_4_.refs_8_ = bf16[2048,1024]{1,0:T(8,128)(2,1)} async-done(((bf16[256,1024]{1,0:T(8,128)(2,1)}), bf16[2048,1024]{1,0:T(8,128)(2,1)}) %all-gather.7.cloned.1.call-update) | async-done | bytes 4194320 | tf_op jit(solution)/shard_map/all_gather | solution.py:850
  213.8 33.3 %experts.2 = (bf16[2048,1024]{1,0:T(8,128)(2,1)}, bf16[2048,2048]{1,0:T(8,128)(2,1)}, bf16[8,2,256,1152]{3,2,1,0:T(8,128)(2,1)}) custom-call(s32[1]{0:T(128)} %bitcast.8.me_ref, bf16[2048,1024]{1,0:T(8,128)(2,1)} %all-gather.7.cloned.1.call-done.x_ref.refs_0_.refs_4_.refs_8_, bf16[8,2,256,1152]{3,2,1,0:T(8,128)(2,1)} %bitcast.22, ...), custom_call_target="tpu_custom_call" | custom-call | tf_op jit(solution)/shard_map/experts/pallas_call | solution.py:476
  247.1 5.7 all-gather.11.cloned.1.call-done.x_ref.refs_2_.refs_6_.refs_10_
  252.8 33.3 %experts.3 = (bf16[2048,1024]{1,0:T(8,128)(2,1)}, bf16[2048,2048]{1,0:T(8,128)(2,1)}, bf16[8,2,256,1152]{3,2,1,0:T(8,128)(2,1)}) custom-call(s32[1]{0:T(128)} %bitcast.8.me_ref, bf16[2048,1024]{1,0:T(8,128)(2,1)} %all-gather.11.cloned.1.call-done.x_ref.refs_2_.refs_6_.refs_10_, bf16[8,2,256,1152]{3,2,1,0:T(8,128)(2,1)} %bitcast.23, ...), custom_call_target="tpu_custom_call", output_to_operand_aliasing={{2}: (5, {})} | custom-call | tf_op jit(solution)/shard_map/experts/pallas_call | solution.py:476
  286.2 12.1 %grads.3.refs_8_ = bf16[8,1,128,512]{3,2,1,0:T(8,128)(2,1)} custom-call(bf16[8,2,256,1152]{3,2,1,0:T(8,128)(2,1)} %bitcast.24, bf16[2048,1024]{1,0:T(8,128)(2,1)} %get-tuple-element.97.refs_1_.refs_0_, bf16[8,2,256,1152]{3,2,1,0:T(8,128)(2,1)} %bitcast.25, bf16[2048,1024]{1,0:T(8,128)(2,1)} %get-tuple-element.99.refs_3_.refs_1_, ...), custom_call_target="tpu_custom_call" | custom-call | flops 1000000000 | bytes 3600000 | tf_op jit(solution)/shard_map/grads/pallas_call | solution.py:559
  302.3 19.3 %grads.4.refs_1_.values_ref = bf16[8,2,128,512]{3,2,1,0:T(8,128)(2,1)} custom-call(bf16[2048,1024]{1,0:T(8,128)(2,1)} %all-gather.7.cloned.1.call-done.x_ref.refs_0_.refs_4_.refs_8_, bf16[2048,2048]{1,0:T(8,128)(2,1)} %get-tuple-element.100.refs_1_.refs_5_.refs_9_, bf16[2048,1024]{1,0:T(8,128)(2,1)} %all-gather.11.cloned.1.call-done.x_ref.refs_2_.refs_6_.refs_10_, ...), custom_call_target="tpu_custom_call" | custom-call | flops 1000000000 | bytes 3600000 | tf_op jit(solution)/shard_map/grads/pallas_call | solution.py:559
  324.7 4.5 all-to-all-start.2
  333.7 26.2 %grads.5.refs_3_.values_ref = bf16[8,3,128,512]{3,2,1,0:T(8,128)(2,1)} custom-call(bf16[8,2,256,1152]{3,2,1,0:T(8,128)(2,1)} %bitcast.26, bf16[2048,1024]{1,0:T(8,128)(2,1)} %get-tuple-element.97.refs_1_.refs_0_, bf16[8,2,256,1152]{3,2,1,0:T(8,128)(2,1)} %bitcast.27, bf16[2048,1024]{1,0:T(8,128)(2,1)} %get-tuple-element.99.refs_3_.refs_1_, ...), custom_call_target="tpu_custom_call" | custom-call | flops 6000000000 | bytes 21600000 | tf_op jit(solution)/shard_map/grads/pallas_call | solution.py:559
  373.5 5.0 all-to-all-start.3
  381.8 14.9 %reduce-scatter.4.cloned.1.call-done.dx_ref = bf16[512,1152]{1,0:T(8,128)(2,1)} async-done(((bf16[4096,1152]{1,0:T(8,128)(2,1)}), bf16[512,1152]{1,0:T(8,128)(2,1)}) %reduce-scatter.4.cloned.1.call-update) | async-done | bytes 1179664 | tf_op jit(solution)/shard_map/reduce_scatter | solution.py:871
  398.5 9.7 %middle_back.1 = (f32[512,1024]{1,0:T(8,128)}, bf16[512,1024]{1,0:T(8,128)(2,1)S(1)}, bf16[1024,1152]{1,0:T(8,128)(2,1)}) custom-call(bf16[512,1152]{1,0:T(8,128)(2,1)} %reduce-scatter.4.cloned.1.call-done.dx_ref, bf16[512,1024]{1,0:T(8,128)(2,1)} %get-tuple-element.96.normed_two_ref, f32[512,1024]{1,0:T(8,128)} %get-tuple-element.95.middle_ref, ...), custom_call_target="tpu_custom_call" | custom-call | flops 30000001024 | bytes 108000000 | tf_op jit(solution)/shard_map/middle_back/pallas_call | solution.py:296
  416.5 33.5 %attention_back.1 = (bf16[1024,3200]{1,0:T(8,128)(2,1)}, f32[512,1024]{1,0:T(8,128)}) custom-call(bf16[512,1024]{1,0:T(8,128)(2,1)S(1)} %copy-done.23, bf16[512,2048]{1,0:T(8,128)(2,1)} %get-tuple-element.109.qkv_ref, f32[512,128]{1,0:T(8,128)S(1)} %copy-done.51, f32[512,512]{1,0:T(8,128)} %fusion.1.bias_ref, f32[512,128]{1,0:T(8,128)S(1)} %get-tuple-element.268.cos_ref, ...), custom_call_target="tpu_custom_call" | custom-call | flops 30000001024 | bytes 108000000 | tf_op jit(solution)/shard_map/attention_back/pallas_call | solution.py:405
  458.2 5.1 collective-permute-start.5
  465.0 7.2 %adam.6 = (f32[16,512,128]{2,1,0:T(8,128)}, f32[16,512,128]{2,1,0:T(8,128)}, f32[16,512,128]{2,1,0:T(8,128)}) custom-call(s32[1]{0:T(128)} %bitcast.10.place_ref, bf16[8,128,512]{2,1,0:T(8,128)(2,1)} %copy-done.46, bf16[8,128,512]{2,1,0:T(8,128)(2,1)} %collective-permute-done.3.refs_1_.r_ref, f32[16,512,128]{2,1,0:T(8,128)} %w_ref.9, f32[16,512,128]{2,1,0:T(8,128)} %m_ref.9, ...), custom_call_target="tpu_custom_call" | custom-call | flops 60000002048 | bytes 216000000 | tf_op jit(solution)/shard_map/adam/pallas_call | solution.py:722
  472.2 13.3 %collective-permute-done.5.refs_1_.r_ref = bf16[8,128,512]{2,1,0:T(8,128)(2,1)} collective-permute-done((bf16[8,128,512]{2,1,0:T(8,128)(2,1)}, bf16[8,128,512]{2,1,0:T(8,128)(2,1)}, u32[]{:S(2)}, u32[]{:S(2)}) %collective-permute-start.5) | collective-permute-done | bytes 1048608 | tf_op jit(solution)/shard_map/ppermute | solution.py:884
  498.3 14.9 %mixture.1.refs_5_ = bf16[8,2,256,1024]{3,2,1,0:T(8,128)(2,1)} custom-call(bf16[2048,1024]{1,0:T(8,128)(2,1)} %get-tuple-element.97.refs_1_.refs_0_, bf16[2048,1024]{1,0:T(8,128)(2,1)} %get-tuple-element.99.refs_3_.refs_1_, bf16[8,2,3,128,512]{4,3,2,1,0:T(8,128)(2,1)} %all-to-all-done.wait_ref.w_ref.refs_2_, ...), custom_call_target="tpu_custom_call" | custom-call | flops 60000002048 | bytes 216000000 | tf_op jit(solution)/shard_map/mixture/pallas_call | solution.py:592
  528.0 8.2 %adam.7 = (f32[16,2,128,512]{3,2,1,0:T(8,128)}, f32[16,2,128,512]{3,2,1,0:T(8,128)}, f32[16,2,128,512]{3,2,1,0:T(8,128)}) custom-call(s32[1]{0:T(128)} %bitcast.10.place_ref, bf16[8,128,512]{2,1,0:T(8,128)(2,1)} %copy-done.44, bf16[8,128,512]{2,1,0:T(8,128)(2,1)} %collective-permute-done.5.refs_1_.r_ref, f32[16,2,128,512]{3,2,1,0:T(8,128)} %w_ref.11, ...), custom_call_target="tpu_custom_call" | custom-call | flops 60000002048 | bytes 216000000 | tf_op jit(solution)/shard_map/adam/pallas_call | solution.py:722
  536.3 8.4 %copy.128.rest_0_ = f32[16,2,128,512]{3,2,1,0:T(8,128)} copy(f32[16,2,128,512]{3,2,1,0:T(8,128)} %get-tuple-element.126.rest_3_) | data formatting | bytes 16777216
  544.7 7.2 %adam.8 = (f32[16,2,128,512]{3,2,1,0:T(8,128)}, f32[16,2,128,512]{3,2,1,0:T(8,128)}, f32[16,2,128,512]{3,2,1,0:T(8,128)}) custom-call(s32[1]{0:T(128)} %bitcast.10.place_ref, bf16[8,128,512]{2,1,0:T(8,128)(2,1)} %copy-done.16, bf16[8,128,512]{2,1,0:T(8,128)(2,1)} %collective-permute-done.7.refs_1_.r_ref, ...), custom_call_target="tpu_custom_call", output_to_operand_aliasing={{0}: (6, {}), {1}: (7, {}), {2}: (8, {})} | custom-call | flops 1000000000 | bytes 3600000 | tf_op jit(solution)/shard_map/adam/pallas_call | solution.py:722
  566.6 7.1 %adam.9 = (f32[16,512,128]{2,1,0:T(8,128)}, f32[16,512,128]{2,1,0:T(8,128)}, f32[16,512,128]{2,1,0:T(8,128)}) custom-call(s32[1]{0:T(128)} %bitcast.10.place_ref, bf16[8,128,512]{2,1,0:T(8,128)(2,1)} %copy-done.45, bf16[8,128,512]{2,1,0:T(8,128)(2,1)} %collective-permute-done.9.refs_1_.r_ref, ...), custom_call_target="tpu_custom_call", output_to_operand_aliasing={{0}: (6, {}), {1}: (7, {}), {2}: (8, {})} | custom-call | flops 60000002048 | bytes 216000000 | tf_op jit(solution)/shard_map/adam/pallas_call | solution.py:722
  573.7 13.3 %collective-permute-done.11.refs_1_.r_ref = bf16[8,128,512]{2,1,0:T(8,128)(2,1)S(1)} collective-permute-done((bf16[8,128,512]{2,1,0:T(8,128)(2,1)}, bf16[8,128,512]{2,1,0:T(8,128)(2,1)S(1)}, u32[]{:S(2)}, u32[]{:S(2)}) %collective-permute-start.11) | collective-permute-done | bytes 1048608 | tf_op jit(solution)/shard_map/ppermute | solution.py:884
  596.7 6.4 collective-permute-start.14
  603.2 7.2 %adam.10 = (f32[16,2,128,512]{3,2,1,0:T(8,128)}, f32[16,2,128,512]{3,2,1,0:T(8,128)}, f32[16,2,128,512]{3,2,1,0:T(8,128)}) custom-call(s32[1]{0:T(128)} %bitcast.10.place_ref, bf16[8,128,512]{2,1,0:T(8,128)(2,1)} %copy-done.47, bf16[8,128,512]{2,1,0:T(8,128)(2,1)} %copy-done.21, ...), custom_call_target="tpu_custom_call", output_to_operand_aliasing={{0}: (6, {}), {1}: (7, {}), {2}: (8, {})} | custom-call | flops 60000002048 | bytes 216000000 | tf_op jit(solution)/shard_map/adam/pallas_call | solution.py:722
  610.4 12.1 %collective-permute-done.14.refs_2_.r_ref = bf16[8,128,512]{2,1,0:T(8,128)(2,1)S(1)} collective-permute-done((bf16[8,128,512]{2,1,0:T(8,128)(2,1)}, bf16[8,128,512]{2,1,0:T(8,128)(2,1)S(1)}, u32[]{:S(2)}, u32[]{:S(2)}) %collective-permute-start.14) | collective-permute-done | bytes 1048608 | tf_op jit(solution)/shard_map/ppermute | solution.py:884
  631.8 7.3 %adam.11 = (f32[16,2,128,512]{3,2,1,0:T(8,128)}, f32[16,2,128,512]{3,2,1,0:T(8,128)}, f32[16,2,128,512]{3,2,1,0:T(8,128)}) custom-call(s32[1]{0:T(128)} %bitcast.10.place_ref, bf16[8,128,512]{2,1,0:T(8,128)(2,1)} %copy-done.48, bf16[8,128,512]{2,1,0:T(8,128)(2,1)} %copy-done.24, ...), custom_call_target="tpu_custom_call", output_to_operand_aliasing={{0}: (6, {}), {1}: (7, {}), {2}: (8, {})} | custom-call | flops 60000002048 | bytes 216000000 | tf_op jit(solution)/shard_map/adam/pallas_call | solution.py:722
  639.1 11.2 %collective-permute-done.15.r_ref = bf16[8,128,512]{2,1,0:T(8,128)(2,1)S(1)} collective-permute-done((bf16[8,128,512]{2,1,0:T(8,128)(2,1)}, bf16[8,128,512]{2,1,0:T(8,128)(2,1)S(1)}, u32[]{:S(2)}, u32[]{:S(2)}) %collective-permute-start.15) | collective-permute-done | bytes 1048608 | tf_op jit(solution)/shard_map/ppermute | solution.py:884
  (213 shorter events, 140.4 us)
Async XLA Ops:
  7.2 106.0 %all-gather.5.cloned.1.call-start = ((), (), s32[]{:S(2)}) async-start(), calls=%async_computation.7 | async-start | bytes 7372800 | tf_op jit(solution)/shard_map/all_gather | solution.py:823
  13.4 161.2 %all-gather.9.cloned.1.call-start = ((), (), s32[]{:S(2)}) async-start(), calls=%async_computation.9 | async-start | bytes 10616832 | tf_op jit(solution)/shard_map/all_gather | solution.py:854
  26.1 93.3 %all-to-all-start = ((bf16[8,2,3,128,512]{4,3,2,1,0:T(8,128)(2,1)}), bf16[8,2,3,128,512]{4,3,2,1,0:T(8,128)(2,1)}, u32[]{:S(2)}, u32[]{:S(2)}) async-start(bf16[8,2,3,128,512]{4,3,2,1,0:T(8,128)(2,1)} %split.1), calls=%async_computation | async-start | bytes 12582912 | tf_op jit(solution)/shard_map/all_to_all | solution.py:827
  30.8 183.0 %all-gather.7.cloned.1.call-start = ((), (), s32[]{:S(2)}) async-start(), calls=%async_computation.8 | async-start | bytes 4718592 | tf_op jit(solution)/shard_map/all_gather | solution.py:850
  31.0 107.6 %copy-start.19 = (f32[512,1]{1,0:T(8,128)}, f32[512,1]{1,0:T(8,128)S(1)}, u32[]{:S(2)}) copy-start(f32[512,1]{1,0:T(8,128)S(1)} %copy.111.alive_ref) | copy-start | bytes 6148
  32.5 106.1 %copy-start.17 = (f32[512,128]{1,0:T(8,128)}, f32[512,128]{1,0:T(8,128)S(1)}, u32[]{:S(2)}) copy-start(f32[512,128]{1,0:T(8,128)S(1)} %get-tuple-element.269.sin_ref) | copy-start | bytes 786436
  138.6 108.5 %copy-start.50 = (f32[512,128]{1,0:T(8,128)}, f32[512,128]{1,0:T(8,128)S(1)}, u32[]{:S(2)}) copy-start(f32[512,128]{1,0:T(8,128)S(1)} %get-tuple-element.110.totals_ref) | copy-start | bytes 786436
  141.0 111.9 %all-gather.11.cloned.1.call-start = ((), (), s32[]{:S(2)}) async-start(), calls=%async_computation.10 | async-start | bytes 4718592 | tf_op jit(solution)/shard_map/all_gather | solution.py:850
  141.6 255.1 %reduce-scatter.4.cloned.1.call-start = ((), (), s32[]{:S(2)}) async-start(), calls=%async_computation.11 | async-start | bytes 10616832 | tf_op jit(solution)/shard_map/reduce_scatter | solution.py:871
  298.3 23.3 %all-to-all-start.1 = ((bf16[8,1,128,512]{3,2,1,0:T(8,128)(2,1)}), bf16[8,1,128,512]{3,2,1,0:T(8,128)(2,1)S(1)}, u32[]{:S(2)}, u32[]{:S(2)}) async-start(bf16[8,1,128,512]{3,2,1,0:T(8,128)(2,1)} %grads.3.refs_8_), calls=%async_computation.1 | async-start | bytes 2097152 | tf_op jit(solution)/shard_map/all_to_all | solution.py:881
  324.7 39.3 %all-to-all-start.2 = ((bf16[8,2,128,512]{3,2,1,0:T(8,128)(2,1)}), bf16[8,2,128,512]{3,2,1,0:T(8,128)(2,1)S(1)}, u32[]{:S(2)}, u32[]{:S(2)}) async-start(bf16[8,2,128,512]{3,2,1,0:T(8,128)(2,1)} %after.2), calls=%async_computation.2 | async-start | bytes 4194304 | tf_op jit(solution)/shard_map/all_to_all | solution.py:881
  329.2 30.8 %collective-permute-start = (bf16[8,128,512]{2,1,0:T(8,128)(2,1)S(1)}, bf16[8,128,512]{2,1,0:T(8,128)(2,1)}, u32[]{:S(2)}, u32[]{:S(2)}) collective-permute-start(bf16[8,128,512]{2,1,0:T(8,128)(2,1)S(1)} %copy-done.11), channel_id=1, source_target_pairs={{0,8},{8,0},{16,24},{24,16},{1,9},{9,1},{17,25},{25,17},{2,10},{10... | collective-permute-start | bytes 3145736 | tf_op jit(solution)/shard_map/ppermute | solution.py:884
  371.8 37.4 %collective-permute-start.2 = (bf16[8,128,512]{2,1,0:T(8,128)(2,1)}, bf16[8,128,512]{2,1,0:T(8,128)(2,1)}, u32[]{:S(2)}, u32[]{:S(2)}) collective-permute-start(bf16[8,128,512]{2,1,0:T(8,128)(2,1)} %get-tuple-element.102.wait_ref.refs_2_), channel_id=1, source_target_pairs={{8,16},{16,8},{9,17},{17,9},{10,18},{18,10},{11,19},{19,11},{12,20... | collective-permute-start | bytes 3145736 | tf_op jit(solution)/shard_map/ppermute | solution.py:887
  373.5 76.6 %all-to-all-start.3 = ((bf16[8,3,128,512]{3,2,1,0:T(8,128)(2,1)}), bf16[8,3,128,512]{3,2,1,0:T(8,128)(2,1)S(1)}, u32[]{:S(2)}, u32[]{:S(2)}) async-start(bf16[8,3,128,512]{3,2,1,0:T(8,128)(2,1)} %after.3), calls=%async_computation.3 | async-start | bytes 6291456 | tf_op jit(solution)/shard_map/all_to_all | solution.py:881
  378.5 173.4 %reduce-scatter.8.cloned.1.call-start = ((), (), s32[]{:S(2)}) async-start(), calls=%async_computation.13 | async-start | bytes 7372800 | tf_op jit(solution)/shard_map/reduce_scatter | solution.py:946
  378.5 30.8 %collective-permute-start.1 = (bf16[8,128,512]{2,1,0:T(8,128)(2,1)}, bf16[8,128,512]{2,1,0:T(8,128)(2,1)}, u32[]{:S(2)}, u32[]{:S(2)}) collective-permute-start(bf16[8,128,512]{2,1,0:T(8,128)(2,1)} %copy-done.49), channel_id=1, source_target_pairs={{0,8},{8,0},{16,24},{24,16},{1,9},{9,1},{17,25},{25,17},{2,10},{10... | collective-permute-start | bytes 3145736 | tf_op jit(solution)/shard_map/ppermute | solution.py:884
  414.6 35.3 %copy-start.46 = (bf16[8,128,512]{2,1,0:T(8,128)(2,1)}, bf16[8,128,512]{2,1,0:T(8,128)(2,1)S(1)}, u32[]{:S(2)}) copy-start(bf16[8,128,512]{2,1,0:T(8,128)(2,1)S(1)} %get-tuple-element.117.t_ref) | copy-start | bytes 3145732
  414.6 35.4 %collective-permute-start.3 = (bf16[8,128,512]{2,1,0:T(8,128)(2,1)}, bf16[8,128,512]{2,1,0:T(8,128)(2,1)}, u32[]{:S(2)}, u32[]{:S(2)}) collective-permute-start(bf16[8,128,512]{2,1,0:T(8,128)(2,1)} %get-tuple-element.107), channel_id=1, source_target_pairs={{0,8},{8,0},{16,24},{24,16},{1,9},{9,1},{17,25},{25,17},{2,10},{10... | collective-permute-start | bytes 3145736 | tf_op jit(solution)/shard_map/ppermute | solution.py:884
  414.7 35.4 %collective-permute-start.4 = (bf16[8,128,512]{2,1,0:T(8,128)(2,1)}, bf16[8,128,512]{2,1,0:T(8,128)(2,1)}, u32[]{:S(2)}, u32[]{:S(2)}) collective-permute-start(bf16[8,128,512]{2,1,0:T(8,128)(2,1)} %get-tuple-element.108.wait_ref.also_ref.refs_2_), channel_id=1, source_target_pairs={{8,16},{16,8},{9,17},{17,9},{10,18},{18,10},{11,19},{19,11},{12,20... | collective-permute-start | bytes 3145736 | tf_op jit(solution)/shard_map/ppermute | solution.py:887
  450.0 212.1 %reduce-scatter.6.cloned.1.call-start = ((), (), s32[]{:S(2)}) async-start(), calls=%async_computation.12 | async-start | bytes 9437184 | tf_op jit(solution)/shard_map/reduce_scatter | solution.py:955
  458.2 27.3 %collective-permute-start.5 = (bf16[8,128,512]{2,1,0:T(8,128)(2,1)}, bf16[8,128,512]{2,1,0:T(8,128)(2,1)}, u32[]{:S(2)}, u32[]{:S(2)}) collective-permute-start(bf16[8,128,512]{2,1,0:T(8,128)(2,1)} %get-tuple-element.115), channel_id=1, source_target_pairs={{0,8},{8,0},{16,24},{24,16},{1,9},{9,1},{17,25},{25,17},{2,10},{10... | collective-permute-start | bytes 3145736 | tf_op jit(solution)/shard_map/ppermute | solution.py:884
  463.3 22.2 %collective-permute-start.6 = (bf16[8,128,512]{2,1,0:T(8,128)(2,1)}, bf16[8,128,512]{2,1,0:T(8,128)(2,1)}, u32[]{:S(2)}, u32[]{:S(2)}) collective-permute-start(bf16[8,128,512]{2,1,0:T(8,128)(2,1)} %get-tuple-element.116.rest_0_.refs_2_), channel_id=1, source_target_pairs={{8,16},{16,8},{9,17},{17,9},{10,18},{18,10},{11,19},{19,11},{12,20... | collective-permute-start | bytes 3145736 | tf_op jit(solution)/shard_map/ppermute | solution.py:887
  492.8 24.9 %collective-permute-start.7 = (bf16[8,128,512]{2,1,0:T(8,128)(2,1)}, bf16[8,128,512]{2,1,0:T(8,128)(2,1)}, u32[]{:S(2)}, u32[]{:S(2)}) collective-permute-start(bf16[8,128,512]{2,1,0:T(8,128)(2,1)} %get-tuple-element.121), channel_id=1, source_target_pairs={{0,8},{8,0},{16,24},{24,16},{1,9},{9,1},{17,25},{25,17},{2,10},{10... | collective-permute-start | bytes 3145736 | tf_op jit(solution)/shard_map/ppermute | solution.py:884
  496.5 21.2 %collective-permute-start.8 = (bf16[8,128,512]{2,1,0:T(8,128)(2,1)}, bf16[8,128,512]{2,1,0:T(8,128)(2,1)}, u32[]{:S(2)}, u32[]{:S(2)}) collective-permute-start(bf16[8,128,512]{2,1,0:T(8,128)(2,1)} %get-tuple-element.119.refs_3_.refs_2_), channel_id=1, source_target_pairs={{8,16},{16,8},{9,17},{17,9},{10,18},{18,10},{11,19},{19,11},{12,20... | collective-permute-start | bytes 3145736 | tf_op jit(solution)/shard_map/ppermute | solution.py:887
  522.8 35.8 %collective-permute-start.9 = (bf16[8,128,512]{2,1,0:T(8,128)(2,1)}, bf16[8,128,512]{2,1,0:T(8,128)(2,1)}, u32[]{:S(2)}, u32[]{:S(2)}) collective-permute-start(bf16[8,128,512]{2,1,0:T(8,128)(2,1)} %get-tuple-element.122), channel_id=1, source_target_pairs={{0,8},{8,0},{16,24},{24,16},{1,9},{9,1},{17,25},{25,17},{2,10},{10... | collective-permute-start | bytes 3145736 | tf_op jit(solution)/shard_map/ppermute | solution.py:884
  526.4 32.2 %collective-permute-start.10 = (bf16[8,128,512]{2,1,0:T(8,128)(2,1)}, bf16[8,128,512]{2,1,0:T(8,128)(2,1)}, u32[]{:S(2)}, u32[]{:S(2)}) collective-permute-start(bf16[8,128,512]{2,1,0:T(8,128)(2,1)} %get-tuple-element.123.rest_0_.refs_2_), channel_id=1, source_target_pairs={{8,16},{16,8},{9,17},{17,9},{10,18},{18,10},{11,19},{19,11},{12,20... | collective-permute-start | bytes 3145736 | tf_op jit(solution)/shard_map/ppermute | solution.py:887
  564.9 22.1 %collective-permute-start.11 = (bf16[8,128,512]{2,1,0:T(8,128)(2,1)}, bf16[8,128,512]{2,1,0:T(8,128)(2,1)S(1)}, u32[]{:S(2)}, u32[]{:S(2)}) collective-permute-start(bf16[8,128,512]{2,1,0:T(8,128)(2,1)} %get-tuple-element.130), channel_id=1, source_target_pairs={{0,8},{8,0},{16,24},{24,16},{1,9},{9,1},{17,25},{25,17},{2,10},{10... | collective-permute-start | bytes 3145736 | tf_op jit(solution)/shard_map/ppermute | solution.py:884
  565.9 21.1 %collective-permute-start.12 = (bf16[8,128,512]{2,1,0:T(8,128)(2,1)}, bf16[8,128,512]{2,1,0:T(8,128)(2,1)S(1)}, u32[]{:S(2)}, u32[]{:S(2)}) collective-permute-start(bf16[8,128,512]{2,1,0:T(8,128)(2,1)} %get-tuple-element.131.rest_3_.refs_2_), channel_id=1, source_target_pairs={{8,16},{16,8},{9,17},{17,9},{10,18},{18,10},{11,19},{19,11},{12,20... | collective-permute-start | bytes 3145736 | tf_op jit(solution)/shard_map/ppermute | solution.py:887
  566.6 21.4 %copy-start.9 = (bf16[128,8,512]{2,0,1:T(8,128)(2,1)S(1)}, bf16[128,8,512]{2,0,1:T(8,128)(2,1)}, u32[]{:S(2)}) copy-start(bf16[128,8,512]{2,0,1:T(8,128)(2,1)} %copy.117) | copy-start | bytes 3145732
  596.0 14.4 %collective-permute-start.13 = (bf16[8,128,512]{2,1,0:T(8,128)(2,1)S(1)}, bf16[8,128,512]{2,1,0:T(8,128)(2,1)S(1)}, u32[]{:S(2)}, u32[]{:S(2)}) collective-permute-start(bf16[8,128,512]{2,1,0:T(8,128)(2,1)S(1)} %get-tuple-element.136.rest_3_.refs_0_), channel_id=1, source_target_pairs={{8,16},{16,8},{9,17},{17,9},{10,18},{18,10},{11,19},{19,11},{12,20... | collective-permute-start | bytes 3145736 | tf_op jit(solution)/shard_map/ppermute | solution.py:887
  596.7 25.7 %collective-permute-start.14 = (bf16[8,128,512]{2,1,0:T(8,128)(2,1)}, bf16[8,128,512]{2,1,0:T(8,128)(2,1)S(1)}, u32[]{:S(2)}, u32[]{:S(2)}) collective-permute-start(bf16[8,128,512]{2,1,0:T(8,128)(2,1)} %get-tuple-element.137), channel_id=1, source_target_pairs={{0,8},{8,0},{16,24},{24,16},{1,9},{9,1},{17,25},{25,17},{2,10},{10... | collective-permute-start | bytes 3145736 | tf_op jit(solution)/shard_map/ppermute | solution.py:884
  630.0 20.4 %collective-permute-start.15 = (bf16[8,128,512]{2,1,0:T(8,128)(2,1)}, bf16[8,128,512]{2,1,0:T(8,128)(2,1)S(1)}, u32[]{:S(2)}, u32[]{:S(2)}) collective-permute-start(bf16[8,128,512]{2,1,0:T(8,128)(2,1)} %get-tuple-element.143), channel_id=1, source_target_pairs={{0,8},{8,0},{16,24},{24,16},{1,9},{9,1},{17,25},{25,17},{2,10},{10... | collective-permute-start | bytes 3145736 | tf_op jit(solution)/shard_map/ppermute | solution.py:884
  (53 other events, 293.5 us)
Sparse Core Ops, SparseCore 0:
  13.5 99.7 all-gather.4
  115.7 58.8 all-gather.8
  177.0 36.7 all-gather.6
  216.1 36.7 all-gather.10
  286.3 110.3 reduce-scatter.3
  450.1 64.3 reduce-scatter.7
  518.4 71.2 reduce-scatter.5

commit v4 on v3

--- a/solution.py
+++ b/solution.py
@@ -190,8 +190,7 @@
 
 
 def front_kernel(
-    x_ref, pack_ref, gains_ref, alive_ref, bias_ref, cos_ref, sin_ref, wait_ref,
-    normed_ref, qkv_ref, mixed_ref, totals_ref, middle_ref, normed_two_ref, linear_ref,
+    x_ref, pack_ref, gains_ref, alive_ref, bias_ref, cos_ref, sin_ref, wait_ref, normed_ref, qkv_ref, mixed_ref, totals_ref, middle_ref, normed_two_ref, linear_ref,
 ):
     rows = x_ref.shape[0]
     scaled, _ = normalize(x_ref[...].astype(jnp.float32))
@@ -692,7 +691,8 @@
 
 
 def adam_kernel(turned, rate, shrink, place_ref, t_ref, r_ref, w_ref, m_ref, v_ref, *rest):
-    m_out, v_out, w_out = rest[-3:]
+    m_out, v_out, w_out, token_ref = rest[-4:]
+    token_ref[...] = jnp.zeros_like(token_ref)
     inner = at_inner(place_ref)
     for k in range(t_ref.shape[0]):
         gradient = jnp.where(inner, t_ref[k].astype(jnp.float32), r_ref[k].astype(jnp.float32))
@@ -725,9 +725,9 @@
             num_scalar_prefetch=1,
             grid=(GROUP // 2,),
             in_specs=[piece, piece, spec, spec, spec] + [ANYWHERE] * (len(held) + 1),
-            out_specs=[spec] * 3,
+            out_specs=[spec] * 3 + [pl.BlockSpec((8, LANES), lambda i, _: (0, 0))],
         ),
-        out_shape=[out(weight.shape, jnp.float32)] * 3,
+        out_shape=[out(weight.shape, jnp.float32)] * 3 + [out((8, LANES), jnp.float32)],
         input_output_aliases={6 + i: i for i in range(len(held))},
         compiler_params=pltpu.CompilerParams(vmem_limit_bytes=60 * MIB),
         cost_estimate=takes(cost),
@@ -824,7 +824,8 @@
     at = PROJECTED + MODEL_WIDTH + EXPERTS
     gains_value = pack[:, at : at + 2].astype(jnp.float32).T
 
-    weights = lax.all_to_all(split_by_owner(gateup_weight, down_weight), "inner", 0, 0)
+    weights_own = split_by_owner(gateup_weight, down_weight)
+    weights = lax.all_to_all(weights_own, "inner", 0, 0)
     if outer > 1:
         weights = lax.all_gather(weights, "outer", axis=0, tiled=True)
 
@@ -856,7 +857,7 @@
     )
 
     normed, qkv, mixed, totals, middle, normed_two = run_front(
-        tokens_in, pack, gains_value, alive, bias, cosine, sine, weights
+        tokens_in, pack, gains_value, alive, bias, cosine, sine, weights_own
     )
 
     x_all, ga_all, dgu_all, dx = ([], [], [], None)
@@ -902,11 +903,11 @@
     def adam_of(k, wait, cost):
         local, side = chunks[k]
         which = side // 2
-        renewed[which] = adam_part(
+        *renewed[which], done = adam_part(
             place, totals_of[k], ends[k], states[which], local, side,
             (F // 16) ** (-0.5) if which else root, renewed[which], wait, cost,
         )
-        return renewed[which][0]
+        return done
 
     first = grads_of(0, (2,), dgu_all[-1], 1)
     token = first
@@ -929,16 +930,20 @@
         elif k == 0:
             got = to_owner(after(second, token))
             mine[1], mine[2] = ((got, 0), (got, 1))
-            third = grads_of(1, (2, 0, 1), token, 6)
+            third = grads_of(1, (2,), token, 3)
             done = third
         elif k == 1:
-            got = to_owner(after(third, token))
-            mine[3], mine[4], mine[5] = ((got, 0), (got, 1), (got, 2))
+            mine[3] = (to_owner(after(third, token)), 0)
+            fourth = grads_of(1, (0, 1), token, 3)
+            done = fourth
+        elif k == 2:
+            got = to_owner(after(fourth, token))
+            mine[4], mine[5] = ((got, 0), (got, 1))
             d_middle, d_mixed, second_grads = run_middle(
                 dx_own, normed_two, middle, cotangent, mask, alive, gains_value, pack, mixed, token
             )
             done = d_mixed
-        elif k == 2:
+        elif k == 3:
             rest_grads, input_gradient = run_back(
                 d_mixed, qkv, totals, bias, cosine, sine, normed, tokens_in, d_middle, gains_value,
                 second_grads, pack, token, token,
@@ -948,8 +953,6 @@
             rest_own = rest_own.reshape(shard, GROUP, F).swapaxes(0, 1)
             mine[last] = (rest_own.reshape(GROUP, 1, shard, F), 0)
             done = input_gradient
-        elif k == 3:
-            done = adam_of(0, token, 60)
         elif k == 4:
             mixture = run_mix(ga_all, weights, part_rows, token, 60)
             mixture_own = lax.psum_scatter(
@@ -960,7 +963,9 @@
             )
             done = mixture
         elif k == 5:
-            done = adam_of(2, adam_of(1, token, 60), 1)
+            done = adam_of(1, adam_of(0, token, 60), 1)
+        elif k == 6:
+            done = adam_of(3, adam_of(2, token, 60), 1)
         elif k - 3 < len(chunks):
             done = adam_of(k - 3, token, 60)
         waits.append(done)

time: 682 us -> 704 us (1.032)
  waiting for transfers between devices: 236 us -> 261 us
  local copies, waits for them, and re-layouts: 65.7 us -> 51.8 us
  starting transfers between devices: 55 us -> 63.4 us
    all_to_all x1, waiting for transfers between devices: 4.84 us -> 95.3 us  [body(): weights = lax.all_to_all(weights_own, 'inner', 0, 0)]
    all_gather x1, waiting for transfers between devices: 79.5 us -> 32.4 us  [body(): pack = lax.all_gather(pack_own, fsdp, axis=0, tiled=True)]
    all_gather x1, waiting for transfers between devices: 32.8 us -> 0.01 us  [body(): lax.all_gather(branch_pack, 'inner', axis=0, tiled=True)]
    all_to_all x3 -> x4, waiting for transfers between devices: 4.05 us -> 30.7 us  [to_owner(): return lax.all_to_all(parts, 'inner', 0, 0)]
    reduce_scatter x1, waiting for transfers between devices: 14.9 us -> 0.01 us  [body(): lax.psum_scatter(dx.reshape(GROUP * count_of_rows, MODEL_WIDTH + EXTRA),...]
    unnamed x124 -> x141, local copies, waits for them, and re-layouts: 54.4 us -> 41.2 us
    ppermute x9, waiting for transfers between devices: 54.4 us -> 63.8 us  [swapped(): return lax.ppermute(values, 'replica', [(0, 1), (1, 0), (2, 3), (3, 2)])]
    all_to_all x3 -> x4, starting transfers between devices: 13.6 us -> 18.3 us  [to_owner(): return lax.all_to_all(parts, 'inner', 0, 0)]
  transfers between devices with their start and end apart: 27 -> 28, of which waited for: 12 -> 14; matrix products, arithmetic and copies ran while one was open for 4% -> 3% of each run, Pallas kernels for 38% -> 32%
where the time goes in v4:
time: 704 us; the launch traced here: 693 us
  Pallas kernels  290 us (41%)
  waiting for transfers between devices  261 us (37%)
  starting transfers between devices  63.4 us (9%)
  local copies, waits for them, and re-layouts  51.8 us (7%)
  between operations  14.9 us (2%)
  other arithmetic  12.1 us (2%)
    all_to_all x1, waiting for transfers between devices, body(): weights = lax.all_to_all(weights_own, 'inner', 0, 0)  95.3 us
    pallas_call x2, Pallas kernels, run_experts(): pl.pallas_call(expert_kernel, grid_spec=pltpu.PrefetchScalarGridSpec(num_...  66.7 us
    ppermute x9, waiting for transfers between devices, swapped(): return lax.ppermute(values, 'replica', [(0, 1), (1, 0), (2, 3), (3, 2)])  63.8 us
    pallas_call x4, Pallas kernels, run_grads(): pl.pallas_call(functools.partial(grads_kernel, steps, sides), grid=(CHUNK...  60.2 us
    pallas_call x6, Pallas kernels, adam_part(): pl.pallas_call(functools.partial(adam_kernel, turned, rate, decay_rate),...  44.2 us
    unnamed x141, local copies, waits for them, and re-layouts  41.2 us
    all_gather x2, waiting for transfers between devices, gathered(): lax.all_gather(values[c * part_rows:(c + 1) * part_rows], 'inner', axis=0...  38.6 us
    pallas_call x1, Pallas kernels, run_back(): pl.pallas_call(back_kernel, grid=(1,), in_specs=[whole(v.shape) for v in...  33.5 us
  transfers between devices with their start and end apart: 28, of which 14 were waited for; matrix products, arithmetic and copies ran while one was open for 3% of the time, Pallas kernels for 32%

profile of v4, /device:TPU:2, one launch (start us, length us, event | category | flops | bytes accessed | tf_op | source)
XLA Modules:
  0.0 693.4 jit_solution(14611534303210636717)
XLA Ops:
  16.4 9.9 %split.1.wait_ref = bf16[8,2,3,128,512]{4,3,2,1,0:T(8,128)(2,1)} custom-call(f32[16,2,128,512]{3,2,1,0:T(8,128)} %w_ref.11, f32[16,512,128]{2,1,0:T(8,128)} %w_ref.9), custom_call_target="tpu_custom_call" | custom-call | tf_op jit(solution)/shard_map/split/pallas_call | solution.py:177
  29.0 32.4 %all-gather.5.cloned.1.call-done.pack_ref.router_ref.output_ref = bf16[1024,3200]{1,0:T(8,128)(2,1)} async-done(((bf16[128,3200]{1,0:T(8,128)(2,1)}), bf16[1024,3200]{1,0:T(8,128)(2,1)}) %all-gather.5.cloned.1.call-update) | async-done | bytes 6553616 | tf_op jit(solution)/shard_map/all_gather | solution.py:823
  62.7 19.2 %front.1 = (bf16[512,1024]{1,0:T(8,128)(2,1)}, bf16[512,2048]{1,0:T(8,128)(2,1)}, bf16[512,1024]{1,0:T(8,128)(2,1)}, f32[512,128]{1,0:T(8,128)S(1)}, f32[512,1024]{1,0:T(8,128)}, /*index=5*/bf16[512,1024]{1,0:T(8,128)(2,1)}) custom-call(bf16[512,1024]{1,0:T(8,128)(2,1)} %x_ref.3, ...), custom_call_target="tpu_custom_call" | custom-call | tf_op jit(solution)/shard_map/front/pallas_call | solution.py:248
  84.8 5.2 all-to-all-start
  90.2 95.3 %all-to-all-done.w_ref.refs_2_ = bf16[8,2,3,128,512]{4,3,2,1,0:T(8,128)(2,1)} async-done(((bf16[8,2,3,128,512]{4,3,2,1,0:T(8,128)(2,1)}), bf16[8,2,3,128,512]{4,3,2,1,0:T(8,128)(2,1)}, u32[]{:S(2)}, u32[]{:S(2)}) %all-to-all-start) | async-done | bytes 6291488 | tf_op jit(solution)/shard_map/all_to_all | solution.py:828
  185.4 32.8 %all-gather.7.cloned.1.call-done.x_ref.refs_0_.refs_4_ = bf16[2048,1024]{1,0:T(8,128)(2,1)} async-done(((bf16[256,1024]{1,0:T(8,128)(2,1)}), bf16[2048,1024]{1,0:T(8,128)(2,1)}) %all-gather.7.cloned.1.call-update) | async-done | bytes 4194320 | tf_op jit(solution)/shard_map/all_gather | solution.py:851
  218.3 33.3 %experts.2 = (bf16[2048,1024]{1,0:T(8,128)(2,1)}, bf16[2048,2048]{1,0:T(8,128)(2,1)}, bf16[8,2,256,1152]{3,2,1,0:T(8,128)(2,1)}) custom-call(s32[1]{0:T(128)} %bitcast.8.me_ref, bf16[2048,1024]{1,0:T(8,128)(2,1)} %all-gather.7.cloned.1.call-done.x_ref.refs_0_.refs_4_, bf16[8,2,256,1152]{3,2,1,0:T(8,128)(2,1)} %bitcast.22, ...), custom_call_target="tpu_custom_call" | custom-call | tf_op jit(solution)/shard_map/experts/pallas_call | solution.py:475
  251.6 5.7 all-gather.11.cloned.1.call-done.x_ref.refs_2_.refs_6_
  257.4 33.3 %experts.3 = (bf16[2048,1024]{1,0:T(8,128)(2,1)}, bf16[2048,2048]{1,0:T(8,128)(2,1)}, bf16[8,2,256,1152]{3,2,1,0:T(8,128)(2,1)}) custom-call(s32[1]{0:T(128)} %bitcast.8.me_ref, bf16[2048,1024]{1,0:T(8,128)(2,1)} %all-gather.11.cloned.1.call-done.x_ref.refs_2_.refs_6_, bf16[8,2,256,1152]{3,2,1,0:T(8,128)(2,1)} %bitcast.23, ...), custom_call_target="tpu_custom_call", output_to_operand_aliasing={{2}: (5, {})} | custom-call | tf_op jit(solution)/shard_map/experts/pallas_call | solution.py:475
  290.7 12.1 %grads.4.refs_8_ = bf16[8,1,128,512]{3,2,1,0:T(8,128)(2,1)} custom-call(bf16[8,2,256,1152]{3,2,1,0:T(8,128)(2,1)} %bitcast.24, bf16[2048,1024]{1,0:T(8,128)(2,1)} %get-tuple-element.102.refs_1_.refs_0_, bf16[8,2,256,1152]{3,2,1,0:T(8,128)(2,1)} %bitcast.25, bf16[2048,1024]{1,0:T(8,128)(2,1)} %get-tuple-element.104.refs_3_.refs_1_, ...), custom_call_target="tpu_custom_call" | custom-call | flops 1000000000 | bytes 3600000 | tf_op jit(solution)/shard_map/grads/pallas_call | solution.py:558
  306.8 18.9 %grads.5.refs_1_.values_ref = bf16[8,2,128,512]{3,2,1,0:T(8,128)(2,1)} custom-call(bf16[2048,1024]{1,0:T(8,128)(2,1)} %all-gather.7.cloned.1.call-done.x_ref.refs_0_.refs_4_, bf16[2048,2048]{1,0:T(8,128)(2,1)} %get-tuple-element.106.refs_1_.refs_5_, bf16[2048,1024]{1,0:T(8,128)(2,1)} %all-gather.11.cloned.1.call-done.x_ref.refs_2_.refs_6_, ...), custom_call_target="tpu_custom_call" | custom-call | flops 1000000000 | bytes 3600000 | tf_op jit(solution)/shard_map/grads/pallas_call | solution.py:558
  334.7 10.3 %grads.6.refs_3_.values_ref = bf16[8,1,128,512]{3,2,1,0:T(8,128)(2,1)S(1)} custom-call(bf16[8,2,256,1152]{3,2,1,0:T(8,128)(2,1)} %bitcast.26, bf16[2048,1024]{1,0:T(8,128)(2,1)} %get-tuple-element.102.refs_1_.refs_0_, bf16[8,2,256,1152]{3,2,1,0:T(8,128)(2,1)} %bitcast.27, bf16[2048,1024]{1,0:T(8,128)(2,1)} %get-tuple-element.104.refs_3_.refs_1_, ...), custom_call_target="tpu_custom_call" | custom-call | flops 3000000000 | bytes 10800000 | tf_op jit(solution)/shard_map/grads/pallas_call | solution.py:558
  346.0 12.4 %collective-permute-done.refs_1_ = bf16[8,128,512]{2,1,0:T(8,128)(2,1)S(1)} collective-permute-done((bf16[8,128,512]{2,1,0:T(8,128)(2,1)S(1)}, bf16[8,128,512]{2,1,0:T(8,128)(2,1)S(1)}, u32[]{:S(2)}, u32[]{:S(2)}) %collective-permute-start) | collective-permute-done | bytes 1048608 | tf_op jit(solution)/shard_map/ppermute | solution.py:885
  359.3 9.2 %all-to-all-done.2.refs_2_.refs_0_.refs_4_ = bf16[8,2,128,512]{3,2,1,0:T(8,128)(2,1)S(1)} async-done(((bf16[8,2,128,512]{3,2,1,0:T(8,128)(2,1)}), bf16[8,2,128,512]{3,2,1,0:T(8,128)(2,1)S(1)}, u32[]{:S(2)}, u32[]{:S(2)}) %all-to-all-start.2) | async-done | bytes 2097184 | tf_op jit(solution)/shard_map/all_to_all | solution.py:882
  377.1 5.7 all-to-all-start.3
  383.9 18.9 %grads.7.refs_5_.values_ref = bf16[8,2,128,512]{3,2,1,0:T(8,128)(2,1)} custom-call(bf16[2048,1024]{1,0:T(8,128)(2,1)} %all-gather.7.cloned.1.call-done.x_ref.refs_0_.refs_4_, bf16[2048,2048]{1,0:T(8,128)(2,1)} %get-tuple-element.106.refs_1_.refs_5_, bf16[2048,1024]{1,0:T(8,128)(2,1)} %all-gather.11.cloned.1.call-done.x_ref.refs_2_.refs_6_, ...), custom_call_target="tpu_custom_call" | custom-call | flops 3000000000 | bytes 10800000 | tf_op jit(solution)/shard_map/grads/pallas_call | solution.py:558
  414.3 9.6 %middle_back.1 = (f32[512,1024]{1,0:T(8,128)}, bf16[512,1024]{1,0:T(8,128)(2,1)S(1)}, bf16[1024,1152]{1,0:T(8,128)(2,1)}) custom-call(bf16[512,1152]{1,0:T(8,128)(2,1)} %reduce-scatter.4.cloned.1.call-done.dx_ref, bf16[512,1024]{1,0:T(8,128)(2,1)} %get-tuple-element.101.normed_two_ref, f32[512,1024]{1,0:T(8,128)} %get-tuple-element.100.middle_ref, ...), custom_call_target="tpu_custom_call" | custom-call | flops 30000001024 | bytes 108000000 | tf_op jit(solution)/shard_map/middle_back/pallas_call | solution.py:295
  424.8 11.6 %collective-permute-done.3.refs_1_.r_ref = bf16[8,128,512]{2,1,0:T(8,128)(2,1)} collective-permute-done((bf16[8,128,512]{2,1,0:T(8,128)(2,1)}, bf16[8,128,512]{2,1,0:T(8,128)(2,1)}, u32[]{:S(2)}, u32[]{:S(2)}) %collective-permute-start.3) | collective-permute-done | bytes 1048608 | tf_op jit(solution)/shard_map/ppermute | solution.py:885
  444.1 33.5 %attention_back.1 = (bf16[1024,3200]{1,0:T(8,128)(2,1)}, f32[512,1024]{1,0:T(8,128)}) custom-call(bf16[512,1024]{1,0:T(8,128)(2,1)S(1)} %copy-done.53, bf16[512,2048]{1,0:T(8,128)(2,1)} %get-tuple-element.116.qkv_ref, f32[512,128]{1,0:T(8,128)S(1)} %copy-done.48, f32[512,512]{1,0:T(8,128)} %fusion.1.bias_ref, f32[512,128]{1,0:T(8,128)S(1)} %get-tuple-element.278.cos_ref, ...), custom_call_target="tpu_custom_call" | custom-call | flops 30000001024 | bytes 108000000 | tf_op jit(solution)/shard_map/attention_back/pallas_call | solution.py:404
  487.5 21.5 %all-to-all-done.4.refs_4_.refs_0_ = bf16[8,2,128,512]{3,2,1,0:T(8,128)(2,1)S(1)} async-done(((bf16[8,2,128,512]{3,2,1,0:T(8,128)(2,1)}), bf16[8,2,128,512]{3,2,1,0:T(8,128)(2,1)S(1)}, u32[]{:S(2)}, u32[]{:S(2)}) %all-to-all-start.4) | async-done | bytes 2097184 | tf_op jit(solution)/shard_map/all_to_all | solution.py:882
  517.2 5.6 collective-permute-start.7
  524.4 15.1 %mixture.1.refs_5_ = bf16[8,2,256,1024]{3,2,1,0:T(8,128)(2,1)} custom-call(bf16[2048,1024]{1,0:T(8,128)(2,1)} %get-tuple-element.102.refs_1_.refs_0_, bf16[2048,1024]{1,0:T(8,128)(2,1)} %get-tuple-element.104.refs_3_.refs_1_, bf16[8,2,3,128,512]{4,3,2,1,0:T(8,128)(2,1)} %all-to-all-done.w_ref.refs_2_, bf16[8,128,512]{2,1,0:T(8,128)(2,1)} %get-tuple-element.122.refs_3_.refs_2_), custom_call_target="tpu_custom_call" | custom-call | flops 60000002048 | bytes 216000000 | tf_op jit(solution)/shard_map/mixture/pallas_call | solution.py:591
  539.5 6.9 collective-permute-done.7.refs_1_.r_ref
  557.3 8.1 %adam.6 = (f32[16,512,128]{2,1,0:T(8,128)}, f32[16,512,128]{2,1,0:T(8,128)}, f32[16,512,128]{2,1,0:T(8,128)}, f32[8,128]{1,0:T(8,128)}) custom-call(s32[1]{0:T(128)} %bitcast.10.place_ref, bf16[8,128,512]{2,1,0:T(8,128)(2,1)} %copy-done.38, bf16[8,128,512]{2,1,0:T(8,128)(2,1)} %collective-permute-done.3.refs_1_.r_ref, f32[16,512,128]{2,1,0:T(8,128)} %w_ref.9, ...), custom_call_target="tpu_custom_call" | custom-call | flops 60000002048 | bytes 216000000 | tf_op jit(solution)/shard_map/adam/pallas_call | solution.py:722
  565.4 7.2 %adam.7 = (f32[16,2,128,512]{3,2,1,0:T(8,128)}, f32[16,2,128,512]{3,2,1,0:T(8,128)}, f32[16,2,128,512]{3,2,1,0:T(8,128)}, f32[8,128]{1,0:T(8,128)}) custom-call(s32[1]{0:T(128)} %bitcast.10.place_ref, bf16[8,128,512]{2,1,0:T(8,128)(2,1)} %copy-done.17, bf16[8,128,512]{2,1,0:T(8,128)(2,1)} %copy-done.6, f32[16,2,128,512]{3,2,1,0:T(8,128)} %w_ref.11, ...), custom_call_target="tpu_custom_call" | custom-call | flops 1000000000 | bytes 3600000 | tf_op jit(solution)/shard_map/adam/pallas_call | solution.py:722
  590.0 7.2 %adam.8 = (f32[16,2,128,512]{3,2,1,0:T(8,128)}, f32[16,2,128,512]{3,2,1,0:T(8,128)}, f32[16,2,128,512]{3,2,1,0:T(8,128)}, f32[8,128]{1,0:T(8,128)}) custom-call(s32[1]{0:T(128)} %bitcast.10.place_ref, bf16[8,128,512]{2,1,0:T(8,128)(2,1)} %copy-done.39, bf16[8,128,512]{2,1,0:T(8,128)(2,1)} %copy-done.18, ...), custom_call_target="tpu_custom_call", output_to_operand_aliasing={{0}: (6, {}), {1}: (7, {}), {2}: (8, {})} | custom-call | flops 60000002048 | bytes 216000000 | tf_op jit(solution)/shard_map/adam/pallas_call | solution.py:722
  597.3 7.1 %adam.9 = (f32[16,512,128]{2,1,0:T(8,128)}, f32[16,512,128]{2,1,0:T(8,128)}, f32[16,512,128]{2,1,0:T(8,128)}, f32[8,128]{1,0:T(8,128)}) custom-call(s32[1]{0:T(128)} %bitcast.10.place_ref, bf16[8,128,512]{2,1,0:T(8,128)(2,1)} %copy-done.19, bf16[8,128,512]{2,1,0:T(8,128)(2,1)} %copy-done.20, ...), custom_call_target="tpu_custom_call", output_to_operand_aliasing={{0}: (6, {}), {1}: (7, {}), {2}: (8, {})} | custom-call | flops 1000000000 | bytes 3600000 | tf_op jit(solution)/shard_map/adam/pallas_call | solution.py:722
  604.4 6.3 collective-permute-done.11.refs_1_.r_ref
  622.9 7.2 %adam.10 = (f32[16,2,128,512]{3,2,1,0:T(8,128)}, f32[16,2,128,512]{3,2,1,0:T(8,128)}, f32[16,2,128,512]{3,2,1,0:T(8,128)}, f32[8,128]{1,0:T(8,128)}) custom-call(s32[1]{0:T(128)} %bitcast.10.place_ref, bf16[8,128,512]{2,1,0:T(8,128)(2,1)} %copy-done.54, bf16[8,128,512]{2,1,0:T(8,128)(2,1)} %copy-done.40, ...), custom_call_target="tpu_custom_call", output_to_operand_aliasing={{0}: (6, {}), {1}: (7, {}), {2}: (8, {})} | custom-call | flops 60000002048 | bytes 216000000 | tf_op jit(solution)/shard_map/adam/pallas_call | solution.py:722
  630.1 13.2 %collective-permute-done.14.refs_2_.r_ref = bf16[8,128,512]{2,1,0:T(8,128)(2,1)S(1)} collective-permute-done((bf16[8,128,512]{2,1,0:T(8,128)(2,1)}, bf16[8,128,512]{2,1,0:T(8,128)(2,1)S(1)}, u32[]{:S(2)}, u32[]{:S(2)}) %collective-permute-start.14) | collective-permute-done | bytes 1048608 | tf_op jit(solution)/shard_map/ppermute | solution.py:885
  651.8 7.3 %adam.11 = (f32[16,2,128,512]{3,2,1,0:T(8,128)}, f32[16,2,128,512]{3,2,1,0:T(8,128)}, f32[16,2,128,512]{3,2,1,0:T(8,128)}, f32[8,128]{1,0:T(8,128)}) custom-call(s32[1]{0:T(128)} %bitcast.10.place_ref, bf16[8,128,512]{2,1,0:T(8,128)(2,1)} %copy-done.55, bf16[8,128,512]{2,1,0:T(8,128)(2,1)} %copy-done.42, ...), custom_call_target="tpu_custom_call", output_to_operand_aliasing={{0}: (6, {}), {1}: (7, {}), {2}: (8, {})} | custom-call | flops 60000002048 | bytes 216000000 | tf_op jit(solution)/shard_map/adam/pallas_call | solution.py:722
  659.2 12.4 %collective-permute-done.15.r_ref = bf16[8,128,512]{2,1,0:T(8,128)(2,1)S(1)} collective-permute-done((bf16[8,128,512]{2,1,0:T(8,128)(2,1)}, bf16[8,128,512]{2,1,0:T(8,128)(2,1)S(1)}, u32[]{:S(2)}, u32[]{:S(2)}) %collective-permute-start.15) | collective-permute-done | bytes 1048608 | tf_op jit(solution)/shard_map/ppermute | solution.py:885
  (234 shorter events, 144.2 us)
Async XLA Ops:
  7.2 54.2 %all-gather.5.cloned.1.call-start = ((), (), s32[]{:S(2)}) async-start(), calls=%async_computation.8 | async-start | bytes 7372800 | tf_op jit(solution)/shard_map/all_gather | solution.py:823
  13.4 172.1 %all-gather.9.cloned.1.call-start = ((), (), s32[]{:S(2)}) async-start(), calls=%async_computation.10 | async-start | bytes 10616832 | tf_op jit(solution)/shard_map/all_gather | solution.py:855
  16.2 202.1 %all-gather.7.cloned.1.call-start = ((), (), s32[]{:S(2)}) async-start(), calls=%async_computation.9 | async-start | bytes 4718592 | tf_op jit(solution)/shard_map/all_gather | solution.py:851
  16.4 46.2 %copy-start.15 = (f32[512,1]{1,0:T(8,128)}, f32[512,1]{1,0:T(8,128)S(1)}, u32[]{:S(2)}) copy-start(f32[512,1]{1,0:T(8,128)S(1)} %copy.112.alive_ref) | copy-start | bytes 6148
  27.8 54.0 %copy-start.13 = (f32[512,128]{1,0:T(8,128)}, f32[512,128]{1,0:T(8,128)S(1)}, u32[]{:S(2)}) copy-start(f32[512,128]{1,0:T(8,128)S(1)} %get-tuple-element.279.sin_ref) | copy-start | bytes 786436
  84.2 173.2 %all-gather.11.cloned.1.call-start = ((), (), s32[]{:S(2)}) async-start(), calls=%async_computation.11 | async-start | bytes 4718592 | tf_op jit(solution)/shard_map/all_gather | solution.py:851
  84.8 100.7 %all-to-all-start = ((bf16[8,2,3,128,512]{4,3,2,1,0:T(8,128)(2,1)}), bf16[8,2,3,128,512]{4,3,2,1,0:T(8,128)(2,1)}, u32[]{:S(2)}, u32[]{:S(2)}) async-start(bf16[8,2,3,128,512]{4,3,2,1,0:T(8,128)(2,1)} %split.1.wait_ref), calls=%async_computation | async-start | bytes 12582912 | tf_op jit(solution)/shard_map/all_to_all | solution.py:828
  90.0 324.3 %reduce-scatter.4.cloned.1.call-start = ((), (), s32[]{:S(2)}) async-start(), calls=%async_computation.12 | async-start | bytes 10616832 | tf_op jit(solution)/shard_map/reduce_scatter | solution.py:872
  302.8 22.9 %all-to-all-start.1 = ((bf16[8,1,128,512]{3,2,1,0:T(8,128)(2,1)}), bf16[8,1,128,512]{3,2,1,0:T(8,128)(2,1)S(1)}, u32[]{:S(2)}, u32[]{:S(2)}) async-start(bf16[8,1,128,512]{3,2,1,0:T(8,128)(2,1)} %grads.4.refs_8_), calls=%async_computation.1 | async-start | bytes 2097152 | tf_op jit(solution)/shard_map/all_to_all | solution.py:882
  328.8 39.7 %all-to-all-start.2 = ((bf16[8,2,128,512]{3,2,1,0:T(8,128)(2,1)}), bf16[8,2,128,512]{3,2,1,0:T(8,128)(2,1)S(1)}, u32[]{:S(2)}, u32[]{:S(2)}) async-start(bf16[8,2,128,512]{3,2,1,0:T(8,128)(2,1)} %after.3), calls=%async_computation.2 | async-start | bytes 4194304 | tf_op jit(solution)/shard_map/all_to_all | solution.py:882
  333.1 25.2 %collective-permute-start = (bf16[8,128,512]{2,1,0:T(8,128)(2,1)S(1)}, bf16[8,128,512]{2,1,0:T(8,128)(2,1)S(1)}, u32[]{:S(2)}, u32[]{:S(2)}) collective-permute-start(bf16[8,128,512]{2,1,0:T(8,128)(2,1)S(1)} %copy-done.8), channel_id=1, source_target_pairs={{0,8},{8,0},{16,24},{24,16},{1,9},{9,1},{17,25},{25,17},{2,10},{10... | collective-permute-start | bytes 3145736 | tf_op jit(solution)/shard_map/ppermute | solution.py:885
  373.8 29.0 %collective-permute-start.1 = (bf16[8,128,512]{2,1,0:T(8,128)(2,1)}, bf16[8,128,512]{2,1,0:T(8,128)(2,1)}, u32[]{:S(2)}, u32[]{:S(2)}) collective-permute-start(bf16[8,128,512]{2,1,0:T(8,128)(2,1)} %get-tuple-element.108), channel_id=1, source_target_pairs={{0,8},{8,0},{16,24},{24,16},{1,9},{9,1},{17,25},{25,17},{2,10},{10... | collective-permute-start | bytes 3145736 | tf_op jit(solution)/shard_map/ppermute | solution.py:885
  375.4 27.5 %collective-permute-start.2 = (bf16[8,128,512]{2,1,0:T(8,128)(2,1)S(1)}, bf16[8,128,512]{2,1,0:T(8,128)(2,1)}, u32[]{:S(2)}, u32[]{:S(2)}) collective-permute-start(bf16[8,128,512]{2,1,0:T(8,128)(2,1)S(1)} %get-tuple-element.107.wait_ref.refs_8_.refs_2_), channel_id=1, source_target_pairs={{8,16},{16,8},{9,17},{17,9},{10,18},{18,10},{11,19},{19,11},{12,20... | collective-permute-start | bytes 3145736 | tf_op jit(solution)/shard_map/ppermute | solution.py:888
  377.1 47.8 %all-to-all-start.3 = ((bf16[8,1,128,512]{3,2,1,0:T(8,128)(2,1)}), bf16[8,1,128,512]{3,2,1,0:T(8,128)(2,1)}, u32[]{:S(2)}, u32[]{:S(2)}) async-start(bf16[8,1,128,512]{3,2,1,0:T(8,128)(2,1)} %after.4), calls=%async_computation.3 | async-start | bytes 2097152 | tf_op jit(solution)/shard_map/all_to_all | solution.py:882
  382.7 189.9 %reduce-scatter.8.cloned.1.call-start = ((), (), s32[]{:S(2)}) async-start(), calls=%async_computation.14 | async-start | bytes 7372800 | tf_op jit(solution)/shard_map/reduce_scatter | solution.py:951
  409.4 27.0 %collective-permute-start.3 = (bf16[8,128,512]{2,1,0:T(8,128)(2,1)}, bf16[8,128,512]{2,1,0:T(8,128)(2,1)}, u32[]{:S(2)}, u32[]{:S(2)}) collective-permute-start(bf16[8,128,512]{2,1,0:T(8,128)(2,1)} %get-tuple-element.109), channel_id=1, source_target_pairs={{0,8},{8,0},{16,24},{24,16},{1,9},{9,1},{17,25},{25,17},{2,10},{10... | collective-permute-start | bytes 3145736 | tf_op jit(solution)/shard_map/ppermute | solution.py:885
  412.6 23.8 %collective-permute-start.4 = (bf16[8,128,512]{2,1,0:T(8,128)(2,1)}, bf16[8,128,512]{2,1,0:T(8,128)(2,1)}, u32[]{:S(2)}, u32[]{:S(2)}) collective-permute-start(bf16[8,128,512]{2,1,0:T(8,128)(2,1)} %get-tuple-element.110.wait_ref.refs_2_), channel_id=1, source_target_pairs={{8,16},{16,8},{9,17},{17,9},{10,18},{18,10},{11,19},{19,11},{12,20... | collective-permute-start | bytes 3145736 | tf_op jit(solution)/shard_map/ppermute | solution.py:888
  477.6 31.3 %all-to-all-start.4 = ((bf16[8,2,128,512]{3,2,1,0:T(8,128)(2,1)}), bf16[8,2,128,512]{3,2,1,0:T(8,128)(2,1)S(1)}, u32[]{:S(2)}, u32[]{:S(2)}) async-start(bf16[8,2,128,512]{3,2,1,0:T(8,128)(2,1)} %after.5), calls=%async_computation.5 | async-start | bytes 4194304 | tf_op jit(solution)/shard_map/all_to_all | solution.py:882
  481.9 201.3 %reduce-scatter.6.cloned.1.call-start = ((), (), s32[]{:S(2)}) async-start(), calls=%async_computation.13 | async-start | bytes 9437184 | tf_op jit(solution)/shard_map/reduce_scatter | solution.py:958
  481.9 27.3 %collective-permute-start.5 = (bf16[8,128,512]{2,1,0:T(8,128)(2,1)}, bf16[8,128,512]{2,1,0:T(8,128)(2,1)S(1)}, u32[]{:S(2)}, u32[]{:S(2)}) collective-permute-start(bf16[8,128,512]{2,1,0:T(8,128)(2,1)} %copy-done.41), channel_id=1, source_target_pairs={{0,8},{8,0},{16,24},{24,16},{1,9},{9,1},{17,25},{25,17},{2,10},{10... | collective-permute-start | bytes 3145736 | tf_op jit(solution)/shard_map/ppermute | solution.py:885
  485.5 23.7 %collective-permute-start.6 = (bf16[8,128,512]{2,1,0:T(8,128)(2,1)}, bf16[8,128,512]{2,1,0:T(8,128)(2,1)}, u32[]{:S(2)}, u32[]{:S(2)}) collective-permute-start(bf16[8,128,512]{2,1,0:T(8,128)(2,1)} %copy-done.21), channel_id=1, source_target_pairs={{8,16},{16,8},{9,17},{17,9},{10,18},{18,10},{11,19},{19,11},{12,20... | collective-permute-start | bytes 3145736 | tf_op jit(solution)/shard_map/ppermute | solution.py:888
  517.2 29.2 %collective-permute-start.7 = (bf16[8,128,512]{2,1,0:T(8,128)(2,1)}, bf16[8,128,512]{2,1,0:T(8,128)(2,1)S(1)}, u32[]{:S(2)}, u32[]{:S(2)}) collective-permute-start(bf16[8,128,512]{2,1,0:T(8,128)(2,1)} %get-tuple-element.124), channel_id=1, source_target_pairs={{0,8},{8,0},{16,24},{24,16},{1,9},{9,1},{17,25},{25,17},{2,10},{10... | collective-permute-start | bytes 3145736 | tf_op jit(solution)/shard_map/ppermute | solution.py:885
  522.8 23.6 %collective-permute-start.8 = (bf16[8,128,512]{2,1,0:T(8,128)(2,1)}, bf16[8,128,512]{2,1,0:T(8,128)(2,1)}, u32[]{:S(2)}, u32[]{:S(2)}) collective-permute-start(bf16[8,128,512]{2,1,0:T(8,128)(2,1)} %get-tuple-element.122.refs_3_.refs_2_), channel_id=1, source_target_pairs={{8,16},{16,8},{9,17},{17,9},{10,18},{18,10},{11,19},{19,11},{12,20... | collective-permute-start | bytes 3145736 | tf_op jit(solution)/shard_map/ppermute | solution.py:888
  551.7 27.6 %collective-permute-start.10 = (bf16[8,128,512]{2,1,0:T(8,128)(2,1)}, bf16[8,128,512]{2,1,0:T(8,128)(2,1)}, u32[]{:S(2)}, u32[]{:S(2)}) collective-permute-start(bf16[8,128,512]{2,1,0:T(8,128)(2,1)} %get-tuple-element.126.rest_0_.refs_2_), channel_id=1, source_target_pairs={{8,16},{16,8},{9,17},{17,9},{10,18},{18,10},{11,19},{19,11},{12,20... | collective-permute-start | bytes 3145736 | tf_op jit(solution)/shard_map/ppermute | solution.py:888
  553.4 26.7 %collective-permute-start.9 = (bf16[8,128,512]{2,1,0:T(8,128)(2,1)}, bf16[8,128,512]{2,1,0:T(8,128)(2,1)S(1)}, u32[]{:S(2)}, u32[]{:S(2)}) collective-permute-start(bf16[8,128,512]{2,1,0:T(8,128)(2,1)} %get-tuple-element.125), channel_id=1, source_target_pairs={{0,8},{8,0},{16,24},{24,16},{1,9},{9,1},{17,25},{25,17},{2,10},{10... | collective-permute-start | bytes 3145736 | tf_op jit(solution)/shard_map/ppermute | solution.py:885
  586.6 24.1 %collective-permute-start.11 = (bf16[8,128,512]{2,1,0:T(8,128)(2,1)}, bf16[8,128,512]{2,1,0:T(8,128)(2,1)S(1)}, u32[]{:S(2)}, u32[]{:S(2)}) collective-permute-start(bf16[8,128,512]{2,1,0:T(8,128)(2,1)} %get-tuple-element.131), channel_id=1, source_target_pairs={{0,8},{8,0},{16,24},{24,16},{1,9},{9,1},{17,25},{25,17},{2,10},{10... | collective-permute-start | bytes 3145736 | tf_op jit(solution)/shard_map/ppermute | solution.py:885
  588.4 22.3 %collective-permute-start.12 = (bf16[8,128,512]{2,1,0:T(8,128)(2,1)}, bf16[8,128,512]{2,1,0:T(8,128)(2,1)}, u32[]{:S(2)}, u32[]{:S(2)}) collective-permute-start(bf16[8,128,512]{2,1,0:T(8,128)(2,1)} %get-tuple-element.132.rest_3_.refs_2_), channel_id=1, source_target_pairs={{8,16},{16,8},{9,17},{17,9},{10,18},{18,10},{11,19},{19,11},{12,20... | collective-permute-start | bytes 3145736 | tf_op jit(solution)/shard_map/ppermute | solution.py:888
  616.2 13.9 %collective-permute-start.13 = (bf16[8,128,512]{2,1,0:T(8,128)(2,1)S(1)}, bf16[8,128,512]{2,1,0:T(8,128)(2,1)}, u32[]{:S(2)}, u32[]{:S(2)}) collective-permute-start(bf16[8,128,512]{2,1,0:T(8,128)(2,1)S(1)} %get-tuple-element.143.rest_3_.refs_0_), channel_id=1, source_target_pairs={{8,16},{16,8},{9,17},{17,9},{10,18},{18,10},{11,19},{19,11},{12,20... | collective-permute-start | bytes 3145736 | tf_op jit(solution)/shard_map/ppermute | solution.py:888
  617.8 25.6 %collective-permute-start.14 = (bf16[8,128,512]{2,1,0:T(8,128)(2,1)}, bf16[8,128,512]{2,1,0:T(8,128)(2,1)S(1)}, u32[]{:S(2)}, u32[]{:S(2)}) collective-permute-start(bf16[8,128,512]{2,1,0:T(8,128)(2,1)} %get-tuple-element.144), channel_id=1, source_target_pairs={{0,8},{8,0},{16,24},{24,16},{1,9},{9,1},{17,25},{25,17},{2,10},{10... | collective-permute-start | bytes 3145736 | tf_op jit(solution)/shard_map/ppermute | solution.py:885
  650.0 21.5 %collective-permute-start.15 = (bf16[8,128,512]{2,1,0:T(8,128)(2,1)}, bf16[8,128,512]{2,1,0:T(8,128)(2,1)S(1)}, u32[]{:S(2)}, u32[]{:S(2)}) collective-permute-start(bf16[8,128,512]{2,1,0:T(8,128)(2,1)} %get-tuple-element.151), channel_id=1, source_target_pairs={{0,8},{8,0},{16,24},{24,16},{1,9},{9,1},{17,25},{25,17},{2,10},{10... | collective-permute-start | bytes 3145736 | tf_op jit(solution)/shard_map/ppermute | solution.py:885
  651.8 19.8 %copy-start.28 = (bf16[8,128,512]{2,1,0:T(8,128)(2,1)S(1)}, bf16[8,128,512]{2,1,0:T(8,128)(2,1)}, u32[]{:S(2)}) copy-start(bf16[8,128,512]{2,1,0:T(8,128)(2,1)} %copy-done.27) | copy-start | bytes 3145732
  651.8 19.8 %copy-start.35 = (f32[2,128]{1,0:T(2,128)S(1)}, f32[2,128]{1,0:T(2,128)}, u32[]{:S(2)}) copy-start(f32[2,128]{1,0:T(2,128)} %refs_0_.1) | copy-start | bytes 3076
  (63 other events, 364.2 us)
Sparse Core Ops, SparseCore 0:
  13.5 47.8 all-gather.4
  63.8 115.2 all-gather.8
  181.6 36.6 all-gather.6
  220.6 36.7 all-gather.10
  290.8 108.8 reduce-scatter.3
  477.7 66.5 reduce-scatter.7
  548.2 71.2 reduce-scatter.5

commit v5 on v4

--- a/solution.py
+++ b/solution.py
@@ -164,29 +164,30 @@
     return jax.ShapeDtypeStruct(shape, dtype)
 
 
-def split_kernel(gateup_ref, down_ref, out_ref):
+def split_kernel(odd_ref, gateup_ref, down_ref, out_ref):
     for k in range(2):
-        out_ref[k, 0, 0] = gateup_ref[k, 0].astype(brain_floating)
-        out_ref[k, 0, 1] = gateup_ref[k, 1].astype(brain_floating)
-        out_ref[k, 0, 2] = down_ref[k].T.astype(brain_floating)
-
-
-def split_by_owner(gateup, down):
+        out_ref[k, 0] = gateup_ref[k, 0].astype(brain_floating)
+        out_ref[k, 1] = gateup_ref[k, 1].astype(brain_floating)
+        out_ref[k, 2] = down_ref[k].T.astype(brain_floating)
+
+
+def split_by_owner(odd, gateup, down):
     shard = gateup.shape[2]
     steps = GROUP // 2
     return pl.pallas_call(
         split_kernel,
-        grid=(EXPERTS // 2,),
-        in_specs=[
-            pl.BlockSpec((2, 2, shard, F), lambda e: (e, 0, 0, 0)),
-            pl.BlockSpec((2, F, shard), lambda e: (e, 0, 0)),
-        ],
-        out_specs=pl.BlockSpec(
-            (2, 1, 3, shard, F), lambda e: (lax.rem(e, steps), e // steps, 0, 0, 0)
+        grid_spec=pltpu.PrefetchScalarGridSpec(
+            num_scalar_prefetch=1,
+            grid=(steps,),
+            in_specs=[
+                pl.BlockSpec((2, 2, shard, F), lambda e, odd: (e + steps * odd[0], 0, 0, 0)),
+                pl.BlockSpec((2, F, shard), lambda e, odd: (e + steps * odd[0], 0, 0)),
+            ],
+            out_specs=pl.BlockSpec((2, 3, shard, F), lambda e, odd: (e, 0, 0, 0)),
         ),
-        out_shape=out((GROUP, LOCAL, 3, shard, F), brain_floating),
+        out_shape=out((GROUP, 3, shard, F), brain_floating),
         name="split",
-    )(gateup, down)
+    )(odd, gateup, down)
 
 
 def front_kernel(
@@ -422,7 +423,7 @@
     )(*held, pack, wait, also)
 
 
-def expert_kernel(me_ref, x_ref, b_ref, w_ref, router_ref, *refs):
+def expert_kernel(me_ref, x_ref, b_ref, w_one_ref, w_two_ref, router_ref, *refs):
     ga_ref, dgu_ref, dx_ref = refs[-3:]
     x = x_ref[...]
     branch = b_ref[:, 0, :, :MODEL_WIDTH].reshape(x.shape)
@@ -432,9 +433,10 @@
     d_gates = jnp.zeros_like(gates)
     dx = jnp.zeros((x.shape[0], MODEL_WIDTH), jnp.float32)
     for local in range(LOCAL):
-        expert = me_ref[0] + GROUP * local
+        expert = me_ref[0] + GROUP * lax.rem(me_ref[1] + local, LOCAL)
+        w_ref = (w_one_ref, w_two_ref)[local]
         gate_weight, up_weight, down_weight = (
-            w_ref[:, local, p].reshape(MODEL_WIDTH, F) for p in range(3)
+            w_ref[:, p].reshape(MODEL_WIDTH, F) for p in range(3)
         )
         gate = jnp.sum(jnp.where(lane == expert, gates, 0.0), axis=1, keepdims=True)
         gate_linear = product(x, gate_weight)
@@ -480,7 +482,8 @@
             in_specs=[
                 rowed(MODEL_WIDTH),
                 pl.BlockSpec((2, 1, part_rows, wide), lambda i, me_ref: (i, c, 0, 0)),
-                whole(weights.shape),
+                whole(weights[0].shape),
+                whole(weights[1].shape),
                 part((MODEL_WIDTH, EXTRA), (0, ROUTER_BLOCK)),
             ]
             + [ANYWHERE] * len(before),
@@ -495,20 +498,20 @@
             out((rows, 2 * LOCAL * F), brain_floating),
             out((rows // part_rows, CHUNKS, part_rows, wide), brain_floating),
         ],
-        input_output_aliases={5 + i: 2 for i in range(len(before))},
+        input_output_aliases={6 + i: 2 for i in range(len(before))},
         compiler_params=pltpu.CompilerParams(vmem_limit_bytes=56 * MIB),
         name="experts",
-    )(me, x, b, weights, pack, *before)
+    )(me, x, b, *weights, pack, *before)
 
 
 def chunked_specs(steps, shape, place):
     def index(c):
-        return lambda i, *_: place(jnp.clip(i - c * steps, 0, steps - 1), c)
+        return lambda i, *scalars: place(jnp.clip(i - c * steps, 0, steps - 1), c, *scalars)
 
     return [pl.BlockSpec(shape, index(c)) for c in range(CHUNKS)]
 
 
-def grads_kernel(steps, sides, *refs):
+def grads_kernel(steps, sides, me_ref, *refs):
     count = len(sides)
     ins, out_ref, sums = (refs[: CHUNKS * 2 * count], refs[-count - 1], refs[-count:])
     blocks, _, shard, _ = out_ref.shape
@@ -535,7 +538,7 @@
             out_ref[:, k] = total[...].astype(brain_floating).reshape(blocks, shard, F)
 
 
-def run_grads(local, sides, shard, xs, b, gas, dgus, wait, cost):
+def run_grads(me, local, sides, shard, xs, b, gas, dgus, wait, cost):
     blocks = MODEL_WIDTH // shard
     rows, part_rows = (xs[0].shape[0], b.shape[2])
     tile = 2 * part_rows
@@ -544,32 +547,39 @@
     for side in sides:
         if side == 2:
             left = chunked_specs(
-                steps, (2, 1, part_rows, MODEL_WIDTH), lambda i, c: (i, c, 0, 0)
+                steps, (2, 1, part_rows, MODEL_WIDTH), lambda i, c, me: (i, c, 0, 0)
             )
-            right = chunked_specs(steps, (tile, F), lambda i, c: (i, local))
+            right = chunked_specs(
+                steps, (tile, F), lambda i, c, me: (i, lax.rem(me[1] + local, LOCAL))
+            )
         else:
-            left = chunked_specs(steps, (tile, MODEL_WIDTH), lambda i, c: (i, 0))
+            left = chunked_specs(steps, (tile, MODEL_WIDTH), lambda i, c, me: (i, 0))
             right = chunked_specs(
-                steps, (tile, F), lambda i, c, side=side: (i, 2 * local + side)
+                steps,
+                (tile, F),
+                lambda i, c, me, side=side: (i, 2 * lax.rem(me[1] + local, LOCAL) + side),
             )
         for c in range(CHUNKS):
             specs += [left[c], right[c]]
             arrays += [b, gas[c]] if side == 2 else [xs[c], dgus[c]]
     return pl.pallas_call(
         functools.partial(grads_kernel, steps, sides),
-        grid=(CHUNKS * steps,),
-        in_specs=specs + [ANYWHERE],
-        out_specs=whole((blocks, len(sides), shard, F)),
+        grid_spec=pltpu.PrefetchScalarGridSpec(
+            num_scalar_prefetch=1,
+            grid=(CHUNKS * steps,),
+            in_specs=specs + [ANYWHERE],
+            out_specs=whole((blocks, len(sides), shard, F)),
+            scratch_shapes=[pltpu.VMEM((MODEL_WIDTH, F), jnp.float32)] * len(sides),
+        ),
         out_shape=out((blocks, len(sides), shard, F), brain_floating),
-        scratch_shapes=[pltpu.VMEM((MODEL_WIDTH, F), jnp.float32)] * len(sides),
         compiler_params=pltpu.CompilerParams(vmem_limit_bytes=52 * MIB),
         cost_estimate=takes(cost),
         name="grads",
-    )(*arrays, wait)
+    )(me, *arrays, wait)
 
 
 def mix_kernel(steps, *refs):
-    gas, w_ref, out_ref = (refs[:CHUNKS], refs[CHUNKS], refs[-1])
+    gas, w_refs, out_ref = (refs[:CHUNKS], refs[CHUNKS : CHUNKS + LOCAL], refs[-1])
     for c in range(CHUNKS):
 
         @pl.when(pl.program_id(0) // steps == c)
@@ -578,7 +588,7 @@
             for local in range(LOCAL):
                 total += times_transposed(
                     gas[c][:, local * F : (local + 1) * F],
-                    w_ref[:, local, 0].reshape(MODEL_WIDTH, F),
+                    w_refs[local][:, 0].reshape(MODEL_WIDTH, F),
                 )
             out_ref[...] = total.astype(brain_floating).reshape(out_ref.shape)
 
@@ -587,12 +597,13 @@
     rows = gas[0].shape[0]
     tile = 2 * part_rows
     steps = rows // tile
-    blocks, _, _, shard, _ = weights.shape
+    blocks, _, shard, _ = weights[0].shape
     return pl.pallas_call(
         functools.partial(mix_kernel, steps),
         grid=(CHUNKS * steps,),
         in_specs=chunked_specs(steps, (tile, LOCAL * F), lambda i, c: (i, 0))
-        + [part((blocks, LOCAL, 1, shard, F), (0, 0, 2, 0, 0)), ANYWHERE],
+        + [part((blocks, 1, shard, F), (0, 2, 0, 0))] * LOCAL
+        + [ANYWHERE],
         out_specs=pl.BlockSpec(
             (2, 1, part_rows, MODEL_WIDTH), lambda i: (lax.rem(i, steps), i // steps, 0, 0)
         ),
@@ -600,7 +611,7 @@
         compiler_params=pltpu.CompilerParams(vmem_limit_bytes=52 * MIB),
         cost_estimate=takes(cost),
         name="mixture",
-    )(*gas, weights, wait)
+    )(*gas, *weights, wait)
 
 
 def at_inner(place_ref):
@@ -805,8 +816,9 @@
     replicas, outer = sizes
     count_of_rows = tokens_in.shape[0]
     shard = query_weight.shape[0]
-    me = lax.axis_index("inner").astype(jnp.int32).reshape(1)
     place = lax.axis_index("replica").astype(jnp.int32).reshape(1)
+    odd = lax.rem(place, LOCAL)
+    me = jnp.concatenate([lax.axis_index("inner").astype(jnp.int32).reshape(1), odd])
 
     pack_own = jnp.concatenate(
         [
@@ -824,10 +836,13 @@
     at = PROJECTED + MODEL_WIDTH + EXPERTS
     gains_value = pack[:, at : at + 2].astype(jnp.float32).T
 
-    weights_own = split_by_owner(gateup_weight, down_weight)
-    weights = lax.all_to_all(weights_own, "inner", 0, 0)
+    weights_own = lax.all_to_all(split_by_owner(odd, gateup_weight, down_weight), "inner", 0, 0)
     if outer > 1:
-        weights = lax.all_gather(weights, "outer", axis=0, tiled=True)
+        weights_own = lax.all_gather(weights_own, "outer", axis=0, tiled=True)
+    weights = (
+        weights_own,
+        lax.ppermute(weights_own, "replica", [(0, 1), (1, 0), (2, 3), (3, 2)]),
+    )
 
     position, alive_mask, allowed = layout(document_lengths[0], count_of_rows)
     cosine, sine = rope_tables(position)
@@ -888,7 +903,7 @@
         return lax.ppermute(values, "replica", [(1, 2), (2, 1)])
 
     def grads_of(local, sides, wait, cost):
-        return run_grads(local, sides, shard, x_all, branch_all, ga_all, dgu_all, wait, cost)
+        return run_grads(me, local, sides, shard, x_all, branch_all, ga_all, dgu_all, wait, cost)
 
     chunks = [(local, side) for local in range(LOCAL) for side in (2, 0, 1)]
     last = len(chunks)
@@ -942,6 +957,7 @@
             d_middle, d_mixed, second_grads = run_middle(
                 dx_own, normed_two, middle, cotangent, mask, alive, gains_value, pack, mixed, token
             )
+            waits.append(got)
             done = d_mixed
         elif k == 3:
             rest_grads, input_gradient = run_back(

time: 704 us -> 676 us (0.960)
  waiting for transfers between devices: 261 us -> 233 us
    all_to_all x1, waiting for transfers between devices: 95.3 us -> 0.01 us  [body(): lax.all_to_all(split_by_owner(odd, gateup_weight, down_weight), 'inner',...]
    ppermute x0 -> x1, waiting for transfers between devices: none -> 68.5 us  [body(): lax.ppermute(weights_own, 'replica', [(0, 1), (1, 0), (2, 3), (3, 2)])]
    all_gather x2, waiting for transfers between devices: 38.6 us -> 11.3 us  [gathered(): lax.all_gather(values[c * part_rows:(c + 1) * part_rows], 'inner', axis=0...]
    all_gather x1, waiting for transfers between devices: 32.4 us -> 58.9 us  [body(): pack = lax.all_gather(pack_own, fsdp, axis=0, tiled=True)]
    all_to_all x4, waiting for transfers between devices: 30.7 us -> 13.8 us  [to_owner(): return lax.all_to_all(parts, 'inner', 0, 0)]
    ppermute x9, waiting for transfers between devices: 63.8 us -> 80.1 us  [swapped(): return lax.ppermute(values, 'replica', [(0, 1), (1, 0), (2, 3), (3, 2)])]
    unnamed x141 -> x147, local copies, waits for them, and re-layouts: 41.2 us -> 44.2 us
  transfers between devices with their start and end apart: 28 -> 29, of which waited for: 14 -> 13; matrix products, arithmetic and copies ran while one was open for 3% -> 3% of each run, Pallas kernels for 32% -> 33%
where the time goes in v5:
time: 676 us; the launch traced here: 666 us
  Pallas kernels  291 us (43%)
  waiting for transfers between devices  233 us (34%)
  starting transfers between devices  58.3 us (9%)
  local copies, waits for them, and re-layouts  55.7 us (8%)
  between operations  14.9 us (2%)
  other arithmetic  12.7 us (2%)
    ppermute x9, waiting for transfers between devices, swapped(): return lax.ppermute(values, 'replica', [(0, 1), (1, 0), (2, 3), (3, 2)])  80.1 us
    ppermute x1, waiting for transfers between devices, body(): lax.ppermute(weights_own, 'replica', [(0, 1), (1, 0), (2, 3), (3, 2)])  68.5 us
    pallas_call x2, Pallas kernels, run_experts(): pl.pallas_call(expert_kernel, grid_spec=pltpu.PrefetchScalarGridSpec(num_...  68.1 us
    pallas_call x4, Pallas kernels, run_grads(): pl.pallas_call(functools.partial(grads_kernel, steps, sides), grid_spec=p...  64 us
    all_gather x1, waiting for transfers between devices, body(): pack = lax.all_gather(pack_own, fsdp, axis=0, tiled=True)  58.9 us
    pallas_call x6, Pallas kernels, adam_part(): pl.pallas_call(functools.partial(adam_kernel, turned, rate, decay_rate),...  44.5 us
    unnamed x147, local copies, waits for them, and re-layouts  44.2 us
    pallas_call x1, Pallas kernels, run_back(): pl.pallas_call(back_kernel, grid=(1,), in_specs=[whole(v.shape) for v in...  33.5 us
  transfers between devices with their start and end apart: 29, of which 13 were waited for; matrix products, arithmetic and copies ran while one was open for 3% of the time, Pallas kernels for 33%

profile of v5, /device:TPU:2, one launch (start us, length us, event | category | flops | bytes accessed | tf_op | source)
XLA Modules:
  0.0 665.8 jit_solution(13795927698291796350)
XLA Ops:
  16.2 5.0 split.1
  28.5 58.9 %all-gather.5.cloned.1.call-done.pack_ref.router_ref.output_ref = bf16[1024,3200]{1,0:T(8,128)(2,1)} async-done(((bf16[128,3200]{1,0:T(8,128)(2,1)}), bf16[1024,3200]{1,0:T(8,128)(2,1)}) %all-gather.5.cloned.1.call-update) | async-done | bytes 6553616 | tf_op jit(solution)/shard_map/all_gather | solution.py:835
  88.7 19.1 %front.1 = (bf16[512,1024]{1,0:T(8,128)(2,1)}, bf16[512,2048]{1,0:T(8,128)(2,1)}, bf16[512,1024]{1,0:T(8,128)(2,1)}, f32[512,128]{1,0:T(8,128)S(1)}, f32[512,1024]{1,0:T(8,128)}, /*index=5*/bf16[512,1024]{1,0:T(8,128)(2,1)}) custom-call(bf16[512,1024]{1,0:T(8,128)(2,1)} %x_ref.3, ...), custom_call_target="tpu_custom_call" | custom-call | tf_op jit(solution)/shard_map/front/pallas_call | solution.py:249
  113.2 68.5 %collective-permute-done.w_two_ref.refs_3_ = bf16[8,3,128,512]{3,2,1,0:T(8,128)(2,1)} collective-permute-done((bf16[8,3,128,512]{3,2,1,0:T(8,128)(2,1)}, bf16[8,3,128,512]{3,2,1,0:T(8,128)(2,1)}, u32[]{:S(2)}, u32[]{:S(2)}) %collective-permute-start) | collective-permute-done | bytes 3145760 | tf_op jit(solution)/shard_map/ppermute | solution.py:844
  181.7 6.3 all-gather.7.cloned.1.call-done.x_ref.refs_0_.refs_4_
  188.0 34.1 %experts.2 = (bf16[2048,1024]{1,0:T(8,128)(2,1)}, bf16[2048,2048]{1,0:T(8,128)(2,1)}, bf16[8,2,256,1152]{3,2,1,0:T(8,128)(2,1)}) custom-call(s32[2]{0:T(128)} %pad_add_fusion.me_ref, bf16[2048,1024]{1,0:T(8,128)(2,1)} %all-gather.7.cloned.1.call-done.x_ref.refs_0_.refs_4_, bf16[8,2,256,1152]{3,2,1,0:T(8,128)(2,1)} %bitcast.22, ...), custom_call_target="tpu_custom_call" | custom-call | tf_op jit(solution)/shard_map/experts/pallas_call | solution.py:477
  222.1 5.0 all-gather.11.cloned.1.call-done.x_ref.refs_2_.refs_6_
  227.0 34.0 %experts.3 = (bf16[2048,1024]{1,0:T(8,128)(2,1)}, bf16[2048,2048]{1,0:T(8,128)(2,1)}, bf16[8,2,256,1152]{3,2,1,0:T(8,128)(2,1)}) custom-call(s32[2]{0:T(128)} %pad_add_fusion.me_ref, bf16[2048,1024]{1,0:T(8,128)(2,1)} %all-gather.11.cloned.1.call-done.x_ref.refs_2_.refs_6_, bf16[8,2,256,1152]{3,2,1,0:T(8,128)(2,1)} %bitcast.23, ...), custom_call_target="tpu_custom_call", output_to_operand_aliasing={{2}: (6, {})} | custom-call | tf_op jit(solution)/shard_map/experts/pallas_call | solution.py:477
  261.7 13.4 %grads.4.refs_8_ = bf16[8,1,128,512]{3,2,1,0:T(8,128)(2,1)} custom-call(s32[2]{0:T(128)S(1)} %copy-done.41, bf16[8,2,256,1152]{3,2,1,0:T(8,128)(2,1)} %bitcast.24, bf16[2048,1024]{1,0:T(8,128)(2,1)} %get-tuple-element.102.refs_1_.refs_0_, bf16[8,2,256,1152]{3,2,1,0:T(8,128)(2,1)} %bitcast.25, bf16[2048,1024]{1,0:T(8,128)(2,1)} %get-tuple-element.104.refs_3_.refs_1_, ...), custom_call_target="tpu_custom_call" | custom-call | flops 1000000000 | bytes 3600000 | tf_op jit(solution)/shard_map/grads/pallas_call | solution.py:565
  279.1 19.8 %grads.5.refs_1_.values_ref = bf16[8,2,128,512]{3,2,1,0:T(8,128)(2,1)} custom-call(s32[2]{0:T(128)S(1)} %copy-done.41, bf16[2048,1024]{1,0:T(8,128)(2,1)} %all-gather.7.cloned.1.call-done.x_ref.refs_0_.refs_4_, bf16[2048,2048]{1,0:T(8,128)(2,1)} %get-tuple-element.106.refs_1_.refs_5_, bf16[2048,1024]{1,0:T(8,128)(2,1)} %all-gather.11.cloned.1.call-done.x_ref.refs_2_.refs_6_, ...), custom_call_target="tpu_custom_call" | custom-call | flops 1000000000 | bytes 3600000 | tf_op jit(solution)/shard_map/grads/pallas_call | solution.py:565
  301.9 4.6 all-to-all-start.2
  308.2 11.0 %grads.6.refs_3_.values_ref = bf16[8,1,128,512]{3,2,1,0:T(8,128)(2,1)S(1)} custom-call(s32[2]{0:T(128)S(1)} %copy-done.41, bf16[8,2,256,1152]{3,2,1,0:T(8,128)(2,1)} %bitcast.26, bf16[2048,1024]{1,0:T(8,128)(2,1)} %get-tuple-element.102.refs_1_.refs_0_, bf16[8,2,256,1152]{3,2,1,0:T(8,128)(2,1)} %bitcast.27, ...), custom_call_target="tpu_custom_call" | custom-call | flops 3000000000 | bytes 10800000 | tf_op jit(solution)/shard_map/grads/pallas_call | solution.py:565
  320.2 11.5 %collective-permute-done.1.refs_1_ = bf16[8,128,512]{2,1,0:T(8,128)(2,1)S(1)} collective-permute-done((bf16[8,128,512]{2,1,0:T(8,128)(2,1)S(1)}, bf16[8,128,512]{2,1,0:T(8,128)(2,1)S(1)}, u32[]{:S(2)}, u32[]{:S(2)}) %collective-permute-start.1) | collective-permute-done | bytes 1048608 | tf_op jit(solution)/shard_map/ppermute | solution.py:900
  332.7 8.1 %all-to-all-done.2.refs_2_.refs_0_.refs_4_ = bf16[8,2,128,512]{3,2,1,0:T(8,128)(2,1)S(1)} async-done(((bf16[8,2,128,512]{3,2,1,0:T(8,128)(2,1)}), bf16[8,2,128,512]{3,2,1,0:T(8,128)(2,1)S(1)}, u32[]{:S(2)}, u32[]{:S(2)}) %all-to-all-start.2) | async-done | bytes 2097184 | tf_op jit(solution)/shard_map/all_to_all | solution.py:897
  349.8 5.7 all-to-all-start.3
  357.6 19.8 %grads.7.refs_5_.values_ref = bf16[8,2,128,512]{3,2,1,0:T(8,128)(2,1)} custom-call(s32[2]{0:T(128)S(1)} %copy-done.41, bf16[2048,1024]{1,0:T(8,128)(2,1)} %all-gather.7.cloned.1.call-done.x_ref.refs_0_.refs_4_, bf16[2048,2048]{1,0:T(8,128)(2,1)} %get-tuple-element.106.refs_1_.refs_5_, bf16[2048,1024]{1,0:T(8,128)(2,1)} %all-gather.11.cloned.1.call-done.x_ref.refs_2_.refs_6_, ...), custom_call_target="tpu_custom_call" | custom-call | flops 3000000000 | bytes 10800000 | tf_op jit(solution)/shard_map/grads/pallas_call | solution.py:565
  394.3 9.6 %middle_back.1 = (f32[512,1024]{1,0:T(8,128)}, bf16[512,1024]{1,0:T(8,128)(2,1)S(1)}, bf16[1024,1152]{1,0:T(8,128)(2,1)}) custom-call(bf16[512,1152]{1,0:T(8,128)(2,1)} %reduce-scatter.4.cloned.1.call-done.dx_ref, bf16[512,1024]{1,0:T(8,128)(2,1)} %get-tuple-element.101.normed_two_ref, f32[512,1024]{1,0:T(8,128)} %get-tuple-element.100.middle_ref, ...), custom_call_target="tpu_custom_call" | custom-call | flops 30000001024 | bytes 108000000 | tf_op jit(solution)/shard_map/middle_back/pallas_call | solution.py:296
  404.9 7.9 %collective-permute-done.4.refs_1_.r_ref = bf16[8,128,512]{2,1,0:T(8,128)(2,1)S(1)} collective-permute-done((bf16[8,128,512]{2,1,0:T(8,128)(2,1)}, bf16[8,128,512]{2,1,0:T(8,128)(2,1)S(1)}, u32[]{:S(2)}, u32[]{:S(2)}) %collective-permute-start.4) | collective-permute-done | bytes 1048608 | tf_op jit(solution)/shard_map/ppermute | solution.py:900
  412.8 5.8 all-to-all-done.4.refs_5_.refs_4_.refs_0_
  427.5 33.5 %attention_back.1 = (bf16[1024,3200]{1,0:T(8,128)(2,1)}, f32[512,1024]{1,0:T(8,128)}) custom-call(bf16[512,1024]{1,0:T(8,128)(2,1)S(1)} %copy-done.24, bf16[512,2048]{1,0:T(8,128)(2,1)} %get-tuple-element.116.qkv_ref, f32[512,128]{1,0:T(8,128)S(1)} %copy-done.55, f32[512,512]{1,0:T(8,128)} %fusion.1.bias_ref, f32[512,128]{1,0:T(8,128)S(1)} %get-tuple-element.278.cos_ref, ...), custom_call_target="tpu_custom_call" | custom-call | flops 30000001024 | bytes 108000000 | tf_op jit(solution)/shard_map/attention_back/pallas_call | solution.py:405
  463.1 23.4 %collective-permute-done.6.refs_1_.r_ref = bf16[8,128,512]{2,1,0:T(8,128)(2,1)S(1)} collective-permute-done((bf16[8,128,512]{2,1,0:T(8,128)(2,1)}, bf16[8,128,512]{2,1,0:T(8,128)(2,1)S(1)}, u32[]{:S(2)}, u32[]{:S(2)}) %collective-permute-start.6) | collective-permute-done | bytes 1048608 | tf_op jit(solution)/shard_map/ppermute | solution.py:900
  499.7 15.2 %mixture.1.refs_5_ = bf16[8,2,256,1024]{3,2,1,0:T(8,128)(2,1)} custom-call(bf16[2048,1024]{1,0:T(8,128)(2,1)} %get-tuple-element.102.refs_1_.refs_0_, bf16[2048,1024]{1,0:T(8,128)(2,1)} %get-tuple-element.104.refs_3_.refs_1_, bf16[8,3,128,512]{3,2,1,0:T(8,128)(2,1)} %all-to-all-done.wait_ref.w_one_ref.refs_2_, ...), custom_call_target="tpu_custom_call" | custom-call | flops 60000002048 | bytes 216000000 | tf_op jit(solution)/shard_map/mixture/pallas_call | solution.py:601
  514.9 5.8 collective-permute-done.8.refs_1_.r_ref
  531.1 7.6 %adam.6 = (f32[16,512,128]{2,1,0:T(8,128)}, f32[16,512,128]{2,1,0:T(8,128)}, f32[16,512,128]{2,1,0:T(8,128)}, f32[8,128]{1,0:T(8,128)}) custom-call(s32[1]{0:T(128)} %bitcast.8.place_ref, bf16[8,128,512]{2,1,0:T(8,128)(2,1)} %copy-done.45, bf16[8,128,512]{2,1,0:T(8,128)(2,1)} %copy-done.15, f32[16,512,128]{2,1,0:T(8,128)} %w_ref.9, f32[16,512,128]{2,1,0:T(8,128)} %m_ref.9, ...), custom_call_target="tpu_custom_call" | custom-call | flops 60000002048 | bytes 216000000 | tf_op jit(solution)/shard_map/adam/pallas_call | solution.py:733
  538.6 7.9 %adam.7 = (f32[16,2,128,512]{3,2,1,0:T(8,128)}, f32[16,2,128,512]{3,2,1,0:T(8,128)}, f32[16,2,128,512]{3,2,1,0:T(8,128)}, f32[8,128]{1,0:T(8,128)}) custom-call(s32[1]{0:T(128)} %bitcast.8.place_ref, bf16[8,128,512]{2,1,0:T(8,128)(2,1)} %copy-done.16, bf16[8,128,512]{2,1,0:T(8,128)(2,1)} %copy-done.8, f32[16,2,128,512]{3,2,1,0:T(8,128)} %w_ref.11, ...), custom_call_target="tpu_custom_call" | custom-call | flops 1000000000 | bytes 3600000 | tf_op jit(solution)/shard_map/adam/pallas_call | solution.py:733
  563.1 7.4 %adam.8 = (f32[16,2,128,512]{3,2,1,0:T(8,128)}, f32[16,2,128,512]{3,2,1,0:T(8,128)}, f32[16,2,128,512]{3,2,1,0:T(8,128)}, f32[8,128]{1,0:T(8,128)}) custom-call(s32[1]{0:T(128)} %bitcast.8.place_ref, bf16[8,128,512]{2,1,0:T(8,128)(2,1)} %copy-done.46, bf16[8,128,512]{2,1,0:T(8,128)(2,1)} %copy-done.17, ...), custom_call_target="tpu_custom_call", output_to_operand_aliasing={{0}: (6, {}), {1}: (7, {}), {2}: (8, {})} | custom-call | flops 60000002048 | bytes 216000000 | tf_op jit(solution)/shard_map/adam/pallas_call | solution.py:733
  570.6 7.1 %adam.9 = (f32[16,512,128]{2,1,0:T(8,128)}, f32[16,512,128]{2,1,0:T(8,128)}, f32[16,512,128]{2,1,0:T(8,128)}, f32[8,128]{1,0:T(8,128)}) custom-call(s32[1]{0:T(128)} %bitcast.8.place_ref, bf16[8,128,512]{2,1,0:T(8,128)(2,1)} %copy-done.18, bf16[8,128,512]{2,1,0:T(8,128)(2,1)} %copy-done.19, ...), custom_call_target="tpu_custom_call", output_to_operand_aliasing={{0}: (6, {}), {1}: (7, {}), {2}: (8, {})} | custom-call | flops 1000000000 | bytes 3600000 | tf_op jit(solution)/shard_map/adam/pallas_call | solution.py:733
  577.6 5.9 collective-permute-done.12.refs_1_.r_ref
  595.1 7.3 %adam.10 = (f32[16,2,128,512]{3,2,1,0:T(8,128)}, f32[16,2,128,512]{3,2,1,0:T(8,128)}, f32[16,2,128,512]{3,2,1,0:T(8,128)}, f32[8,128]{1,0:T(8,128)}) custom-call(s32[1]{0:T(128)} %bitcast.8.place_ref, bf16[8,128,512]{2,1,0:T(8,128)(2,1)} %copy-done.58, bf16[8,128,512]{2,1,0:T(8,128)(2,1)} %copy-done.47, ...), custom_call_target="tpu_custom_call", output_to_operand_aliasing={{0}: (6, {}), {1}: (7, {}), {2}: (8, {})} | custom-call | flops 60000002048 | bytes 216000000 | tf_op jit(solution)/shard_map/adam/pallas_call | solution.py:733
  602.4 13.2 %collective-permute-done.15.refs_2_.r_ref = bf16[8,128,512]{2,1,0:T(8,128)(2,1)S(1)} collective-permute-done((bf16[8,128,512]{2,1,0:T(8,128)(2,1)}, bf16[8,128,512]{2,1,0:T(8,128)(2,1)S(1)}, u32[]{:S(2)}, u32[]{:S(2)}) %collective-permute-start.15) | collective-permute-done | bytes 1048608 | tf_op jit(solution)/shard_map/ppermute | solution.py:900
  624.1 7.3 %adam.11 = (f32[16,2,128,512]{3,2,1,0:T(8,128)}, f32[16,2,128,512]{3,2,1,0:T(8,128)}, f32[16,2,128,512]{3,2,1,0:T(8,128)}, f32[8,128]{1,0:T(8,128)}) custom-call(s32[1]{0:T(128)} %bitcast.8.place_ref, bf16[8,128,512]{2,1,0:T(8,128)(2,1)} %copy-done.59, bf16[8,128,512]{2,1,0:T(8,128)(2,1)} %copy-done.49, ...), custom_call_target="tpu_custom_call", output_to_operand_aliasing={{0}: (6, {}), {1}: (7, {}), {2}: (8, {})} | custom-call | flops 60000002048 | bytes 216000000 | tf_op jit(solution)/shard_map/adam/pallas_call | solution.py:733
  631.5 12.5 %collective-permute-done.16.r_ref = bf16[8,128,512]{2,1,0:T(8,128)(2,1)S(1)} collective-permute-done((bf16[8,128,512]{2,1,0:T(8,128)(2,1)}, bf16[8,128,512]{2,1,0:T(8,128)(2,1)S(1)}, u32[]{:S(2)}, u32[]{:S(2)}) %collective-permute-start.16) | collective-permute-done | bytes 1048608 | tf_op jit(solution)/shard_map/ppermute | solution.py:900
  (243 shorter events, 148.9 us)
Async XLA Ops:
  7.2 80.2 %all-gather.5.cloned.1.call-start = ((), (), s32[]{:S(2)}) async-start(), calls=%async_computation.8 | async-start | bytes 7372800 | tf_op jit(solution)/shard_map/all_gather | solution.py:835
  13.4 168.3 %all-gather.9.cloned.1.call-start = ((), (), s32[]{:S(2)}) async-start(), calls=%async_computation.10 | async-start | bytes 10616832 | tf_op jit(solution)/shard_map/all_gather | solution.py:870
  21.2 67.5 %all-to-all-start = ((bf16[8,3,128,512]{3,2,1,0:T(8,128)(2,1)}), bf16[8,3,128,512]{3,2,1,0:T(8,128)(2,1)}, u32[]{:S(2)}, u32[]{:S(2)}) async-start(bf16[8,3,128,512]{3,2,1,0:T(8,128)(2,1)} %split.1), calls=%async_computation | async-start | bytes 6291456 | tf_op jit(solution)/shard_map/all_to_all | solution.py:839
  25.6 162.3 %all-gather.7.cloned.1.call-start = ((), (), s32[]{:S(2)}) async-start(), calls=%async_computation.9 | async-start | bytes 4718592 | tf_op jit(solution)/shard_map/all_gather | solution.py:866
  25.8 82.0 %copy-start.27 = (f32[512,1]{1,0:T(8,128)}, f32[512,1]{1,0:T(8,128)S(1)}, u32[]{:S(2)}) copy-start(f32[512,1]{1,0:T(8,128)S(1)} %copy.112.alive_ref) | copy-start | bytes 6148
  27.4 80.5 %copy-start.25 = (f32[512,128]{1,0:T(8,128)}, f32[512,128]{1,0:T(8,128)S(1)}, u32[]{:S(2)}) copy-start(f32[512,128]{1,0:T(8,128)S(1)} %get-tuple-element.279.sin_ref) | copy-start | bytes 786436
  107.9 114.2 %copy-start.54 = (f32[512,128]{1,0:T(8,128)}, f32[512,128]{1,0:T(8,128)S(1)}, u32[]{:S(2)}) copy-start(f32[512,128]{1,0:T(8,128)S(1)} %get-tuple-element.117.totals_ref) | copy-start | bytes 786436
  110.2 116.8 %all-gather.11.cloned.1.call-start = ((), (), s32[]{:S(2)}) async-start(), calls=%async_computation.11 | async-start | bytes 4718592 | tf_op jit(solution)/shard_map/all_gather | solution.py:866
  110.8 282.6 %reduce-scatter.4.cloned.1.call-start = ((), (), s32[]{:S(2)}) async-start(), calls=%async_computation.12 | async-start | bytes 10616832 | tf_op jit(solution)/shard_map/reduce_scatter | solution.py:887
  111.0 70.6 %collective-permute-start = (bf16[8,3,128,512]{3,2,1,0:T(8,128)(2,1)}, bf16[8,3,128,512]{3,2,1,0:T(8,128)(2,1)}, u32[]{:S(2)}, u32[]{:S(2)}) collective-permute-start(bf16[8,3,128,512]{3,2,1,0:T(8,128)(2,1)} %all-to-all-done.wait_ref.w_one_ref.refs_2_), channel_id=1, source_target_pairs={{0,8},{8,0},{16,24},{24,16},{1,9},{9,1},{17,25},{25,17},{2,10},{10... | collective-permute-start | bytes 9437192 | tf_op jit(solution)/shard_map/ppermute | solution.py:844
  275.1 23.9 %all-to-all-start.1 = ((bf16[8,1,128,512]{3,2,1,0:T(8,128)(2,1)}), bf16[8,1,128,512]{3,2,1,0:T(8,128)(2,1)S(1)}, u32[]{:S(2)}, u32[]{:S(2)}) async-start(bf16[8,1,128,512]{3,2,1,0:T(8,128)(2,1)} %grads.4.refs_8_), calls=%async_computation.1 | async-start | bytes 2097152 | tf_op jit(solution)/shard_map/all_to_all | solution.py:897
  301.9 38.9 %all-to-all-start.2 = ((bf16[8,2,128,512]{3,2,1,0:T(8,128)(2,1)}), bf16[8,2,128,512]{3,2,1,0:T(8,128)(2,1)S(1)}, u32[]{:S(2)}, u32[]{:S(2)}) async-start(bf16[8,2,128,512]{3,2,1,0:T(8,128)(2,1)} %after.3), calls=%async_computation.2 | async-start | bytes 4194304 | tf_op jit(solution)/shard_map/all_to_all | solution.py:897
  306.6 25.2 %collective-permute-start.1 = (bf16[8,128,512]{2,1,0:T(8,128)(2,1)S(1)}, bf16[8,128,512]{2,1,0:T(8,128)(2,1)S(1)}, u32[]{:S(2)}, u32[]{:S(2)}) collective-permute-start(bf16[8,128,512]{2,1,0:T(8,128)(2,1)S(1)} %copy-done.10), channel_id=1, source_target_pairs={{0,8},{8,0},{16,24},{24,16},{1,9},{9,1},{17,25},{25,17},{2,10},{10... | collective-permute-start | bytes 3145736 | tf_op jit(solution)/shard_map/ppermute | solution.py:900
  346.6 30.8 %collective-permute-start.2 = (bf16[8,128,512]{2,1,0:T(8,128)(2,1)}, bf16[8,128,512]{2,1,0:T(8,128)(2,1)}, u32[]{:S(2)}, u32[]{:S(2)}) collective-permute-start(bf16[8,128,512]{2,1,0:T(8,128)(2,1)} %get-tuple-element.108), channel_id=1, source_target_pairs={{0,8},{8,0},{16,24},{24,16},{1,9},{9,1},{17,25},{25,17},{2,10},{10... | collective-permute-start | bytes 3145736 | tf_op jit(solution)/shard_map/ppermute | solution.py:900
  348.1 29.3 %collective-permute-start.3 = (bf16[8,128,512]{2,1,0:T(8,128)(2,1)S(1)}, bf16[8,128,512]{2,1,0:T(8,128)(2,1)}, u32[]{:S(2)}, u32[]{:S(2)}) collective-permute-start(bf16[8,128,512]{2,1,0:T(8,128)(2,1)S(1)} %get-tuple-element.107.wait_ref.refs_8_.refs_2_), channel_id=1, source_target_pairs={{8,16},{16,8},{9,17},{17,9},{10,18},{18,10},{11,19},{19,11},{12,20... | collective-permute-start | bytes 3145736 | tf_op jit(solution)/shard_map/ppermute | solution.py:903
  349.8 39.4 %all-to-all-start.3 = ((bf16[8,1,128,512]{3,2,1,0:T(8,128)(2,1)}), bf16[8,1,128,512]{3,2,1,0:T(8,128)(2,1)}, u32[]{:S(2)}, u32[]{:S(2)}) async-start(bf16[8,1,128,512]{3,2,1,0:T(8,128)(2,1)} %after.4), calls=%async_computation.3 | async-start | bytes 2097152 | tf_op jit(solution)/shard_map/all_to_all | solution.py:897
  383.9 28.9 %collective-permute-start.5 = (bf16[8,128,512]{2,1,0:T(8,128)(2,1)}, bf16[8,128,512]{2,1,0:T(8,128)(2,1)}, u32[]{:S(2)}, u32[]{:S(2)}) collective-permute-start(bf16[8,128,512]{2,1,0:T(8,128)(2,1)} %get-tuple-element.110.wait_ref.refs_2_), channel_id=1, source_target_pairs={{8,16},{16,8},{9,17},{17,9},{10,18},{18,10},{11,19},{19,11},{12,20... | collective-permute-start | bytes 3145736 | tf_op jit(solution)/shard_map/ppermute | solution.py:903
  385.5 27.2 %collective-permute-start.4 = (bf16[8,128,512]{2,1,0:T(8,128)(2,1)}, bf16[8,128,512]{2,1,0:T(8,128)(2,1)S(1)}, u32[]{:S(2)}, u32[]{:S(2)}) collective-permute-start(bf16[8,128,512]{2,1,0:T(8,128)(2,1)} %get-tuple-element.109), channel_id=1, source_target_pairs={{0,8},{8,0},{16,24},{24,16},{1,9},{9,1},{17,25},{25,17},{2,10},{10... | collective-permute-start | bytes 3145736 | tf_op jit(solution)/shard_map/ppermute | solution.py:900
  389.1 29.4 %all-to-all-start.4 = ((bf16[8,2,128,512]{3,2,1,0:T(8,128)(2,1)}), bf16[8,2,128,512]{3,2,1,0:T(8,128)(2,1)S(1)}, u32[]{:S(2)}, u32[]{:S(2)}) async-start(bf16[8,2,128,512]{3,2,1,0:T(8,128)(2,1)} %after.5), calls=%async_computation.4 | async-start | bytes 4194304 | tf_op jit(solution)/shard_map/all_to_all | solution.py:897
  393.4 153.1 %reduce-scatter.8.cloned.1.call-start = ((), (), s32[]{:S(2)}) async-start(), calls=%async_computation.14 | async-start | bytes 7372800 | tf_op jit(solution)/shard_map/reduce_scatter | solution.py:967
  461.0 194.6 %reduce-scatter.6.cloned.1.call-start = ((), (), s32[]{:S(2)}) async-start(), calls=%async_computation.13 | async-start | bytes 9437184 | tf_op jit(solution)/shard_map/reduce_scatter | solution.py:974
  461.1 25.4 %collective-permute-start.6 = (bf16[8,128,512]{2,1,0:T(8,128)(2,1)}, bf16[8,128,512]{2,1,0:T(8,128)(2,1)S(1)}, u32[]{:S(2)}, u32[]{:S(2)}) collective-permute-start(bf16[8,128,512]{2,1,0:T(8,128)(2,1)} %copy-done.48), channel_id=1, source_target_pairs={{0,8},{8,0},{16,24},{24,16},{1,9},{9,1},{17,25},{25,17},{2,10},{10... | collective-permute-start | bytes 3145736 | tf_op jit(solution)/shard_map/ppermute | solution.py:900
  461.2 25.3 %collective-permute-start.7 = (bf16[8,128,512]{2,1,0:T(8,128)(2,1)}, bf16[8,128,512]{2,1,0:T(8,128)(2,1)}, u32[]{:S(2)}, u32[]{:S(2)}) collective-permute-start(bf16[8,128,512]{2,1,0:T(8,128)(2,1)} %copy-done.20), channel_id=1, source_target_pairs={{8,16},{16,8},{9,17},{17,9},{10,18},{18,10},{11,19},{19,11},{12,20... | collective-permute-start | bytes 3145736 | tf_op jit(solution)/shard_map/ppermute | solution.py:903
  494.5 26.2 %collective-permute-start.8 = (bf16[8,128,512]{2,1,0:T(8,128)(2,1)}, bf16[8,128,512]{2,1,0:T(8,128)(2,1)S(1)}, u32[]{:S(2)}, u32[]{:S(2)}) collective-permute-start(bf16[8,128,512]{2,1,0:T(8,128)(2,1)} %get-tuple-element.124), channel_id=1, source_target_pairs={{0,8},{8,0},{16,24},{24,16},{1,9},{9,1},{17,25},{25,17},{2,10},{10... | collective-permute-start | bytes 3145736 | tf_op jit(solution)/shard_map/ppermute | solution.py:900
  498.1 22.7 %collective-permute-start.9 = (bf16[8,128,512]{2,1,0:T(8,128)(2,1)}, bf16[8,128,512]{2,1,0:T(8,128)(2,1)}, u32[]{:S(2)}, u32[]{:S(2)}) collective-permute-start(bf16[8,128,512]{2,1,0:T(8,128)(2,1)} %get-tuple-element.122.refs_4_.refs_2_), channel_id=1, source_target_pairs={{8,16},{16,8},{9,17},{17,9},{10,18},{18,10},{11,19},{19,11},{12,20... | collective-permute-start | bytes 3145736 | tf_op jit(solution)/shard_map/ppermute | solution.py:903
  526.0 27.2 %collective-permute-start.10 = (bf16[8,128,512]{2,1,0:T(8,128)(2,1)}, bf16[8,128,512]{2,1,0:T(8,128)(2,1)S(1)}, u32[]{:S(2)}, u32[]{:S(2)}) collective-permute-start(bf16[8,128,512]{2,1,0:T(8,128)(2,1)} %get-tuple-element.125), channel_id=1, source_target_pairs={{0,8},{8,0},{16,24},{24,16},{1,9},{9,1},{17,25},{25,17},{2,10},{10... | collective-permute-start | bytes 3145736 | tf_op jit(solution)/shard_map/ppermute | solution.py:900
  529.4 23.8 %collective-permute-start.11 = (bf16[8,128,512]{2,1,0:T(8,128)(2,1)}, bf16[8,128,512]{2,1,0:T(8,128)(2,1)}, u32[]{:S(2)}, u32[]{:S(2)}) collective-permute-start(bf16[8,128,512]{2,1,0:T(8,128)(2,1)} %get-tuple-element.126.rest_0_.refs_2_), channel_id=1, source_target_pairs={{8,16},{16,8},{9,17},{17,9},{10,18},{18,10},{11,19},{19,11},{12,20... | collective-permute-start | bytes 3145736 | tf_op jit(solution)/shard_map/ppermute | solution.py:903
  559.7 23.8 %collective-permute-start.12 = (bf16[8,128,512]{2,1,0:T(8,128)(2,1)}, bf16[8,128,512]{2,1,0:T(8,128)(2,1)S(1)}, u32[]{:S(2)}, u32[]{:S(2)}) collective-permute-start(bf16[8,128,512]{2,1,0:T(8,128)(2,1)} %get-tuple-element.131), channel_id=1, source_target_pairs={{0,8},{8,0},{16,24},{24,16},{1,9},{9,1},{17,25},{25,17},{2,10},{10... | collective-permute-start | bytes 3145736 | tf_op jit(solution)/shard_map/ppermute | solution.py:900
  561.5 22.0 %collective-permute-start.13 = (bf16[8,128,512]{2,1,0:T(8,128)(2,1)}, bf16[8,128,512]{2,1,0:T(8,128)(2,1)}, u32[]{:S(2)}, u32[]{:S(2)}) collective-permute-start(bf16[8,128,512]{2,1,0:T(8,128)(2,1)} %get-tuple-element.132.rest_3_.refs_2_), channel_id=1, source_target_pairs={{8,16},{16,8},{9,17},{17,9},{10,18},{18,10},{11,19},{19,11},{12,20... | collective-permute-start | bytes 3145736 | tf_op jit(solution)/shard_map/ppermute | solution.py:903
  589.0 13.3 %collective-permute-start.14 = (bf16[8,128,512]{2,1,0:T(8,128)(2,1)S(1)}, bf16[8,128,512]{2,1,0:T(8,128)(2,1)}, u32[]{:S(2)}, u32[]{:S(2)}) collective-permute-start(bf16[8,128,512]{2,1,0:T(8,128)(2,1)S(1)} %get-tuple-element.143.rest_3_.refs_0_), channel_id=1, source_target_pairs={{8,16},{16,8},{9,17},{17,9},{10,18},{18,10},{11,19},{19,11},{12,20... | collective-permute-start | bytes 3145736 | tf_op jit(solution)/shard_map/ppermute | solution.py:903
  590.7 24.9 %collective-permute-start.15 = (bf16[8,128,512]{2,1,0:T(8,128)(2,1)}, bf16[8,128,512]{2,1,0:T(8,128)(2,1)S(1)}, u32[]{:S(2)}, u32[]{:S(2)}) collective-permute-start(bf16[8,128,512]{2,1,0:T(8,128)(2,1)} %get-tuple-element.144), channel_id=1, source_target_pairs={{0,8},{8,0},{16,24},{24,16},{1,9},{9,1},{17,25},{25,17},{2,10},{10... | collective-permute-start | bytes 3145736 | tf_op jit(solution)/shard_map/ppermute | solution.py:900
  622.3 21.6 %collective-permute-start.16 = (bf16[8,128,512]{2,1,0:T(8,128)(2,1)}, bf16[8,128,512]{2,1,0:T(8,128)(2,1)S(1)}, u32[]{:S(2)}, u32[]{:S(2)}) collective-permute-start(bf16[8,128,512]{2,1,0:T(8,128)(2,1)} %get-tuple-element.151), channel_id=1, source_target_pairs={{0,8},{8,0},{16,24},{24,16},{1,9},{9,1},{17,25},{25,17},{2,10},{10... | collective-permute-start | bytes 3145736 | tf_op jit(solution)/shard_map/ppermute | solution.py:900
  (67 other events, 375.5 us)
Sparse Core Ops, SparseCore 0:
  13.5 73.9 all-gather.4
  89.9 58.8 all-gather.8
  151.2 36.7 all-gather.6
  190.3 36.7 all-gather.10
  261.2 105.1 reduce-scatter.3
  461.2 62.5 reduce-scatter.7
  527.6 71.2 reduce-scatter.5

commit v6 on v5

--- a/solution.py
+++ b/solution.py
@@ -513,8 +513,7 @@
 
 def grads_kernel(steps, sides, me_ref, *refs):
     count = len(sides)
-    ins, out_ref, sums = (refs[: CHUNKS * 2 * count], refs[-count - 1], refs[-count:])
-    blocks, _, shard, _ = out_ref.shape
+    ins, outs, sums = (refs[: CHUNKS * 2 * count], refs[-2 * count : -count], refs[-count:])
     i = pl.program_id(0)
 
     @pl.when(i == 0)
@@ -534,8 +533,8 @@
 
     @pl.when(i == CHUNKS * steps - 1)
     def _():
-        for k, total in enumerate(sums):
-            out_ref[:, k] = total[...].astype(brain_floating).reshape(blocks, shard, F)
+        for result, total in zip(outs, sums):
+            result[...] = total[...].astype(brain_floating).reshape(result.shape)
 
 
 def run_grads(me, local, sides, shard, xs, b, gas, dgus, wait, cost):
@@ -568,10 +567,10 @@
             num_scalar_prefetch=1,
             grid=(CHUNKS * steps,),
             in_specs=specs + [ANYWHERE],
-            out_specs=whole((blocks, len(sides), shard, F)),
+            out_specs=[whole((blocks, shard, F))] * len(sides),
             scratch_shapes=[pltpu.VMEM((MODEL_WIDTH, F), jnp.float32)] * len(sides),
         ),
-        out_shape=out((blocks, len(sides), shard, F), brain_floating),
+        out_shape=[out((blocks, shard, F), brain_floating)] * len(sides),
         compiler_params=pltpu.CompilerParams(vmem_limit_bytes=52 * MIB),
         cost_estimate=takes(cost),
         name="grads",
@@ -618,23 +617,26 @@
     return (place_ref[0] == 1) | (place_ref[0] == 2)
 
 
+def as_chunk(values):
+    if values.ndim == 2:
+        return jnp.stack([values[:, :F], values[:, F:]])
+    return values
+
+
 def round_kernel(kinds, waits, place_ref, *refs):
     has_own, has_pair, has_next = kinds
     refs = list(refs)
 
     def take(count):
         taken, refs[:count] = (refs[:count], [])
-        return [ref[...].astype(jnp.float32) for ref in taken]
+        return [as_chunk(ref[...].astype(jnp.float32)) for ref in taken]
 
     own = take(2) if has_own else None
     pair = take(2) if has_pair else None
-    following = take(1) if has_next else None
+    edge = take(1)[0] if has_next else None
     outs = refs[waits:]
-    edge = None
-    if has_next:
-        edge = following[0].reshape(outs[-1].shape)
     if has_own:
-        outs.pop(0)[...] = (own[0].reshape(own[1].shape) + own[1]).astype(brain_floating)
+        outs.pop(0)[...] = (own[0] + own[1]).astype(brain_floating)
     if has_pair:
         total = pair[0] + pair[1]
         outs.pop(0)[...] = total.astype(brain_floating)
@@ -646,32 +648,29 @@
     steps = GROUP // 2
     arrays, specs, count = ([], [], 0)
 
-    def chunk_spec(source):
-        values, at = source
-        _, _, shard, width = values.shape
-        return pl.BlockSpec((2, 1, shard, width), lambda i, _: (i, at, 0, 0))
-
-    flat = None
-    for source in (own[:1] if own else ()) + ((following,) if following else ()):
-        flat = (GROUP,) + source[0].shape[2:]
-    if pair:
-        flat = pair[0].shape
+    flat = pair[0].shape if pair else following.shape
     piece = pl.BlockSpec((2,) + flat[1:], lambda i, _: (i, 0, 0))
+
+    def chunk_spec(values):
+        if values.ndim == 2:
+            return pl.BlockSpec((values.shape[0], 2 * F), lambda i, _: (0, i))
+        return piece
+
     if own:
-        arrays += [own[0][0], own[1]]
+        arrays += list(own)
         specs += [chunk_spec(own[0]), piece]
         count += 1
     if pair:
         arrays += list(pair)
         specs += [piece] * 2
         count += 1
-    if following:
-        arrays.append(following[0])
+    if following is not None:
+        arrays.append(following)
         specs.append(chunk_spec(following))
     count += 1
     return pl.pallas_call(
         functools.partial(
-            round_kernel, (bool(own), bool(pair), bool(following)), len(waits)
+            round_kernel, (bool(own), bool(pair), following is not None), len(waits)
         ),
         grid_spec=pltpu.PrefetchScalarGridSpec(
             num_scalar_prefetch=1,
@@ -924,9 +923,9 @@
         )
         return done
 
-    first = grads_of(0, (2,), dgu_all[-1], 1)
-    token = first
-    mine = {0: (to_owner(first), 0)}
+    ready = grads_of(0, (2,), dgu_all[-1], 1)
+    token = ready[0]
+    mine = {0: to_owner(token)}
     for k in range(-1, last + 3):
         own, pair, following, waits = (None, None, None, [])
         if k in edges:
@@ -939,38 +938,31 @@
         if k - 1 in by_pairs:
             pair = (by_pairs[k - 1], across(by_pairs[k - 1]))
 
+        if 0 <= k < len(chunks) - 1:
+            mine[k + 1] = to_owner(after(ready[k + 1], token))
         if k == -1:
-            second = grads_of(0, (0, 1), token, 1)
-            done = second
+            ready += grads_of(0, (0, 1), token, 1)
+            done = ready[1]
         elif k == 0:
-            got = to_owner(after(second, token))
-            mine[1], mine[2] = ((got, 0), (got, 1))
-            third = grads_of(1, (2,), token, 3)
-            done = third
+            ready += grads_of(1, (2,), token, 3)
+            done = ready[3]
         elif k == 1:
-            mine[3] = (to_owner(after(third, token)), 0)
-            fourth = grads_of(1, (0, 1), token, 3)
-            done = fourth
+            ready += grads_of(1, (0, 1), token, 3)
+            done = ready[4]
         elif k == 2:
-            got = to_owner(after(fourth, token))
-            mine[4], mine[5] = ((got, 0), (got, 1))
             d_middle, d_mixed, second_grads = run_middle(
                 dx_own, normed_two, middle, cotangent, mask, alive, gains_value, pack, mixed, token
             )
-            waits.append(got)
             done = d_mixed
         elif k == 3:
             rest_grads, input_gradient = run_back(
                 d_mixed, qkv, totals, bias, cosine, sine, normed, tokens_in, d_middle, gains_value,
                 second_grads, pack, token, token,
             )
-            rest_own = lax.psum_scatter(rest_grads, fsdp, scatter_dimension=0, tiled=True)
-            rest_own = jnp.pad(rest_own, ((0, 0), (0, GROUP * F - rest_own.shape[1])))
-            rest_own = rest_own.reshape(shard, GROUP, F).swapaxes(0, 1)
-            mine[last] = (rest_own.reshape(GROUP, 1, shard, F), 0)
+            mine[last] = lax.psum_scatter(rest_grads, fsdp, scatter_dimension=0, tiled=True)
             done = input_gradient
         elif k == 4:
-            mixture = run_mix(ga_all, weights, part_rows, token, 60)
+            mixture = run_mix(ga_all, weights, part_rows, token, 300)
             mixture_own = lax.psum_scatter(
                 mixture.reshape(GROUP * count_of_rows, MODEL_WIDTH),
                 "inner",
@@ -979,11 +971,11 @@
             )
             done = mixture
         elif k == 5:
-            done = adam_of(1, adam_of(0, token, 60), 1)
+            done = adam_of(1, adam_of(0, token, 300), 1)
         elif k == 6:
-            done = adam_of(3, adam_of(2, token, 60), 1)
+            done = adam_of(3, adam_of(2, token, 300), 1)
         elif k - 3 < len(chunks):
-            done = adam_of(k - 3, token, 60)
+            done = adam_of(k - 3, token, 300)
         waits.append(done)
 
         if k + 1 <= last:

time: 676 us -> 662 us (0.979)
  waiting for transfers between devices: 233 us -> 211 us
  local copies, waits for them, and re-layouts: 55.7 us -> 41.8 us
  Pallas kernels: 291 us -> 302 us
  starting transfers between devices: 58.3 us -> 68 us
    ppermute x9, waiting for transfers between devices: 80.1 us -> 60.7 us  [swapped(): return lax.ppermute(values, 'replica', [(0, 1), (1, 0), (2, 3), (3, 2)])]
    pallas_call x4, Pallas kernels: 64 us -> 73.3 us  [run_grads(): pl.pallas_call(functools.partial(grads_kernel, steps, sides), grid_spec=p...]
    unnamed x147 -> x138, local copies, waits for them, and re-layouts: 44.2 us -> 35 us
    all_to_all x4 -> x6, starting transfers between devices: 18.6 us -> 27.2 us  [to_owner(): return lax.all_to_all(parts, 'inner', 0, 0)]
    all_to_all x4 -> x6, waiting for transfers between devices: 13.8 us -> 11.8 us  [to_owner(): return lax.all_to_all(parts, 'inner', 0, 0)]
  transfers between devices with their start and end apart: 29 -> 31, of which waited for: 13 -> 14; matrix products, arithmetic and copies ran while one was open for 3% -> 2% of each run, Pallas kernels for 33% -> 41%
where the time goes in v6:
time: 662 us; the launch traced here: 650 us
  Pallas kernels  302 us (46%)
  waiting for transfers between devices  211 us (32%)
  starting transfers between devices  68 us (10%)
  local copies, waits for them, and re-layouts  41.8 us (6%)
  between operations  15.2 us (2%)
  other arithmetic  12.7 us (2%)
    pallas_call x4, Pallas kernels, run_grads(): pl.pallas_call(functools.partial(grads_kernel, steps, sides), grid_spec=p...  73.3 us
    ppermute x1, waiting for transfers between devices, body(): lax.ppermute(weights_own, 'replica', [(0, 1), (1, 0), (2, 3), (3, 2)])  68.4 us
    pallas_call x2, Pallas kernels, run_experts(): pl.pallas_call(expert_kernel, grid_spec=pltpu.PrefetchScalarGridSpec(num_...  68.2 us
    ppermute x9, waiting for transfers between devices, swapped(): return lax.ppermute(values, 'replica', [(0, 1), (1, 0), (2, 3), (3, 2)])  60.7 us
    all_gather x1, waiting for transfers between devices, body(): pack = lax.all_gather(pack_own, fsdp, axis=0, tiled=True)  58.9 us
    pallas_call x6, Pallas kernels, adam_part(): pl.pallas_call(functools.partial(adam_kernel, turned, rate, decay_rate),...  44 us
    unnamed x138, local copies, waits for them, and re-layouts  35 us
    pallas_call x1, Pallas kernels, run_back(): pl.pallas_call(back_kernel, grid=(1,), in_specs=[whole(v.shape) for v in...  33.7 us
  transfers between devices with their start and end apart: 31, of which 14 were waited for; matrix products, arithmetic and copies ran while one was open for 2% of the time, Pallas kernels for 41%

profile of v6, /device:TPU:2, one launch (start us, length us, event | category | flops | bytes accessed | tf_op | source)
XLA Modules:
  0.0 650.4 jit_solution(54495362319658150)
XLA Ops:
  16.2 5.0 split.1
  28.6 58.9 %all-gather.5.cloned.1.call-done.pack_ref.router_ref.output_ref = bf16[1024,3200]{1,0:T(8,128)(2,1)} async-done(((bf16[128,3200]{1,0:T(8,128)(2,1)}), bf16[1024,3200]{1,0:T(8,128)(2,1)}) %all-gather.5.cloned.1.call-update) | async-done | bytes 6553616 | tf_op jit(solution)/shard_map/all_gather | solution.py:834
  88.7 19.1 %front.1 = (bf16[512,1024]{1,0:T(8,128)(2,1)}, bf16[512,2048]{1,0:T(8,128)(2,1)}, bf16[512,1024]{1,0:T(8,128)(2,1)}, f32[512,128]{1,0:T(8,128)S(1)}, f32[512,1024]{1,0:T(8,128)}, /*index=5*/bf16[512,1024]{1,0:T(8,128)(2,1)}) custom-call(bf16[512,1024]{1,0:T(8,128)(2,1)} %x_ref.3, ...), custom_call_target="tpu_custom_call" | custom-call | tf_op jit(solution)/shard_map/front/pallas_call | solution.py:249
  113.8 68.4 %collective-permute-done.w_two_ref.refs_3_ = bf16[8,3,128,512]{3,2,1,0:T(8,128)(2,1)S(1)} collective-permute-done((bf16[8,3,128,512]{3,2,1,0:T(8,128)(2,1)}, bf16[8,3,128,512]{3,2,1,0:T(8,128)(2,1)S(1)}, u32[]{:S(2)}, u32[]{:S(2)}) %collective-permute-start) | collective-permute-done | bytes 3145760 | tf_op jit(solution)/shard_map/ppermute | solution.py:843
  182.2 5.7 all-gather.7.cloned.1.call-done.x_ref.refs_0_.refs_4_
  188.0 34.1 %experts.2 = (bf16[2048,1024]{1,0:T(8,128)(2,1)}, bf16[2048,2048]{1,0:T(8,128)(2,1)}, bf16[8,2,256,1152]{3,2,1,0:T(8,128)(2,1)}) custom-call(s32[2]{0:T(128)} %pad_add_fusion.me_ref, bf16[2048,1024]{1,0:T(8,128)(2,1)} %all-gather.7.cloned.1.call-done.x_ref.refs_0_.refs_4_, bf16[8,2,256,1152]{3,2,1,0:T(8,128)(2,1)} %bitcast.16, ...), custom_call_target="tpu_custom_call" | custom-call | tf_op jit(solution)/shard_map/experts/pallas_call | solution.py:477
  222.1 5.0 all-gather.11.cloned.1.call-done.x_ref.refs_2_.refs_6_
  227.0 34.1 %experts.3 = (bf16[2048,1024]{1,0:T(8,128)(2,1)}, bf16[2048,2048]{1,0:T(8,128)(2,1)}, bf16[8,2,256,1152]{3,2,1,0:T(8,128)(2,1)}) custom-call(s32[2]{0:T(128)} %pad_add_fusion.me_ref, bf16[2048,1024]{1,0:T(8,128)(2,1)} %all-gather.11.cloned.1.call-done.x_ref.refs_2_.refs_6_, bf16[8,2,256,1152]{3,2,1,0:T(8,128)(2,1)} %bitcast.17, ...), custom_call_target="tpu_custom_call", output_to_operand_aliasing={{2}: (6, {})} | custom-call | tf_op jit(solution)/shard_map/experts/pallas_call | solution.py:477
  261.8 23.5 %grads.4.refs_8_ = bf16[8,128,512]{2,1,0:T(8,128)(2,1)} custom-call(s32[2]{0:T(128)S(1)} %copy-done.34, bf16[8,2,256,1152]{3,2,1,0:T(8,128)(2,1)} %bitcast.18, bf16[2048,1024]{1,0:T(8,128)(2,1)} %get-tuple-element.106.refs_1_.refs_0_, bf16[8,2,256,1152]{3,2,1,0:T(8,128)(2,1)} %bitcast.19, bf16[2048,1024]{1,0:T(8,128)(2,1)} %get-tuple-element.108.refs_3_.refs_1_, ...), custom_call_target="tpu_custom_call" | custom-call | flops 1000000000 | bytes 3600000 | tf_op jit(solution)/shard_map/grads/pallas_call | solution.py:564
  289.3 19.5 %grads.5 = (bf16[8,128,512]{2,1,0:T(8,128)(2,1)S(1)}, bf16[8,128,512]{2,1,0:T(8,128)(2,1)}) custom-call(s32[2]{0:T(128)S(1)} %copy-done.34, bf16[2048,1024]{1,0:T(8,128)(2,1)} %all-gather.7.cloned.1.call-done.x_ref.refs_0_.refs_4_, bf16[2048,2048]{1,0:T(8,128)(2,1)} %get-tuple-element.110.refs_1_.refs_5_, ...), custom_call_target="tpu_custom_call" | custom-call | flops 1000000000 | bytes 3600000 | tf_op jit(solution)/shard_map/grads/pallas_call | solution.py:564
  308.8 4.7 all-to-all-done.1.refs_0_
  315.2 6.3 all-to-all-start.2
  321.5 10.9 %grads.6.refs_3_.values_ref = bf16[8,128,512]{2,1,0:T(8,128)(2,1)S(1)} custom-call(s32[2]{0:T(128)S(1)} %copy-done.34, bf16[8,2,256,1152]{3,2,1,0:T(8,128)(2,1)} %bitcast.20, bf16[2048,1024]{1,0:T(8,128)(2,1)} %get-tuple-element.106.refs_1_.refs_0_, bf16[8,2,256,1152]{3,2,1,0:T(8,128)(2,1)} %bitcast.21, ...), custom_call_target="tpu_custom_call" | custom-call | flops 3000000000 | bytes 10800000 | tf_op jit(solution)/shard_map/grads/pallas_call | solution.py:564
  332.4 4.6 all-to-all-done.2.refs_2_.refs_0_
  352.0 19.4 %grads.7 = (bf16[8,128,512]{2,1,0:T(8,128)(2,1)S(1)}, bf16[8,128,512]{2,1,0:T(8,128)(2,1)}) custom-call(s32[2]{0:T(128)S(1)} %copy-done.34, bf16[2048,1024]{1,0:T(8,128)(2,1)} %all-gather.7.cloned.1.call-done.x_ref.refs_0_.refs_4_, bf16[2048,2048]{1,0:T(8,128)(2,1)} %get-tuple-element.110.refs_1_.refs_5_, ...), custom_call_target="tpu_custom_call" | custom-call | flops 3000000000 | bytes 10800000 | tf_op jit(solution)/shard_map/grads/pallas_call | solution.py:564
  388.3 9.7 %middle_back.1 = (f32[512,1024]{1,0:T(8,128)}, bf16[512,1024]{1,0:T(8,128)(2,1)S(1)}, bf16[1024,1152]{1,0:T(8,128)(2,1)}) custom-call(bf16[512,1152]{1,0:T(8,128)(2,1)} %reduce-scatter.4.cloned.1.call-done.dx_ref, bf16[512,1024]{1,0:T(8,128)(2,1)} %get-tuple-element.105.normed_two_ref, f32[512,1024]{1,0:T(8,128)} %get-tuple-element.104.middle_ref, ...), custom_call_target="tpu_custom_call" | custom-call | flops 30000001024 | bytes 108000000 | tf_op jit(solution)/shard_map/middle_back/pallas_call | solution.py:296
  398.9 13.1 %collective-permute-done.4.refs_1_.r_ref = bf16[8,128,512]{2,1,0:T(8,128)(2,1)} collective-permute-done((bf16[8,128,512]{2,1,0:T(8,128)(2,1)}, bf16[8,128,512]{2,1,0:T(8,128)(2,1)}, u32[]{:S(2)}, u32[]{:S(2)}) %collective-permute-start.4) | collective-permute-done | bytes 1048608 | tf_op jit(solution)/shard_map/ppermute | solution.py:899
  432.4 33.7 %attention_back.1 = (bf16[1024,3200]{1,0:T(8,128)(2,1)}, f32[512,1024]{1,0:T(8,128)}) custom-call(bf16[512,1024]{1,0:T(8,128)(2,1)S(1)} %copy-done.51, bf16[512,2048]{1,0:T(8,128)(2,1)} %get-tuple-element.123.qkv_ref, f32[512,128]{1,0:T(8,128)S(1)} %copy-done.43, f32[512,512]{1,0:T(8,128)} %fusion.1.bias_ref, f32[512,128]{1,0:T(8,128)S(1)} %get-tuple-element.286.cos_ref, ...), custom_call_target="tpu_custom_call" | custom-call | flops 30000001024 | bytes 108000000 | tf_op jit(solution)/shard_map/attention_back/pallas_call | solution.py:405
  481.5 14.7 %mixture.1.refs_5_ = bf16[8,2,256,1024]{3,2,1,0:T(8,128)(2,1)} custom-call(bf16[2048,1024]{1,0:T(8,128)(2,1)} %get-tuple-element.106.refs_1_.refs_0_, bf16[2048,1024]{1,0:T(8,128)(2,1)} %get-tuple-element.108.refs_3_.refs_1_, bf16[8,3,128,512]{3,2,1,0:T(8,128)(2,1)} %all-to-all-done.wait_ref.w_one_ref.refs_2_, bf16[8,3,128,512]{3,2,1,0:T(8,128)(2,1)} %copy-done.55, ...), custom_call_target="tpu_custom_call" | custom-call | flops 299999985664 | bytes 1080000000 | tf_op jit(solution)/shard_map/mixture/pallas_call | solution.py:600
  498.7 8.0 %collective-permute-done.8.refs_1_.r_ref = bf16[8,128,512]{2,1,0:T(8,128)(2,1)} collective-permute-done((bf16[8,128,512]{2,1,0:T(8,128)(2,1)}, bf16[8,128,512]{2,1,0:T(8,128)(2,1)}, u32[]{:S(2)}, u32[]{:S(2)}) %collective-permute-start.8) | collective-permute-done | bytes 1048608 | tf_op jit(solution)/shard_map/ppermute | solution.py:899
  514.0 7.7 %adam.6 = (f32[16,512,128]{2,1,0:T(8,128)}, f32[16,512,128]{2,1,0:T(8,128)}, f32[16,512,128]{2,1,0:T(8,128)}, f32[8,128]{1,0:T(8,128)}) custom-call(s32[1]{0:T(128)} %bitcast.8.place_ref, bf16[8,128,512]{2,1,0:T(8,128)(2,1)} %copy-done.48, bf16[8,128,512]{2,1,0:T(8,128)(2,1)} %collective-permute-done.4.refs_1_.r_ref, f32[16,512,128]{2,1,0:T(8,128)} %w_ref.9, ...), custom_call_target="tpu_custom_call" | custom-call | flops 299999985664 | bytes 1080000000 | tf_op jit(solution)/shard_map/adam/pallas_call | solution.py:732
  521.7 7.2 %adam.7 = (f32[16,2,128,512]{3,2,1,0:T(8,128)}, f32[16,2,128,512]{3,2,1,0:T(8,128)}, f32[16,2,128,512]{3,2,1,0:T(8,128)}, f32[8,128]{1,0:T(8,128)}) custom-call(s32[1]{0:T(128)} %bitcast.8.place_ref, bf16[8,128,512]{2,1,0:T(8,128)(2,1)} %copy-done.7, bf16[8,128,512]{2,1,0:T(8,128)(2,1)} %copy-done.8, f32[16,2,128,512]{3,2,1,0:T(8,128)} %w_ref.11, ...), custom_call_target="tpu_custom_call" | custom-call | flops 1000000000 | bytes 3600000 | tf_op jit(solution)/shard_map/adam/pallas_call | solution.py:732
  528.9 7.7 %collective-permute-done.10.refs_1_.r_ref = bf16[8,128,512]{2,1,0:T(8,128)(2,1)} collective-permute-done((bf16[8,128,512]{2,1,0:T(8,128)(2,1)}, bf16[8,128,512]{2,1,0:T(8,128)(2,1)}, u32[]{:S(2)}, u32[]{:S(2)}) %collective-permute-start.10) | collective-permute-done | bytes 1048608 | tf_op jit(solution)/shard_map/ppermute | solution.py:899
  549.2 7.3 %adam.8 = (f32[16,2,128,512]{3,2,1,0:T(8,128)}, f32[16,2,128,512]{3,2,1,0:T(8,128)}, f32[16,2,128,512]{3,2,1,0:T(8,128)}, f32[8,128]{1,0:T(8,128)}) custom-call(s32[1]{0:T(128)} %bitcast.8.place_ref, bf16[8,128,512]{2,1,0:T(8,128)(2,1)} %copy-done.47, ...), custom_call_target="tpu_custom_call", output_to_operand_aliasing={{0}: (6, {}), {1}: (7, {}), {2}: (8, {})} | custom-call | flops 299999985664 | bytes 1080000000 | tf_op jit(solution)/shard_map/adam/pallas_call | solution.py:732
  556.6 7.1 %adam.9 = (f32[16,512,128]{2,1,0:T(8,128)}, f32[16,512,128]{2,1,0:T(8,128)}, f32[16,512,128]{2,1,0:T(8,128)}, f32[8,128]{1,0:T(8,128)}) custom-call(s32[1]{0:T(128)} %bitcast.8.place_ref, bf16[8,128,512]{2,1,0:T(8,128)(2,1)} %copy-done.9, ...), custom_call_target="tpu_custom_call", output_to_operand_aliasing={{0}: (6, {}), {1}: (7, {}), {2}: (8, {})} | custom-call | flops 1000000000 | bytes 3600000 | tf_op jit(solution)/shard_map/adam/pallas_call | solution.py:732
  563.7 5.2 collective-permute-done.12.refs_1_.r_ref
  576.3 5.4 collective-permute-start.15
  581.7 7.2 %adam.10 = (f32[16,2,128,512]{3,2,1,0:T(8,128)}, f32[16,2,128,512]{3,2,1,0:T(8,128)}, f32[16,2,128,512]{3,2,1,0:T(8,128)}, f32[8,128]{1,0:T(8,128)}) custom-call(s32[1]{0:T(128)} %bitcast.8.place_ref, bf16[8,128,512]{2,1,0:T(8,128)(2,1)} %copy-done.52, ...), custom_call_target="tpu_custom_call", output_to_operand_aliasing={{0}: (6, {}), {1}: (7, {}), {2}: (8, {})} | custom-call | flops 299999985664 | bytes 1080000000 | tf_op jit(solution)/shard_map/adam/pallas_call | solution.py:732
  588.9 13.3 %collective-permute-done.15.refs_2_.r_ref = bf16[8,128,512]{2,1,0:T(8,128)(2,1)} collective-permute-done((bf16[8,128,512]{2,1,0:T(8,128)(2,1)}, bf16[8,128,512]{2,1,0:T(8,128)(2,1)}, u32[]{:S(2)}, u32[]{:S(2)}) %collective-permute-start.15) | collective-permute-done | bytes 1048608 | tf_op jit(solution)/shard_map/ppermute | solution.py:899
  609.4 7.3 %adam.11 = (f32[16,2,128,512]{3,2,1,0:T(8,128)}, f32[16,2,128,512]{3,2,1,0:T(8,128)}, f32[16,2,128,512]{3,2,1,0:T(8,128)}, f32[8,128]{1,0:T(8,128)}) custom-call(s32[1]{0:T(128)} %bitcast.8.place_ref, bf16[8,128,512]{2,1,0:T(8,128)(2,1)} %copy-done.53, ...), custom_call_target="tpu_custom_call", output_to_operand_aliasing={{0}: (6, {}), {1}: (7, {}), {2}: (8, {})} | custom-call | flops 299999985664 | bytes 1080000000 | tf_op jit(solution)/shard_map/adam/pallas_call | solution.py:732
  616.7 12.4 %collective-permute-done.16.r_ref = bf16[8,128,512]{2,1,0:T(8,128)(2,1)} collective-permute-done((bf16[8,128,512]{2,1,0:T(8,128)(2,1)}, bf16[8,128,512]{2,1,0:T(8,128)(2,1)}, u32[]{:S(2)}, u32[]{:S(2)}) %collective-permute-start.16) | collective-permute-done | bytes 1048608 | tf_op jit(solution)/shard_map/ppermute | solution.py:899
  633.4 4.5 adam_rest.1
  (238 shorter events, 144.4 us)
Async XLA Ops:
  7.2 80.2 %all-gather.5.cloned.1.call-start = ((), (), s32[]{:S(2)}) async-start(), calls=%async_computation.10 | async-start | bytes 7372800 | tf_op jit(solution)/shard_map/all_gather | solution.py:834
  13.4 168.9 %all-gather.9.cloned.1.call-start = ((), (), s32[]{:S(2)}) async-start(), calls=%async_computation.12 | async-start | bytes 10616832 | tf_op jit(solution)/shard_map/all_gather | solution.py:869
  21.2 67.5 %all-to-all-start = ((bf16[8,3,128,512]{3,2,1,0:T(8,128)(2,1)}), bf16[8,3,128,512]{3,2,1,0:T(8,128)(2,1)}, u32[]{:S(2)}, u32[]{:S(2)}) async-start(bf16[8,3,128,512]{3,2,1,0:T(8,128)(2,1)} %split.1), calls=%async_computation | async-start | bytes 6291456 | tf_op jit(solution)/shard_map/all_to_all | solution.py:838
  25.6 162.3 %all-gather.7.cloned.1.call-start = ((), (), s32[]{:S(2)}) async-start(), calls=%async_computation.11 | async-start | bytes 4718592 | tf_op jit(solution)/shard_map/all_gather | solution.py:865
  25.9 82.0 %copy-start.16 = (f32[512,1]{1,0:T(8,128)}, f32[512,1]{1,0:T(8,128)S(1)}, u32[]{:S(2)}) copy-start(f32[512,1]{1,0:T(8,128)S(1)} %copy.110.alive_ref) | copy-start | bytes 6148
  110.8 116.2 %all-gather.11.cloned.1.call-start = ((), (), s32[]{:S(2)}) async-start(), calls=%async_computation.13 | async-start | bytes 4718592 | tf_op jit(solution)/shard_map/all_gather | solution.py:865
  111.4 276.9 %reduce-scatter.4.cloned.1.call-start = ((), (), s32[]{:S(2)}) async-start(), calls=%async_computation.14 | async-start | bytes 10616832 | tf_op jit(solution)/shard_map/reduce_scatter | solution.py:886
  111.7 70.5 %collective-permute-start = (bf16[8,3,128,512]{3,2,1,0:T(8,128)(2,1)}, bf16[8,3,128,512]{3,2,1,0:T(8,128)(2,1)S(1)}, u32[]{:S(2)}, u32[]{:S(2)}) collective-permute-start(bf16[8,3,128,512]{3,2,1,0:T(8,128)(2,1)} %all-to-all-done.wait_ref.w_one_ref.refs_2_), channel_id=1, source_target_pairs={{0,8},{8,0},{16,24},{24,16},{1,9},{9,1},{17,25},{25,17},{2,10},{10... | collective-permute-start | bytes 9437192 | tf_op jit(solution)/shard_map/ppermute | solution.py:843
  285.3 28.2 %all-to-all-start.1 = ((bf16[8,128,512]{2,1,0:T(8,128)(2,1)}), bf16[8,128,512]{2,1,0:T(8,128)(2,1)S(1)}, u32[]{:S(2)}, u32[]{:S(2)}) async-start(bf16[8,128,512]{2,1,0:T(8,128)(2,1)} %grads.4.refs_8_), calls=%async_computation.1 | async-start | bytes 2097152 | tf_op jit(solution)/shard_map/all_to_all | solution.py:896
  313.6 24.3 %collective-permute-start.1 = (bf16[8,128,512]{2,1,0:T(8,128)(2,1)S(1)}, bf16[8,128,512]{2,1,0:T(8,128)(2,1)}, u32[]{:S(2)}, u32[]{:S(2)}) collective-permute-start(bf16[8,128,512]{2,1,0:T(8,128)(2,1)S(1)} %round.9.refs_4_.wait_ref), channel_id=1, source_target_pairs={{0,8},{8,0},{16,24},{24,16},{1,9},{9,1},{17,25},{25,17},{2,10},{10... | collective-permute-start | bytes 3145736 | tf_op jit(solution)/shard_map/ppermute | solution.py:899
  315.2 21.8 %all-to-all-start.2 = ((bf16[8,128,512]{2,1,0:T(8,128)(2,1)}), bf16[8,128,512]{2,1,0:T(8,128)(2,1)S(1)}, u32[]{:S(2)}, u32[]{:S(2)}) async-start(bf16[8,128,512]{2,1,0:T(8,128)(2,1)} %after.5), calls=%async_computation.2 | async-start | bytes 2097152 | tf_op jit(solution)/shard_map/all_to_all | solution.py:896
  342.9 28.6 %collective-permute-start.2 = (bf16[8,128,512]{2,1,0:T(8,128)(2,1)}, bf16[8,128,512]{2,1,0:T(8,128)(2,1)}, u32[]{:S(2)}, u32[]{:S(2)}) collective-permute-start(bf16[8,128,512]{2,1,0:T(8,128)(2,1)} %get-tuple-element.112), channel_id=1, source_target_pairs={{0,8},{8,0},{16,24},{24,16},{1,9},{9,1},{17,25},{25,17},{2,10},{10... | collective-permute-start | bytes 3145736 | tf_op jit(solution)/shard_map/ppermute | solution.py:899
  344.5 27.0 %collective-permute-start.3 = (bf16[8,128,512]{2,1,0:T(8,128)(2,1)}, bf16[8,128,512]{2,1,0:T(8,128)(2,1)}, u32[]{:S(2)}, u32[]{:S(2)}) collective-permute-start(bf16[8,128,512]{2,1,0:T(8,128)(2,1)} %get-tuple-element.113.wait_ref.refs_8_.refs_2_), channel_id=1, source_target_pairs={{8,16},{16,8},{9,17},{17,9},{10,18},{18,10},{11,19},{19,11},{12,20... | collective-permute-start | bytes 3145736 | tf_op jit(solution)/shard_map/ppermute | solution.py:902
  346.2 25.3 %all-to-all-start.3 = ((bf16[8,128,512]{2,1,0:T(8,128)(2,1)}), bf16[8,128,512]{2,1,0:T(8,128)(2,1)S(1)}, u32[]{:S(2)}, u32[]{:S(2)}) async-start(bf16[8,128,512]{2,1,0:T(8,128)(2,1)} %after.6), calls=%async_computation.3 | async-start | bytes 2097152 | tf_op jit(solution)/shard_map/all_to_all | solution.py:896
  378.7 33.3 %collective-permute-start.5 = (bf16[8,128,512]{2,1,0:T(8,128)(2,1)}, bf16[8,128,512]{2,1,0:T(8,128)(2,1)}, u32[]{:S(2)}, u32[]{:S(2)}) collective-permute-start(bf16[8,128,512]{2,1,0:T(8,128)(2,1)} %copy-done.12), channel_id=1, source_target_pairs={{8,16},{16,8},{9,17},{17,9},{10,18},{18,10},{11,19},{19,11},{12,20... | collective-permute-start | bytes 3145736 | tf_op jit(solution)/shard_map/ppermute | solution.py:902
  380.5 18.4 %all-to-all-start.4 = ((bf16[8,128,512]{2,1,0:T(8,128)(2,1)}), bf16[8,128,512]{2,1,0:T(8,128)(2,1)S(1)}, u32[]{:S(2)}, u32[]{:S(2)}) async-start(bf16[8,128,512]{2,1,0:T(8,128)(2,1)} %after.7), calls=%async_computation.4 | async-start | bytes 2097152 | tf_op jit(solution)/shard_map/all_to_all | solution.py:896
  384.7 27.4 %collective-permute-start.4 = (bf16[8,128,512]{2,1,0:T(8,128)(2,1)}, bf16[8,128,512]{2,1,0:T(8,128)(2,1)}, u32[]{:S(2)}, u32[]{:S(2)}) collective-permute-start(bf16[8,128,512]{2,1,0:T(8,128)(2,1)} %copy-done.39), channel_id=1, source_target_pairs={{0,8},{8,0},{16,24},{24,16},{1,9},{9,1},{17,25},{25,17},{2,10},{10... | collective-permute-start | bytes 3145736 | tf_op jit(solution)/shard_map/ppermute | solution.py:899
  421.1 45.0 %collective-permute-start.7 = (bf16[8,128,512]{2,1,0:T(8,128)(2,1)}, bf16[8,128,512]{2,1,0:T(8,128)(2,1)}, u32[]{:S(2)}, u32[]{:S(2)}) collective-permute-start(bf16[8,128,512]{2,1,0:T(8,128)(2,1)} %copy-done.10), channel_id=1, source_target_pairs={{8,16},{16,8},{9,17},{17,9},{10,18},{18,10},{11,19},{19,11},{12,20... | collective-permute-start | bytes 3145736 | tf_op jit(solution)/shard_map/ppermute | solution.py:902
  422.9 43.2 %all-to-all-start.5 = ((bf16[8,128,512]{2,1,0:T(8,128)(2,1)}), bf16[8,128,512]{2,1,0:T(8,128)(2,1)S(1)}, u32[]{:S(2)}, u32[]{:S(2)}) async-start(bf16[8,128,512]{2,1,0:T(8,128)(2,1)} %after.8), calls=%async_computation.6 | async-start | bytes 2097152 | tf_op jit(solution)/shard_map/all_to_all | solution.py:896
  427.1 109.5 %reduce-scatter.8.cloned.1.call-start = ((), (), s32[]{:S(2)}) async-start(), calls=%async_computation.16 | async-start | bytes 7372800 | tf_op jit(solution)/shard_map/reduce_scatter | solution.py:962
  427.1 39.0 %collective-permute-start.6 = (bf16[8,128,512]{2,1,0:T(8,128)(2,1)}, bf16[8,128,512]{2,1,0:T(8,128)(2,1)S(1)}, u32[]{:S(2)}, u32[]{:S(2)}) collective-permute-start(bf16[8,128,512]{2,1,0:T(8,128)(2,1)} %copy-done.38), channel_id=1, source_target_pairs={{0,8},{8,0},{16,24},{24,16},{1,9},{9,1},{17,25},{25,17},{2,10},{10... | collective-permute-start | bytes 3145736 | tf_op jit(solution)/shard_map/ppermute | solution.py:899
  475.2 31.5 %collective-permute-start.9 = (bf16[8,128,512]{2,1,0:T(8,128)(2,1)}, bf16[8,128,512]{2,1,0:T(8,128)(2,1)}, u32[]{:S(2)}, u32[]{:S(2)}) collective-permute-start(bf16[8,128,512]{2,1,0:T(8,128)(2,1)} %get-tuple-element.129.refs_4_.wait_ref.refs_2_), channel_id=1, source_target_pairs={{8,16},{16,8},{9,17},{17,9},{10,18},{18,10},{11,19},{19,11},{12,20... | collective-permute-start | bytes 3145736 | tf_op jit(solution)/shard_map/ppermute | solution.py:902
  476.9 21.8 %all-to-all-start.6 = ((bf16[8,128,512]{2,1,0:T(8,128)(2,1)}), bf16[8,128,512]{2,1,0:T(8,128)(2,1)}, u32[]{:S(2)}, u32[]{:S(2)}) async-start(bf16[8,128,512]{2,1,0:T(8,128)(2,1)} %after.9), calls=%async_computation.9 | async-start | bytes 2097152 | tf_op jit(solution)/shard_map/all_to_all | solution.py:896
  481.2 158.8 %reduce-scatter.6.cloned.1.call-start = ((), (), s32[]{:S(2)}) async-start(), calls=%async_computation.15 | async-start | bytes 9437184 | tf_op jit(solution)/shard_map/reduce_scatter | solution.py:966
  481.2 25.5 %collective-permute-start.8 = (bf16[8,128,512]{2,1,0:T(8,128)(2,1)}, bf16[8,128,512]{2,1,0:T(8,128)(2,1)}, u32[]{:S(2)}, u32[]{:S(2)}) collective-permute-start(bf16[8,128,512]{2,1,0:T(8,128)(2,1)} %get-tuple-element.132), channel_id=1, source_target_pairs={{0,8},{8,0},{16,24},{24,16},{1,9},{9,1},{17,25},{25,17},{2,10},{10... | collective-permute-start | bytes 3145736 | tf_op jit(solution)/shard_map/ppermute | solution.py:899
  512.0 24.6 %collective-permute-start.10 = (bf16[8,128,512]{2,1,0:T(8,128)(2,1)}, bf16[8,128,512]{2,1,0:T(8,128)(2,1)}, u32[]{:S(2)}, u32[]{:S(2)}) collective-permute-start(bf16[8,128,512]{2,1,0:T(8,128)(2,1)} %get-tuple-element.133), channel_id=1, source_target_pairs={{0,8},{8,0},{16,24},{24,16},{1,9},{9,1},{17,25},{25,17},{2,10},{10... | collective-permute-start | bytes 3145736 | tf_op jit(solution)/shard_map/ppermute | solution.py:899
  512.3 24.3 %collective-permute-start.11 = (bf16[8,128,512]{2,1,0:T(8,128)(2,1)}, bf16[8,128,512]{2,1,0:T(8,128)(2,1)}, u32[]{:S(2)}, u32[]{:S(2)}) collective-permute-start(bf16[8,128,512]{2,1,0:T(8,128)(2,1)} %get-tuple-element.134.rest_0_.refs_2_), channel_id=1, source_target_pairs={{8,16},{16,8},{9,17},{17,9},{10,18},{18,10},{11,19},{19,11},{12,20... | collective-permute-start | bytes 3145736 | tf_op jit(solution)/shard_map/ppermute | solution.py:902
  543.6 25.3 %collective-permute-start.12 = (bf16[8,128,512]{2,1,0:T(8,128)(2,1)}, bf16[8,128,512]{2,1,0:T(8,128)(2,1)}, u32[]{:S(2)}, u32[]{:S(2)}) collective-permute-start(bf16[8,128,512]{2,1,0:T(8,128)(2,1)} %get-tuple-element.139), channel_id=1, source_target_pairs={{0,8},{8,0},{16,24},{24,16},{1,9},{9,1},{17,25},{25,17},{2,10},{10... | collective-permute-start | bytes 3145736 | tf_op jit(solution)/shard_map/ppermute | solution.py:899
  547.6 21.3 %collective-permute-start.13 = (bf16[8,128,512]{2,1,0:T(8,128)(2,1)}, bf16[8,128,512]{2,1,0:T(8,128)(2,1)}, u32[]{:S(2)}, u32[]{:S(2)}) collective-permute-start(bf16[8,128,512]{2,1,0:T(8,128)(2,1)} %get-tuple-element.140.rest_3_.refs_2_), channel_id=1, source_target_pairs={{8,16},{16,8},{9,17},{17,9},{10,18},{18,10},{11,19},{19,11},{12,20... | collective-permute-start | bytes 3145736 | tf_op jit(solution)/shard_map/ppermute | solution.py:902
  574.7 14.2 %collective-permute-start.14 = (bf16[8,128,512]{2,1,0:T(8,128)(2,1)}, bf16[8,128,512]{2,1,0:T(8,128)(2,1)}, u32[]{:S(2)}, u32[]{:S(2)}) collective-permute-start(bf16[8,128,512]{2,1,0:T(8,128)(2,1)} %get-tuple-element.151.rest_3_.refs_0_), channel_id=1, source_target_pairs={{8,16},{16,8},{9,17},{17,9},{10,18},{18,10},{11,19},{19,11},{12,20... | collective-permute-start | bytes 3145736 | tf_op jit(solution)/shard_map/ppermute | solution.py:902
  576.3 25.9 %collective-permute-start.15 = (bf16[8,128,512]{2,1,0:T(8,128)(2,1)}, bf16[8,128,512]{2,1,0:T(8,128)(2,1)}, u32[]{:S(2)}, u32[]{:S(2)}) collective-permute-start(bf16[8,128,512]{2,1,0:T(8,128)(2,1)} %get-tuple-element.152), channel_id=1, source_target_pairs={{0,8},{8,0},{16,24},{24,16},{1,9},{9,1},{17,25},{25,17},{2,10},{10... | collective-permute-start | bytes 3145736 | tf_op jit(solution)/shard_map/ppermute | solution.py:899
  607.6 21.6 %collective-permute-start.16 = (bf16[8,128,512]{2,1,0:T(8,128)(2,1)}, bf16[8,128,512]{2,1,0:T(8,128)(2,1)}, u32[]{:S(2)}, u32[]{:S(2)}) collective-permute-start(bf16[8,128,512]{2,1,0:T(8,128)(2,1)} %get-tuple-element.159), channel_id=1, source_target_pairs={{0,8},{8,0},{16,24},{24,16},{1,9},{9,1},{17,25},{25,17},{2,10},{10... | collective-permute-start | bytes 3145736 | tf_op jit(solution)/shard_map/ppermute | solution.py:899
  (65 other events, 511.7 us)
Sparse Core Ops, SparseCore 0:
  13.5 73.9 all-gather.4
  89.9 58.8 all-gather.8
  151.2 36.7 all-gather.6
  190.3 36.7 all-gather.10
  261.3 92.5 reduce-scatter.3
  466.2 64.1 reduce-scatter.7
  534.2 71.2 reduce-scatter.5

commit v7 on v6

--- a/solution.py
+++ b/solution.py
@@ -320,10 +320,10 @@
 
 
 def back_kernel(
-    d_mixed_ref, qkv_ref, totals_ref, bias_ref, cos_ref, sin_ref, normed_ref, x_ref, d_middle_ref,
-    gains_ref, other_ref, pack_ref, wait_ref, also_ref, grads_ref, d_input_ref, d_linear_ref, d_keys_ref, d_values_ref,
+    d_mixed_ref, qkv_ref, totals_ref, bias_ref, cos_ref, sin_ref, wait_ref, d_linear_ref,
+    d_keys_ref, d_values_ref,
 ):
-    rows = x_ref.shape[0]
+    rows = d_mixed_ref.shape[0]
     cosine, sine = (cos_ref[...], -sin_ref[...])
 
     @pl.loop(0, KEYVALUE_HEADS // 2)
@@ -380,6 +380,27 @@
         ).astype(brain_floating)
         d_linear_ref[:, pl.ds(WIDTH + KV_WIDTH + at, LANES)] = pair_values.astype(brain_floating)
 
+
+def run_back(d_mixed, qkv, totals, bias, cosine, sine, wait):
+    rows = d_mixed.shape[0]
+    held = (d_mixed, qkv, totals, bias, cosine, sine)
+    return pl.pallas_call(
+        back_kernel,
+        grid=(1,),
+        in_specs=[whole(v.shape) for v in held] + [ANYWHERE],
+        out_specs=whole((rows, PROJECTED)),
+        out_shape=out((rows, PROJECTED), brain_floating),
+        scratch_shapes=[pltpu.VMEM((rows, LANES), jnp.float32)] * 2,
+        compiler_params=pltpu.CompilerParams(vmem_limit_bytes=52 * MIB),
+        cost_estimate=takes(30),
+        name="attention_back",
+    )(*held, wait)
+
+
+def projection_kernel(
+    d_linear_ref, normed_ref, x_ref, d_middle_ref, gains_ref, other_ref, pack_ref, wait_ref,
+    grads_ref, d_input_ref,
+):
     normed = normed_ref[...]
     for at in range(0, PROJECTED, 512):
         grads_ref[:, at : at + 512] = transposed_times(
@@ -396,31 +417,24 @@
     d_input_ref[...] = d_middle_ref[...] + norm_back(d_normed, scaled, inverse, gains_ref[0:1, :])
 
 
-def run_back(
-    d_mixed, qkv, totals, bias, cosine, sine, normed, x, d_middle, gains, other, pack, wait, also
-):
+def run_projection(d_linear, normed, x, d_middle, gains, other, pack, wait):
     rows = x.shape[0]
-    held = (d_mixed, qkv, totals, bias, cosine, sine, normed, x, d_middle, gains, other)
+    held = (d_linear, normed, x, d_middle, gains, other)
     width = PROJECTED + other.shape[1]
     return pl.pallas_call(
-        back_kernel,
+        projection_kernel,
         grid=(1,),
         in_specs=[whole(v.shape) for v in held]
-        + [part((MODEL_WIDTH, PROJECTED), (0, 0)), ANYWHERE, ANYWHERE],
+        + [part((MODEL_WIDTH, PROJECTED), (0, 0)), ANYWHERE],
         out_specs=[whole((MODEL_WIDTH, width)), whole((rows, MODEL_WIDTH))],
         out_shape=[
             out((MODEL_WIDTH, width), brain_floating),
             out((rows, MODEL_WIDTH), jnp.float32),
         ],
-        scratch_shapes=[
-            pltpu.VMEM((rows, PROJECTED), brain_floating),
-            pltpu.VMEM((rows, LANES), jnp.float32),
-            pltpu.VMEM((rows, LANES), jnp.float32),
-        ],
         compiler_params=pltpu.CompilerParams(vmem_limit_bytes=52 * MIB),
         cost_estimate=takes(30),
-        name="attention_back",
-    )(*held, pack, wait, also)
+        name="projection_back",
+    )(*held, pack, wait)
 
 
 def expert_kernel(me_ref, x_ref, b_ref, w_one_ref, w_two_ref, router_ref, *refs):
@@ -953,11 +967,11 @@
             d_middle, d_mixed, second_grads = run_middle(
                 dx_own, normed_two, middle, cotangent, mask, alive, gains_value, pack, mixed, token
             )
-            done = d_mixed
+            d_linear = run_back(d_mixed, qkv, totals, bias, cosine, sine, token)
+            done = d_linear
         elif k == 3:
-            rest_grads, input_gradient = run_back(
-                d_mixed, qkv, totals, bias, cosine, sine, normed, tokens_in, d_middle, gains_value,
-                second_grads, pack, token, token,
+            rest_grads, input_gradient = run_projection(
+                d_linear, normed, tokens_in, d_middle, gains_value, second_grads, pack, token
             )
             mine[last] = lax.psum_scatter(rest_grads, fsdp, scatter_dimension=0, tiled=True)
             done = input_gradient
@@ -974,6 +988,11 @@
             done = adam_of(1, adam_of(0, token, 300), 1)
         elif k == 6:
             done = adam_of(3, adam_of(2, token, 300), 1)
+        elif k == last + 2:
+            block_output = (middle + alive * mixture_own.astype(jnp.float32)).astype(
+                brain_floating
+            )
+            done = adam_of(k - 3, block_output, 300)
         elif k - 3 < len(chunks):
             done = adam_of(k - 3, token, 300)
         waits.append(done)
@@ -989,8 +1008,6 @@
         if pair:
             totals_of[k - 1] = results.pop(0)
         edges[k + 1] = results.pop(0)
-
-    block_output = (middle + alive * mixture_own.astype(jnp.float32)).astype(brain_floating)
 
     rest_states = (
         (norm_gains, gains_first, gains_second),

time: 662 us -> 655 us (0.989)
  Pallas kernels: 302 us -> 293 us
    pallas_call x0 -> x1, Pallas kernels: none -> 13.9 us  [run_projection(): pl.pallas_call(projection_kernel, grid=(1,), in_specs=[whole(v.shape) for...]
    pallas_call x1, Pallas kernels: 33.7 us -> 22.2 us  [run_back(): pl.pallas_call(back_kernel, grid=(1,), in_specs=[whole(v.shape) for v in...]
    pallas_call x4, Pallas kernels: 73.3 us -> 63.1 us  [run_grads(): pl.pallas_call(functools.partial(grads_kernel, steps, sides), grid_spec=p...]
    all_to_all x6, waiting for transfers between devices: 11.8 us -> 19.9 us  [to_owner(): return lax.all_to_all(parts, 'inner', 0, 0)]
    unnamed x138 -> x124, local copies, waits for them, and re-layouts: 35 us -> 31.6 us
  transfers between devices with their start and end apart: 31 -> 31, of which waited for: 14 -> 12; matrix products, arithmetic and copies ran while one was open for 2% -> 2% of each run, Pallas kernels for 41% -> 39%
where the time goes in v7:
time: 655 us; the launch traced here: 645 us
  Pallas kernels  293 us (45%)
  waiting for transfers between devices  215 us (33%)
  starting transfers between devices  70.8 us (11%)
  local copies, waits for them, and re-layouts  38.7 us (6%)
  between operations  14.9 us (2%)
  other arithmetic  12.7 us (2%)
    ppermute x1, waiting for transfers between devices, body(): lax.ppermute(weights_own, 'replica', [(0, 1), (1, 0), (2, 3), (3, 2)])  68.5 us
    pallas_call x2, Pallas kernels, run_experts(): pl.pallas_call(expert_kernel, grid_spec=pltpu.PrefetchScalarGridSpec(num_...  68.1 us
    pallas_call x4, Pallas kernels, run_grads(): pl.pallas_call(functools.partial(grads_kernel, steps, sides), grid_spec=p...  63.1 us
    all_gather x1, waiting for transfers between devices, body(): pack = lax.all_gather(pack_own, fsdp, axis=0, tiled=True)  58.9 us
    ppermute x9, waiting for transfers between devices, swapped(): return lax.ppermute(values, 'replica', [(0, 1), (1, 0), (2, 3), (3, 2)])  56.2 us
    pallas_call x6, Pallas kernels, adam_part(): pl.pallas_call(functools.partial(adam_kernel, turned, rate, decay_rate),...  43 us
    unnamed x124, local copies, waits for them, and re-layouts  31.6 us
    pallas_call x9, Pallas kernels, run_round(): pl.pallas_call(functools.partial(round_kernel, (bool(own), bool(pair), fo...  29.5 us
  transfers between devices with their start and end apart: 31, of which 12 were waited for; matrix products, arithmetic and copies ran while one was open for 2% of the time, Pallas kernels for 39%

profile of v7, /device:TPU:2, one launch (start us, length us, event | category | flops | bytes accessed | tf_op | source)
XLA Modules:
  0.0 645.4 jit_solution(7282789339672656355)
XLA Ops:
  16.2 5.0 split.1
  28.6 58.9 %all-gather.5.cloned.1.call-done.pack_ref.router_ref.output_ref = bf16[1024,3200]{1,0:T(8,128)(2,1)} async-done(((bf16[128,3200]{1,0:T(8,128)(2,1)}), bf16[1024,3200]{1,0:T(8,128)(2,1)}) %all-gather.5.cloned.1.call-update) | async-done | bytes 6553616 | tf_op jit(solution)/shard_map/all_gather | solution.py:848
  88.7 19.1 %front.1 = (bf16[512,1024]{1,0:T(8,128)(2,1)}, bf16[512,2048]{1,0:T(8,128)(2,1)}, bf16[512,1024]{1,0:T(8,128)(2,1)}, f32[512,128]{1,0:T(8,128)S(1)}, f32[512,1024]{1,0:T(8,128)}, /*index=5*/bf16[512,1024]{1,0:T(8,128)(2,1)}) custom-call(bf16[512,1024]{1,0:T(8,128)(2,1)} %x_ref.3, ...), custom_call_target="tpu_custom_call" | custom-call | tf_op jit(solution)/shard_map/front/pallas_call | solution.py:249
  113.1 68.5 %collective-permute-done.w_two_ref.refs_3_ = bf16[8,3,128,512]{3,2,1,0:T(8,128)(2,1)} collective-permute-done((bf16[8,3,128,512]{3,2,1,0:T(8,128)(2,1)}, bf16[8,3,128,512]{3,2,1,0:T(8,128)(2,1)}, u32[]{:S(2)}, u32[]{:S(2)}) %collective-permute-start) | collective-permute-done | bytes 3145760 | tf_op jit(solution)/shard_map/ppermute | solution.py:857
  181.6 6.3 all-gather.7.cloned.1.call-done.x_ref.refs_0_.refs_4_
  188.0 34.1 %experts.2 = (bf16[2048,1024]{1,0:T(8,128)(2,1)}, bf16[2048,2048]{1,0:T(8,128)(2,1)}, bf16[8,2,256,1152]{3,2,1,0:T(8,128)(2,1)}) custom-call(s32[2]{0:T(128)} %pad_add_fusion.me_ref, bf16[2048,1024]{1,0:T(8,128)(2,1)} %all-gather.7.cloned.1.call-done.x_ref.refs_0_.refs_4_, bf16[8,2,256,1152]{3,2,1,0:T(8,128)(2,1)} %bitcast.16, ...), custom_call_target="tpu_custom_call" | custom-call | tf_op jit(solution)/shard_map/experts/pallas_call | solution.py:491
  222.0 5.0 all-gather.11.cloned.1.call-done.x_ref.refs_2_.refs_6_
  227.0 34.1 %experts.3 = (bf16[2048,1024]{1,0:T(8,128)(2,1)}, bf16[2048,2048]{1,0:T(8,128)(2,1)}, bf16[8,2,256,1152]{3,2,1,0:T(8,128)(2,1)}) custom-call(s32[2]{0:T(128)} %pad_add_fusion.me_ref, bf16[2048,1024]{1,0:T(8,128)(2,1)} %all-gather.11.cloned.1.call-done.x_ref.refs_2_.refs_6_, bf16[8,2,256,1152]{3,2,1,0:T(8,128)(2,1)} %bitcast.17, ...), custom_call_target="tpu_custom_call", output_to_operand_aliasing={{2}: (6, {})} | custom-call | tf_op jit(solution)/shard_map/experts/pallas_call | solution.py:491
  261.8 13.3 %grads.4.refs_8_ = bf16[8,128,512]{2,1,0:T(8,128)(2,1)} custom-call(s32[2]{0:T(128)S(1)} %copy-done.30, bf16[8,2,256,1152]{3,2,1,0:T(8,128)(2,1)} %bitcast.18, bf16[2048,1024]{1,0:T(8,128)(2,1)} %get-tuple-element.106.refs_1_.refs_0_, bf16[8,2,256,1152]{3,2,1,0:T(8,128)(2,1)} %bitcast.19, bf16[2048,1024]{1,0:T(8,128)(2,1)} %get-tuple-element.108.refs_3_.refs_1_, ...), custom_call_target="tpu_custom_call" | custom-call | flops 1000000000 | bytes 3600000 | tf_op jit(solution)/shard_map/grads/pallas_call | solution.py:578
  278.9 19.5 %grads.5 = (bf16[8,128,512]{2,1,0:T(8,128)(2,1)S(1)}, bf16[8,128,512]{2,1,0:T(8,128)(2,1)}) custom-call(s32[2]{0:T(128)S(1)} %copy-done.30, bf16[2048,1024]{1,0:T(8,128)(2,1)} %all-gather.7.cloned.1.call-done.x_ref.refs_0_.refs_4_, bf16[2048,2048]{1,0:T(8,128)(2,1)} %get-tuple-element.110.refs_1_.refs_5_, ...), custom_call_target="tpu_custom_call" | custom-call | flops 1000000000 | bytes 3600000 | tf_op jit(solution)/shard_map/grads/pallas_call | solution.py:578
  304.4 11.0 %grads.6.refs_3_.values_ref = bf16[8,128,512]{2,1,0:T(8,128)(2,1)S(1)} custom-call(s32[2]{0:T(128)S(1)} %copy-done.30, bf16[8,2,256,1152]{3,2,1,0:T(8,128)(2,1)} %bitcast.20, bf16[2048,1024]{1,0:T(8,128)(2,1)} %get-tuple-element.106.refs_1_.refs_0_, bf16[8,2,256,1152]{3,2,1,0:T(8,128)(2,1)} %bitcast.21, ...), custom_call_target="tpu_custom_call" | custom-call | flops 3000000000 | bytes 10800000 | tf_op jit(solution)/shard_map/grads/pallas_call | solution.py:578
  315.4 12.8 %all-to-all-done.2.refs_2_.refs_0_ = bf16[8,128,512]{2,1,0:T(8,128)(2,1)S(1)} async-done(((bf16[8,128,512]{2,1,0:T(8,128)(2,1)}), bf16[8,128,512]{2,1,0:T(8,128)(2,1)S(1)}, u32[]{:S(2)}, u32[]{:S(2)}) %all-to-all-start.2) | async-done | bytes 1048608 | tf_op jit(solution)/shard_map/all_to_all | solution.py:910
  336.4 6.1 all-to-all-start.3
  343.4 19.4 %grads.7 = (bf16[8,128,512]{2,1,0:T(8,128)(2,1)S(1)}, bf16[8,128,512]{2,1,0:T(8,128)(2,1)}) custom-call(s32[2]{0:T(128)S(1)} %copy-done.30, bf16[2048,1024]{1,0:T(8,128)(2,1)} %all-gather.7.cloned.1.call-done.x_ref.refs_0_.refs_4_, bf16[2048,2048]{1,0:T(8,128)(2,1)} %get-tuple-element.110.refs_1_.refs_5_, ...), custom_call_target="tpu_custom_call" | custom-call | flops 3000000000 | bytes 10800000 | tf_op jit(solution)/shard_map/grads/pallas_call | solution.py:578
  371.8 4.6 all-to-all-start.4
  380.2 9.6 %middle_back.1 = (f32[512,1024]{1,0:T(8,128)}, bf16[512,1024]{1,0:T(8,128)(2,1)S(1)}, bf16[1024,1152]{1,0:T(8,128)(2,1)}) custom-call(bf16[512,1152]{1,0:T(8,128)(2,1)} %reduce-scatter.4.cloned.1.call-done.dx_ref, bf16[512,1024]{1,0:T(8,128)(2,1)} %get-tuple-element.105.normed_two_ref, f32[512,1024]{1,0:T(8,128)} %get-tuple-element.104.middle_ref, ...), custom_call_target="tpu_custom_call" | custom-call | flops 30000001024 | bytes 108000000 | tf_op jit(solution)/shard_map/middle_back/pallas_call | solution.py:296
  389.9 22.2 %attention_back.1.refs_5_.d_linear_ref = bf16[512,2048]{1,0:T(8,128)(2,1)} custom-call(bf16[512,1024]{1,0:T(8,128)(2,1)S(1)} %get-tuple-element.120.d_mixed_ref, bf16[512,2048]{1,0:T(8,128)(2,1)} %get-tuple-element.121.qkv_ref, f32[512,128]{1,0:T(8,128)S(1)} %copy-done.40, f32[512,512]{1,0:T(8,128)} %fusion.1.bias_ref, ...), custom_call_target="tpu_custom_call" | custom-call | flops 30000001024 | bytes 108000000 | tf_op jit(solution)/shard_map/attention_back/pallas_call | solution.py:387
  430.6 13.9 %projection_back.1 = (bf16[1024,3200]{1,0:T(8,128)(2,1)}, f32[512,1024]{1,0:T(8,128)}) custom-call(bf16[512,2048]{1,0:T(8,128)(2,1)} %attention_back.1.refs_5_.d_linear_ref, bf16[512,1024]{1,0:T(8,128)(2,1)S(1)} %copy-done.34, bf16[512,1024]{1,0:T(8,128)(2,1)} %x_ref.3, f32[512,1024]{1,0:T(8,128)} %get-tuple-element.126.d_middle_ref, ...), custom_call_target="tpu_custom_call" | custom-call | flops 30000001024 | bytes 108000000 | tf_op jit(solution)/shard_map/projection_back/pallas_call | solution.py:424
  444.5 8.6 %collective-permute-done.6.refs_1_.r_ref = bf16[8,128,512]{2,1,0:T(8,128)(2,1)S(1)} collective-permute-done((bf16[8,128,512]{2,1,0:T(8,128)(2,1)}, bf16[8,128,512]{2,1,0:T(8,128)(2,1)S(1)}, u32[]{:S(2)}, u32[]{:S(2)}) %collective-permute-start.6) | collective-permute-done | bytes 1048608 | tf_op jit(solution)/shard_map/ppermute | solution.py:913
  469.8 14.6 %mixture.1.refs_5_ = bf16[8,2,256,1024]{3,2,1,0:T(8,128)(2,1)} custom-call(bf16[2048,1024]{1,0:T(8,128)(2,1)} %get-tuple-element.106.refs_1_.refs_0_, bf16[2048,1024]{1,0:T(8,128)(2,1)} %get-tuple-element.108.refs_3_.refs_1_, bf16[8,3,128,512]{3,2,1,0:T(8,128)(2,1)} %all-to-all-done.wait_ref.w_one_ref.refs_2_, ...), custom_call_target="tpu_custom_call" | custom-call | flops 299999985664 | bytes 1080000000 | tf_op jit(solution)/shard_map/mixture/pallas_call | solution.py:614
  484.4 7.1 %all-to-all-done.6.refs_4_.refs_0_ = bf16[8,128,512]{2,1,0:T(8,128)(2,1)} async-done(((bf16[8,128,512]{2,1,0:T(8,128)(2,1)}), bf16[8,128,512]{2,1,0:T(8,128)(2,1)}, u32[]{:S(2)}, u32[]{:S(2)}) %all-to-all-start.6) | async-done | bytes 1048608 | tf_op jit(solution)/shard_map/all_to_all | solution.py:910
  502.1 7.0 %adam.6 = (f32[16,512,128]{2,1,0:T(8,128)}, f32[16,512,128]{2,1,0:T(8,128)}, f32[16,512,128]{2,1,0:T(8,128)}, f32[8,128]{1,0:T(8,128)}) custom-call(s32[1]{0:T(128)} %bitcast.8.place_ref, bf16[8,128,512]{2,1,0:T(8,128)(2,1)} %copy-done.46, bf16[8,128,512]{2,1,0:T(8,128)(2,1)} %collective-permute-done.4.refs_1_.r_ref, f32[16,512,128]{2,1,0:T(8,128)} %w_ref.9, ...), custom_call_target="tpu_custom_call" | custom-call | flops 299999985664 | bytes 1080000000 | tf_op jit(solution)/shard_map/adam/pallas_call | solution.py:746
  509.1 7.2 %adam.7 = (f32[16,2,128,512]{3,2,1,0:T(8,128)}, f32[16,2,128,512]{3,2,1,0:T(8,128)}, f32[16,2,128,512]{3,2,1,0:T(8,128)}, f32[8,128]{1,0:T(8,128)}) custom-call(s32[1]{0:T(128)} %bitcast.8.place_ref, bf16[8,128,512]{2,1,0:T(8,128)(2,1)} %copy-done.7, bf16[8,128,512]{2,1,0:T(8,128)(2,1)} %copy-done.8, f32[16,2,128,512]{3,2,1,0:T(8,128)} %w_ref.11, ...), custom_call_target="tpu_custom_call" | custom-call | flops 1000000000 | bytes 3600000 | tf_op jit(solution)/shard_map/adam/pallas_call | solution.py:746
  516.3 7.4 %collective-permute-done.10.refs_1_.r_ref = bf16[8,128,512]{2,1,0:T(8,128)(2,1)} collective-permute-done((bf16[8,128,512]{2,1,0:T(8,128)(2,1)}, bf16[8,128,512]{2,1,0:T(8,128)(2,1)}, u32[]{:S(2)}, u32[]{:S(2)}) %collective-permute-start.10) | collective-permute-done | bytes 1048608 | tf_op jit(solution)/shard_map/ppermute | solution.py:913
  536.9 7.3 %adam.8 = (f32[16,2,128,512]{3,2,1,0:T(8,128)}, f32[16,2,128,512]{3,2,1,0:T(8,128)}, f32[16,2,128,512]{3,2,1,0:T(8,128)}, f32[8,128]{1,0:T(8,128)}) custom-call(s32[1]{0:T(128)} %bitcast.8.place_ref, bf16[8,128,512]{2,1,0:T(8,128)(2,1)} %copy-done.45, ...), custom_call_target="tpu_custom_call", output_to_operand_aliasing={{0}: (6, {}), {1}: (7, {}), {2}: (8, {})} | custom-call | flops 299999985664 | bytes 1080000000 | tf_op jit(solution)/shard_map/adam/pallas_call | solution.py:746
  544.1 7.1 %adam.9 = (f32[16,512,128]{2,1,0:T(8,128)}, f32[16,512,128]{2,1,0:T(8,128)}, f32[16,512,128]{2,1,0:T(8,128)}, f32[8,128]{1,0:T(8,128)}) custom-call(s32[1]{0:T(128)} %bitcast.8.place_ref, bf16[8,128,512]{2,1,0:T(8,128)(2,1)} %copy-done.9, ...), custom_call_target="tpu_custom_call", output_to_operand_aliasing={{0}: (6, {}), {1}: (7, {}), {2}: (8, {})} | custom-call | flops 1000000000 | bytes 3600000 | tf_op jit(solution)/shard_map/adam/pallas_call | solution.py:746
  551.2 6.1 collective-permute-done.12.refs_1_.r_ref
  568.5 7.3 %adam.10 = (f32[16,2,128,512]{3,2,1,0:T(8,128)}, f32[16,2,128,512]{3,2,1,0:T(8,128)}, f32[16,2,128,512]{3,2,1,0:T(8,128)}, f32[8,128]{1,0:T(8,128)}) custom-call(s32[1]{0:T(128)} %bitcast.8.place_ref, bf16[8,128,512]{2,1,0:T(8,128)(2,1)} %copy-done.47, ...), custom_call_target="tpu_custom_call", output_to_operand_aliasing={{0}: (6, {}), {1}: (7, {}), {2}: (8, {})} | custom-call | flops 299999985664 | bytes 1080000000 | tf_op jit(solution)/shard_map/adam/pallas_call | solution.py:746
  575.9 12.0 %collective-permute-done.15.refs_2_.r_ref = bf16[8,128,512]{2,1,0:T(8,128)(2,1)} collective-permute-done((bf16[8,128,512]{2,1,0:T(8,128)(2,1)}, bf16[8,128,512]{2,1,0:T(8,128)(2,1)}, u32[]{:S(2)}, u32[]{:S(2)}) %collective-permute-start.15) | collective-permute-done | bytes 1048608 | tf_op jit(solution)/shard_map/ppermute | solution.py:913
  596.2 20.0 %collective-permute-done.16.r_ref = bf16[8,128,512]{2,1,0:T(8,128)(2,1)} collective-permute-done((bf16[8,128,512]{2,1,0:T(8,128)(2,1)}, bf16[8,128,512]{2,1,0:T(8,128)(2,1)}, u32[]{:S(2)}, u32[]{:S(2)}) %collective-permute-start.16) | collective-permute-done | bytes 1048608 | tf_op jit(solution)/shard_map/ppermute | solution.py:913
  621.5 4.5 adam_rest.1
  631.2 7.2 %adam.11 = (f32[16,2,128,512]{3,2,1,0:T(8,128)}, f32[16,2,128,512]{3,2,1,0:T(8,128)}, f32[16,2,128,512]{3,2,1,0:T(8,128)}, f32[8,128]{1,0:T(8,128)}) custom-call(s32[1]{0:T(128)} %bitcast.8.place_ref, bf16[8,128,512]{2,1,0:T(8,128)(2,1)} %copy-done.48, ...), custom_call_target="tpu_custom_call", output_to_operand_aliasing={{0}: (6, {}), {1}: (7, {}), {2}: (8, {})} | custom-call | flops 299999985664 | bytes 1080000000 | tf_op jit(solution)/shard_map/adam/pallas_call | solution.py:746
  (225 shorter events, 143.8 us)
Async XLA Ops:
  7.2 80.2 %all-gather.5.cloned.1.call-start = ((), (), s32[]{:S(2)}) async-start(), calls=%async_computation.10 | async-start | bytes 7372800 | tf_op jit(solution)/shard_map/all_gather | solution.py:848
  13.4 168.3 %all-gather.9.cloned.1.call-start = ((), (), s32[]{:S(2)}) async-start(), calls=%async_computation.12 | async-start | bytes 10616832 | tf_op jit(solution)/shard_map/all_gather | solution.py:883
  21.2 67.5 %all-to-all-start = ((bf16[8,3,128,512]{3,2,1,0:T(8,128)(2,1)}), bf16[8,3,128,512]{3,2,1,0:T(8,128)(2,1)}, u32[]{:S(2)}, u32[]{:S(2)}) async-start(bf16[8,3,128,512]{3,2,1,0:T(8,128)(2,1)} %split.1), calls=%async_computation | async-start | bytes 6291456 | tf_op jit(solution)/shard_map/all_to_all | solution.py:852
  25.6 162.3 %all-gather.7.cloned.1.call-start = ((), (), s32[]{:S(2)}) async-start(), calls=%async_computation.11 | async-start | bytes 4718592 | tf_op jit(solution)/shard_map/all_gather | solution.py:879
  107.8 114.2 %copy-start.39 = (f32[512,128]{1,0:T(8,128)}, f32[512,128]{1,0:T(8,128)S(1)}, u32[]{:S(2)}) copy-start(f32[512,128]{1,0:T(8,128)S(1)} %get-tuple-element.122.totals_ref) | copy-start | bytes 786436
  110.2 116.9 %all-gather.11.cloned.1.call-start = ((), (), s32[]{:S(2)}) async-start(), calls=%async_computation.13 | async-start | bytes 4718592 | tf_op jit(solution)/shard_map/all_gather | solution.py:879
  110.8 269.4 %reduce-scatter.4.cloned.1.call-start = ((), (), s32[]{:S(2)}) async-start(), calls=%async_computation.14 | async-start | bytes 10616832 | tf_op jit(solution)/shard_map/reduce_scatter | solution.py:900
  111.0 70.7 %collective-permute-start = (bf16[8,3,128,512]{3,2,1,0:T(8,128)(2,1)}, bf16[8,3,128,512]{3,2,1,0:T(8,128)(2,1)}, u32[]{:S(2)}, u32[]{:S(2)}) collective-permute-start(bf16[8,3,128,512]{3,2,1,0:T(8,128)(2,1)} %all-to-all-done.wait_ref.w_one_ref.refs_2_), channel_id=1, source_target_pairs={{0,8},{8,0},{16,24},{24,16},{1,9},{9,1},{17,25},{25,17},{2,10},{10... | collective-permute-start | bytes 9437192 | tf_op jit(solution)/shard_map/ppermute | solution.py:857
  275.0 23.3 %all-to-all-start.1 = ((bf16[8,128,512]{2,1,0:T(8,128)(2,1)}), bf16[8,128,512]{2,1,0:T(8,128)(2,1)S(1)}, u32[]{:S(2)}, u32[]{:S(2)}) async-start(bf16[8,128,512]{2,1,0:T(8,128)(2,1)} %grads.4.refs_8_), calls=%async_computation.1 | async-start | bytes 2097152 | tf_op jit(solution)/shard_map/all_to_all | solution.py:910
  298.5 29.8 %collective-permute-start.1 = (bf16[8,128,512]{2,1,0:T(8,128)(2,1)S(1)}, bf16[8,128,512]{2,1,0:T(8,128)(2,1)}, u32[]{:S(2)}, u32[]{:S(2)}) collective-permute-start(bf16[8,128,512]{2,1,0:T(8,128)(2,1)S(1)} %round.9.refs_4_.wait_ref), channel_id=1, source_target_pairs={{0,8},{8,0},{16,24},{24,16},{1,9},{9,1},{17,25},{25,17},{2,10},{10... | collective-permute-start | bytes 3145736 | tf_op jit(solution)/shard_map/ppermute | solution.py:913
  300.2 28.1 %all-to-all-start.2 = ((bf16[8,128,512]{2,1,0:T(8,128)(2,1)}), bf16[8,128,512]{2,1,0:T(8,128)(2,1)S(1)}, u32[]{:S(2)}, u32[]{:S(2)}) async-start(bf16[8,128,512]{2,1,0:T(8,128)(2,1)} %after.5), calls=%async_computation.2 | async-start | bytes 2097152 | tf_op jit(solution)/shard_map/all_to_all | solution.py:910
  333.1 29.8 %collective-permute-start.2 = (bf16[8,128,512]{2,1,0:T(8,128)(2,1)}, bf16[8,128,512]{2,1,0:T(8,128)(2,1)}, u32[]{:S(2)}, u32[]{:S(2)}) collective-permute-start(bf16[8,128,512]{2,1,0:T(8,128)(2,1)} %get-tuple-element.112), channel_id=1, source_target_pairs={{0,8},{8,0},{16,24},{24,16},{1,9},{9,1},{17,25},{25,17},{2,10},{10... | collective-permute-start | bytes 3145736 | tf_op jit(solution)/shard_map/ppermute | solution.py:913
  334.7 28.1 %collective-permute-start.3 = (bf16[8,128,512]{2,1,0:T(8,128)(2,1)}, bf16[8,128,512]{2,1,0:T(8,128)(2,1)}, u32[]{:S(2)}, u32[]{:S(2)}) collective-permute-start(bf16[8,128,512]{2,1,0:T(8,128)(2,1)} %get-tuple-element.113.wait_ref.refs_8_.refs_2_), channel_id=1, source_target_pairs={{8,16},{16,8},{9,17},{17,9},{10,18},{18,10},{11,19},{19,11},{12,20... | collective-permute-start | bytes 3145736 | tf_op jit(solution)/shard_map/ppermute | solution.py:916
  336.4 26.4 %all-to-all-start.3 = ((bf16[8,128,512]{2,1,0:T(8,128)(2,1)}), bf16[8,128,512]{2,1,0:T(8,128)(2,1)S(1)}, u32[]{:S(2)}, u32[]{:S(2)}) async-start(bf16[8,128,512]{2,1,0:T(8,128)(2,1)} %after.6), calls=%async_computation.3 | async-start | bytes 2097152 | tf_op jit(solution)/shard_map/all_to_all | solution.py:910
  370.1 42.0 %collective-permute-start.5 = (bf16[8,128,512]{2,1,0:T(8,128)(2,1)}, bf16[8,128,512]{2,1,0:T(8,128)(2,1)}, u32[]{:S(2)}, u32[]{:S(2)}) collective-permute-start(bf16[8,128,512]{2,1,0:T(8,128)(2,1)} %copy-done.12), channel_id=1, source_target_pairs={{8,16},{16,8},{9,17},{17,9},{10,18},{18,10},{11,19},{19,11},{12,20... | collective-permute-start | bytes 3145736 | tf_op jit(solution)/shard_map/ppermute | solution.py:916
  371.8 40.2 %all-to-all-start.4 = ((bf16[8,128,512]{2,1,0:T(8,128)(2,1)}), bf16[8,128,512]{2,1,0:T(8,128)(2,1)S(1)}, u32[]{:S(2)}, u32[]{:S(2)}) async-start(bf16[8,128,512]{2,1,0:T(8,128)(2,1)} %after.7), calls=%async_computation.4 | async-start | bytes 2097152 | tf_op jit(solution)/shard_map/all_to_all | solution.py:910
  376.5 35.6 %collective-permute-start.4 = (bf16[8,128,512]{2,1,0:T(8,128)(2,1)}, bf16[8,128,512]{2,1,0:T(8,128)(2,1)}, u32[]{:S(2)}, u32[]{:S(2)}) collective-permute-start(bf16[8,128,512]{2,1,0:T(8,128)(2,1)} %copy-done.35), channel_id=1, source_target_pairs={{0,8},{8,0},{16,24},{24,16},{1,9},{9,1},{17,25},{25,17},{2,10},{10... | collective-permute-start | bytes 3145736 | tf_op jit(solution)/shard_map/ppermute | solution.py:913
  420.9 32.1 %collective-permute-start.7 = (bf16[8,128,512]{2,1,0:T(8,128)(2,1)}, bf16[8,128,512]{2,1,0:T(8,128)(2,1)}, u32[]{:S(2)}, u32[]{:S(2)}) collective-permute-start(bf16[8,128,512]{2,1,0:T(8,128)(2,1)} %copy-done.10), channel_id=1, source_target_pairs={{8,16},{16,8},{9,17},{17,9},{10,18},{18,10},{11,19},{19,11},{12,20... | collective-permute-start | bytes 3145736 | tf_op jit(solution)/shard_map/ppermute | solution.py:916
  422.6 21.9 %all-to-all-start.5 = ((bf16[8,128,512]{2,1,0:T(8,128)(2,1)}), bf16[8,128,512]{2,1,0:T(8,128)(2,1)S(1)}, u32[]{:S(2)}, u32[]{:S(2)}) async-start(bf16[8,128,512]{2,1,0:T(8,128)(2,1)} %after.8), calls=%async_computation.6 | async-start | bytes 2097152 | tf_op jit(solution)/shard_map/all_to_all | solution.py:910
  426.8 96.9 %reduce-scatter.8.cloned.1.call-start = ((), (), s32[]{:S(2)}) async-start(), calls=%async_computation.16 | async-start | bytes 7372800 | tf_op jit(solution)/shard_map/reduce_scatter | solution.py:976
  427.0 26.1 %collective-permute-start.6 = (bf16[8,128,512]{2,1,0:T(8,128)(2,1)}, bf16[8,128,512]{2,1,0:T(8,128)(2,1)S(1)}, u32[]{:S(2)}, u32[]{:S(2)}) collective-permute-start(bf16[8,128,512]{2,1,0:T(8,128)(2,1)} %copy-done.36), channel_id=1, source_target_pairs={{0,8},{8,0},{16,24},{24,16},{1,9},{9,1},{17,25},{25,17},{2,10},{10... | collective-permute-start | bytes 3145736 | tf_op jit(solution)/shard_map/ppermute | solution.py:913
  461.4 32.2 %collective-permute-start.9 = (bf16[8,128,512]{2,1,0:T(8,128)(2,1)}, bf16[8,128,512]{2,1,0:T(8,128)(2,1)}, u32[]{:S(2)}, u32[]{:S(2)}) collective-permute-start(bf16[8,128,512]{2,1,0:T(8,128)(2,1)} %get-tuple-element.129.refs_4_.wait_ref.refs_2_), channel_id=1, source_target_pairs={{8,16},{16,8},{9,17},{17,9},{10,18},{18,10},{11,19},{19,11},{12,20... | collective-permute-start | bytes 3145736 | tf_op jit(solution)/shard_map/ppermute | solution.py:916
  463.0 28.4 %all-to-all-start.6 = ((bf16[8,128,512]{2,1,0:T(8,128)(2,1)}), bf16[8,128,512]{2,1,0:T(8,128)(2,1)}, u32[]{:S(2)}, u32[]{:S(2)}) async-start(bf16[8,128,512]{2,1,0:T(8,128)(2,1)} %after.9), calls=%async_computation.9 | async-start | bytes 2097152 | tf_op jit(solution)/shard_map/all_to_all | solution.py:910
  467.5 160.5 %reduce-scatter.6.cloned.1.call-start = ((), (), s32[]{:S(2)}) async-start(), calls=%async_computation.15 | async-start | bytes 9437184 | tf_op jit(solution)/shard_map/reduce_scatter | solution.py:980
  467.5 26.0 %collective-permute-start.8 = (bf16[8,128,512]{2,1,0:T(8,128)(2,1)}, bf16[8,128,512]{2,1,0:T(8,128)(2,1)}, u32[]{:S(2)}, u32[]{:S(2)}) collective-permute-start(bf16[8,128,512]{2,1,0:T(8,128)(2,1)} %get-tuple-element.132), channel_id=1, source_target_pairs={{0,8},{8,0},{16,24},{24,16},{1,9},{9,1},{17,25},{25,17},{2,10},{10... | collective-permute-start | bytes 3145736 | tf_op jit(solution)/shard_map/ppermute | solution.py:913
  498.7 25.0 %collective-permute-start.10 = (bf16[8,128,512]{2,1,0:T(8,128)(2,1)}, bf16[8,128,512]{2,1,0:T(8,128)(2,1)}, u32[]{:S(2)}, u32[]{:S(2)}) collective-permute-start(bf16[8,128,512]{2,1,0:T(8,128)(2,1)} %get-tuple-element.133), channel_id=1, source_target_pairs={{0,8},{8,0},{16,24},{24,16},{1,9},{9,1},{17,25},{25,17},{2,10},{10... | collective-permute-start | bytes 3145736 | tf_op jit(solution)/shard_map/ppermute | solution.py:913
  500.4 23.3 %collective-permute-start.11 = (bf16[8,128,512]{2,1,0:T(8,128)(2,1)}, bf16[8,128,512]{2,1,0:T(8,128)(2,1)}, u32[]{:S(2)}, u32[]{:S(2)}) collective-permute-start(bf16[8,128,512]{2,1,0:T(8,128)(2,1)} %get-tuple-element.134.rest_0_.refs_2_), channel_id=1, source_target_pairs={{8,16},{16,8},{9,17},{17,9},{10,18},{18,10},{11,19},{19,11},{12,20... | collective-permute-start | bytes 3145736 | tf_op jit(solution)/shard_map/ppermute | solution.py:916
  530.8 26.6 %collective-permute-start.12 = (bf16[8,128,512]{2,1,0:T(8,128)(2,1)}, bf16[8,128,512]{2,1,0:T(8,128)(2,1)}, u32[]{:S(2)}, u32[]{:S(2)}) collective-permute-start(bf16[8,128,512]{2,1,0:T(8,128)(2,1)} %get-tuple-element.139), channel_id=1, source_target_pairs={{0,8},{8,0},{16,24},{24,16},{1,9},{9,1},{17,25},{25,17},{2,10},{10... | collective-permute-start | bytes 3145736 | tf_op jit(solution)/shard_map/ppermute | solution.py:913
  535.2 22.1 %collective-permute-start.13 = (bf16[8,128,512]{2,1,0:T(8,128)(2,1)}, bf16[8,128,512]{2,1,0:T(8,128)(2,1)}, u32[]{:S(2)}, u32[]{:S(2)}) collective-permute-start(bf16[8,128,512]{2,1,0:T(8,128)(2,1)} %get-tuple-element.140.rest_3_.refs_2_), channel_id=1, source_target_pairs={{8,16},{16,8},{9,17},{17,9},{10,18},{18,10},{11,19},{19,11},{12,20... | collective-permute-start | bytes 3145736 | tf_op jit(solution)/shard_map/ppermute | solution.py:916
  563.1 24.8 %collective-permute-start.15 = (bf16[8,128,512]{2,1,0:T(8,128)(2,1)}, bf16[8,128,512]{2,1,0:T(8,128)(2,1)}, u32[]{:S(2)}, u32[]{:S(2)}) collective-permute-start(bf16[8,128,512]{2,1,0:T(8,128)(2,1)} %get-tuple-element.152), channel_id=1, source_target_pairs={{0,8},{8,0},{16,24},{24,16},{1,9},{9,1},{17,25},{25,17},{2,10},{10... | collective-permute-start | bytes 3145736 | tf_op jit(solution)/shard_map/ppermute | solution.py:913
  566.7 21.2 %collective-permute-start.14 = (bf16[8,128,512]{2,1,0:T(8,128)(2,1)}, bf16[8,128,512]{2,1,0:T(8,128)(2,1)}, u32[]{:S(2)}, u32[]{:S(2)}) collective-permute-start(bf16[8,128,512]{2,1,0:T(8,128)(2,1)} %get-tuple-element.151.rest_3_.refs_0_), channel_id=1, source_target_pairs={{8,16},{16,8},{9,17},{17,9},{10,18},{18,10},{11,19},{19,11},{12,20... | collective-permute-start | bytes 3145736 | tf_op jit(solution)/shard_map/ppermute | solution.py:916
  592.3 23.9 %collective-permute-start.16 = (bf16[8,128,512]{2,1,0:T(8,128)(2,1)}, bf16[8,128,512]{2,1,0:T(8,128)(2,1)}, u32[]{:S(2)}, u32[]{:S(2)}) collective-permute-start(bf16[8,128,512]{2,1,0:T(8,128)(2,1)} %get-tuple-element.159), channel_id=1, source_target_pairs={{0,8},{8,0},{16,24},{24,16},{1,9},{9,1},{17,25},{25,17},{2,10},{10... | collective-permute-start | bytes 3145736 | tf_op jit(solution)/shard_map/ppermute | solution.py:913
  (58 other events, 697.1 us)
Sparse Core Ops, SparseCore 0:
  13.5 73.9 all-gather.4
  89.9 58.8 all-gather.8
  151.2 36.7 all-gather.6
  190.3 36.7 all-gather.10
  261.2 102.4 reduce-scatter.3
  444.6 72.5 reduce-scatter.7
  521.1 71.2 reduce-scatter.5
